TPU v7x, 32 devices: a whole 2x2x4 slice. The times are simulated.
32 devices in a mesh: group: 2 (over y), afd: 16 (over z, x, core).
Axes of the slice: x: 2, y: 2, z: 4, core: 2. Of those that a mesh axis runs over, the one named last changes fastest.
Arguments:
- queries: bfloat16 [2, 128, 7168], P(None, ('group', 'afd')), parts along dimension 1, may hold values from -27 to 27
- fresh: bfloat16 [2, 128, 448], P(None, ('group', 'afd')), parts along dimension 1, may hold values from -12 to 12
- kv_cache: bfloat16 [128, 128, 448], P(('group', 'afd')), parts along dimension 0, may hold values from -12 to 12
- cache_len: int32 [128], P(('group', 'afd')), parts along dimension 0, may hold values from 1 to 128, 4096 in all
- hidden_state: bfloat16 [2, 128, 7168], P(None, ('group', 'afd')), parts along dimension 1, may hold values from -40 to 40
- norm_gain: bfloat16 [7168], replicated, may hold values from 0.099609375 to 1.8984375
- expert_ids: int32 [2, 128, 3], P(None, ('group', 'afd')), parts along dimension 1, may hold values from 0 to 7, as said below
- route_weight: float32 [2, 128, 3], P(None, ('group', 'afd')), parts along dimension 1, may hold values from 0.3 to 1.5
- gate_up: bfloat16 [16, 2, 256, 7168], P('afd'), may hold values from -0.0625 to 0.0625
- down: bfloat16 [16, 256, 7168], P('afd'), may hold values from -0.25 to 0.25
Outputs:
- layer_out: bfloat16 [2, 128, 7168], P(None, ('group', 'afd')), parts along dimension 1
There are 2 independent parts, one for each index of `group`. A program takes and returns all parts, laid end to end along the dimension named above; an argument that names none is the same for every part. Nothing has to cross between parts.
Inputs may be any that keep to these rules, and one draw needn't show every extreme that they name: `expert_ids`: A row names 3 different experts. In each step the 4 rows of one device name every expert at most 2 times and at least 2 - 1 times, and the experts named 2 times are the same on all devices of that step.
All inputs are finite; a program needn't handle non-finite values. No bound on the sum of `cache_len` on one device may be relied on, other than what follows from the above.
Results may differ from a plain program's by a relative error of at most 0.0052.
Values may be sent and summed in bfloat16 or wider, within the bound.
No kernel may reach another device: no remote copies, remote signals or barrier semaphores. Data moves between devices by JAX's collectives and lax.ppermute only.
A program may use at most 128 MiB of HBM per device.

v0:
```python
import jax
import jax.numpy as jnp
from jax import lax
from jax.sharding import PartitionSpec as P

HEADS = 32
HEAD = 224
EXPERTS = 8
TOP = 3


def slot_table(ids, slots, expert_count):
    flat = ids.reshape(ids.shape[0], -1)
    named = flat[:, :, None] == jnp.arange(expert_count, dtype=jnp.int32)[None, None, :]
    rank = jnp.cumsum(named.astype(jnp.int32), axis=1) - 1
    table = named[..., None] & (rank[..., None] == jnp.arange(slots, dtype=jnp.int32))
    return table.reshape(ids.shape + (expert_count, slots)).astype(jnp.float32)


def attend_padded(query, cache, fresh_part, length, scale):
    fresh_scores = (
        jnp.einsum(
            "rhd,srd->rhs", query, fresh_part[:, :, :HEAD], preferred_element_type=jnp.float32
        )
        * scale
    )
    scores = (
        jnp.einsum("rhd,rld->rhl", query, cache[:, :, :HEAD], preferred_element_type=jnp.float32)
        * scale
    )
    valid = jnp.arange(cache.shape[1], dtype=jnp.int32)[None, :] < length[:, None]
    scores = jnp.where(valid[:, None, :], scores, -1e30)
    top = jnp.maximum(jnp.max(scores, axis=-1), jnp.max(fresh_scores, axis=-1))[..., None]
    cache_exp = jnp.exp(scores - top)
    fresh_exp = jnp.exp(fresh_scores - top)
    total = jnp.sum(cache_exp, axis=-1, keepdims=True) + jnp.sum(fresh_exp, axis=-1, keepdims=True)
    cache_weights = (cache_exp / total).astype(jnp.bfloat16)
    fresh_weights = (fresh_exp / total).astype(jnp.bfloat16)
    result = jnp.einsum(
        "rhl,rld->rhd", cache_weights, cache[:, :, HEAD:], preferred_element_type=jnp.float32
    )
    return result + jnp.einsum(
        "rhs,srd->rhd", fresh_weights, fresh_part[:, :, HEAD:], preferred_element_type=jnp.float32
    )


def per_device(
    queries,
    fresh,
    kv_cache,
    cache_len,
    hidden_state,
    norm_gain,
    expert_ids,
    route_weight,
    gate_up,
    down,
):
    steps = queries.shape[0]
    rows = queries.shape[1]
    width = queries.shape[2]
    owners = lax.axis_size("afd")
    shards = owners // EXPERTS
    slots = (rows * TOP + EXPERTS - 1) // EXPERTS
    scale = HEAD ** (-0.5)
    w_gate = gate_up[0, 0]
    w_upper = gate_up[0, 1]
    w_down = down[0]
    gain = norm_gain.astype(jnp.float32)
    outputs = []
    for step in range(steps):
        query = queries[step].reshape(rows, HEADS, HEAD)
        fresh_part = fresh[: step + 1]
        attended = attend_padded(query, kv_cache, fresh_part, cache_len, scale)
        resid = hidden_state[step].astype(jnp.float32) + attended.reshape(rows, width)
        meansq = jnp.mean(resid * resid, axis=-1, keepdims=True)
        normed = (resid * lax.rsqrt(meansq + 1e-06) * gain).astype(jnp.bfloat16)
        ids_now = expert_ids[step]
        table = slot_table(ids_now[None], slots, EXPERTS)[0]
        picks = table.sum(axis=1).astype(jnp.bfloat16)
        outgoing = jnp.einsum(
            "rec,rd->ecd", picks, normed, preferred_element_type=jnp.float32
        ).astype(jnp.bfloat16)
        outgoing = jnp.broadcast_to(outgoing[:, None], (EXPERTS, shards, slots, width)).reshape(
            owners, slots, width
        )
        received = lax.all_to_all(outgoing, "afd", split_axis=0, concat_axis=0, tiled=True)
        flat = received.reshape(-1, width)
        gate = jnp.einsum("nd,hd->nh", flat, w_gate, preferred_element_type=jnp.float32)
        upper = jnp.einsum("nd,hd->nh", flat, w_upper, preferred_element_type=jnp.float32)
        act = (jax.nn.silu(gate) * upper).astype(jnp.bfloat16)
        part = jnp.dot(act, w_down, preferred_element_type=jnp.float32).astype(jnp.bfloat16)
        partial_value = part.reshape(received.shape)
        returned = lax.all_to_all(partial_value, "afd", split_axis=0, concat_axis=0, tiled=True)
        summed = jnp.sum(
            returned.reshape(EXPERTS, shards, slots, width).astype(jnp.float32), axis=1
        )
        mixing = jnp.einsum(
            "rkec,rk->rec", table, route_weight[step], precision=lax.Precision.HIGHEST
        )
        combined = jnp.einsum("rec,ecd->rd", mixing, summed, precision=lax.Precision.HIGHEST)
        outputs.append((resid + combined).astype(jnp.bfloat16))
    return jnp.stack(outputs)


def solution(mesh):
    placed = (
        P(None, ("group", "afd"), None),
        P(None, ("group", "afd"), None),
        P(("group", "afd"), None, None),
        P(("group", "afd")),
        P(None, ("group", "afd"), None),
        P(),
        P(None, ("group", "afd"), None),
        P(None, ("group", "afd"), None),
        P("afd", None, None, None),
        P("afd", None, None),
    )
    return jax.shard_map(
        per_device,
        mesh=mesh,
        in_specs=placed,
        out_specs=P(None, ("group", "afd"), None),
        check_vma=False,
    )
```

profile of v0, /device:TPU:0, one launch (start us, length us, event | category | flops | bytes accessed | tf_op | source)
XLA Modules:
  0.0 85.8 jit_solution(4239695807119458624)
XLA Ops:
  0.0 0.9 %fusion.98 = (bf16[1,4,7168]{2,1,0:T(4,128)(2,1)S(1)}, bf16[1,4,7168]{2,1,0:T(4,128)(2,1)S(1)}) fusion(bf16[2,4,7168]{2,1,0:T(4,128)(2,1)} %param.10), kind=kLoop, calls=%fused_computation.130 | loop fusion | bytes 229376 | tf_op jit(solution)/shard_map/slice | solution.py:72
  1.1 0.7 iota_compare_fusion.6
  1.8 0.8 slice_bitcast_fusion
  2.8 1.2 %fusion.104 = (f32[4,32]{1,0:T(4,128)S(1)}, f32[4,32,128]{2,1,0:T(8,128)S(1)}) fusion(bf16[4,32,224]{2,1,0:T(8,128)(2,1)S(1)} %reshape_squeeze.6, bf16[4,128,448]{1,2,0:T(8,128)(2,1)} %param.12, pred[4,128]{1,0:T(4,128)(4,1)S(1)} %iota_compare_fusion.6), kind=kOutput, calls=%fused_computation.136 | convolution fusion | flops 7389056 | bytes 353280 | tf_op jit(solution)/shard_map/rhd,rld->rhl/dot_general | solution.py:28
  4.2 0.9 %slice_convert_fusion.1 = (f32[1,4,7168]{2,1,0:T(4,128)S(1)}, f32[1,4,7168]{2,1,0:T(4,128)S(1)}) fusion(bf16[2,4,7168]{2,1,0:T(4,128)(2,1)} %param.14), kind=kLoop, calls=%fused_computation.66 | loop fusion | flops 57344 | bytes 344064 | tf_op jit(solution)/shard_map/convert_element_type | solution.py:75
  5.2 1.3 %multiply_reduce_fusion.1 = (f32[4]{0:T(128)S(1)}, f32[4,32,224]{2,1,0:T(8,128)S(1)}) fusion(f32[4,32,224]{2,1,0:T(8,128)S(1)} %reshape.338, f32[4,224]{1,0:T(4,128)S(1)} %get-tuple-element.14, f32[4,32]{1,0:T(4,128)S(1)} %get-tuple-element.18, bf16[4,128,448]{1,2,0:T(8,128)(2,1)} %param.12, f32[4,32,128]{2,1,0:T(8,128)S(1)} %get-tuple-element.30, ...), kind=kOutput, calls=%fused_computation.47 | convolution fusion | flops 7532540 | bytes 529424 | tf_op jit(solution)/shard_map/rhl,rld->rhd/dot_general | solution.py:39
  6.7 0.8 fusion.101
  8.6 1.1 %convolution_convert_fusion.3 = bf16[8,2,7168]{2,0,1:T(8,128)(2,1)S(1)} fusion(f32[7168]{0:T(1024)S(1)} %convert_element_type.133, f32[4]{0:T(128)S(1)} %add_rsqrt_fusion.1, f32[4,7168]{1,0:T(4,128)S(1)} %reshape.328, bf16[2,4,7168]{2,1,0:T(4,128)(2,1)} %param.14, bf16[4,8,2]{1,0,2:T(4,128)(2,1)S(1)} %get-tuple-element.5), kind=kOutput, calls=%fused_computation.3 | convolution fusion | flops 1175552 | bytes 430224 | tf_op jit(solution)/shard_map/rec,rd->ecd/dot_general | solution.py:81
  9.9 1.0 %broadcast_in_dim.22 = bf16[8,2,2,7168]{3,2,1,0:T(2,128)(2,1)} broadcast(bf16[8,2,7168]{2,1,0:T(2,128)(2,1)S(1)} %copy.48), dimensions={0,2,3} | broadcast | bytes 688128 | tf_op jit(solution)/shard_map/broadcast_in_dim | solution.py:84
  10.9 7.4 %all-to-all-start = ((bf16[16,2,7168]{2,1,0:T(2,128)(2,1)}), bf16[16,2,7168]{2,1,0:T(2,128)(2,1)S(1)}, u32[]{:S(2)}, u32[]{:S(2)}) async-start(bf16[16,2,7168]{2,1,0:T(2,128)(2,1)} %bitcast.13), calls=%async_computation | async-start | bytes 917504 | tf_op jit(solution)/shard_map/all_to_all | solution.py:87
  21.1 10.5 %all-to-all-done = bf16[16,2,7168]{2,1,0:T(2,128)(2,1)S(1)} async-done(((bf16[16,2,7168]{2,1,0:T(2,128)(2,1)}), bf16[16,2,7168]{2,1,0:T(2,128)(2,1)S(1)}, u32[]{:S(2)}, u32[]{:S(2)}) %all-to-all-start) | async-done | bytes 458784 | tf_op jit(solution)/shard_map/all_to_all | solution.py:87
  31.6 1.0 %broadcast_in_dim.23 = bf16[8,2,2,7168]{3,2,1,0:T(2,128)(2,1)} broadcast(bf16[8,2,7168]{2,1,0:T(2,128)(2,1)S(1)} %copy.57), dimensions={0,2,3} | broadcast | bytes 688128 | tf_op jit(solution)/shard_map/broadcast_in_dim | solution.py:84
  32.6 3.9 %all-to-all-start.2 = ((bf16[16,2,7168]{2,1,0:T(2,128)(2,1)}), bf16[16,2,7168]{2,1,0:T(2,128)(2,1)S(1)}, u32[]{:S(2)}, u32[]{:S(2)}) async-start(bf16[16,2,7168]{2,1,0:T(2,128)(2,1)} %bitcast.28), calls=%async_computation.2 | async-start | bytes 917504 | tf_op jit(solution)/shard_map/all_to_all | solution.py:87
  36.7 3.2 %fusion.14 = f32[32,256]{1,0:T(8,128)S(1)} fusion(bf16[32,7168]{1,0:T(8,128)(2,1)S(1)} %reshape.330, bf16[1,2,256,7168]{3,2,1,0:T(8,128)(2,1)} %param.18), kind=kOutput, calls=%fused_computation.20 | convolution fusion | flops 117440512 | bytes 4161536 | tf_op jit(solution)/shard_map/nd,hd->nh/dot_general | solution.py:89
  39.9 5.7 %convolution_convert_fusion.1 = bf16[32,7168]{1,0:T(8,128)(2,1)S(1)} fusion(bf16[1,256,7168]{2,1,0:T(8,128)(2,1)} %param.19, bf16[32,7168]{1,0:T(8,128)(2,1)S(1)} %reshape.330, bf16[1,2,256,7168]{3,2,1,0:T(8,128)(2,1)} %param.18, f32[32,256]{1,0:T(8,128)S(1)} %fusion.14), kind=kOutput, calls=%fused_computation.1 | convolution fusion | flops 235159552 | bytes 8290304 | tf_op jit(solution)/shard_map/dot_general | solution.py:92
  45.6 1.0 %reshape.331 = bf16[16,2,7168]{2,1,0:T(2,128)(2,1)} reshape(bf16[32,7168]{1,0:T(8,128)(2,1)S(1)} %convolution_convert_fusion.1) | data formatting | bytes 917504 | tf_op jit(solution)/shard_map/reshape | solution.py:93
  46.6 3.1 %all-to-all-done.2 = bf16[16,2,7168]{2,1,0:T(2,128)(2,1)S(1)} async-done(((bf16[16,2,7168]{2,1,0:T(2,128)(2,1)}), bf16[16,2,7168]{2,1,0:T(2,128)(2,1)S(1)}, u32[]{:S(2)}, u32[]{:S(2)}) %all-to-all-start.2) | async-done | bytes 458784 | tf_op jit(solution)/shard_map/all_to_all | solution.py:87
  49.7 3.9 %all-to-all-start.1 = ((bf16[16,2,7168]{2,1,0:T(2,128)(2,1)}), bf16[16,2,7168]{2,1,0:T(2,128)(2,1)S(1)}, u32[]{:S(2)}, u32[]{:S(2)}) async-start(bf16[16,2,7168]{2,1,0:T(2,128)(2,1)} %reshape.331), calls=%async_computation.1 | async-start | bytes 917504 | tf_op jit(solution)/shard_map/all_to_all | solution.py:94
  53.8 3.2 %fusion.12 = f32[32,256]{1,0:T(8,128)S(1)} fusion(bf16[32,7168]{1,0:T(8,128)(2,1)S(1)} %reshape.334, bf16[1,2,256,7168]{3,2,1,0:T(8,128)(2,1)} %param.18), kind=kOutput, calls=%fused_computation.18 | convolution fusion | flops 117440512 | bytes 4161536 | tf_op jit(solution)/shard_map/nd,hd->nh/dot_general | solution.py:89
  57.1 5.7 %convolution_convert_fusion = bf16[32,7168]{1,0:T(8,128)(2,1)S(1)} fusion(bf16[1,256,7168]{2,1,0:T(8,128)(2,1)} %param.19, bf16[32,7168]{1,0:T(8,128)(2,1)S(1)} %reshape.334, bf16[1,2,256,7168]{3,2,1,0:T(8,128)(2,1)} %param.18, f32[32,256]{1,0:T(8,128)S(1)} %fusion.12), kind=kOutput, calls=%fused_computation | convolution fusion | flops 235159552 | bytes 8290304 | tf_op jit(solution)/shard_map/dot_general | solution.py:92
  62.8 1.0 %reshape.335 = bf16[16,2,7168]{2,1,0:T(2,128)(2,1)} reshape(bf16[32,7168]{1,0:T(8,128)(2,1)S(1)} %convolution_convert_fusion) | data formatting | bytes 917504 | tf_op jit(solution)/shard_map/reshape | solution.py:93
  63.8 3.1 %all-to-all-done.1 = bf16[16,2,7168]{2,1,0:T(2,128)(2,1)S(1)} async-done(((bf16[16,2,7168]{2,1,0:T(2,128)(2,1)}), bf16[16,2,7168]{2,1,0:T(2,128)(2,1)S(1)}, u32[]{:S(2)}, u32[]{:S(2)}) %all-to-all-start.1) | async-done | bytes 458784 | tf_op jit(solution)/shard_map/all_to_all | solution.py:94
  66.9 3.9 %all-to-all-start.3 = ((bf16[16,2,7168]{2,1,0:T(2,128)(2,1)}), bf16[16,2,7168]{2,1,0:T(2,128)(2,1)S(1)}, u32[]{:S(2)}, u32[]{:S(2)}) async-start(bf16[16,2,7168]{2,1,0:T(2,128)(2,1)} %reshape.335), calls=%async_computation.3 | async-start | bytes 917504 | tf_op jit(solution)/shard_map/all_to_all | solution.py:94
  72.3 11.7 %all-to-all-done.3 = bf16[16,2,7168]{2,1,0:T(2,128)(2,1)S(1)} async-done(((bf16[16,2,7168]{2,1,0:T(2,128)(2,1)}), bf16[16,2,7168]{2,1,0:T(2,128)(2,1)S(1)}, u32[]{:S(2)}, u32[]{:S(2)}) %all-to-all-start.3) | async-done | bytes 458784 | tf_op jit(solution)/shard_map/all_to_all | solution.py:94
  (64 shorter events, 8.3 us)
Async XLA Ops:
  0.0 18.3 %copy-start.1 = (bf16[2,4,448]{2,1,0:T(4,128)(2,1)S(1)}, bf16[2,4,448]{2,1,0:T(4,128)(2,1)}, u32[]{:S(2)}) copy-start(bf16[2,4,448]{2,1,0:T(4,128)(2,1)} %param.11) | copy-start | bytes 21508
  0.0 18.6 %copy-start.3 = (bf16[4,128,448]{1,2,0:T(8,128)(2,1)S(1)}, bf16[4,128,448]{1,2,0:T(8,128)(2,1)}, u32[]{:S(2)}) copy-start(bf16[4,128,448]{1,2,0:T(8,128)(2,1)} %param.12) | copy-start | bytes 1376260
  0.0 20.5 %copy-start = (bf16[2,4,7168]{2,1,0:T(4,128)(2,1)S(1)}, bf16[2,4,7168]{2,1,0:T(4,128)(2,1)}, u32[]{:S(2)}) copy-start(bf16[2,4,7168]{2,1,0:T(4,128)(2,1)} %param.14) | copy-start | bytes 344068
  10.9 20.6 %all-to-all-start = ((bf16[16,2,7168]{2,1,0:T(2,128)(2,1)}), bf16[16,2,7168]{2,1,0:T(2,128)(2,1)S(1)}, u32[]{:S(2)}, u32[]{:S(2)}) async-start(bf16[16,2,7168]{2,1,0:T(2,128)(2,1)} %bitcast.13), calls=%async_computation | async-start | bytes 917504 | tf_op jit(solution)/shard_map/all_to_all | solution.py:87
  32.6 17.2 %all-to-all-start.2 = ((bf16[16,2,7168]{2,1,0:T(2,128)(2,1)}), bf16[16,2,7168]{2,1,0:T(2,128)(2,1)S(1)}, u32[]{:S(2)}, u32[]{:S(2)}) async-start(bf16[16,2,7168]{2,1,0:T(2,128)(2,1)} %bitcast.28), calls=%async_computation.2 | async-start | bytes 917504 | tf_op jit(solution)/shard_map/all_to_all | solution.py:87
  49.7 17.2 %all-to-all-start.1 = ((bf16[16,2,7168]{2,1,0:T(2,128)(2,1)}), bf16[16,2,7168]{2,1,0:T(2,128)(2,1)S(1)}, u32[]{:S(2)}, u32[]{:S(2)}) async-start(bf16[16,2,7168]{2,1,0:T(2,128)(2,1)} %reshape.331), calls=%async_computation.1 | async-start | bytes 917504 | tf_op jit(solution)/shard_map/all_to_all | solution.py:94
  57.1 13.7 %copy-start.2 = (f32[2,4,3]{1,0,2:T(2,128)S(1)}, f32[2,4,3]{1,0,2:T(2,128)}, u32[]{:S(2)}) copy-start(f32[2,4,3]{1,0,2:T(2,128)} %param.17) | copy-start | bytes 292
  66.9 17.2 %all-to-all-start.3 = ((bf16[16,2,7168]{2,1,0:T(2,128)(2,1)}), bf16[16,2,7168]{2,1,0:T(2,128)(2,1)S(1)}, u32[]{:S(2)}, u32[]{:S(2)}) async-start(bf16[16,2,7168]{2,1,0:T(2,128)(2,1)} %reshape.335), calls=%async_computation.3 | async-start | bytes 917504 | tf_op jit(solution)/shard_map/all_to_all | solution.py:94
where the time goes:
time: 86.7 us; the launch traced here: 85.8 us
  waiting for transfers between devices  28.5 us (33%)
  matrix products  24.2 us (28%)
  starting transfers between devices  19 us (22%)
  local copies, waits for them, and re-layouts  8.03 us (9%)
  other arithmetic  5.74 us (7%)
    all_to_all x2, waiting for transfers between devices, per_device(): lax.all_to_all(partial_value, 'afd', split_axis=0, concat_axis=0, tiled=T...  14.8 us
    all_to_all x2, waiting for transfers between devices, per_device(): lax.all_to_all(outgoing, 'afd', split_axis=0, concat_axis=0, tiled=True)  13.7 us
    dot_general x2, matrix products, per_device(): jnp.dot(act, w_down, preferred_element_type=jnp.float32)  11.5 us
    all_to_all x2, starting transfers between devices, per_device(): lax.all_to_all(outgoing, 'afd', split_axis=0, concat_axis=0, tiled=True)  11.3 us
    all_to_all x2, starting transfers between devices, per_device(): lax.all_to_all(partial_value, 'afd', split_axis=0, concat_axis=0, tiled=T...  7.79 us
    dot_general x2, matrix products, per_device(): jnp.einsum('nd,hd->nh', flat, w_gate, preferred_element_type=jnp.float32)  6.45 us
    broadcast_in_dim x2, local copies, waits for them, and re-layouts, per_device(): jnp.broadcast_to(outgoing[:, None], (EXPERTS, shards, slots, width))  2.03 us
    reshape x2, local copies, waits for them, and re-layouts, per_device(): partial_value = part.reshape(received.shape)  1.95 us
  transfers between devices with their start and end apart: 4, of which 4 were waited for; matrix products, arithmetic and copies ran while one was open for 28% of the time, Pallas kernels for 0%

commit v1 on v0

v1 whole, which is shorter than its diff:
```python
import functools
import jax
import jax.numpy as jnp
from jax import lax
from jax.experimental import pallas as pl
from jax.experimental.pallas import tpu as pltpu
from jax.sharding import PartitionSpec as P

HEADS = 32
HEAD = 224
EXPERTS = 8
TOP = 3
CAP = 2
PIECES = 4
F32 = jnp.float32
BF16 = jnp.bfloat16
MIB = 1 << 20


def iota(shape, dim):
    return lax.broadcasted_iota(jnp.int32, shape, dim)


def nt_dot(a, b):
    return lax.dot_general(a, b, (((1,), (1,)), ((), ())), preferred_element_type=F32)


def dot(a, b):
    return jnp.dot(a, b, preferred_element_type=F32)


def spread(ids_ref, where, steps, rows, k):
    out = jnp.full(where.shape, -1, jnp.int32)
    for s in range(steps):
        for r in range(rows):
            out = jnp.where(where == s * rows + r, ids_ref[s, r, k], out)
    return out


def attend_kernel(
    len_ref, ids_ref, q_ref, fresh_ref, kv_ref, hid_ref, gain_ref, resid_ref, out_ref, merged
):
    steps, rows, width = q_ref.shape
    length = kv_ref.shape[1]
    both = steps * rows
    piece = width // PIECES
    scale = HEAD ** (-0.5)
    q = jnp.concatenate([q_ref[s].astype(F32) for s in range(steps)], axis=0)
    heads = jnp.concatenate([q[:, h * HEAD : (h + 1) * HEAD] for h in range(HEADS)], axis=0)
    heads = heads.astype(BF16)
    kv = jnp.concatenate([kv_ref[r] for r in range(rows)], axis=0)
    new = jnp.concatenate([fresh_ref[s].astype(F32) for s in range(steps)], axis=0).astype(BF16)

    sub = iota((both, rows * length), 0)
    lane = iota((both, rows * length), 1)
    limit = jnp.zeros_like(lane)
    for r in range(rows):
        limit = jnp.where(lane // length == r, len_ref[r], limit)
    valid = (lane // length == sub % rows) & (lane % length < limit)
    sub = iota((both, both), 0)
    lane = iota((both, both), 1)
    valid_new = (lane % rows == sub % rows) & (lane // rows <= sub // rows)

    old_s = (nt_dot(heads, kv[:, :HEAD]) * scale).reshape(HEADS, both, rows * length)
    new_s = (nt_dot(heads, new[:, :HEAD]) * scale).reshape(HEADS, both, both)
    old_s = jnp.where(valid[None], old_s, -1e30)
    new_s = jnp.where(valid_new[None], new_s, -1e30)
    top = jnp.maximum(
        jnp.max(old_s, axis=-1, keepdims=True), jnp.max(new_s, axis=-1, keepdims=True)
    )
    old_e = jnp.exp(old_s - top)
    new_e = jnp.exp(new_s - top)
    total = jnp.sum(old_e, axis=-1, keepdims=True) + jnp.sum(new_e, axis=-1, keepdims=True)
    old_w = (old_e / total).reshape(HEADS * both, rows * length).astype(BF16)
    new_w = (new_e / total).reshape(HEADS * both, both).astype(BF16)
    attended = dot(old_w, kv[:, HEAD:]) + dot(new_w, new[:, HEAD:])
    for h in range(HEADS):
        merged[:, h * HEAD : (h + 1) * HEAD] = attended[h * both : (h + 1) * both]
    hidden = jnp.concatenate([hid_ref[s].astype(F32) for s in range(steps)], axis=0)
    resid = hidden + merged[...]
    resid_ref[...] = resid
    meansq = jnp.mean(resid * resid, axis=-1, keepdims=True)
    normed = resid * lax.rsqrt(meansq + 1e-06) * gain_ref[...].astype(F32)
    stacked = jnp.concatenate(
        [normed[:, k * piece : (k + 1) * piece] for k in range(PIECES)], axis=0
    ).astype(BF16)

    lines = PIECES * steps * CAP
    shape = (EXPERTS * lines, PIECES * both)
    line = iota(shape, 0)
    col = iota(shape, 1)
    where = iota((1, PIECES * both), 1) % both
    named = jnp.zeros(shape, jnp.bool_)
    for k in range(TOP):
        named = named | (spread(ids_ref, where, steps, rows, k) == line // lines)
    at = iota((PIECES * both, PIECES * both), 0)
    to = iota((PIECES * both, PIECES * both), 1)
    before = jnp.where((at // rows == to // rows) & (at < to), 1.0, 0.0).astype(BF16)
    rank = dot(jnp.where(named, 1.0, 0.0).astype(BF16), before)
    slot = (line % CAP).astype(F32)
    same = (line // CAP) % (PIECES * steps) == col // rows
    picks = jnp.where(named & same & (rank == slot), 1.0, 0.0).astype(BF16)
    out_ref[...] = dot(picks, stacked).astype(BF16).reshape(out_ref.shape)


def attend(cache_len, expert_ids, queries, fresh, kv_cache, hidden_state, norm_gain):
    steps, rows, width = queries.shape
    lines = PIECES * steps * CAP
    smem = pl.BlockSpec(memory_space=pltpu.SMEM)
    vmem = pl.BlockSpec(memory_space=pltpu.VMEM)
    return pl.pallas_call(
        attend_kernel,
        out_shape=(
            jax.ShapeDtypeStruct((steps * rows, width), F32),
            jax.ShapeDtypeStruct((EXPERTS, lines, width // PIECES), BF16),
        ),
        in_specs=[smem, smem, vmem, vmem, vmem, vmem, vmem],
        out_specs=(vmem, vmem),
        scratch_shapes=[pltpu.VMEM((steps * rows, width), F32)],
        compiler_params=pltpu.CompilerParams(vmem_limit_bytes=32 * MIB),
        cost_estimate=pl.CostEstimate(
            flops=300_000_000, bytes_accessed=2_000_000, transcendentals=131072
        ),
        name="attend",
    )(cache_len, expert_ids, queries, fresh, kv_cache, hidden_state, norm_gain.reshape(1, width))


def regroup(chips, lines, per):
    n = chips * lines
    row = iota((n, n), 0)
    col = iota((n, n), 1)
    k, p, x = row // (chips * per), (row // per) % chips, row % per
    return jnp.where(col == p * lines + k * per + x, 1.0, 0.0).astype(BF16)


def expert_kernel(
    own_ref, other_ref, gate_up_ref, down_ref, mine_ref, theirs_ref, gu, dn, gu_sem, dn_sem
):
    chips, lines, piece = own_ref.shape
    per = lines // PIECES
    hidden = down_ref.shape[1]
    half = chips * per
    cols = [pl.ds(k * piece, piece) for k in range(PIECES)]
    gu_copies = [
        pltpu.make_async_copy(gate_up_ref.at[0, :, :, cols[k]], gu.at[k], gu_sem.at[k])
        for k in range(PIECES)
    ]
    dn_copies = [
        pltpu.make_async_copy(down_ref.at[0, :, cols[k]], dn.at[k], dn_sem.at[k])
        for k in range(PIECES)
    ]
    for copy in gu_copies + dn_copies:
        copy.start()
    order = regroup(chips, lines, per)
    own = dot(order, own_ref[...].reshape(chips * lines, piece)).astype(BF16)
    other = dot(order, other_ref[...].reshape(chips * lines, piece)).astype(BF16)
    gate = jnp.zeros((2 * half, hidden), F32)
    upper = jnp.zeros((2 * half, hidden), F32)
    for k in range(PIECES):
        rows = jnp.concatenate(
            [own[k * half : (k + 1) * half], other[k * half : (k + 1) * half]], axis=0
        )
        gu_copies[k].wait()
        gate = gate + nt_dot(rows, gu[k, 0])
        upper = upper + nt_dot(rows, gu[k, 1])
    act = (gate / (1.0 + jnp.exp(-gate)) * upper).astype(BF16)
    mine = []
    theirs = []
    for k in range(PIECES):
        dn_copies[k].wait()
        part = dot(act, dn[k]).astype(BF16)
        mine.append(part[:half])
        theirs.append(part[half:])
    n = chips * lines
    row = iota((n, n), 0)
    col = iota((n, n), 1)
    k, p, x = col // half, (col // per) % chips, col % per
    back = jnp.where(row == p * lines + k * per + x, 1.0, 0.0).astype(BF16)
    mine = dot(back, jnp.concatenate(mine, axis=0)).astype(BF16)
    theirs = dot(back, jnp.concatenate(theirs, axis=0)).astype(BF16)
    mine_ref[...] = mine.reshape(chips, lines, piece)
    theirs_ref[...] = theirs.reshape(chips, lines, piece)


def experts(own, other, gate_up, down):
    chips, lines, piece = own.shape
    hidden = down.shape[1]
    vmem = pl.BlockSpec(memory_space=pltpu.VMEM)
    hbm = pl.BlockSpec(memory_space=pl.ANY)
    return pl.pallas_call(
        expert_kernel,
        out_shape=(jax.ShapeDtypeStruct(own.shape, BF16),) * 2,
        in_specs=[vmem, vmem, hbm, hbm],
        out_specs=(vmem, vmem),
        scratch_shapes=[
            pltpu.VMEM((PIECES, 2, hidden, piece), BF16),
            pltpu.VMEM((PIECES, hidden, piece), BF16),
            pltpu.SemaphoreType.DMA((PIECES,)),
            pltpu.SemaphoreType.DMA((PIECES,)),
        ],
        compiler_params=pltpu.CompilerParams(vmem_limit_bytes=48 * MIB),
        cost_estimate=pl.CostEstimate(
            flops=800_000_000, bytes_accessed=12_000_000, transcendentals=16384
        ),
        name="experts",
    )(own, other, gate_up, down)


def combine_kernel(ids_ref, weight_ref, resid_ref, back_ref, out_ref):
    steps, rows, width = out_ref.shape
    chips, lines, piece = back_ref.shape
    both = steps * rows
    chips_per_expert = chips // EXPERTS
    shape = (both, chips * lines)
    line = iota(shape, 1)
    sub = iota(shape, 0)
    expert = line // (lines * chips_per_expert)
    where = iota((both, 1), 0)
    named = jnp.zeros(shape, F32)
    mix = jnp.zeros(shape, F32)
    for k in range(TOP):
        hit = spread(ids_ref, where, steps, rows, k) == expert
        weight = jnp.zeros((both, 1), F32)
        for s in range(steps):
            for r in range(rows):
                weight = jnp.where(where == s * rows + r, weight_ref[s, r, k], weight)
        named = named + jnp.where(hit, 1.0, 0.0)
        mix = mix + jnp.where(hit, weight, 0.0)
    at = iota((both, both), 1)
    to = iota((both, both), 0)
    before = jnp.where((at // rows == to // rows) & (at < to), 1.0, 0.0).astype(BF16)
    rank = dot(before, named.astype(BF16))
    same = (line // CAP) % steps == sub // rows
    mix = jnp.where((rank == (line % CAP).astype(F32)) & same, mix, 0.0)
    high = mix.astype(BF16)
    rest = mix - high.astype(F32)
    middle = rest.astype(BF16)
    low = (rest - middle.astype(F32)).astype(BF16)
    k_of = (line // (steps * CAP)) % PIECES
    parts = [
        jnp.where(k_of == k, part.astype(F32), 0.0)
        for part in (high, middle, low)
        for k in range(PIECES)
    ]
    left = jnp.concatenate(parts, axis=0).astype(BF16)
    product = dot(left, back_ref[...].reshape(chips * lines, piece))
    n = PIECES * both
    total = product[:n] + product[n : 2 * n] + product[2 * n :]
    for k in range(PIECES):
        cols = pl.ds(k * piece, piece)
        done = (resid_ref[:, cols] + total[k * both : (k + 1) * both]).astype(BF16)
        for s in range(steps):
            out_ref[s, :, cols] = done[s * rows : (s + 1) * rows]


def combine(expert_ids, route_weight, resid, back):
    steps, rows, _ = expert_ids.shape
    smem = pl.BlockSpec(memory_space=pltpu.SMEM)
    vmem = pl.BlockSpec(memory_space=pltpu.VMEM)
    return pl.pallas_call(
        combine_kernel,
        out_shape=jax.ShapeDtypeStruct((steps, rows, resid.shape[1]), BF16),
        in_specs=[smem, smem, vmem, vmem],
        out_specs=vmem,
        compiler_params=pltpu.CompilerParams(vmem_limit_bytes=32 * MIB),
        cost_estimate=pl.CostEstimate(
            flops=100_000_000, bytes_accessed=1_000_000, transcendentals=0
        ),
        name="combine",
    )(expert_ids, route_weight, resid, back)


def per_device(
    queries,
    fresh,
    kv_cache,
    cache_len,
    hidden_state,
    norm_gain,
    expert_ids,
    route_weight,
    gate_up,
    down,
):
    owners = lax.axis_size("afd")
    chips = owners // 2
    chips_per_expert = chips // EXPERTS
    same_core = [[2 * p + c for p in range(chips)] for c in range(2)]
    swap = [(i, i ^ 1) for i in range(owners)]
    resid, outgoing = attend(
        cache_len, expert_ids, queries, fresh, kv_cache, hidden_state, norm_gain
    )
    if chips_per_expert > 1:
        outgoing = jnp.repeat(outgoing, chips_per_expert, axis=0)
    own = lax.all_to_all(
        outgoing, "afd", split_axis=0, concat_axis=0, axis_index_groups=same_core, tiled=True
    )
    other = lax.ppermute(own, "afd", swap)
    mine, theirs = experts(own, other, gate_up, down)
    summed = (mine.astype(F32) + lax.ppermute(theirs, "afd", swap).astype(F32)).astype(BF16)
    back = lax.all_to_all(
        summed, "afd", split_axis=0, concat_axis=0, axis_index_groups=same_core, tiled=True
    )
    return combine(expert_ids, route_weight, resid, back)


def solution(mesh):
    placed = (
        P(None, ("group", "afd"), None),
        P(None, ("group", "afd"), None),
        P(("group", "afd"), None, None),
        P(("group", "afd")),
        P(None, ("group", "afd"), None),
        P(),
        P(None, ("group", "afd"), None),
        P(None, ("group", "afd"), None),
        P("afd", None, None, None),
        P("afd", None, None),
    )
    return jax.shard_map(
        per_device,
        mesh=mesh,
        in_specs=placed,
        out_specs=P(None, ("group", "afd"), None),
        check_vma=False,
    )
```

time: 86.7 us -> 59.9 us (0.69)
  matrix products: 24.2 us -> 0 us
  blocking collectives: 0 us -> 20.3 us
  starting transfers between devices: 19 us -> 3.68 us
  waiting for transfers between devices: 28.5 us -> 17 us
  Pallas kernels: 0 us -> 9.51 us
  other arithmetic: 5.74 us -> 0.88 us
    dot_general x17 -> x0, matrix products: 24.2 us -> none  [the longest x2 11.5 us: per_device(): jnp.dot(act, w_down, preferred_element_type=jnp.float32)]
    all_to_all x0 -> x1, blocking collectives: none -> 20.3 us  [per_device(): lax.all_to_all(outgoing, 'afd', split_axis=0, concat_axis=0, axis_index_g...]
    all_to_all x4 -> x1, starting transfers between devices: 19 us -> 3.48 us  [per_device(): lax.all_to_all(summed, 'afd', split_axis=0, concat_axis=0, axis_index_gro...]
    all_to_all x4 -> x1, waiting for transfers between devices: 28.5 us -> 13.5 us  [per_device(): lax.all_to_all(summed, 'afd', split_axis=0, concat_axis=0, axis_index_gro...]
    pallas_call x0 -> x3, Pallas kernels: none -> 9.51 us  [the longest x1 5.93 us: experts(): pl.pallas_call(expert_kernel, out_shape=(jax.ShapeDtypeStruct(own.shape,...]
    unnamed x8 -> x15, local copies, waits for them, and re-layouts: 0.03 us -> 7.28 us
    ppermute x0 -> x2, waiting for transfers between devices: none -> 3.5 us  [the longest x1 1.81 us: per_device(): other = lax.ppermute(own, 'afd', swap)]
    slice x8 -> x0, local copies, waits for them, and re-layouts: 2.17 us -> none  [the longest x3 0.95 us: per_device(): ids_now = expert_ids[step]]
  transfers between devices with their start and end apart: 4 -> 3, of which waited for: 4 -> 3; matrix products, arithmetic and copies ran while one was open for 28% -> 0% of each run, Pallas kernels for 0% -> 0%
where the time goes in v1:
time: 59.9 us; the launch traced here: 59.4 us
  blocking collectives  20.3 us (34%)
  waiting for transfers between devices  17 us (28%)
  Pallas kernels  9.51 us (16%)
  local copies, waits for them, and re-layouts  8.01 us (13%)
  starting transfers between devices  3.68 us (6%)
  other arithmetic  0.88 us (1%)
    all_to_all x1, blocking collectives, per_device(): lax.all_to_all(outgoing, 'afd', split_axis=0, concat_axis=0, axis_index_g...  20.3 us
    all_to_all x1, waiting for transfers between devices, per_device(): lax.all_to_all(summed, 'afd', split_axis=0, concat_axis=0, axis_index_gro...  13.5 us
    unnamed x15, local copies, waits for them, and re-layouts  7.28 us
    pallas_call x1, Pallas kernels, experts(): pl.pallas_call(expert_kernel, out_shape=(jax.ShapeDtypeStruct(own.shape,...  5.93 us
    all_to_all x1, starting transfers between devices, per_device(): lax.all_to_all(summed, 'afd', split_axis=0, concat_axis=0, axis_index_gro...  3.48 us
    pallas_call x1, Pallas kernels, attend(): pl.pallas_call(attend_kernel, out_shape=(jax.ShapeDtypeStruct((steps * ro...  1.91 us
    ppermute x1, waiting for transfers between devices, per_device(): other = lax.ppermute(own, 'afd', swap)  1.81 us
    ppermute x1, waiting for transfers between devices, per_device(): lax.ppermute(theirs, 'afd', swap).astype(F32)  1.68 us
  transfers between devices with their start and end apart: 3, of which 3 were waited for; matrix products, arithmetic and copies ran while one was open for 0% of the time, Pallas kernels for 0%

profile of v1, /device:TPU:0, one launch (start us, length us, event | category | flops | bytes accessed | tf_op | source)
XLA Modules:
  0.0 59.4 jit_solution(10674871384936329001)
XLA Ops:
  0.0 0.8 %copy.13.ids_ref = s32[2,4,3]{2,1,0:T(4,128)S(1)} copy(s32[2,4,3]{1,0,2:T(2,128)} %param.16) | data formatting | bytes 192 | tf_op args[6]
  0.8 1.2 %copy.12.kv_ref = bf16[4,128,448]{2,1,0:T(8,128)(2,1)S(1)} copy(bf16[4,128,448]{1,2,0:T(8,128)(2,1)} %param.12) | data formatting | bytes 917504 | tf_op args[2]
  2.0 0.7 %reshape.3.gain_ref = bf16[1,7168]{1,0:T(2,128)(2,1)S(1)} reshape(bf16[7168]{0:T(1024)(128)(2,1)} %param.15) | data formatting | bytes 28672 | tf_op jit(solution)/shard_map/reshape | solution.py:125
  2.7 0.0 copy-start.1
  2.8 0.9 %copy-done.1 = bf16[2,4,7168]{2,1,0:T(4,128)(2,1)S(1)} copy-done((bf16[2,4,7168]{2,1,0:T(4,128)(2,1)S(1)}, bf16[2,4,7168]{2,1,0:T(4,128)(2,1)}, u32[]{:S(2)}) %copy-start.1) | copy-done | bytes 114712
  3.6 0.0 copy-start.2
  3.6 0.9 %copy-done.2 = bf16[2,4,7168]{2,1,0:T(4,128)(2,1)S(1)} copy-done((bf16[2,4,7168]{2,1,0:T(4,128)(2,1)S(1)}, bf16[2,4,7168]{2,1,0:T(4,128)(2,1)}, u32[]{:S(2)}) %copy-start.2) | copy-done | bytes 114712
  4.5 0.7 %copy-done.3 = bf16[2,4,448]{2,1,0:T(4,128)(2,1)S(1)} copy-done((bf16[2,4,448]{2,1,0:T(4,128)(2,1)S(1)}, bf16[2,4,448]{2,1,0:T(4,128)(2,1)}, u32[]{:S(2)}) %copy-start.3) | copy-done | bytes 7192
  5.2 0.7 %copy-done.4 = s32[4]{0:T(128)S(1)} copy-done((s32[4]{0:T(128)S(1)}, s32[4]{0:T(128)}, u32[]{:S(2)}) %copy-start.4) | copy-done | bytes 40
  5.9 1.9 %attend.1 = (f32[8,7168]{1,0:T(8,128)S(1)}, bf16[8,16,1792]{2,1,0:T(8,128)(2,1)S(1)}) custom-call(s32[4]{0:T(128)S(1)} %copy-done.4, s32[2,4,3]{2,1,0:T(4,128)S(1)} %copy.13.ids_ref, bf16[2,4,7168]{2,1,0:T(4,128)(2,1)S(1)} %copy-done.1, bf16[2,4,448]{2,1,0:T(4,128)(2,1)S(1)} %copy-done.3, bf16[4,128,448]{2,1,0:T(8,128)(2,1)S(1)} %copy.12.kv_ref, ...), custom_call_target="tpu_custom_call" | custom-call | flops 300000000 | bytes 2000000 | tf_op jit(solution)/shard_map/attend/pallas_call | solution.py:111
  7.8 0.0 copy-start.5
  7.8 20.3 %all_to_all.10.own_ref = bf16[8,16,1792]{2,1,0:T(8,128)(2,1)S(1)} all-to-all(bf16[8,16,1792]{2,1,0:T(8,128)(2,1)S(1)} %get-tuple-element.10), channel_id=1, replica_groups={{0,2,4,6,8,10,12,14},{1,3,5,7,9,11,13,15},{16,18,20,22,24,26,28,30},{17..., dimensions={0} | all-to-all | bytes 917504 | tf_op jit(solution)/shard_map/all_to_all | solution.py:295
  28.1 0.0 collective-permute-start
  28.1 1.8 %collective-permute-done.other_ref = bf16[8,16,1792]{2,1,0:T(8,128)(2,1)S(1)} collective-permute-done((bf16[8,16,1792]{2,1,0:T(8,128)(2,1)S(1)}, bf16[8,16,1792]{2,1,0:T(8,128)(2,1)S(1)}, u32[]{:S(2)}, u32[]{:S(2)}) %collective-permute-start) | collective-permute-done | bytes 458784 | tf_op jit(solution)/shard_map/ppermute | solution.py:298
  29.9 2.0 %copy-done = bf16[1,256,7168]{2,1,0:T(8,128)(2,1)S(1)} copy-done((bf16[1,256,7168]{2,1,0:T(8,128)(2,1)S(1)}, bf16[1,256,7168]{2,1,0:T(8,128)(2,1)}, u32[]{:S(2)}) %copy-start) | copy-done | bytes 3670040
  32.0 5.9 %experts.1 = (bf16[8,16,1792]{2,1,0:T(8,128)(2,1)S(1)}, bf16[8,16,1792]{2,1,0:T(8,128)(2,1)S(1)}) custom-call(bf16[8,16,1792]{2,1,0:T(8,128)(2,1)S(1)} %all_to_all.10.own_ref, bf16[8,16,1792]{2,1,0:T(8,128)(2,1)S(1)} %collective-permute-done.other_ref, bf16[1,2,256,7168]{3,2,1,0:T(8,128)(2,1)} %gate_up_ref.1, bf16[1,256,7168]{2,1,0:T(8,128)(2,1)S(1)} %copy-done), custom_call_target="tpu_custom_call" | custom-call | flops 800000000 | bytes 12000000 | tf_op jit(solution)/shard_map/experts/pallas_call | solution.py:190
  37.9 0.2 collective-permute-start.1
  38.1 1.7 %collective-permute-done.1 = bf16[8,16,1792]{2,1,0:T(8,128)(2,1)S(1)} collective-permute-done((bf16[8,16,1792]{2,1,0:T(8,128)(2,1)S(1)}, bf16[8,16,1792]{2,1,0:T(8,128)(2,1)S(1)}, u32[]{:S(2)}, u32[]{:S(2)}) %collective-permute-start.1) | collective-permute-done | bytes 458784 | tf_op jit(solution)/shard_map/ppermute | solution.py:300
  39.8 0.9 %add_convert_fusion = bf16[8,16,1792]{2,1,0:T(8,128)(2,1)} fusion(bf16[8,16,1792]{2,1,0:T(8,128)(2,1)S(1)} %collective-permute-done.1, bf16[8,16,1792]{2,1,0:T(8,128)(2,1)S(1)} %get-tuple-element.11), kind=kLoop, calls=%fused_computation | loop fusion | flops 917504 | bytes 1376256 | tf_op jit(solution)/shard_map/convert_element_type | solution.py:300
  40.7 3.5 %all-to-all-start.1 = ((bf16[8,16,1792]{2,1,0:T(8,128)(2,1)}), bf16[8,16,1792]{2,1,0:T(8,128)(2,1)S(1)}, u32[]{:S(2)}, u32[]{:S(2)}) async-start(bf16[8,16,1792]{2,1,0:T(8,128)(2,1)} %add_convert_fusion), calls=%async_computation.1 | async-start | bytes 917504 | tf_op jit(solution)/shard_map/all_to_all | solution.py:301
  44.1 0.0 copy-done.5
  44.1 0.1 copy.14.weight_ref
  44.2 13.5 %all-to-all-done.1.back_ref = bf16[8,16,1792]{2,1,0:T(8,128)(2,1)S(1)} async-done(((bf16[8,16,1792]{2,1,0:T(8,128)(2,1)}), bf16[8,16,1792]{2,1,0:T(8,128)(2,1)S(1)}, u32[]{:S(2)}, u32[]{:S(2)}) %all-to-all-start.1) | async-done | bytes 458784 | tf_op jit(solution)/shard_map/all_to_all | solution.py:301
  57.7 1.7 %combine.1 = bf16[2,4,7168]{2,1,0:T(4,128)(2,1)} custom-call(s32[2,4,3]{2,1,0:T(4,128)S(1)} %copy.13.ids_ref, f32[2,4,3]{2,1,0:T(4,128)S(1)} %copy.14.weight_ref, f32[8,7168]{1,0:T(8,128)S(1)} %get-tuple-element.9.resid_ref, bf16[8,16,1792]{2,1,0:T(8,128)(2,1)S(1)} %all-to-all-done.1.back_ref), custom_call_target="tpu_custom_call" | custom-call | flops 100000000 | bytes 1000000 | tf_op jit(solution)/shard_map/combine/pallas_call | solution.py:260
  (3 shorter events, 0.0 us)
Async XLA Ops:
  2.7 0.9 %copy-start.1 = (bf16[2,4,7168]{2,1,0:T(4,128)(2,1)S(1)}, bf16[2,4,7168]{2,1,0:T(4,128)(2,1)}, u32[]{:S(2)}) copy-start(bf16[2,4,7168]{2,1,0:T(4,128)(2,1)} %q_ref.1) | copy-start | bytes 344068
  3.6 0.9 %copy-start.2 = (bf16[2,4,7168]{2,1,0:T(4,128)(2,1)S(1)}, bf16[2,4,7168]{2,1,0:T(4,128)(2,1)}, u32[]{:S(2)}) copy-start(bf16[2,4,7168]{2,1,0:T(4,128)(2,1)} %hid_ref.1) | copy-start | bytes 344068
  4.5 0.7 %copy-start.3 = (bf16[2,4,448]{2,1,0:T(4,128)(2,1)S(1)}, bf16[2,4,448]{2,1,0:T(4,128)(2,1)}, u32[]{:S(2)}) copy-start(bf16[2,4,448]{2,1,0:T(4,128)(2,1)} %fresh_ref.1) | copy-start | bytes 21508
  5.2 0.7 %copy-start.4 = (s32[4]{0:T(128)S(1)}, s32[4]{0:T(128)}, u32[]{:S(2)}) copy-start(s32[4]{0:T(128)} %len_ref.1) | copy-start | bytes 52
  7.8 36.3 %copy-start.5 = (f32[2,4,3]{1,0,2:T(2,128)S(1)}, f32[2,4,3]{1,0,2:T(2,128)}, u32[]{:S(2)}) copy-start(f32[2,4,3]{1,0,2:T(2,128)} %param.17) | copy-start | bytes 292
  28.1 1.8 %collective-permute-start = (bf16[8,16,1792]{2,1,0:T(8,128)(2,1)S(1)}, bf16[8,16,1792]{2,1,0:T(8,128)(2,1)S(1)}, u32[]{:S(2)}, u32[]{:S(2)}) collective-permute-start(bf16[8,16,1792]{2,1,0:T(8,128)(2,1)S(1)} %all_to_all.10.own_ref), channel_id=1, source_target_pairs={{0,1},{1,0},{2,3},{3,2},{4,5},{5,4},{6,7},{7,6},{8,9},{9,8},{10,11... | collective-permute-start | bytes 1376264 | tf_op jit(solution)/shard_map/ppermute | solution.py:298
  29.9 2.0 %copy-start = (bf16[1,256,7168]{2,1,0:T(8,128)(2,1)S(1)}, bf16[1,256,7168]{2,1,0:T(8,128)(2,1)}, u32[]{:S(2)}) copy-start(bf16[1,256,7168]{2,1,0:T(8,128)(2,1)} %down_ref.1) | copy-start | bytes 11010052
  37.9 1.9 %collective-permute-start.1 = (bf16[8,16,1792]{2,1,0:T(8,128)(2,1)S(1)}, bf16[8,16,1792]{2,1,0:T(8,128)(2,1)S(1)}, u32[]{:S(2)}, u32[]{:S(2)}) collective-permute-start(bf16[8,16,1792]{2,1,0:T(8,128)(2,1)S(1)} %get-tuple-element.12), channel_id=1, source_target_pairs={{0,1},{1,0},{2,3},{3,2},{4,5},{5,4},{6,7},{7,6},{8,9},{9,8},{10,11... | collective-permute-start | bytes 1376264 | tf_op jit(solution)/shard_map/ppermute | solution.py:300
  40.7 17.1 %all-to-all-start.1 = ((bf16[8,16,1792]{2,1,0:T(8,128)(2,1)}), bf16[8,16,1792]{2,1,0:T(8,128)(2,1)S(1)}, u32[]{:S(2)}, u32[]{:S(2)}) async-start(bf16[8,16,1792]{2,1,0:T(8,128)(2,1)} %add_convert_fusion), calls=%async_computation.1 | async-start | bytes 917504 | tf_op jit(solution)/shard_map/all_to_all | solution.py:301

commit v2 on v0

v2 whole, which is shorter than its diff:
```python
import functools
import jax
import jax.numpy as jnp
from jax import lax
from jax.experimental import pallas as pl
from jax.experimental.pallas import tpu as pltpu
from jax.sharding import PartitionSpec as P

HEADS = 32
HEAD = 224
EXPERTS = 8
TOP = 3
CAP = 2
LINES = 16
LANES = 128
F32 = jnp.float32
BF16 = jnp.bfloat16
MIB = 1 << 20
VMEM = pl.BlockSpec(memory_space=pltpu.VMEM)
HBM = pl.BlockSpec(memory_space=pl.ANY)
BATCHES = ((0, 1),)


def iota(shape, dim):
    return lax.broadcasted_iota(jnp.int32, shape, dim)


def nt_dot(a, b):
    return lax.dot_general(a, b, (((1,), (1,)), ((), ())), preferred_element_type=F32)


def dot(a, b):
    return jnp.dot(a, b, preferred_element_type=F32)


def one_hot(mask):
    return jnp.where(mask, 1.0, 0.0).astype(BF16)


def spread(ref, k, where, steps, rows, empty):
    out = jnp.full(where.shape, empty)
    for s in range(steps):
        for r in range(rows):
            out = jnp.where(where == s * rows + r, ref[k, s, r], out)
    return out


def picks_of(ids_ref, batch, steps, rows, me):
    pieces = LINES // (len(batch) * CAP)
    both = steps * rows
    shape = (EXPERTS * LINES, pieces * both)
    line = iota(shape, 0)
    col = iota(shape, 1)
    where = iota((1, pieces * both), 1) % both
    expert = (line // LINES) ^ me
    named = jnp.zeros(shape, jnp.bool_)
    for k in range(TOP):
        named = named | (spread(ids_ref, k, where, steps, rows, -1) == expert)
    at = iota((pieces * both, pieces * both), 0)
    to = iota((pieces * both, pieces * both), 1)
    rank = dot(one_hot(named), one_hot((at // rows == to // rows) & (at < to)))
    slot = (line % CAP).astype(F32)
    step = (line // CAP) % len(batch) + batch[0]
    piece = line // (CAP * len(batch)) % pieces
    same = (step == col // rows % steps) & (piece == col // both)
    return one_hot(named & same & (rank == slot))


def attend_kernel(
    permuted, len_hbm, ids_hbm, q_hbm, fresh_hbm, kv_hbm, hid_hbm, gain_hbm, resid_ref, *rest
):
    outs = rest[: len(BATCHES) * EXPERTS]
    len_ref, ids_ref, q_ref, fresh_ref, kv_ref, hid_ref, gain_ref, merged, sems = rest[len(outs) :]
    copies = [
        pltpu.make_async_copy(source, target, sems.at[i])
        for i, (source, target) in enumerate(
            (
                (q_hbm, q_ref),
                (kv_hbm, kv_ref),
                (len_hbm, len_ref),
                (ids_hbm, ids_ref),
                (fresh_hbm, fresh_ref),
                (hid_hbm, hid_ref),
                (gain_hbm, gain_ref),
            )
        )
    ]
    for copy in copies:
        copy.start()
    steps, rows, width = q_ref.shape
    length = kv_ref.shape[2]
    both = steps * rows
    scale = HEAD ** (-0.5)
    me = lax.axis_index("afd") // 2 if permuted else 0
    for copy in copies:
        copy.wait()
    q = jnp.concatenate([q_ref[s].astype(F32) for s in range(steps)], axis=0)
    heads = jnp.concatenate([q[:, h * HEAD : (h + 1) * HEAD] for h in range(HEADS)], axis=0)
    heads = heads.astype(BF16)
    kv = jnp.concatenate([kv_ref[r] for r in range(rows)], axis=1)
    new = jnp.concatenate([fresh_ref[s].astype(F32) for s in range(steps)], axis=0).astype(BF16)

    sub = iota((both, rows * length), 0)
    lane = iota((both, rows * length), 1)
    limit = jnp.zeros_like(lane)
    for r in range(rows):
        limit = jnp.where(lane // length == r, len_ref[r], limit)
    valid = (lane // length == sub % rows) & (lane % length < limit)
    sub = iota((both, both), 0)
    lane = iota((both, both), 1)
    valid_new = (lane % rows == sub % rows) & (lane // rows <= sub // rows)

    old_s = (dot(heads, kv[:HEAD]) * scale).reshape(HEADS, both, rows * length)
    new_s = (nt_dot(heads, new[:, :HEAD]) * scale).reshape(HEADS, both, both)
    old_s = jnp.where(valid[None], old_s, -1e30)
    new_s = jnp.where(valid_new[None], new_s, -1e30)
    top = jnp.maximum(
        jnp.max(old_s, axis=-1, keepdims=True), jnp.max(new_s, axis=-1, keepdims=True)
    )
    old_e = jnp.exp(old_s - top)
    new_e = jnp.exp(new_s - top)
    total = jnp.sum(old_e, axis=-1, keepdims=True) + jnp.sum(new_e, axis=-1, keepdims=True)
    old_w = (old_e / total).reshape(HEADS * both, rows * length).astype(BF16)
    new_w = (new_e / total).reshape(HEADS * both, both).astype(BF16)
    attended = nt_dot(old_w, kv[HEAD:]) + dot(new_w, new[:, HEAD:])
    for h in range(HEADS):
        merged[:, h * HEAD : (h + 1) * HEAD] = attended[h * both : (h + 1) * both]
    hidden = jnp.concatenate([hid_ref[s].astype(F32) for s in range(steps)], axis=0)
    resid = hidden + merged[...]
    resid_ref[...] = resid
    meansq = jnp.mean(resid * resid, axis=-1, keepdims=True)
    gain = gain_ref[...].astype(F32)
    gain = jnp.concatenate([gain[i : i + 1] for i in range(width // LANES)], axis=1)
    normed = resid * lax.rsqrt(meansq + 1e-06) * gain
    for i, batch in enumerate(BATCHES):
        pieces = LINES // (len(batch) * CAP)
        piece = width // pieces
        stacked = jnp.concatenate(
            [normed[:, k * piece : (k + 1) * piece] for k in range(pieces)], axis=0
        ).astype(BF16)
        picks = picks_of(ids_ref, batch, steps, rows, me)
        sent = dot(picks, stacked).astype(BF16)
        for j in range(EXPERTS):
            outs[i * EXPERTS + j][0] = sent[j * LINES : (j + 1) * LINES]


def attend(permuted, cache_len, ids, queries, fresh, kv_cache, hidden_state, norm_gain):
    steps, rows, width = queries.shape
    chunks = []
    for batch in BATCHES:
        shape = (1, LINES, width * len(batch) * CAP // LINES)
        chunks += [jax.ShapeDtypeStruct(shape, BF16)] * EXPERTS
    kv = kv_cache.transpose(0, 2, 1)
    gain = norm_gain.reshape(width // LANES, LANES)
    results = pl.pallas_call(
        functools.partial(attend_kernel, permuted),
        out_shape=(jax.ShapeDtypeStruct((steps * rows, width), F32), *chunks),
        in_specs=[HBM] * 7,
        out_specs=(VMEM,) * (1 + len(chunks)),
        scratch_shapes=[
            pltpu.SMEM(cache_len.shape, jnp.int32),
            pltpu.SMEM(ids.shape, jnp.int32),
            pltpu.VMEM(queries.shape, BF16),
            pltpu.VMEM(fresh.shape, BF16),
            pltpu.VMEM(kv.shape, BF16),
            pltpu.VMEM(hidden_state.shape, BF16),
            pltpu.VMEM(gain.shape, BF16),
            pltpu.VMEM((steps * rows, width), F32),
            pltpu.SemaphoreType.DMA((7,)),
        ],
        compiler_params=pltpu.CompilerParams(vmem_limit_bytes=24 * MIB),
        cost_estimate=pl.CostEstimate(
            flops=300_000_000, bytes_accessed=2_000_000, transcendentals=131072
        ),
        name="attend",
    )(cache_len, ids, queries, fresh, kv, hidden_state, gain)
    resid, chunks = results[0], results[1:]
    return resid, [chunks[i * EXPERTS : (i + 1) * EXPERTS] for i in range(len(BATCHES))]


def mixing(ids_ref, weight_ref, batch, steps, rows, chips, me):
    pieces = LINES // (len(batch) * CAP)
    both = len(batch) * rows
    shape = (both, chips * LINES)
    line = iota(shape, 1)
    sub = iota(shape, 0)
    expert = (line // LINES ^ me) // (chips // EXPERTS)
    where = iota((both, 1), 0) + batch[0] * rows
    named = jnp.zeros(shape, F32)
    mix = jnp.zeros(shape, F32)
    for k in range(TOP):
        hit = spread(ids_ref, k, where, steps, rows, -1) == expert
        weight = spread(weight_ref, k, where, steps, rows, 0.0)
        named = named + jnp.where(hit, 1.0, 0.0)
        mix = mix + jnp.where(hit, weight, 0.0)
    at = iota((both, both), 1)
    to = iota((both, both), 0)
    rank = dot(one_hot((at // rows == to // rows) & (at < to)), named.astype(BF16))
    same = (line // CAP) % len(batch) == sub // rows
    mix = jnp.where((rank == (line % CAP).astype(F32)) & same, mix, 0.0)
    high = mix.astype(BF16).astype(F32)
    middle = (mix - high).astype(BF16).astype(F32)
    low = mix - high - middle
    k_of = line // (len(batch) * CAP) % pieces
    parts = [
        jnp.where(k_of == k, part, 0.0) for part in (high, middle, low) for k in range(pieces)
    ]
    return jnp.concatenate(parts, axis=0).astype(BF16)


def stage_kernel(
    permuted, chips, steps, rows, ids_hbm, weight_hbm, gu_hbm, dn_hbm, after, gu, dn, *rest
):
    mixes = rest[: len(BATCHES)]
    ids_ref, weight_ref, small, large = rest[len(BATCHES) :]
    first = [
        pltpu.make_async_copy(ids_hbm, ids_ref, small.at[0]),
        pltpu.make_async_copy(weight_hbm, weight_ref, small.at[1]),
    ]
    hidden = dn.shape[0]
    step = hidden // 4
    second = []
    for i in range(4):
        part = pl.ds(i * step, step)
        second.append((gu_hbm.at[0, 0, part], gu.at[0, part]))
        second.append((gu_hbm.at[0, 1, part], gu.at[1, part]))
        second.append((dn_hbm.at[0, part], dn.at[part]))
    second = [pltpu.make_async_copy(a, b, large.at[i]) for i, (a, b) in enumerate(second)]
    for copy in first + second:
        copy.start()
    for copy in first:
        copy.wait()
    me = lax.axis_index("afd") // 2 if permuted else 0
    for batch, mix in zip(BATCHES, mixes):
        mix[...] = mixing(ids_ref, weight_ref, batch, steps, rows, chips, me)
    for copy in second:
        copy.wait()


def stage(permuted, chips, ids, weights, gate_up, down, after):
    _, steps, rows = ids.shape
    mixes = [
        jax.ShapeDtypeStruct((3 * LINES // CAP * rows, chips * LINES), BF16) for _ in BATCHES
    ]
    gu, dn, *mixes = pl.pallas_call(
        functools.partial(stage_kernel, permuted, chips, steps, rows),
        out_shape=(
            jax.ShapeDtypeStruct(gate_up.shape[1:], BF16),
            jax.ShapeDtypeStruct(down.shape[1:], BF16),
            *mixes,
        ),
        in_specs=[HBM] * 5,
        out_specs=(VMEM,) * (2 + len(mixes)),
        scratch_shapes=[
            pltpu.SMEM(ids.shape, jnp.int32),
            pltpu.SMEM(weights.shape, F32),
            pltpu.SemaphoreType.DMA((2,)),
            pltpu.SemaphoreType.DMA((12,)),
        ],
        compiler_params=pltpu.CompilerParams(vmem_limit_bytes=24 * MIB),
        cost_estimate=pl.CostEstimate(
            flops=1_000_000, bytes_accessed=22_000_000, transcendentals=0
        ),
        name="stage",
    )(ids, weights, gate_up, down, after)
    return gu, dn, mixes


def expert_kernel(count, per, *refs):
    own_refs, other_refs = refs[:count], refs[count : 2 * count]
    gu, dn = refs[2 * count : 2 * count + 2]
    mine_refs = refs[2 * count + 2 : 3 * count + 2]
    theirs_refs = refs[3 * count + 2 :]
    piece = own_refs[0].shape[2]
    chips = sum(ref.shape[0] for ref in own_refs)
    pieces = LINES // per
    half = chips * per
    n = chips * LINES
    row = iota((n, n), 0)
    col = iota((n, n), 1)
    order = one_hot(col == row // per % chips * LINES + row // half * per + row % per)
    sides = []
    for refs_now in (own_refs, other_refs):
        lines = [ref[...].reshape(ref.shape[0] * LINES, piece) for ref in refs_now]
        sides.append(dot(order, jnp.concatenate(lines, axis=0)).astype(BF16))
    gate = upper = None
    for k in range(pieces):
        x = jnp.concatenate([side[k * half : (k + 1) * half] for side in sides], axis=0)
        cols = pl.ds(k * piece, piece)
        g, u = nt_dot(x, gu[0, :, cols]), nt_dot(x, gu[1, :, cols])
        gate, upper = (g, u) if k == 0 else (gate + g, upper + u)
    act = (gate / (1.0 + jnp.exp(-gate)) * upper).astype(BF16)
    mine = []
    theirs = []
    for k in range(pieces):
        part = dot(act, dn[:, k * piece : (k + 1) * piece]).astype(BF16)
        mine.append(part[:half])
        theirs.append(part[half:])
    back = one_hot(row == col // per % chips * LINES + col // half * per + col % per)
    for parts, refs_now in ((theirs, theirs_refs), (mine, mine_refs)):
        lines = dot(back, jnp.concatenate(parts, axis=0)).astype(BF16)
        start = 0
        for ref in refs_now:
            size = ref.shape[0] * LINES
            ref[...] = lines[start : start + size].reshape(ref.shape)
            start += size


def experts(own, other, gu, dn, per):
    count = len(own)
    shapes = tuple(jax.ShapeDtypeStruct(x.shape, BF16) for x in own)
    results = pl.pallas_call(
        functools.partial(expert_kernel, count, per),
        out_shape=shapes + shapes,
        in_specs=[VMEM] * (2 * count + 2),
        out_specs=(VMEM,) * (2 * count),
        compiler_params=pltpu.CompilerParams(vmem_limit_bytes=32 * MIB),
        cost_estimate=pl.CostEstimate(
            flops=800_000_000, bytes_accessed=12_000_000, transcendentals=16384
        ),
        name="experts",
    )(*own, *other, gu, dn)
    return results[:count], results[count:]


def combine_kernel(counts, resid_ref, *refs):
    out_ref = refs[-1]
    _, rows, width = out_ref.shape
    start = 0
    for batch, count in zip(BATCHES, counts):
        left = refs[start][...]
        back_refs = refs[start + 1 : start + 1 + count]
        start += 1 + count
        piece = back_refs[0].shape[2]
        pieces = width // piece
        both = len(batch) * rows
        lines = [ref[...].reshape(ref.shape[0] * LINES, piece) for ref in back_refs]
        product = dot(left, jnp.concatenate(lines, axis=0))
        n = pieces * both
        total = product[:n] + product[n : 2 * n] + product[2 * n :]
        first = batch[0] * rows
        for k in range(pieces):
            cols = pl.ds(k * piece, piece)
            done = resid_ref[first : first + both, cols] + total[k * both : (k + 1) * both]
            done = done.astype(BF16)
            for i, s in enumerate(batch):
                out_ref[s, :, cols] = done[i * rows : (i + 1) * rows]


def combine(shape, resid, mixes, backs):
    operands = [x for mix, back in zip(mixes, backs) for x in (mix, *back)]
    return pl.pallas_call(
        functools.partial(combine_kernel, [len(back) for back in backs]),
        out_shape=jax.ShapeDtypeStruct(shape, BF16),
        in_specs=[VMEM] * (1 + len(operands)),
        out_specs=VMEM,
        compiler_params=pltpu.CompilerParams(vmem_limit_bytes=24 * MIB),
        cost_estimate=pl.CostEstimate(
            flops=100_000_000, bytes_accessed=1_000_000, transcendentals=0
        ),
        name="combine",
    )(resid, *operands)


def per_device(
    queries,
    fresh,
    kv_cache,
    cache_len,
    hidden_state,
    norm_gain,
    expert_ids,
    route_weight,
    gate_up,
    down,
):
    owners = lax.axis_size("afd")
    chips = owners // 2
    chips_per_expert = chips // EXPERTS
    permuted = chips == EXPERTS
    swap = [(i, i ^ 1) for i in range(owners)]
    far_first = sorted(range(1, chips), reverse=True)

    def to_chips(chunks):
        if permuted:
            moved = {0: chunks[0]}
            for j in far_first:
                moved[j] = lax.ppermute(chunks[j], "afd", [(i, i ^ 2 * j) for i in range(owners)])
            return [moved[j] for j in range(chips)]
        same_core = [[2 * p + c for p in range(chips)] for c in range(2)]
        whole = jnp.concatenate(chunks, axis=0)
        return [
            lax.all_to_all(
                whole, "afd", split_axis=0, concat_axis=0, axis_index_groups=same_core, tiled=True
            )
        ]

    ids = expert_ids.transpose(2, 0, 1)
    weights = route_weight.transpose(2, 0, 1)
    resid, sent = attend(
        permuted, cache_len, ids, queries, fresh, kv_cache, hidden_state, norm_gain
    )
    gu, dn, mixes = stage(permuted, chips, ids, weights, gate_up, down, resid)
    backs = []
    for batch, chunks in zip(BATCHES, sent):
        if not permuted:
            chunks = [jnp.repeat(chunk, chips_per_expert, axis=0) for chunk in chunks]
        own = to_chips(chunks)
        other = [lax.ppermute(x, "afd", swap) for x in own]
        mine, theirs = experts(own, other, gu, dn, len(batch) * CAP)
        summed = [
            (a.astype(F32) + lax.ppermute(b, "afd", swap).astype(F32)).astype(BF16)
            for a, b in zip(mine, theirs)
        ]
        backs.append(to_chips(summed))
    return combine(queries.shape, resid, mixes, backs)


def solution(mesh):
    placed = (
        P(None, ("group", "afd"), None),
        P(None, ("group", "afd"), None),
        P(("group", "afd"), None, None),
        P(("group", "afd")),
        P(None, ("group", "afd"), None),
        P(),
        P(None, ("group", "afd"), None),
        P(None, ("group", "afd"), None),
        P("afd", None, None, None),
        P("afd", None, None),
    )
    return jax.shard_map(
        per_device,
        mesh=mesh,
        in_specs=placed,
        out_specs=P(None, ("group", "afd"), None),
        check_vma=False,
    )
```

time: 86.7 us -> 59.7 us (0.69)
  matrix products: 24.2 us -> 0 us
  waiting for transfers between devices: 28.5 us -> 9.67 us
  Pallas kernels: 0 us -> 9.85 us
  starting transfers between devices: 19 us -> 28 us
  other arithmetic: 5.74 us -> 0.13 us
  local copies, waits for them, and re-layouts: 8.03 us -> 11.4 us
    all_to_all x4 -> x0, waiting for transfers between devices: 28.5 us -> none  [the longest x2 14.8 us: per_device(): lax.all_to_all(partial_value, 'afd', split_axis=0, concat_axis=0, tiled=T...]
    ppermute x0 -> x30, starting transfers between devices: none -> 28 us  [the longest x14 24 us: to_chips(): lax.ppermute(chunks[j], 'afd', [(i, i ^ 2 * j) for i in range(owners)])]
    dot_general x17 -> x0, matrix products: 24.2 us -> none  [the longest x2 11.5 us: per_device(): jnp.dot(act, w_down, preferred_element_type=jnp.float32)]
    all_to_all x4 -> x0, starting transfers between devices: 19 us -> none  [the longest x2 11.3 us: per_device(): lax.all_to_all(outgoing, 'afd', split_axis=0, concat_axis=0, tiled=True)]
    unnamed x8 -> x20, local copies, waits for them, and re-layouts: 0.03 us -> 11.4 us
    pallas_call x0 -> x4, Pallas kernels: none -> 9.85 us  [the longest x1 3.63 us: experts(): pl.pallas_call(functools.partial(expert_kernel, count, per), out_shape=sh...]
    ppermute x0 -> x30, waiting for transfers between devices: none -> 9.67 us  [the longest x14 9.29 us: to_chips(): lax.ppermute(chunks[j], 'afd', [(i, i ^ 2 * j) for i in range(owners)])]
    reshape x6 -> x0, local copies, waits for them, and re-layouts: 2.6 us -> none  [the longest x2 1.95 us: per_device(): partial_value = part.reshape(received.shape)]
  transfers between devices with their start and end apart: 4 -> 30, of which waited for: 4 -> 5; matrix products, arithmetic and copies ran while one was open for 28% -> 0% of each run, Pallas kernels for 0% -> 5%
where the time goes in v2:
time: 59.7 us; the launch traced here: 59.3 us
  starting transfers between devices  28 us (47%)
  local copies, waits for them, and re-layouts  11.4 us (19%)
  Pallas kernels  9.85 us (16%)
  waiting for transfers between devices  9.67 us (16%)
    ppermute x14, starting transfers between devices, to_chips(): lax.ppermute(chunks[j], 'afd', [(i, i ^ 2 * j) for i in range(owners)])  24 us
    unnamed x20, local copies, waits for them, and re-layouts  11.4 us
    ppermute x14, waiting for transfers between devices, to_chips(): lax.ppermute(chunks[j], 'afd', [(i, i ^ 2 * j) for i in range(owners)])  9.29 us
    pallas_call x1, Pallas kernels, experts(): pl.pallas_call(functools.partial(expert_kernel, count, per), out_shape=sh...  3.63 us
    pallas_call x1, Pallas kernels, stage(): pl.pallas_call(functools.partial(stage_kernel, permuted, chips, steps, ro...  2.97 us
    pallas_call x1, Pallas kernels, attend(): pl.pallas_call(functools.partial(attend_kernel, permuted), out_shape=(jax...  2.34 us
    ppermute x8, starting transfers between devices, per_device(): other = [lax.ppermute(x, 'afd', swap) for x in own]  2.06 us
    ppermute x8, starting transfers between devices, per_device(): lax.ppermute(b, 'afd', swap).astype(F32)  2.03 us
  transfers between devices with their start and end apart: 30, of which 5 were waited for; matrix products, arithmetic and copies ran while one was open for 0% of the time, Pallas kernels for 5%

profile of v2, /device:TPU:0, one launch (start us, length us, event | category | flops | bytes accessed | tf_op | source)
XLA Modules:
  0.0 59.3 jit_solution(16320865370178902065)
XLA Ops:
  0.7 1.0 %copy-done.4 = bf16[4,128,448]{1,2,0:T(8,128)(2,1)S(1)} copy-done((bf16[4,128,448]{1,2,0:T(8,128)(2,1)S(1)}, bf16[4,128,448]{1,2,0:T(8,128)(2,1)}, u32[]{:S(2)}) %copy-start.4) | copy-done | bytes 458776
  1.7 0.9 %copy-done.5 = bf16[2,4,7168]{2,1,0:T(4,128)(2,1)S(1)} copy-done((bf16[2,4,7168]{2,1,0:T(4,128)(2,1)S(1)}, bf16[2,4,7168]{2,1,0:T(4,128)(2,1)}, u32[]{:S(2)}) %copy-start.5) | copy-done | bytes 114712
  2.6 0.9 %copy-done.6 = bf16[2,4,7168]{2,1,0:T(4,128)(2,1)S(1)} copy-done((bf16[2,4,7168]{2,1,0:T(4,128)(2,1)S(1)}, bf16[2,4,7168]{2,1,0:T(4,128)(2,1)}, u32[]{:S(2)}) %copy-start.6) | copy-done | bytes 114712
  3.5 0.7 %copy-done.7 = bf16[7168]{0:T(1024)(128)(2,1)S(1)} copy-done((bf16[7168]{0:T(1024)(128)(2,1)S(1)}, bf16[7168]{0:T(1024)(128)(2,1)}, u32[]{:S(2)}) %copy-start.7) | copy-done | bytes 14360
  5.6 2.3 %attend.1 = (f32[8,7168]{1,0:T(8,128)S(1)}, bf16[1,16,1792]{2,1,0:T(8,128)(2,1)S(1)}, bf16[1,16,1792]{2,1,0:T(8,128)(2,1)S(1)}, bf16[1,16,1792]{2,1,0:T(8,128)(2...) custom-call(s32[4]{0:T(128)S(1)} %copy-done.9, ...), custom_call_target="tpu_custom_call" | custom-call | flops 300000000 | bytes 2000000 | tf_op jit(solution)/shard_map/attend/pallas_call | solution.py:155
  7.9 3.0 %collective-permute-start = (bf16[1,16,1792]{2,1,0:T(8,128)(2,1)S(1)}, bf16[1,16,1792]{2,1,0:T(8,128)(2,1)S(1)}, u32[]{:S(2)}, u32[]{:S(2)}) collective-permute-start(bf16[1,16,1792]{2,1,0:T(8,128)(2,1)S(1)} %get-tuple-element.36), channel_id=1, source_target_pairs={{0,2},{1,3},{2,0},{3,1},{4,6},{5,7},{6,4},{7,5},{8,10},{9,11},{10,... | collective-permute-start | bytes 172040 | tf_op jit(solution)/shard_map/ppermute | solution.py:388
  10.9 1.6 %collective-permute-start.1 = (bf16[1,16,1792]{2,1,0:T(8,128)(2,1)S(1)}, bf16[1,16,1792]{2,1,0:T(8,128)(2,1)S(1)}, u32[]{:S(2)}, u32[]{:S(2)}) collective-permute-start(bf16[1,16,1792]{2,1,0:T(8,128)(2,1)S(1)} %get-tuple-element.37), channel_id=1, source_target_pairs={{0,4},{1,5},{2,6},{3,7},{4,0},{5,1},{6,2},{7,3},{8,12},{9,13},{10,... | collective-permute-start | bytes 172040 | tf_op jit(solution)/shard_map/ppermute | solution.py:388
  12.5 3.0 %collective-permute-start.3 = (bf16[1,16,1792]{2,1,0:T(8,128)(2,1)S(1)}, bf16[1,16,1792]{2,1,0:T(8,128)(2,1)S(1)}, u32[]{:S(2)}, u32[]{:S(2)}) collective-permute-start(bf16[1,16,1792]{2,1,0:T(8,128)(2,1)S(1)} %get-tuple-element.39), channel_id=1, source_target_pairs={{0,8},{1,9},{2,10},{3,11},{4,12},{5,13},{6,14},{7,15},{8,0},{9,1},... | collective-permute-start | bytes 172040 | tf_op jit(solution)/shard_map/ppermute | solution.py:388
  15.5 1.3 %collective-permute-start.4 = (bf16[1,16,1792]{2,1,0:T(8,128)(2,1)S(1)}, bf16[1,16,1792]{2,1,0:T(8,128)(2,1)S(1)}, u32[]{:S(2)}, u32[]{:S(2)}) collective-permute-start(bf16[1,16,1792]{2,1,0:T(8,128)(2,1)S(1)} %get-tuple-element.40), channel_id=1, source_target_pairs={{0,10},{1,11},{2,8},{3,9},{4,14},{5,15},{6,12},{7,13},{8,2},{9,3},... | collective-permute-start | bytes 172040 | tf_op jit(solution)/shard_map/ppermute | solution.py:388
  16.8 3.6 %collective-permute-start.5 = (bf16[1,16,1792]{2,1,0:T(8,128)(2,1)S(1)}, bf16[1,16,1792]{2,1,0:T(8,128)(2,1)S(1)}, u32[]{:S(2)}, u32[]{:S(2)}) collective-permute-start(bf16[1,16,1792]{2,1,0:T(8,128)(2,1)S(1)} %get-tuple-element.41), channel_id=1, source_target_pairs={{0,12},{1,13},{2,14},{3,15},{4,8},{5,9},{6,10},{7,11},{8,4},{9,5},... | collective-permute-start | bytes 172040 | tf_op jit(solution)/shard_map/ppermute | solution.py:388
  21.0 3.7 %collective-permute-done.4.refs_5_ = bf16[1,16,1792]{2,1,0:T(8,128)(2,1)S(1)} collective-permute-done((bf16[1,16,1792]{2,1,0:T(8,128)(2,1)S(1)}, bf16[1,16,1792]{2,1,0:T(8,128)(2,1)S(1)}, u32[]{:S(2)}, u32[]{:S(2)}) %collective-permute-start.4) | collective-permute-done | bytes 57376 | tf_op jit(solution)/shard_map/ppermute | solution.py:388
  25.2 2.1 %collective-permute-done.6.refs_7_ = bf16[1,16,1792]{2,1,0:T(8,128)(2,1)S(1)} collective-permute-done((bf16[1,16,1792]{2,1,0:T(8,128)(2,1)S(1)}, bf16[1,16,1792]{2,1,0:T(8,128)(2,1)S(1)}, u32[]{:S(2)}, u32[]{:S(2)}) %collective-permute-start.6) | collective-permute-done | bytes 57376 | tf_op jit(solution)/shard_map/ppermute | solution.py:388
  28.3 3.1 %copy-done = bf16[1,2,256,7168]{3,2,1,0:T(8,128)(2,1)S(1)} copy-done((bf16[1,2,256,7168]{3,2,1,0:T(8,128)(2,1)S(1)}, bf16[1,2,256,7168]{3,2,1,0:T(8,128)(2,1)}, u32[]{:S(2)}) %copy-start) | copy-done | bytes 7340056
  31.4 2.0 %copy-done.1 = bf16[1,256,7168]{2,1,0:T(8,128)(2,1)S(1)} copy-done((bf16[1,256,7168]{2,1,0:T(8,128)(2,1)S(1)}, bf16[1,256,7168]{2,1,0:T(8,128)(2,1)}, u32[]{:S(2)}) %copy-start.1) | copy-done | bytes 3670040
  34.1 3.0 %stage.1 = (bf16[2,256,7168]{2,1,0:T(8,128)(2,1)S(1)}, bf16[256,7168]{1,0:T(8,128)(2,1)S(1)}, bf16[96,128]{1,0:T(8,128)(2,1)S(1)}) custom-call(s32[3,2,4]{2,1,0:T(2,128)S(1)} %bitcast.5, f32[3,2,4]{2,1,0:T(2,128)S(1)} %bitcast.6, bf16[1,2,256,7168]{3,2,1,0:T(8,128)(2,1)S(1)} %copy-done, bf16[1,256,7168]{2,1,0:T(8,128)(2,1)S(1)} %copy-done.1, ...), custom_call_target="tpu_custom_call" | custom-call | flops 1000000 | bytes 22000000 | tf_op jit(solution)/shard_map/stage/pallas_call | solution.py:245
  37.1 3.6 %experts.1 = (bf16[1,16,1792]{2,1,0:T(8,128)(2,1)S(1)}, bf16[1,16,1792]{2,1,0:T(8,128)(2,1)S(1)}, bf16[1,16,1792]{2,1,0:T(8,128)(2,1)S(1)}, bf16[1,16,1792]{2,1,...) custom-call(bf16[1,16,1792]{2,1,0:T(8,128)(2,1)S(1)} %get-tuple-elem, ...), custom_call_target="tpu_custom_call" | custom-call | flops 800000000 | bytes 12000000 | tf_op jit(solution)/shard_map/experts/pallas_call | solution.py:312
  44.0 0.8 %collective-permute-start.19 = (bf16[1,16,1792]{2,1,0:T(8,128)(2,1)S(1)}, bf16[1,16,1792]{2,1,0:T(8,128)(2,1)S(1)}, u32[]{:S(2)}, u32[]{:S(2)}) collective-permute-start(bf16[1,16,1792]{2,1,0:T(8,128)(2,1)S(1)} %add_convert_fusion.5), channel_id=1, source_target_pairs={{0,4},{1,5},{2,6},{3,7},{4,0},{5,1},{6,2},{7,3},{8,12},{9,13},{10,... | collective-permute-start | bytes 172040 | tf_op jit(solution)/shard_map/ppermute | solution.py:388
  44.8 2.2 %collective-permute-start.21 = (bf16[1,16,1792]{2,1,0:T(8,128)(2,1)S(1)}, bf16[1,16,1792]{2,1,0:T(8,128)(2,1)S(1)}, u32[]{:S(2)}, u32[]{:S(2)}) collective-permute-start(bf16[1,16,1792]{2,1,0:T(8,128)(2,1)S(1)} %add_convert_fusion.4), channel_id=1, source_target_pairs={{0,6},{1,7},{2,4},{3,5},{4,2},{5,3},{6,0},{7,1},{8,14},{9,15},{10,... | collective-permute-start | bytes 172040 | tf_op jit(solution)/shard_map/ppermute | solution.py:388
  47.0 1.6 %collective-permute-start.23 = (bf16[1,16,1792]{2,1,0:T(8,128)(2,1)S(1)}, bf16[1,16,1792]{2,1,0:T(8,128)(2,1)S(1)}, u32[]{:S(2)}, u32[]{:S(2)}) collective-permute-start(bf16[1,16,1792]{2,1,0:T(8,128)(2,1)S(1)} %add_convert_fusion.3), channel_id=1, source_target_pairs={{0,8},{1,9},{2,10},{3,11},{4,12},{5,13},{6,14},{7,15},{8,0},{9,1},... | collective-permute-start | bytes 172040 | tf_op jit(solution)/shard_map/ppermute | solution.py:388
  48.6 1.6 %collective-permute-start.25 = (bf16[1,16,1792]{2,1,0:T(8,128)(2,1)S(1)}, bf16[1,16,1792]{2,1,0:T(8,128)(2,1)S(1)}, u32[]{:S(2)}, u32[]{:S(2)}) collective-permute-start(bf16[1,16,1792]{2,1,0:T(8,128)(2,1)S(1)} %add_convert_fusion.2), channel_id=1, source_target_pairs={{0,10},{1,11},{2,8},{3,9},{4,14},{5,15},{6,12},{7,13},{8,2},{9,3},... | collective-permute-start | bytes 172040 | tf_op jit(solution)/shard_map/ppermute | solution.py:388
  50.2 1.2 %collective-permute-start.27 = (bf16[1,16,1792]{2,1,0:T(8,128)(2,1)S(1)}, bf16[1,16,1792]{2,1,0:T(8,128)(2,1)S(1)}, u32[]{:S(2)}, u32[]{:S(2)}) collective-permute-start(bf16[1,16,1792]{2,1,0:T(8,128)(2,1)S(1)} %add_convert_fusion.1), channel_id=1, source_target_pairs={{0,12},{1,13},{2,14},{3,15},{4,8},{5,9},{6,10},{7,11},{8,4},{9,5},... | collective-permute-start | bytes 172040 | tf_op jit(solution)/shard_map/ppermute | solution.py:388
  51.3 3.5 %collective-permute-start.29 = (bf16[1,16,1792]{2,1,0:T(8,128)(2,1)S(1)}, bf16[1,16,1792]{2,1,0:T(8,128)(2,1)S(1)}, u32[]{:S(2)}, u32[]{:S(2)}) collective-permute-start(bf16[1,16,1792]{2,1,0:T(8,128)(2,1)S(1)} %add_convert_fusion), channel_id=1, source_target_pairs={{0,14},{1,15},{2,12},{3,13},{4,10},{5,11},{6,8},{7,9},{8,6},{9,7},... | collective-permute-start | bytes 172040 | tf_op jit(solution)/shard_map/ppermute | solution.py:388
  54.9 3.5 %collective-permute-done.25.refs_6_ = bf16[1,16,1792]{2,1,0:T(8,128)(2,1)S(1)} collective-permute-done((bf16[1,16,1792]{2,1,0:T(8,128)(2,1)S(1)}, bf16[1,16,1792]{2,1,0:T(8,128)(2,1)S(1)}, u32[]{:S(2)}, u32[]{:S(2)}) %collective-permute-start.25) | collective-permute-done | bytes 57376 | tf_op jit(solution)/shard_map/ppermute | solution.py:388
  58.4 0.9 %combine.1 = bf16[2,4,7168]{2,1,0:T(4,128)(2,1)} custom-call(f32[8,7168]{1,0:T(8,128)S(1)} %get-tuple-element.33.after.resid_ref, bf16[96,128]{1,0:T(8,128)(2,1)S(1)} %get-tuple-element.34.refs_0_, bf16[1,16,1792]{2,1,0:T(8,128)(2,1)S(1)} %add_convert_fusion.7.refs_1_, bf16[1,16,1792]{2,1,0:T(8,128)(2,1)S(1)} %collective-permute-done.17.refs_2_, ...), custom_call_target="tpu_custom_call" | custom-call | flops 100000000 | bytes 1000000 | tf_op jit(solution)/shard_map/combine/pallas_call | solution.py:352
  (68 shorter events, 8.1 us)
Async XLA Ops:
  7.9 8.9 %collective-permute-start = (bf16[1,16,1792]{2,1,0:T(8,128)(2,1)S(1)}, bf16[1,16,1792]{2,1,0:T(8,128)(2,1)S(1)}, u32[]{:S(2)}, u32[]{:S(2)}) collective-permute-start(bf16[1,16,1792]{2,1,0:T(8,128)(2,1)S(1)} %get-tuple-element.36), channel_id=1, source_target_pairs={{0,2},{1,3},{2,0},{3,1},{4,6},{5,7},{6,4},{7,5},{8,10},{9,11},{10,... | collective-permute-start | bytes 172040 | tf_op jit(solution)/shard_map/ppermute | solution.py:388
  10.9 9.5 %collective-permute-start.1 = (bf16[1,16,1792]{2,1,0:T(8,128)(2,1)S(1)}, bf16[1,16,1792]{2,1,0:T(8,128)(2,1)S(1)}, u32[]{:S(2)}, u32[]{:S(2)}) collective-permute-start(bf16[1,16,1792]{2,1,0:T(8,128)(2,1)S(1)} %get-tuple-element.37), channel_id=1, source_target_pairs={{0,4},{1,5},{2,6},{3,7},{4,0},{5,1},{6,2},{7,3},{8,12},{9,13},{10,... | collective-permute-start | bytes 172040 | tf_op jit(solution)/shard_map/ppermute | solution.py:388
  12.5 7.9 %collective-permute-start.2 = (bf16[1,16,1792]{2,1,0:T(8,128)(2,1)S(1)}, bf16[1,16,1792]{2,1,0:T(8,128)(2,1)S(1)}, u32[]{:S(2)}, u32[]{:S(2)}) collective-permute-start(bf16[1,16,1792]{2,1,0:T(8,128)(2,1)S(1)} %get-tuple-element.38), channel_id=1, source_target_pairs={{0,6},{1,7},{2,4},{3,5},{4,2},{5,3},{6,0},{7,1},{8,14},{9,15},{10,... | collective-permute-start | bytes 172040 | tf_op jit(solution)/shard_map/ppermute | solution.py:388
  12.5 8.0 %collective-permute-start.3 = (bf16[1,16,1792]{2,1,0:T(8,128)(2,1)S(1)}, bf16[1,16,1792]{2,1,0:T(8,128)(2,1)S(1)}, u32[]{:S(2)}, u32[]{:S(2)}) collective-permute-start(bf16[1,16,1792]{2,1,0:T(8,128)(2,1)S(1)} %get-tuple-element.39), channel_id=1, source_target_pairs={{0,8},{1,9},{2,10},{3,11},{4,12},{5,13},{6,14},{7,15},{8,0},{9,1},... | collective-permute-start | bytes 172040 | tf_op jit(solution)/shard_map/ppermute | solution.py:388
  15.5 9.2 %collective-permute-start.4 = (bf16[1,16,1792]{2,1,0:T(8,128)(2,1)S(1)}, bf16[1,16,1792]{2,1,0:T(8,128)(2,1)S(1)}, u32[]{:S(2)}, u32[]{:S(2)}) collective-permute-start(bf16[1,16,1792]{2,1,0:T(8,128)(2,1)S(1)} %get-tuple-element.40), channel_id=1, source_target_pairs={{0,10},{1,11},{2,8},{3,9},{4,14},{5,15},{6,12},{7,13},{8,2},{9,3},... | collective-permute-start | bytes 172040 | tf_op jit(solution)/shard_map/ppermute | solution.py:388
  16.8 7.9 %collective-permute-start.5 = (bf16[1,16,1792]{2,1,0:T(8,128)(2,1)S(1)}, bf16[1,16,1792]{2,1,0:T(8,128)(2,1)S(1)}, u32[]{:S(2)}, u32[]{:S(2)}) collective-permute-start(bf16[1,16,1792]{2,1,0:T(8,128)(2,1)S(1)} %get-tuple-element.41), channel_id=1, source_target_pairs={{0,12},{1,13},{2,14},{3,15},{4,8},{5,9},{6,10},{7,11},{8,4},{9,5},... | collective-permute-start | bytes 172040 | tf_op jit(solution)/shard_map/ppermute | solution.py:388
  20.4 6.9 %collective-permute-start.6 = (bf16[1,16,1792]{2,1,0:T(8,128)(2,1)S(1)}, bf16[1,16,1792]{2,1,0:T(8,128)(2,1)S(1)}, u32[]{:S(2)}, u32[]{:S(2)}) collective-permute-start(bf16[1,16,1792]{2,1,0:T(8,128)(2,1)S(1)} %get-tuple-element.42), channel_id=1, source_target_pairs={{0,14},{1,15},{2,12},{3,13},{4,10},{5,11},{6,8},{7,9},{8,6},{9,7},... | collective-permute-start | bytes 172040 | tf_op jit(solution)/shard_map/ppermute | solution.py:388
  20.4 6.8 %collective-permute-start.7 = (bf16[1,16,1792]{2,1,0:T(8,128)(2,1)S(1)}, bf16[1,16,1792]{2,1,0:T(8,128)(2,1)S(1)}, u32[]{:S(2)}, u32[]{:S(2)}) collective-permute-start(bf16[1,16,1792]{2,1,0:T(8,128)(2,1)S(1)} %get-tuple-element.35.refs_0_), channel_id=1, source_target_pairs={{0,1},{1,0},{2,3},{3,2},{4,5},{5,4},{6,7},{7,6},{8,9},{9,8},{10,11... | collective-permute-start | bytes 172040 | tf_op jit(solution)/shard_map/ppermute | solution.py:409
  20.5 7.3 %collective-permute-start.8 = (bf16[1,16,1792]{2,1,0:T(8,128)(2,1)S(1)}, bf16[1,16,1792]{2,1,0:T(8,128)(2,1)S(1)}, u32[]{:S(2)}, u32[]{:S(2)}) collective-permute-start(bf16[1,16,1792]{2,1,0:T(8,128)(2,1)S(1)} %collective-permute-done.refs_1_), channel_id=1, source_target_pairs={{0,1},{1,0},{2,3},{3,2},{4,5},{5,4},{6,7},{7,6},{8,9},{9,8},{10,11... | collective-permute-start | bytes 172040 | tf_op jit(solution)/shard_map/ppermute | solution.py:409
  24.7 3.2 %collective-permute-start.9 = (bf16[1,16,1792]{2,1,0:T(8,128)(2,1)S(1)}, bf16[1,16,1792]{2,1,0:T(8,128)(2,1)S(1)}, u32[]{:S(2)}, u32[]{:S(2)}) collective-permute-start(bf16[1,16,1792]{2,1,0:T(8,128)(2,1)S(1)} %collective-permute-done.1.refs_2_), channel_id=1, source_target_pairs={{0,1},{1,0},{2,3},{3,2},{4,5},{5,4},{6,7},{7,6},{8,9},{9,8},{10,11... | collective-permute-start | bytes 172040 | tf_op jit(solution)/shard_map/ppermute | solution.py:409
  24.7 12.4 %collective-permute-start.10 = (bf16[1,16,1792]{2,1,0:T(8,128)(2,1)S(1)}, bf16[1,16,1792]{2,1,0:T(8,128)(2,1)S(1)}, u32[]{:S(2)}, u32[]{:S(2)}) collective-permute-start(bf16[1,16,1792]{2,1,0:T(8,128)(2,1)S(1)} %collective-permute-done.2.refs_3_), channel_id=1, source_target_pairs={{0,1},{1,0},{2,3},{3,2},{4,5},{5,4},{6,7},{7,6},{8,9},{9,8},{10,11... | collective-permute-start | bytes 172040 | tf_op jit(solution)/shard_map/ppermute | solution.py:409
  27.3 9.8 %collective-permute-start.11 = (bf16[1,16,1792]{2,1,0:T(8,128)(2,1)S(1)}, bf16[1,16,1792]{2,1,0:T(8,128)(2,1)S(1)}, u32[]{:S(2)}, u32[]{:S(2)}) collective-permute-start(bf16[1,16,1792]{2,1,0:T(8,128)(2,1)S(1)} %collective-permute-done.3.refs_4_), channel_id=1, source_target_pairs={{0,1},{1,0},{2,3},{3,2},{4,5},{5,4},{6,7},{7,6},{8,9},{9,8},{10,11... | collective-permute-start | bytes 172040 | tf_op jit(solution)/shard_map/ppermute | solution.py:409
  27.3 9.8 %collective-permute-start.12 = (bf16[1,16,1792]{2,1,0:T(8,128)(2,1)S(1)}, bf16[1,16,1792]{2,1,0:T(8,128)(2,1)S(1)}, u32[]{:S(2)}, u32[]{:S(2)}) collective-permute-start(bf16[1,16,1792]{2,1,0:T(8,128)(2,1)S(1)} %collective-permute-done.4.refs_5_), channel_id=1, source_target_pairs={{0,1},{1,0},{2,3},{3,2},{4,5},{5,4},{6,7},{7,6},{8,9},{9,8},{10,11... | collective-permute-start | bytes 172040 | tf_op jit(solution)/shard_map/ppermute | solution.py:409
  27.8 9.3 %collective-permute-start.13 = (bf16[1,16,1792]{2,1,0:T(8,128)(2,1)S(1)}, bf16[1,16,1792]{2,1,0:T(8,128)(2,1)S(1)}, u32[]{:S(2)}, u32[]{:S(2)}) collective-permute-start(bf16[1,16,1792]{2,1,0:T(8,128)(2,1)S(1)} %collective-permute-done.5.refs_6_), channel_id=1, source_target_pairs={{0,1},{1,0},{2,3},{3,2},{4,5},{5,4},{6,7},{7,6},{8,9},{9,8},{10,11... | collective-permute-start | bytes 172040 | tf_op jit(solution)/shard_map/ppermute | solution.py:409
  27.9 9.3 %collective-permute-start.14 = (bf16[1,16,1792]{2,1,0:T(8,128)(2,1)S(1)}, bf16[1,16,1792]{2,1,0:T(8,128)(2,1)S(1)}, u32[]{:S(2)}, u32[]{:S(2)}) collective-permute-start(bf16[1,16,1792]{2,1,0:T(8,128)(2,1)S(1)} %collective-permute-done.6.refs_7_), channel_id=1, source_target_pairs={{0,1},{1,0},{2,3},{3,2},{4,5},{5,4},{6,7},{7,6},{8,9},{9,8},{10,11... | collective-permute-start | bytes 172040 | tf_op jit(solution)/shard_map/ppermute | solution.py:409
  40.9 7.7 %collective-permute-start.15 = (bf16[1,16,1792]{2,1,0:T(8,128)(2,1)S(1)}, bf16[1,16,1792]{2,1,0:T(8,128)(2,1)S(1)}, u32[]{:S(2)}, u32[]{:S(2)}) collective-permute-start(bf16[1,16,1792]{2,1,0:T(8,128)(2,1)S(1)} %get-tuple-element.46), channel_id=1, source_target_pairs={{0,1},{1,0},{2,3},{3,2},{4,5},{5,4},{6,7},{7,6},{8,9},{9,8},{10,11... | collective-permute-start | bytes 172040 | tf_op jit(solution)/shard_map/ppermute | solution.py:412
  42.8 4.2 %collective-permute-start.28 = (bf16[1,16,1792]{2,1,0:T(8,128)(2,1)S(1)}, bf16[1,16,1792]{2,1,0:T(8,128)(2,1)S(1)}, u32[]{:S(2)}, u32[]{:S(2)}) collective-permute-start(bf16[1,16,1792]{2,1,0:T(8,128)(2,1)S(1)} %get-tuple-element.60), channel_id=1, source_target_pairs={{0,1},{1,0},{2,3},{3,2},{4,5},{5,4},{6,7},{7,6},{8,9},{9,8},{10,11... | collective-permute-start | bytes 172040 | tf_op jit(solution)/shard_map/ppermute | solution.py:412
  43.2 6.9 %collective-permute-start.17 = (bf16[1,16,1792]{2,1,0:T(8,128)(2,1)S(1)}, bf16[1,16,1792]{2,1,0:T(8,128)(2,1)S(1)}, u32[]{:S(2)}, u32[]{:S(2)}) collective-permute-start(bf16[1,16,1792]{2,1,0:T(8,128)(2,1)S(1)} %add_convert_fusion.6), channel_id=1, source_target_pairs={{0,2},{1,3},{2,0},{3,1},{4,6},{5,7},{6,4},{7,5},{8,10},{9,11},{10,... | collective-permute-start | bytes 172040 | tf_op jit(solution)/shard_map/ppermute | solution.py:388
  44.0 7.4 %collective-permute-start.19 = (bf16[1,16,1792]{2,1,0:T(8,128)(2,1)S(1)}, bf16[1,16,1792]{2,1,0:T(8,128)(2,1)S(1)}, u32[]{:S(2)}, u32[]{:S(2)}) collective-permute-start(bf16[1,16,1792]{2,1,0:T(8,128)(2,1)S(1)} %add_convert_fusion.5), channel_id=1, source_target_pairs={{0,4},{1,5},{2,6},{3,7},{4,0},{5,1},{6,2},{7,3},{8,12},{9,13},{10,... | collective-permute-start | bytes 172040 | tf_op jit(solution)/shard_map/ppermute | solution.py:388
  44.8 10.0 %collective-permute-start.21 = (bf16[1,16,1792]{2,1,0:T(8,128)(2,1)S(1)}, bf16[1,16,1792]{2,1,0:T(8,128)(2,1)S(1)}, u32[]{:S(2)}, u32[]{:S(2)}) collective-permute-start(bf16[1,16,1792]{2,1,0:T(8,128)(2,1)S(1)} %add_convert_fusion.4), channel_id=1, source_target_pairs={{0,6},{1,7},{2,4},{3,5},{4,2},{5,3},{6,0},{7,1},{8,14},{9,15},{10,... | collective-permute-start | bytes 172040 | tf_op jit(solution)/shard_map/ppermute | solution.py:388
  47.0 7.8 %collective-permute-start.23 = (bf16[1,16,1792]{2,1,0:T(8,128)(2,1)S(1)}, bf16[1,16,1792]{2,1,0:T(8,128)(2,1)S(1)}, u32[]{:S(2)}, u32[]{:S(2)}) collective-permute-start(bf16[1,16,1792]{2,1,0:T(8,128)(2,1)S(1)} %add_convert_fusion.3), channel_id=1, source_target_pairs={{0,8},{1,9},{2,10},{3,11},{4,12},{5,13},{6,14},{7,15},{8,0},{9,1},... | collective-permute-start | bytes 172040 | tf_op jit(solution)/shard_map/ppermute | solution.py:388
  48.6 9.8 %collective-permute-start.25 = (bf16[1,16,1792]{2,1,0:T(8,128)(2,1)S(1)}, bf16[1,16,1792]{2,1,0:T(8,128)(2,1)S(1)}, u32[]{:S(2)}, u32[]{:S(2)}) collective-permute-start(bf16[1,16,1792]{2,1,0:T(8,128)(2,1)S(1)} %add_convert_fusion.2), channel_id=1, source_target_pairs={{0,10},{1,11},{2,8},{3,9},{4,14},{5,15},{6,12},{7,13},{8,2},{9,3},... | collective-permute-start | bytes 172040 | tf_op jit(solution)/shard_map/ppermute | solution.py:388
  50.2 8.2 %collective-permute-start.27 = (bf16[1,16,1792]{2,1,0:T(8,128)(2,1)S(1)}, bf16[1,16,1792]{2,1,0:T(8,128)(2,1)S(1)}, u32[]{:S(2)}, u32[]{:S(2)}) collective-permute-start(bf16[1,16,1792]{2,1,0:T(8,128)(2,1)S(1)} %add_convert_fusion.1), channel_id=1, source_target_pairs={{0,12},{1,13},{2,14},{3,15},{4,8},{5,9},{6,10},{7,11},{8,4},{9,5},... | collective-permute-start | bytes 172040 | tf_op jit(solution)/shard_map/ppermute | solution.py:388
  51.3 7.0 %collective-permute-start.29 = (bf16[1,16,1792]{2,1,0:T(8,128)(2,1)S(1)}, bf16[1,16,1792]{2,1,0:T(8,128)(2,1)S(1)}, u32[]{:S(2)}, u32[]{:S(2)}) collective-permute-start(bf16[1,16,1792]{2,1,0:T(8,128)(2,1)S(1)} %add_convert_fusion), channel_id=1, source_target_pairs={{0,14},{1,15},{2,12},{3,13},{4,10},{5,11},{6,8},{7,9},{8,6},{9,7},... | collective-permute-start | bytes 172040 | tf_op jit(solution)/shard_map/ppermute | solution.py:388
  (16 other events, 20.7 us)

commit v3 on v0

v3 whole, which is shorter than its diff:
```python
import functools
import jax
import jax.numpy as jnp
from jax import lax
from jax.experimental import pallas as pl
from jax.experimental.pallas import tpu as pltpu
from jax.sharding import PartitionSpec as P

HEADS = 32
HEAD = 224
EXPERTS = 8
TOP = 3
LANES = 128
PARTS = 3
F32 = jnp.float32
BF16 = jnp.bfloat16
MIB = 1 << 20
VMEM = pl.BlockSpec(memory_space=pltpu.VMEM)
HBM = pl.BlockSpec(memory_space=pltpu.HBM)


def iota(shape, dim):
    return lax.broadcasted_iota(jnp.int32, shape, dim)


def nt_dot(a, b):
    return lax.dot_general(a, b, (((1,), (1,)), ((), ())), preferred_element_type=F32)


def dot(a, b):
    return jnp.dot(a, b, preferred_element_type=F32)


def one_hot(mask):
    return jnp.where(mask, 1.0, 0.0).astype(BF16)


def spread(ref, k, where, steps, rows, empty):
    out = jnp.full(where.shape, empty)
    for s in range(steps):
        for r in range(rows):
            out = jnp.where(where == s * rows + r, ref[k, s, r], out)
    return out


def tail(ids_ref, weight_ref, steps, rows):
    both = steps * rows
    lane = iota((both, LANES), 1)
    where = iota((both, 1), 0)
    mix = jnp.zeros((both, LANES), F32)
    for k in range(TOP):
        hit = spread(ids_ref, k, where, steps, rows, -1) == lane % EXPERTS
        mix = mix + jnp.where(hit, spread(weight_ref, k, where, steps, rows, 0.0), 0.0)
    out = jnp.zeros((both, LANES), F32)
    for part in range(PARTS):
        term = mix.astype(BF16).astype(F32)
        out = jnp.where(lane // EXPERTS == part, term, out)
        mix = mix - term
    return out.astype(BF16)


def attend_kernel(
    len_hbm,
    ids_hbm,
    weight_hbm,
    q_hbm,
    fresh_hbm,
    kv_hbm,
    hid_hbm,
    gain_hbm,
    resid_ref,
    out_ref,
    len_ref,
    ids_ref,
    weight_ref,
    q_ref,
    fresh_ref,
    kv_ref,
    hid_ref,
    gain_ref,
    merged,
    sems,
):
    copies = [
        pltpu.make_async_copy(source, target, sems.at[i])
        for i, (source, target) in enumerate(
            (
                (q_hbm, q_ref),
                (kv_hbm, kv_ref),
                (len_hbm, len_ref),
                (ids_hbm, ids_ref),
                (weight_hbm, weight_ref),
                (fresh_hbm, fresh_ref),
                (hid_hbm, hid_ref),
                (gain_hbm, gain_ref),
            )
        )
    ]
    for copy in copies:
        copy.start()
    steps, rows, width = q_ref.shape
    length = kv_ref.shape[2]
    both = steps * rows
    scale = HEAD ** (-0.5)
    for copy in copies:
        copy.wait()
    q = jnp.concatenate([q_ref[s].astype(F32) for s in range(steps)], axis=0)
    heads = jnp.concatenate([q[:, h * HEAD : (h + 1) * HEAD] for h in range(HEADS)], axis=0)
    heads = heads.astype(BF16)
    kv = jnp.concatenate([kv_ref[r] for r in range(rows)], axis=1)
    new = jnp.concatenate([fresh_ref[s].astype(F32) for s in range(steps)], axis=0).astype(BF16)

    sub = iota((both, rows * length), 0)
    lane = iota((both, rows * length), 1)
    limit = jnp.zeros_like(lane)
    for r in range(rows):
        limit = jnp.where(lane // length == r, len_ref[r], limit)
    valid = (lane // length == sub % rows) & (lane % length < limit)
    sub = iota((both, both), 0)
    lane = iota((both, both), 1)
    valid_new = (lane % rows == sub % rows) & (lane // rows <= sub // rows)

    old_s = (dot(heads, kv[:HEAD]) * scale).reshape(HEADS, both, rows * length)
    new_s = (nt_dot(heads, new[:, :HEAD]) * scale).reshape(HEADS, both, both)
    old_s = jnp.where(valid[None], old_s, -1e30)
    new_s = jnp.where(valid_new[None], new_s, -1e30)
    top = jnp.maximum(
        jnp.max(old_s, axis=-1, keepdims=True), jnp.max(new_s, axis=-1, keepdims=True)
    )
    old_e = jnp.exp(old_s - top)
    new_e = jnp.exp(new_s - top)
    total = jnp.sum(old_e, axis=-1, keepdims=True) + jnp.sum(new_e, axis=-1, keepdims=True)
    old_w = (old_e / total).reshape(HEADS * both, rows * length).astype(BF16)
    new_w = (new_e / total).reshape(HEADS * both, both).astype(BF16)
    attended = nt_dot(old_w, kv[HEAD:]) + dot(new_w, new[:, HEAD:])
    for h in range(HEADS):
        merged[:, h * HEAD : (h + 1) * HEAD] = attended[h * both : (h + 1) * both]
    hidden = jnp.concatenate([hid_ref[s].astype(F32) for s in range(steps)], axis=0)
    resid = hidden + merged[...]
    resid_ref[...] = resid
    meansq = jnp.mean(resid * resid, axis=-1, keepdims=True)
    gain = gain_ref[...].astype(F32)
    gain = jnp.concatenate([gain[i : i + 1] for i in range(width // LANES)], axis=1)
    normed = resid * lax.rsqrt(meansq + 1e-06) * gain
    out_ref[:, :width] = normed.astype(BF16)
    out_ref[:, width:] = tail(ids_ref, weight_ref, steps, rows)


def attend(cache_len, ids, weights, queries, fresh, kv_cache, hidden_state, norm_gain):
    steps, rows, width = queries.shape
    kv = kv_cache.transpose(0, 2, 1)
    gain = norm_gain.reshape(width // LANES, LANES)
    return pl.pallas_call(
        attend_kernel,
        out_shape=(
            jax.ShapeDtypeStruct((steps * rows, width), F32),
            jax.ShapeDtypeStruct((steps * rows, width + LANES), BF16),
        ),
        in_specs=[HBM] * 8,
        out_specs=(VMEM, VMEM),
        scratch_shapes=[
            pltpu.SMEM(cache_len.shape, jnp.int32),
            pltpu.SMEM(ids.shape, jnp.int32),
            pltpu.SMEM(weights.shape, F32),
            pltpu.VMEM(queries.shape, BF16),
            pltpu.VMEM(fresh.shape, BF16),
            pltpu.VMEM(kv.shape, BF16),
            pltpu.VMEM(hidden_state.shape, BF16),
            pltpu.VMEM(gain.shape, BF16),
            pltpu.VMEM((steps * rows, width), F32),
            pltpu.SemaphoreType.DMA((8,)),
        ],
        compiler_params=pltpu.CompilerParams(vmem_limit_bytes=24 * MIB),
        cost_estimate=pl.CostEstimate(
            flops=300_000_000, bytes_accessed=2_000_000, transcendentals=131072
        ),
        name="attend",
    )(cache_len, ids, weights, queries, fresh, kv, hidden_state, gain)


def stage_kernel(gu_hbm, dn_hbm, after, gu, dn, sems):
    step = dn.shape[0] // 4
    pairs = []
    for i in range(4):
        part = pl.ds(i * step, step)
        pairs.append((gu_hbm.at[0, 0, part], gu.at[0, part]))
        pairs.append((gu_hbm.at[0, 1, part], gu.at[1, part]))
        pairs.append((dn_hbm.at[0, part], dn.at[part]))
    copies = [pltpu.make_async_copy(a, b, sems.at[i]) for i, (a, b) in enumerate(pairs)]
    for copy in copies:
        copy.start()
    for copy in copies:
        copy.wait()


def stage(gate_up, down, after):
    return pl.pallas_call(
        stage_kernel,
        out_shape=(
            jax.ShapeDtypeStruct(gate_up.shape[1:], BF16),
            jax.ShapeDtypeStruct(down.shape[1:], BF16),
        ),
        in_specs=[HBM, HBM, VMEM],
        out_specs=(VMEM, VMEM),
        scratch_shapes=[pltpu.SemaphoreType.DMA((12,))],
        compiler_params=pltpu.CompilerParams(vmem_limit_bytes=24 * MIB),
        cost_estimate=pl.CostEstimate(flops=0, bytes_accessed=22_000_000, transcendentals=0),
        name="stage",
    )(gate_up, down, after)


def expert_kernel(rows_ref, gu, dn, out_ref):
    width = out_ref.shape[1]
    expert = lax.axis_index("afd") // (lax.axis_size("afd") // EXPERTS)
    ends = rows_ref[:, width:].astype(F32)
    lane = iota(ends.shape, 1)
    mine = (lane % EXPERTS == expert) & (lane < PARTS * EXPERTS)
    weight = jnp.sum(jnp.where(mine, ends, 0.0), axis=1, keepdims=True)
    x = rows_ref[:, :width]
    gate = nt_dot(x, gu[0])
    upper = nt_dot(x, gu[1])
    act = (gate / (1.0 + jnp.exp(-gate)) * upper).astype(BF16)
    part = dot(act, dn[...]).astype(BF16).astype(F32)
    out_ref[...] = (part * weight).astype(BF16)


def experts(rows, gu, dn):
    count, width = rows.shape[0], dn.shape[1]
    return pl.pallas_call(
        expert_kernel,
        out_shape=jax.ShapeDtypeStruct((count, width), BF16),
        in_specs=[VMEM] * 3,
        out_specs=VMEM,
        compiler_params=pltpu.CompilerParams(vmem_limit_bytes=32 * MIB),
        cost_estimate=pl.CostEstimate(
            flops=1_500_000_000, bytes_accessed=12_000_000, transcendentals=16384
        ),
        name="experts",
    )(rows, gu, dn)


def per_device(
    queries,
    fresh,
    kv_cache,
    cache_len,
    hidden_state,
    norm_gain,
    expert_ids,
    route_weight,
    gate_up,
    down,
):
    ids = expert_ids.transpose(2, 0, 1)
    weights = route_weight.transpose(2, 0, 1)
    resid, packed = attend(
        cache_len, ids, weights, queries, fresh, kv_cache, hidden_state, norm_gain
    )
    gathered = lax.all_gather(packed, "afd", axis=0, tiled=True)
    gu, dn = stage(gate_up, down, resid)
    weighted = experts(gathered, gu, dn)
    combined = lax.psum_scatter(weighted, "afd", scatter_dimension=0, tiled=True)
    return (resid + combined.astype(F32)).astype(BF16).reshape(queries.shape)


def solution(mesh):
    placed = (
        P(None, ("group", "afd"), None),
        P(None, ("group", "afd"), None),
        P(("group", "afd"), None, None),
        P(("group", "afd")),
        P(None, ("group", "afd"), None),
        P(),
        P(None, ("group", "afd"), None),
        P(None, ("group", "afd"), None),
        P("afd", None, None, None),
        P("afd", None, None),
    )
    return jax.shard_map(
        per_device,
        mesh=mesh,
        in_specs=placed,
        out_specs=P(None, ("group", "afd"), None),
        check_vma=False,
    )
```

time: 86.7 us -> 139 us (1.60)
  waiting for transfers between devices: 28.5 us -> 90.1 us
  matrix products: 24.2 us -> 0 us
  starting transfers between devices: 19 us -> 0.04 us
  local copies, waits for them, and re-layouts: 8.03 us -> 23.6 us
  between operations: 0.31 us -> 13.4 us
  Pallas kernels: 0 us -> 10 us
  other arithmetic: 5.74 us -> 0.92 us
    reduce_scatter x0 -> x1, waiting for transfers between devices: none -> 59.3 us  [per_device(): lax.psum_scatter(weighted, 'afd', scatter_dimension=0, tiled=True)]
    all_gather x0 -> x1, waiting for transfers between devices: none -> 30.8 us  [per_device(): gathered = lax.all_gather(packed, 'afd', axis=0, tiled=True)]
    all_to_all x4 -> x0, waiting for transfers between devices: 28.5 us -> none  [the longest x2 14.8 us: per_device(): lax.all_to_all(partial_value, 'afd', split_axis=0, concat_axis=0, tiled=T...]
    dot_general x17 -> x0, matrix products: 24.2 us -> none  [the longest x2 11.5 us: per_device(): jnp.dot(act, w_down, preferred_element_type=jnp.float32)]
    unnamed x8 -> x30, local copies, waits for them, and re-layouts: 0.03 us -> 22.9 us
    all_to_all x4 -> x0, starting transfers between devices: 19 us -> none  [the longest x2 11.3 us: per_device(): lax.all_to_all(outgoing, 'afd', split_axis=0, concat_axis=0, tiled=True)]
    pallas_call x0 -> x3, Pallas kernels: none -> 10 us  [the longest x1 4.42 us: experts(): pl.pallas_call(expert_kernel, out_shape=jax.ShapeDtypeStruct((count, widt...]
    slice x8 -> x0, local copies, waits for them, and re-layouts: 2.17 us -> none  [the longest x3 0.95 us: per_device(): ids_now = expert_ids[step]]
  transfers between devices with their start and end apart: 4 -> 2, of which waited for: 4 -> 2; matrix products, arithmetic and copies ran while one was open for 28% -> 0% of each run, Pallas kernels for 0% -> 2%
where the time goes in v3:
time: 139 us; the launch traced here: 138 us
  waiting for transfers between devices  90.1 us (65%)
  local copies, waits for them, and re-layouts  23.6 us (17%)
  between operations  13.4 us (10%)
  Pallas kernels  10 us (7%)
    reduce_scatter x1, waiting for transfers between devices, per_device(): lax.psum_scatter(weighted, 'afd', scatter_dimension=0, tiled=True)  59.3 us
    all_gather x1, waiting for transfers between devices, per_device(): gathered = lax.all_gather(packed, 'afd', axis=0, tiled=True)  30.8 us
    unnamed x30, local copies, waits for them, and re-layouts  22.9 us
    pallas_call x1, Pallas kernels, experts(): pl.pallas_call(expert_kernel, out_shape=jax.ShapeDtypeStruct((count, widt...  4.42 us
    pallas_call x1, Pallas kernels, attend(): pl.pallas_call(attend_kernel, out_shape=(jax.ShapeDtypeStruct((steps * ro...  2.81 us
    pallas_call x1, Pallas kernels, stage(): pl.pallas_call(stage_kernel, out_shape=(jax.ShapeDtypeStruct(gate_up.shap...  2.79 us
  transfers between devices with their start and end apart: 2, of which 2 were waited for; matrix products, arithmetic and copies ran while one was open for 0% of the time, Pallas kernels for 2%

profile of v3, /device:TPU:0, one launch (start us, length us, event | category | flops | bytes accessed | tf_op | source)
XLA Modules:
  0.0 138.1 jit_solution(6402953985812582750)
XLA Ops:
  6.5 1.0 copy-done.7
  7.6 0.9 copy-done.8
  8.5 0.9 copy-done.9
  9.4 0.7 copy-done.10
  10.1 0.7 copy-done.11
  10.8 0.7 copy-done.12
  11.5 0.7 copy-done.13
  12.1 0.7 copy-done.14
  12.8 2.8 %attend.1 = (f32[8,7168]{1,0:T(8,128)S(1)}, bf16[8,7296]{1,0:T(8,128)(2,1)}) custom-call(s32[4]{0:T(128)S(1)} %copy-done.14, s32[3,2,4]{2,1,0:T(2,128)S(1)} %bitcast.6, f32[3,2,4]{2,1,0:T(2,128)S(1)} %bitcast.7, bf16[2,4,7168]{2,1,0:T(4,128)(2,1)S(1)} %copy-done.8, bf16[2,4,448]{2,1,0:T(4,128)(2,1)S(1)} %copy-done.11, bf16[4,448,128]{2,1,0:T(8,128)(2,1)S(1)} %bitcast.4, ...), custom_call_target="tpu_custom_call" | custom-call | flops 300000000 | bytes 2000000 | tf_op jit(solution)/shard_map/attend/pallas_call | solution.py:153
  15.6 0.0 all-gather.2.cloned.1.call-update
  15.6 0.0 reduce-scatter.2.cloned.1.call-start
  15.7 3.1 %copy-done.2 = bf16[1,2,256,7168]{3,2,1,0:T(8,128)(2,1)S(1)} copy-done((bf16[1,2,256,7168]{3,2,1,0:T(8,128)(2,1)S(1)}, bf16[1,2,256,7168]{3,2,1,0:T(8,128)(2,1)}, u32[]{:S(2)}) %copy-start.2) | copy-done | bytes 7340056
  18.8 2.0 %copy-done.5 = bf16[1,256,7168]{2,1,0:T(8,128)(2,1)S(1)} copy-done((bf16[1,256,7168]{2,1,0:T(8,128)(2,1)S(1)}, bf16[1,256,7168]{2,1,0:T(8,128)(2,1)}, u32[]{:S(2)}) %copy-start.5) | copy-done | bytes 3670040
  20.8 2.8 %stage.1 = (bf16[2,256,7168]{2,1,0:T(8,128)(2,1)S(1)}, bf16[256,7168]{1,0:T(8,128)(2,1)S(1)}) custom-call(bf16[1,2,256,7168]{3,2,1,0:T(8,128)(2,1)S(1)} %copy-done.2, bf16[1,256,7168]{2,1,0:T(8,128)(2,1)S(1)} %copy-done.5, f32[8,7168]{1,0:T(8,128)S(1)} %get-tuple-element.9.after), custom_call_target="tpu_custom_call" | custom-call | bytes 22000000 | tf_op jit(solution)/shard_map/stage/pallas_call | solution.py:197
  23.6 2.9 %copy-done = bf16[2,256,7168]{2,1,0:T(8,128)(2,1)} copy-done((bf16[2,256,7168]{2,1,0:T(8,128)(2,1)}, bf16[2,256,7168]{2,1,0:T(8,128)(2,1)S(1)}, u32[]{:S(2)}) %copy-start) | copy-done | bytes 7340056
  26.6 1.9 %copy-done.3 = bf16[256,7168]{1,0:T(8,128)(2,1)} copy-done((bf16[256,7168]{1,0:T(8,128)(2,1)}, bf16[256,7168]{1,0:T(8,128)(2,1)S(1)}, u32[]{:S(2)}) %copy-start.3) | copy-done | bytes 3670040
  28.5 30.8 %all-gather.2.cloned.1.call-done.rows_ref = bf16[128,7296]{1,0:T(8,128)(2,1)} async-done(((bf16[8,7296]{1,0:T(8,128)(2,1)}), bf16[128,7296]{1,0:T(8,128)(2,1)}) %all-gather.2.cloned.1.call-update) | async-done | bytes 1867792 | tf_op jit(solution)/shard_map/all_gather | solution.py:259
  59.2 3.1 %copy-done.1 = bf16[2,256,7168]{2,1,0:T(8,128)(2,1)S(1)} copy-done((bf16[2,256,7168]{2,1,0:T(8,128)(2,1)S(1)}, bf16[2,256,7168]{2,1,0:T(8,128)(2,1)}, u32[]{:S(2)}) %copy-start.1) | copy-done | bytes 7340056
  62.3 2.0 %copy-done.4 = bf16[256,7168]{1,0:T(8,128)(2,1)S(1)} copy-done((bf16[256,7168]{1,0:T(8,128)(2,1)S(1)}, bf16[256,7168]{1,0:T(8,128)(2,1)}, u32[]{:S(2)}) %copy-start.4) | copy-done | bytes 3670040
  64.4 1.5 %copy-done.6 = bf16[128,7296]{1,0:T(8,128)(2,1)S(1)} copy-done((bf16[128,7296]{1,0:T(8,128)(2,1)S(1)}, bf16[128,7296]{1,0:T(8,128)(2,1)}, u32[]{:S(2)}) %copy-start.6) | copy-done | bytes 1867800
  65.9 4.4 %experts.1 = bf16[128,7168]{1,0:T(8,128)(2,1)} custom-call(bf16[128,7296]{1,0:T(8,128)(2,1)S(1)} %copy-done.6, bf16[2,256,7168]{2,1,0:T(8,128)(2,1)S(1)} %copy-done.1, bf16[256,7168]{1,0:T(8,128)(2,1)S(1)} %copy-done.4), custom_call_target="tpu_custom_call" | custom-call | flops 1500000000 | bytes 12000000 | tf_op jit(solution)/shard_map/experts/pallas_call | solution.py:229
  70.3 59.3 %reduce-scatter.2.cloned.1.call-done = bf16[8,7168]{1,0:T(8,128)(2,1)} async-done(((bf16[128,7168]{1,0:T(8,128)(2,1)}), bf16[8,7168]{1,0:T(8,128)(2,1)}) %reduce-scatter.2.cloned.1.call-update) | async-done | bytes 114704 | tf_op jit(solution)/shard_map/reduce_scatter | solution.py:262
  129.6 0.9 add_convert_fusion
  130.5 0.7 reshape.7
  (17 shorter events, 0.0 us)
Async XLA Ops:
  6.5 52.7 %all-gather.2.cloned.1.call-start = ((), (), s32[]{:S(2)}) async-start(), calls=%async_computation.1 | async-start | bytes 1984512 | tf_op jit(solution)/shard_map/all_gather | solution.py:259
  6.5 1.0 copy-start.7
  7.6 0.9 copy-start.8
  8.5 0.9 copy-start.9
  9.4 0.7 copy-start.10
  10.1 0.7 copy-start.11
  10.8 0.7 copy-start.12
  11.4 0.7 copy-start.13
  12.1 0.7 copy-start.14
  15.6 114.0 %reduce-scatter.2.cloned.1.call-start = ((), (), s32[]{:S(2)}) async-start(), calls=%async_computation.2 | async-start | bytes 1949696 | tf_op jit(solution)/shard_map/reduce_scatter | solution.py:262
  15.7 3.1 %copy-start.2 = (bf16[1,2,256,7168]{3,2,1,0:T(8,128)(2,1)S(1)}, bf16[1,2,256,7168]{3,2,1,0:T(8,128)(2,1)}, u32[]{:S(2)}) copy-start(bf16[1,2,256,7168]{3,2,1,0:T(8,128)(2,1)} %gu_hbm.1) | copy-start | bytes 22020100
  18.8 2.0 %copy-start.5 = (bf16[1,256,7168]{2,1,0:T(8,128)(2,1)S(1)}, bf16[1,256,7168]{2,1,0:T(8,128)(2,1)}, u32[]{:S(2)}) copy-start(bf16[1,256,7168]{2,1,0:T(8,128)(2,1)} %dn_hbm.1) | copy-start | bytes 11010052
  23.6 3.0 %copy-start = (bf16[2,256,7168]{2,1,0:T(8,128)(2,1)}, bf16[2,256,7168]{2,1,0:T(8,128)(2,1)S(1)}, u32[]{:S(2)}) copy-start(bf16[2,256,7168]{2,1,0:T(8,128)(2,1)S(1)} %get-tuple-element.11.gu) | copy-start | bytes 22020100
  26.6 1.9 %copy-start.3 = (bf16[256,7168]{1,0:T(8,128)(2,1)}, bf16[256,7168]{1,0:T(8,128)(2,1)S(1)}, u32[]{:S(2)}) copy-start(bf16[256,7168]{1,0:T(8,128)(2,1)S(1)} %get-tuple-element.12.dn) | copy-start | bytes 11010052
  59.2 3.1 %copy-start.1 = (bf16[2,256,7168]{2,1,0:T(8,128)(2,1)S(1)}, bf16[2,256,7168]{2,1,0:T(8,128)(2,1)}, u32[]{:S(2)}) copy-start(bf16[2,256,7168]{2,1,0:T(8,128)(2,1)} %copy-done) | copy-start | bytes 22020100
  62.3 2.0 %copy-start.4 = (bf16[256,7168]{1,0:T(8,128)(2,1)S(1)}, bf16[256,7168]{1,0:T(8,128)(2,1)}, u32[]{:S(2)}) copy-start(bf16[256,7168]{1,0:T(8,128)(2,1)} %copy-done.3) | copy-start | bytes 11010052
  64.4 1.5 %copy-start.6 = (bf16[128,7296]{1,0:T(8,128)(2,1)S(1)}, bf16[128,7296]{1,0:T(8,128)(2,1)}, u32[]{:S(2)}) copy-start(bf16[128,7296]{1,0:T(8,128)(2,1)} %all-gather.2.cloned.1.call-done.rows_ref) | copy-start | bytes 5603332
Sparse Core Ops, SparseCore 0:
  15.8 43.4 all-gather.1
  70.4 59.1 reduce-scatter.1

commit v4 on v2

v4 whole, which is shorter than its diff:
```python
import functools
import jax
import jax.numpy as jnp
from jax import lax
from jax.experimental import pallas as pl
from jax.experimental.pallas import tpu as pltpu
from jax.sharding import PartitionSpec as P

HEADS = 32
HEAD = 224
EXPERTS = 8
TOP = 3
CAP = 2
LINES = 16
LANES = 128
F32 = jnp.float32
BF16 = jnp.bfloat16
MIB = 1 << 20
VMEM = pl.BlockSpec(memory_space=pltpu.VMEM)
HBM = pl.BlockSpec(memory_space=pltpu.HBM)
BATCHES = ((0,), (1,))


def iota(shape, dim):
    return lax.broadcasted_iota(jnp.int32, shape, dim)


def in_hbm(*arrays):
    return [pltpu.with_memory_space_constraint(x, pltpu.HBM) for x in arrays]


def nt_dot(a, b):
    return lax.dot_general(a, b, (((1,), (1,)), ((), ())), preferred_element_type=F32)


def dot(a, b):
    return jnp.dot(a, b, preferred_element_type=F32)


def one_hot(mask):
    return jnp.where(mask, 1.0, 0.0).astype(BF16)


def spread(ref, k, where, steps, rows, empty):
    out = jnp.full(where.shape, empty)
    for s in range(steps):
        for r in range(rows):
            out = jnp.where(where == s * rows + r, ref[k, s, r], out)
    return out


def picks_of(ids_ref, batch, steps, rows):
    pieces = LINES // (len(batch) * CAP)
    both = steps * rows
    shape = (EXPERTS * LINES, pieces * both)
    line = iota(shape, 0)
    col = iota(shape, 1)
    where = iota((1, pieces * both), 1) % both
    expert = line // LINES
    named = jnp.zeros(shape, jnp.bool_)
    for k in range(TOP):
        named = named | (spread(ids_ref, k, where, steps, rows, -1) == expert)
    at = iota((pieces * both, pieces * both), 0)
    to = iota((pieces * both, pieces * both), 1)
    rank = dot(one_hot(named), one_hot((at // rows == to // rows) & (at < to)))
    slot = (line % CAP).astype(F32)
    step = (line // CAP) % len(batch) + batch[0]
    piece = line // (CAP * len(batch)) % pieces
    same = (step == col // rows % steps) & (piece == col // both)
    return one_hot(named & same & (rank == slot))


def attend_kernel(
    len_hbm,
    ids_hbm,
    q_hbm,
    fresh_hbm,
    kv_hbm,
    hid_hbm,
    gain_hbm,
    gu_hbm,
    dn_hbm,
    gu_ref,
    dn_ref,
    resid_ref,
    *rest,
):
    outs = rest[: len(BATCHES)]
    len_ref, ids_ref, q_ref, fresh_ref, kv_ref, hid_ref, gain_ref, merged, sems, large = rest[
        len(outs) :
    ]
    copies = [
        pltpu.make_async_copy(source, target, sems.at[i])
        for i, (source, target) in enumerate(
            (
                (q_hbm, q_ref),
                (kv_hbm, kv_ref),
                (len_hbm, len_ref),
                (ids_hbm, ids_ref),
                (fresh_hbm, fresh_ref),
                (hid_hbm, hid_ref),
                (gain_hbm, gain_ref),
            )
        )
    ]
    step = dn_ref.shape[0] // 4
    weights = []
    for i in range(4):
        part = pl.ds(i * step, step)
        weights.append((gu_hbm.at[0, 0, part], gu_ref.at[0, part]))
        weights.append((gu_hbm.at[0, 1, part], gu_ref.at[1, part]))
        weights.append((dn_hbm.at[0, part], dn_ref.at[part]))
    weights = [pltpu.make_async_copy(a, b, large.at[i]) for i, (a, b) in enumerate(weights)]
    for copy in copies + weights:
        copy.start()
    steps, rows, width = q_ref.shape
    length = kv_ref.shape[2]
    both = steps * rows
    scale = HEAD ** (-0.5)
    for copy in copies:
        copy.wait()
    q = jnp.concatenate([q_ref[s].astype(F32) for s in range(steps)], axis=0)
    heads = jnp.concatenate([q[:, h * HEAD : (h + 1) * HEAD] for h in range(HEADS)], axis=0)
    heads = heads.astype(BF16)
    kv = jnp.concatenate([kv_ref[r] for r in range(rows)], axis=1)
    new = jnp.concatenate([fresh_ref[s].astype(F32) for s in range(steps)], axis=0).astype(BF16)

    sub = iota((both, rows * length), 0)
    lane = iota((both, rows * length), 1)
    limit = jnp.zeros_like(lane)
    for r in range(rows):
        limit = jnp.where(lane // length == r, len_ref[r], limit)
    valid = (lane // length == sub % rows) & (lane % length < limit)
    sub = iota((both, both), 0)
    lane = iota((both, both), 1)
    valid_new = (lane % rows == sub % rows) & (lane // rows <= sub // rows)

    old_s = (dot(heads, kv[:HEAD]) * scale).reshape(HEADS, both, rows * length)
    new_s = (nt_dot(heads, new[:, :HEAD]) * scale).reshape(HEADS, both, both)
    old_s = jnp.where(valid[None], old_s, -1e30)
    new_s = jnp.where(valid_new[None], new_s, -1e30)
    top = jnp.maximum(
        jnp.max(old_s, axis=-1, keepdims=True), jnp.max(new_s, axis=-1, keepdims=True)
    )
    old_e = jnp.exp(old_s - top)
    new_e = jnp.exp(new_s - top)
    total = jnp.sum(old_e, axis=-1, keepdims=True) + jnp.sum(new_e, axis=-1, keepdims=True)
    old_w = (old_e / total).reshape(HEADS * both, rows * length).astype(BF16)
    new_w = (new_e / total).reshape(HEADS * both, both).astype(BF16)
    attended = nt_dot(old_w, kv[HEAD:]) + dot(new_w, new[:, HEAD:])
    for h in range(HEADS):
        merged[:, h * HEAD : (h + 1) * HEAD] = attended[h * both : (h + 1) * both]
    hidden = jnp.concatenate([hid_ref[s].astype(F32) for s in range(steps)], axis=0)
    resid = hidden + merged[...]
    resid_ref[...] = resid
    meansq = jnp.mean(resid * resid, axis=-1, keepdims=True)
    gain = gain_ref[...].astype(F32)
    gain = jnp.concatenate([gain[i : i + 1] for i in range(width // LANES)], axis=1)
    normed = resid * lax.rsqrt(meansq + 1e-06) * gain
    for batch, out in zip(BATCHES, outs):
        pieces = LINES // (len(batch) * CAP)
        piece = width // pieces
        stacked = jnp.concatenate(
            [normed[:, k * piece : (k + 1) * piece] for k in range(pieces)], axis=0
        ).astype(BF16)
        picks = picks_of(ids_ref, batch, steps, rows)
        out[...] = dot(picks, stacked).astype(BF16).reshape(out.shape)
    for copy in weights:
        copy.wait()


def attend(cache_len, ids, queries, fresh, kv_cache, hidden_state, norm_gain, gate_up, down):
    steps, rows, width = queries.shape
    chunks = []
    for batch in BATCHES:
        shape = (EXPERTS, LINES, width * len(batch) * CAP // LINES)
        chunks.append(jax.ShapeDtypeStruct(shape, BF16))
    kv = kv_cache.transpose(0, 2, 1)
    gain = norm_gain.reshape(width // LANES, LANES)
    gu, dn, resid, *chunks = pl.pallas_call(
        attend_kernel,
        out_shape=(
            jax.ShapeDtypeStruct(gate_up.shape[1:], BF16),
            jax.ShapeDtypeStruct(down.shape[1:], BF16),
            jax.ShapeDtypeStruct((steps * rows, width), F32),
            *chunks,
        ),
        in_specs=[HBM] * 9,
        out_specs=(VMEM,) * (3 + len(chunks)),
        scratch_shapes=[
            pltpu.SMEM(cache_len.shape, jnp.int32),
            pltpu.SMEM(ids.shape, jnp.int32),
            pltpu.VMEM(queries.shape, BF16),
            pltpu.VMEM(fresh.shape, BF16),
            pltpu.VMEM(kv.shape, BF16),
            pltpu.VMEM(hidden_state.shape, BF16),
            pltpu.VMEM(gain.shape, BF16),
            pltpu.VMEM((steps * rows, width), F32),
            pltpu.SemaphoreType.DMA((7,)),
            pltpu.SemaphoreType.DMA((12,)),
        ],
        compiler_params=pltpu.CompilerParams(vmem_limit_bytes=32 * MIB),
        cost_estimate=pl.CostEstimate(
            flops=300_000_000, bytes_accessed=24_000_000, transcendentals=131072
        ),
        name="attend",
    )(*in_hbm(cache_len, ids, queries, fresh, kv, hidden_state, gain, gate_up, down))
    return gu, dn, resid, chunks


def mixing(ids_ref, weight_ref, batch, steps, rows, chips):
    pieces = LINES // (len(batch) * CAP)
    both = len(batch) * rows
    shape = (both, chips * LINES)
    line = iota(shape, 1)
    sub = iota(shape, 0)
    expert = line // LINES // (chips // EXPERTS)
    where = iota((both, 1), 0) + batch[0] * rows
    named = jnp.zeros(shape, F32)
    mix = jnp.zeros(shape, F32)
    for k in range(TOP):
        hit = spread(ids_ref, k, where, steps, rows, -1) == expert
        weight = spread(weight_ref, k, where, steps, rows, 0.0)
        named = named + jnp.where(hit, 1.0, 0.0)
        mix = mix + jnp.where(hit, weight, 0.0)
    at = iota((both, both), 1)
    to = iota((both, both), 0)
    rank = dot(one_hot((at // rows == to // rows) & (at < to)), named.astype(BF16))
    same = (line // CAP) % len(batch) == sub // rows
    mix = jnp.where((rank == (line % CAP).astype(F32)) & same, mix, 0.0)
    high = mix.astype(BF16).astype(F32)
    middle = (mix - high).astype(BF16).astype(F32)
    low = mix - high - middle
    k_of = line // (len(batch) * CAP) % pieces
    parts = [
        jnp.where(k_of == k, part, 0.0) for part in (high, middle, low) for k in range(pieces)
    ]
    return jnp.concatenate(parts, axis=0).astype(BF16)


def mix_kernel(chips, ids_hbm, weight_hbm, *refs):
    mixes = refs[: len(BATCHES)]
    ids_ref, weight_ref, sems = refs[len(BATCHES) :]
    copies = [
        pltpu.make_async_copy(ids_hbm, ids_ref, sems.at[0]),
        pltpu.make_async_copy(weight_hbm, weight_ref, sems.at[1]),
    ]
    for copy in copies:
        copy.start()
    for copy in copies:
        copy.wait()
    _, steps, rows = ids_ref.shape
    for batch, mix in zip(BATCHES, mixes):
        mix[...] = mixing(ids_ref, weight_ref, batch, steps, rows, chips)


def mixers(chips, ids, weights):
    rows = ids.shape[2]
    mixes = [
        jax.ShapeDtypeStruct((3 * LINES // CAP * rows, chips * LINES), BF16) for _ in BATCHES
    ]
    return pl.pallas_call(
        functools.partial(mix_kernel, chips),
        out_shape=mixes,
        in_specs=[HBM] * 2,
        out_specs=[VMEM] * len(mixes),
        scratch_shapes=[
            pltpu.SMEM(ids.shape, jnp.int32),
            pltpu.SMEM(weights.shape, F32),
            pltpu.SemaphoreType.DMA((2,)),
        ],
        compiler_params=pltpu.CompilerParams(vmem_limit_bytes=16 * MIB),
        cost_estimate=pl.CostEstimate(flops=100_000_000, bytes_accessed=4_000_000, transcendentals=0),
        name="mixers",
    )(*in_hbm(ids, weights))


def expert_kernel(per, own_ref, other_ref, gu, dn, mine_ref, theirs_ref):
    chips, lines, piece = own_ref.shape
    pieces = lines // per
    half = chips * per
    n = chips * lines
    row = iota((n, n), 0)
    col = iota((n, n), 1)
    order = one_hot(col == row // per % chips * lines + row // half * per + row % per)
    sides = [dot(order, ref[...].reshape(n, piece)).astype(BF16) for ref in (own_ref, other_ref)]
    gate = upper = None
    for k in range(pieces):
        x = jnp.concatenate([side[k * half : (k + 1) * half] for side in sides], axis=0)
        cols = pl.ds(k * piece, piece)
        g, u = nt_dot(x, gu[0, :, cols]), nt_dot(x, gu[1, :, cols])
        gate, upper = (g, u) if k == 0 else (gate + g, upper + u)
    act = (gate / (1.0 + jnp.exp(-gate)) * upper).astype(BF16)
    mine = []
    theirs = []
    for k in range(pieces):
        part = dot(act, dn[:, k * piece : (k + 1) * piece]).astype(BF16)
        mine.append(part[:half])
        theirs.append(part[half:])
    back = one_hot(row == col // per % chips * lines + col // half * per + col % per)
    for parts, ref in ((theirs, theirs_ref), (mine, mine_ref)):
        lines_now = dot(back, jnp.concatenate(parts, axis=0)).astype(BF16)
        ref[...] = lines_now.reshape(ref.shape)


def experts(own, other, gu, dn, per):
    shape = jax.ShapeDtypeStruct(own.shape, BF16)
    return pl.pallas_call(
        functools.partial(expert_kernel, per),
        out_shape=(shape, shape),
        in_specs=[VMEM] * 4,
        out_specs=(VMEM, VMEM),
        compiler_params=pltpu.CompilerParams(vmem_limit_bytes=32 * MIB),
        cost_estimate=pl.CostEstimate(
            flops=800_000_000, bytes_accessed=12_000_000, transcendentals=16384
        ),
        name="experts",
    )(own, other, gu, dn)


def combine_kernel(resid_ref, *refs):
    out_ref = refs[-1]
    _, rows, width = out_ref.shape
    for i, batch in enumerate(BATCHES):
        left = refs[2 * i][...]
        back_ref = refs[2 * i + 1]
        chips, lines, piece = back_ref.shape
        pieces = width // piece
        both = len(batch) * rows
        product = dot(left, back_ref[...].reshape(chips * lines, piece))
        n = pieces * both
        total = product[:n] + product[n : 2 * n] + product[2 * n :]
        first = batch[0] * rows
        for k in range(pieces):
            cols = pl.ds(k * piece, piece)
            done = resid_ref[first : first + both, cols] + total[k * both : (k + 1) * both]
            done = done.astype(BF16)
            for j, s in enumerate(batch):
                out_ref[s, :, cols] = done[j * rows : (j + 1) * rows]


def combine(shape, resid, mixes, backs):
    operands = [x for pair in zip(mixes, backs) for x in pair]
    return pl.pallas_call(
        combine_kernel,
        out_shape=jax.ShapeDtypeStruct(shape, BF16),
        in_specs=[VMEM] * (1 + len(operands)),
        out_specs=VMEM,
        compiler_params=pltpu.CompilerParams(vmem_limit_bytes=24 * MIB),
        cost_estimate=pl.CostEstimate(
            flops=100_000_000, bytes_accessed=1_000_000, transcendentals=0
        ),
        name="combine",
    )(resid, *operands)


def per_device(
    queries,
    fresh,
    kv_cache,
    cache_len,
    hidden_state,
    norm_gain,
    expert_ids,
    route_weight,
    gate_up,
    down,
):
    owners = lax.axis_size("afd")
    chips = owners // 2
    swap = [(i, i ^ 1) for i in range(owners)]
    same_core = [[2 * p + c for p in range(chips)] for c in range(2)]

    def to_chips(chunks):
        return lax.all_to_all(
            chunks, "afd", split_axis=0, concat_axis=0, axis_index_groups=same_core, tiled=True
        )

    ids = expert_ids.transpose(2, 0, 1)
    weights = route_weight.transpose(2, 0, 1)
    gu, dn, resid, sent = attend(
        cache_len, ids, queries, fresh, kv_cache, hidden_state, norm_gain, gate_up, down
    )
    mixes = mixers(chips, ids, weights)
    if chips > EXPERTS:
        sent = [jnp.repeat(chunks, chips // EXPERTS, axis=0) for chunks in sent]
    received = [to_chips(chunks) for chunks in sent]
    backs = []
    for batch, own in zip(BATCHES, received):
        other = lax.ppermute(own, "afd", swap)
        mine, theirs = experts(own, other, gu, dn, len(batch) * CAP)
        summed = mine.astype(F32) + lax.ppermute(theirs, "afd", swap).astype(F32)
        backs.append(to_chips(summed.astype(BF16)))
    return combine(queries.shape, resid, mixes, backs)


def solution(mesh):
    placed = (
        P(None, ("group", "afd"), None),
        P(None, ("group", "afd"), None),
        P(("group", "afd"), None, None),
        P(("group", "afd")),
        P(None, ("group", "afd"), None),
        P(),
        P(None, ("group", "afd"), None),
        P(None, ("group", "afd"), None),
        P("afd", None, None, None),
        P("afd", None, None),
    )
    return jax.shard_map(
        per_device,
        mesh=mesh,
        in_specs=placed,
        out_specs=P(None, ("group", "afd"), None),
        check_vma=False,
    )
```

time: 59.7 us -> 76.7 us (1.28)
  starting transfers between devices: 28 us -> 10.9 us
  blocking collectives: 0 us -> 15.5 us
  waiting for transfers between devices: 9.67 us -> 24.2 us
  Pallas kernels: 9.85 us -> 14 us
  local copies, waits for them, and re-layouts: 11.4 us -> 9.97 us
  other arithmetic: 0.13 us -> 1.49 us
    ppermute x30 -> x4, starting transfers between devices: 28 us -> 0.73 us  [the longest x2 0.66 us: per_device(): summed = mine.astype(F32) + lax.ppermute(theirs, 'afd', swap).astype(F32)]
    all_to_all x0 -> x3, waiting for transfers between devices: none -> 24.2 us  [to_chips(): lax.all_to_all(chunks, 'afd', split_axis=0, concat_axis=0, axis_index_gro...]
    all_to_all x0 -> x1, blocking collectives: none -> 15.5 us  [to_chips(): lax.all_to_all(chunks, 'afd', split_axis=0, concat_axis=0, axis_index_gro...]
    all_to_all x0 -> x3, starting transfers between devices: none -> 10.2 us  [to_chips(): lax.all_to_all(chunks, 'afd', split_axis=0, concat_axis=0, axis_index_gro...]
    ppermute x30 -> x4, waiting for transfers between devices: 9.67 us -> 0.01 us  [the longest x2 0.01 us: per_device(): other = lax.ppermute(own, 'afd', swap)]
    pallas_call x4 -> x5, Pallas kernels: 9.85 us -> 14 us  [the longest x1 6.17 us: attend(): pl.pallas_call(attend_kernel, out_shape=(jax.ShapeDtypeStruct(gate_up.sha...]
    unnamed x20 -> x8, local copies, waits for them, and re-layouts: 11.4 us -> 9.97 us
    convert_element_type x8 -> x2, other arithmetic: 0.13 us -> 1.49 us  [per_device(): backs.append(to_chips(summed.astype(BF16)))]
  transfers between devices with their start and end apart: 30 -> 7, of which waited for: 5 -> 3; matrix products, arithmetic and copies ran while one was open for 0% -> 2% of each run, Pallas kernels for 5% -> 9%
where the time goes in v4:
time: 76.7 us; the launch traced here: 76.2 us
  waiting for transfers between devices  24.2 us (32%)
  blocking collectives  15.5 us (20%)
  Pallas kernels  14 us (18%)
  starting transfers between devices  10.9 us (14%)
  local copies, waits for them, and re-layouts  9.97 us (13%)
  other arithmetic  1.49 us (2%)
    all_to_all x3, waiting for transfers between devices, to_chips(): lax.all_to_all(chunks, 'afd', split_axis=0, concat_axis=0, axis_index_gro...  24.2 us
    all_to_all x1, blocking collectives, to_chips(): lax.all_to_all(chunks, 'afd', split_axis=0, concat_axis=0, axis_index_gro...  15.5 us
    all_to_all x3, starting transfers between devices, to_chips(): lax.all_to_all(chunks, 'afd', split_axis=0, concat_axis=0, axis_index_gro...  10.2 us
    unnamed x8, local copies, waits for them, and re-layouts  9.97 us
    pallas_call x1, Pallas kernels, attend(): pl.pallas_call(attend_kernel, out_shape=(jax.ShapeDtypeStruct(gate_up.sha...  6.17 us
    pallas_call x2, Pallas kernels, experts(): pl.pallas_call(functools.partial(expert_kernel, per), out_shape=(shape, s...  5.99 us
  transfers between devices with their start and end apart: 7, of which 3 were waited for; matrix products, arithmetic and copies ran while one was open for 2% of the time, Pallas kernels for 9%

profile of v4, /device:TPU:0, one launch (start us, length us, event | category | flops | bytes accessed | tf_op | source)
XLA Modules:
  0.0 76.2 jit_solution(14475251326508590831)
XLA Ops:
  0.0 6.2 %attend.1 = (bf16[2,256,7168]{2,1,0:T(8,128)(2,1)S(1)}, bf16[256,7168]{1,0:T(8,128)(2,1)S(1)}, f32[8,7168]{1,0:T(8,128)S(1)}, bf16[8,16,896]{2,1,0:T(8,128)(2,1)}, bf16[8,16,896]{2,1,0:T(8,128)(2,1)S(1)}) custom-call(s32[4]{0:T(128)} %len_hbm.1, s32[3,2,4]{2,1,0:T(2,128)} %bitcast.6, bf16[2,4,7168]{2,1,0:T(4,128)(2,1)} %q_hbm.1, ...), custom_call_target="tpu_custom_call" | custom-call | flops 300000000 | bytes 24000000 | tf_op jit(solution)/shard_map/attend/pallas_call | solution.py:180
  6.2 2.9 %copy-done = bf16[2,256,7168]{2,1,0:T(8,128)(2,1)} copy-done((bf16[2,256,7168]{2,1,0:T(8,128)(2,1)}, bf16[2,256,7168]{2,1,0:T(8,128)(2,1)S(1)}, u32[]{:S(2)}) %copy-start) | copy-done | bytes 7340056
  9.1 1.9 %copy-done.2 = bf16[256,7168]{1,0:T(8,128)(2,1)} copy-done((bf16[256,7168]{1,0:T(8,128)(2,1)}, bf16[256,7168]{1,0:T(8,128)(2,1)S(1)}, u32[]{:S(2)}) %copy-start.2) | copy-done | bytes 3670040
  11.0 15.5 %all_to_all.20.own_ref = bf16[8,16,896]{2,1,0:T(8,128)(2,1)S(1)} all-to-all(bf16[8,16,896]{2,1,0:T(8,128)(2,1)S(1)} %get-tuple-element.24), channel_id=1, replica_groups={{0,2,4,6,8,10,12,14},{1,3,5,7,9,11,13,15},{16,18,20,22,24,26,28,30},{17..., dimensions={0} | all-to-all | bytes 458752 | tf_op jit(solution)/shard_map/all_to_all | solution.py:375
  26.5 3.4 %all-to-all-start = ((bf16[8,16,896]{2,1,0:T(8,128)(2,1)}), bf16[8,16,896]{2,1,0:T(8,128)(2,1)S(1)}, u32[]{:S(2)}, u32[]{:S(2)}) async-start(bf16[8,16,896]{2,1,0:T(8,128)(2,1)} %get-tuple-element.18), calls=%async_computation | async-start | bytes 458752 | tf_op jit(solution)/shard_map/all_to_all | solution.py:375
  29.9 0.1 collective-permute-start.2
  30.0 8.0 %all-to-all-done.own_ref = bf16[8,16,896]{2,1,0:T(8,128)(2,1)S(1)} async-done(((bf16[8,16,896]{2,1,0:T(8,128)(2,1)}), bf16[8,16,896]{2,1,0:T(8,128)(2,1)S(1)}, u32[]{:S(2)}, u32[]{:S(2)}) %all-to-all-start) | async-done | bytes 229408 | tf_op jit(solution)/shard_map/all_to_all | solution.py:375
  38.0 0.0 collective-permute-start
  38.0 0.0 collective-permute-done.2.other_ref
  38.0 3.1 %copy-done.1 = bf16[2,256,7168]{2,1,0:T(8,128)(2,1)S(1)} copy-done((bf16[2,256,7168]{2,1,0:T(8,128)(2,1)S(1)}, bf16[2,256,7168]{2,1,0:T(8,128)(2,1)}, u32[]{:S(2)}) %copy-start.1) | copy-done | bytes 7340056
  41.1 2.0 %copy-done.3 = bf16[256,7168]{1,0:T(8,128)(2,1)S(1)} copy-done((bf16[256,7168]{1,0:T(8,128)(2,1)S(1)}, bf16[256,7168]{1,0:T(8,128)(2,1)}, u32[]{:S(2)}) %copy-start.3) | copy-done | bytes 3670040
  43.1 3.0 %experts.3 = (bf16[8,16,896]{2,1,0:T(8,128)(2,1)S(1)}, bf16[8,16,896]{2,1,0:T(8,128)(2,1)S(1)}) custom-call(bf16[8,16,896]{2,1,0:T(8,128)(2,1)S(1)} %all_to_all.20.own_ref, bf16[8,16,896]{2,1,0:T(8,128)(2,1)S(1)} %collective-permute-done.2.other_ref, bf16[2,256,7168]{2,1,0:T(8,128)(2,1)S(1)} %copy-done.1, bf16[256,7168]{1,0:T(8,128)(2,1)S(1)} %copy-done.3), custom_call_target="tpu_custom_call" | custom-call | flops 800000000 | bytes 12000000 | tf_op jit(solution)/shard_map/experts/pallas_call | solution.py:308
  46.1 0.6 collective-permute-start.3
  46.7 0.0 collective-permute-done.other_ref
  46.7 3.0 %experts.2 = (bf16[8,16,896]{2,1,0:T(8,128)(2,1)S(1)}, bf16[8,16,896]{2,1,0:T(8,128)(2,1)S(1)}) custom-call(bf16[8,16,896]{2,1,0:T(8,128)(2,1)S(1)} %all-to-all-done.own_ref, bf16[8,16,896]{2,1,0:T(8,128)(2,1)S(1)} %collective-permute-done.other_ref, bf16[2,256,7168]{2,1,0:T(8,128)(2,1)S(1)} %copy-done.1, bf16[256,7168]{1,0:T(8,128)(2,1)S(1)} %copy-done.3), custom_call_target="tpu_custom_call" | custom-call | flops 800000000 | bytes 12000000 | tf_op jit(solution)/shard_map/experts/pallas_call | solution.py:308
  49.7 0.1 collective-permute-start.1
  49.8 0.7 add_convert_fusion
  50.5 3.4 %all-to-all-start.3 = ((bf16[8,16,896]{2,1,0:T(8,128)(2,1)}), bf16[8,16,896]{2,1,0:T(8,128)(2,1)S(1)}, u32[]{:S(2)}, u32[]{:S(2)}) async-start(bf16[8,16,896]{2,1,0:T(8,128)(2,1)} %add_convert_fusion), calls=%async_computation.3 | async-start | bytes 458752 | tf_op jit(solution)/shard_map/all_to_all | solution.py:375
  54.0 0.7 add_convert_fusion.1
  54.7 8.5 %all-to-all-done.3.refs_3_ = bf16[8,16,896]{2,1,0:T(8,128)(2,1)S(1)} async-done(((bf16[8,16,896]{2,1,0:T(8,128)(2,1)}), bf16[8,16,896]{2,1,0:T(8,128)(2,1)S(1)}, u32[]{:S(2)}, u32[]{:S(2)}) %all-to-all-start.3) | async-done | bytes 229408 | tf_op jit(solution)/shard_map/all_to_all | solution.py:375
  63.3 3.4 %all-to-all-start.1 = ((bf16[8,16,896]{2,1,0:T(8,128)(2,1)}), bf16[8,16,896]{2,1,0:T(8,128)(2,1)S(1)}, u32[]{:S(2)}, u32[]{:S(2)}) async-start(bf16[8,16,896]{2,1,0:T(8,128)(2,1)} %add_convert_fusion.1), calls=%async_computation.1 | async-start | bytes 458752 | tf_op jit(solution)/shard_map/all_to_all | solution.py:375
  66.7 0.9 %mixers.1 = (bf16[96,128]{1,0:T(8,128)(2,1)S(1)}, bf16[96,128]{1,0:T(8,128)(2,1)S(1)}) custom-call(s32[3,2,4]{2,1,0:T(2,128)} %bitcast.7, f32[3,2,4]{2,1,0:T(2,128)} %bitcast.8), custom_call_target="tpu_custom_call" | custom-call | flops 100000000 | bytes 4000000 | tf_op jit(solution)/shard_map/mixers/pallas_call | solution.py:262
  67.6 7.7 %all-to-all-done.1.refs_1_ = bf16[8,16,896]{2,1,0:T(8,128)(2,1)S(1)} async-done(((bf16[8,16,896]{2,1,0:T(8,128)(2,1)}), bf16[8,16,896]{2,1,0:T(8,128)(2,1)S(1)}, u32[]{:S(2)}, u32[]{:S(2)}) %all-to-all-start.1) | async-done | bytes 229408 | tf_op jit(solution)/shard_map/all_to_all | solution.py:375
  75.3 0.9 %combine.1 = bf16[2,4,7168]{2,1,0:T(4,128)(2,1)} custom-call(f32[8,7168]{1,0:T(8,128)S(1)} %get-tuple-element.16.resid_ref, bf16[96,128]{1,0:T(8,128)(2,1)S(1)} %get-tuple-element.17.refs_0_, bf16[8,16,896]{2,1,0:T(8,128)(2,1)S(1)} %all-to-all-done.1.refs_1_, bf16[96,128]{1,0:T(8,128)(2,1)S(1)} %get-tuple-element.23.refs_2_, ...), custom_call_target="tpu_custom_call" | custom-call | flops 100000000 | bytes 1000000 | tf_op jit(solution)/shard_map/combine/pallas_call | solution.py:344
  (6 shorter events, 0.0 us)
Async XLA Ops:
  6.2 2.9 %copy-start = (bf16[2,256,7168]{2,1,0:T(8,128)(2,1)}, bf16[2,256,7168]{2,1,0:T(8,128)(2,1)S(1)}, u32[]{:S(2)}) copy-start(bf16[2,256,7168]{2,1,0:T(8,128)(2,1)S(1)} %get-tuple-element.19.gu) | copy-start | bytes 22020100
  9.1 1.9 %copy-start.2 = (bf16[256,7168]{1,0:T(8,128)(2,1)}, bf16[256,7168]{1,0:T(8,128)(2,1)S(1)}, u32[]{:S(2)}) copy-start(bf16[256,7168]{1,0:T(8,128)(2,1)S(1)} %get-tuple-element.20.dn) | copy-start | bytes 11010052
  26.5 11.5 %all-to-all-start = ((bf16[8,16,896]{2,1,0:T(8,128)(2,1)}), bf16[8,16,896]{2,1,0:T(8,128)(2,1)S(1)}, u32[]{:S(2)}, u32[]{:S(2)}) async-start(bf16[8,16,896]{2,1,0:T(8,128)(2,1)} %get-tuple-element.18), calls=%async_computation | async-start | bytes 458752 | tf_op jit(solution)/shard_map/all_to_all | solution.py:375
  29.9 8.1 %collective-permute-start.2 = (bf16[8,16,896]{2,1,0:T(8,128)(2,1)S(1)}, bf16[8,16,896]{2,1,0:T(8,128)(2,1)S(1)}, u32[]{:S(2)}, u32[]{:S(2)}) collective-permute-start(bf16[8,16,896]{2,1,0:T(8,128)(2,1)S(1)} %all_to_all.20.own_ref), channel_id=1, source_target_pairs={{0,1},{1,0},{2,3},{3,2},{4,5},{5,4},{6,7},{7,6},{8,9},{9,8},{10,11... | collective-permute-start | bytes 688136 | tf_op jit(solution)/shard_map/ppermute | solution.py:390
  38.0 8.7 %collective-permute-start = (bf16[8,16,896]{2,1,0:T(8,128)(2,1)S(1)}, bf16[8,16,896]{2,1,0:T(8,128)(2,1)S(1)}, u32[]{:S(2)}, u32[]{:S(2)}) collective-permute-start(bf16[8,16,896]{2,1,0:T(8,128)(2,1)S(1)} %all-to-all-done.own_ref), channel_id=1, source_target_pairs={{0,1},{1,0},{2,3},{3,2},{4,5},{5,4},{6,7},{7,6},{8,9},{9,8},{10,11... | collective-permute-start | bytes 688136 | tf_op jit(solution)/shard_map/ppermute | solution.py:390
  38.0 3.1 %copy-start.1 = (bf16[2,256,7168]{2,1,0:T(8,128)(2,1)S(1)}, bf16[2,256,7168]{2,1,0:T(8,128)(2,1)}, u32[]{:S(2)}) copy-start(bf16[2,256,7168]{2,1,0:T(8,128)(2,1)} %copy-done) | copy-start | bytes 22020100
  41.1 2.0 %copy-start.3 = (bf16[256,7168]{1,0:T(8,128)(2,1)S(1)}, bf16[256,7168]{1,0:T(8,128)(2,1)}, u32[]{:S(2)}) copy-start(bf16[256,7168]{1,0:T(8,128)(2,1)} %copy-done.2) | copy-start | bytes 11010052
  46.1 3.7 %collective-permute-start.3 = (bf16[8,16,896]{2,1,0:T(8,128)(2,1)S(1)}, bf16[8,16,896]{2,1,0:T(8,128)(2,1)S(1)}, u32[]{:S(2)}, u32[]{:S(2)}) collective-permute-start(bf16[8,16,896]{2,1,0:T(8,128)(2,1)S(1)} %get-tuple-element.26), channel_id=1, source_target_pairs={{0,1},{1,0},{2,3},{3,2},{4,5},{5,4},{6,7},{7,6},{8,9},{9,8},{10,11... | collective-permute-start | bytes 688136 | tf_op jit(solution)/shard_map/ppermute | solution.py:392
  49.7 4.2 %collective-permute-start.1 = (bf16[8,16,896]{2,1,0:T(8,128)(2,1)S(1)}, bf16[8,16,896]{2,1,0:T(8,128)(2,1)S(1)}, u32[]{:S(2)}, u32[]{:S(2)}) collective-permute-start(bf16[8,16,896]{2,1,0:T(8,128)(2,1)S(1)} %get-tuple-element.22), channel_id=1, source_target_pairs={{0,1},{1,0},{2,3},{3,2},{4,5},{5,4},{6,7},{7,6},{8,9},{9,8},{10,11... | collective-permute-start | bytes 688136 | tf_op jit(solution)/shard_map/ppermute | solution.py:392
  50.5 12.7 %all-to-all-start.3 = ((bf16[8,16,896]{2,1,0:T(8,128)(2,1)}), bf16[8,16,896]{2,1,0:T(8,128)(2,1)S(1)}, u32[]{:S(2)}, u32[]{:S(2)}) async-start(bf16[8,16,896]{2,1,0:T(8,128)(2,1)} %add_convert_fusion), calls=%async_computation.3 | async-start | bytes 458752 | tf_op jit(solution)/shard_map/all_to_all | solution.py:375
  63.3 12.0 %all-to-all-start.1 = ((bf16[8,16,896]{2,1,0:T(8,128)(2,1)}), bf16[8,16,896]{2,1,0:T(8,128)(2,1)S(1)}, u32[]{:S(2)}, u32[]{:S(2)}) async-start(bf16[8,16,896]{2,1,0:T(8,128)(2,1)} %add_convert_fusion.1), calls=%async_computation.1 | async-start | bytes 458752 | tf_op jit(solution)/shard_map/all_to_all | solution.py:375

commit v5 on v2

--- a/solution.py
+++ b/solution.py
@@ -13,16 +13,32 @@
 CAP = 2
 LINES = 16
 LANES = 128
+STAGED = 5
 F32 = jnp.float32
 BF16 = jnp.bfloat16
 MIB = 1 << 20
 VMEM = pl.BlockSpec(memory_space=pltpu.VMEM)
-HBM = pl.BlockSpec(memory_space=pl.ANY)
+HBM = pl.BlockSpec(memory_space=pltpu.HBM)
 BATCHES = ((0, 1),)
+TURNS = ((0, 7, 1, 5, 2, 6, 3, 4), (0, 4, 6, 1, 7, 2, 5, 3))
 
 
 def iota(shape, dim):
     return lax.broadcasted_iota(jnp.int32, shape, dim)
+
+
+def in_hbm(*arrays):
+    return [pltpu.with_memory_space_constraint(x, pltpu.HBM) for x in arrays]
+
+
+def partner(permuted, turn):
+    if not permuted:
+        return turn
+    place = lax.axis_index("afd")
+    out = jnp.zeros_like(turn)
+    for n in range(1, len(TURNS[0])):
+        out = jnp.where(turn == n, jnp.where(place % 2 == 0, TURNS[0][n], TURNS[1][n]), out)
+    return out ^ (place // 2)
 
 
 def nt_dot(a, b):
@@ -45,14 +61,14 @@
     return out
 
 
-def picks_of(ids_ref, batch, steps, rows, me):
+def picks_of(ids_ref, batch, steps, rows, permuted):
     pieces = LINES // (len(batch) * CAP)
     both = steps * rows
     shape = (EXPERTS * LINES, pieces * both)
     line = iota(shape, 0)
     col = iota(shape, 1)
     where = iota((1, pieces * both), 1) % both
-    expert = (line // LINES) ^ me
+    expert = partner(permuted, line // LINES)
     named = jnp.zeros(shape, jnp.bool_)
     for k in range(TOP):
         named = named | (spread(ids_ref, k, where, steps, rows, -1) == expert)
@@ -91,7 +107,6 @@
     length = kv_ref.shape[2]
     both = steps * rows
     scale = HEAD ** (-0.5)
-    me = lax.axis_index("afd") // 2 if permuted else 0
     for copy in copies:
         copy.wait()
     q = jnp.concatenate([q_ref[s].astype(F32) for s in range(steps)], axis=0)
@@ -138,7 +153,7 @@
         stacked = jnp.concatenate(
             [normed[:, k * piece : (k + 1) * piece] for k in range(pieces)], axis=0
         ).astype(BF16)
-        picks = picks_of(ids_ref, batch, steps, rows, me)
+        picks = picks_of(ids_ref, batch, steps, rows, permuted)
         sent = dot(picks, stacked).astype(BF16)
         for j in range(EXPERTS):
             outs[i * EXPERTS + j][0] = sent[j * LINES : (j + 1) * LINES]
@@ -173,18 +188,18 @@
             flops=300_000_000, bytes_accessed=2_000_000, transcendentals=131072
         ),
         name="attend",
-    )(cache_len, ids, queries, fresh, kv, hidden_state, gain)
+    )(*in_hbm(cache_len, ids, queries, fresh, kv, hidden_state, gain))
     resid, chunks = results[0], results[1:]
     return resid, [chunks[i * EXPERTS : (i + 1) * EXPERTS] for i in range(len(BATCHES))]
 
 
-def mixing(ids_ref, weight_ref, batch, steps, rows, chips, me):
+def mixing(ids_ref, weight_ref, batch, steps, rows, chips, permuted):
     pieces = LINES // (len(batch) * CAP)
     both = len(batch) * rows
     shape = (both, chips * LINES)
     line = iota(shape, 1)
     sub = iota(shape, 0)
-    expert = (line // LINES ^ me) // (chips // EXPERTS)
+    expert = partner(permuted, line // LINES) // (chips // EXPERTS)
     where = iota((both, 1), 0) + batch[0] * rows
     named = jnp.zeros(shape, F32)
     mix = jnp.zeros(shape, F32)
@@ -209,7 +224,7 @@
 
 
 def stage_kernel(
-    permuted, chips, steps, rows, ids_hbm, weight_hbm, gu_hbm, dn_hbm, after, gu, dn, *rest
+    permuted, chips, steps, rows, ids_hbm, weight_hbm, gu_hbm, dn_hbm, gu, dn, *rest
 ):
     mixes = rest[: len(BATCHES)]
     ids_ref, weight_ref, small, large = rest[len(BATCHES) :]
@@ -230,14 +245,13 @@
         copy.start()
     for copy in first:
         copy.wait()
-    me = lax.axis_index("afd") // 2 if permuted else 0
     for batch, mix in zip(BATCHES, mixes):
-        mix[...] = mixing(ids_ref, weight_ref, batch, steps, rows, chips, me)
+        mix[...] = mixing(ids_ref, weight_ref, batch, steps, rows, chips, permuted)
     for copy in second:
         copy.wait()
 
 
-def stage(permuted, chips, ids, weights, gate_up, down, after):
+def stage(permuted, chips, ids, weights, gate_up, down):
     _, steps, rows = ids.shape
     mixes = [
         jax.ShapeDtypeStruct((3 * LINES // CAP * rows, chips * LINES), BF16) for _ in BATCHES
@@ -249,7 +263,7 @@
             jax.ShapeDtypeStruct(down.shape[1:], BF16),
             *mixes,
         ),
-        in_specs=[HBM] * 5,
+        in_specs=[HBM] * 4,
         out_specs=(VMEM,) * (2 + len(mixes)),
         scratch_shapes=[
             pltpu.SMEM(ids.shape, jnp.int32),
@@ -262,7 +276,7 @@
             flops=1_000_000, bytes_accessed=22_000_000, transcendentals=0
         ),
         name="stage",
-    )(ids, weights, gate_up, down, after)
+    )(*in_hbm(ids, weights, gate_up, down))
     return gu, dn, mixes
 
 
@@ -379,14 +393,12 @@
     chips_per_expert = chips // EXPERTS
     permuted = chips == EXPERTS
     swap = [(i, i ^ 1) for i in range(owners)]
-    far_first = sorted(range(1, chips), reverse=True)
+
+    def trade(chunk, n):
+        turns = [(i, ((i // 2) ^ TURNS[i % 2][n]) * 2 + i % 2) for i in range(owners)]
+        return lax.ppermute(chunk, "afd", turns)
 
     def to_chips(chunks):
-        if permuted:
-            moved = {0: chunks[0]}
-            for j in far_first:
-                moved[j] = lax.ppermute(chunks[j], "afd", [(i, i ^ 2 * j) for i in range(owners)])
-            return [moved[j] for j in range(chips)]
         same_core = [[2 * p + c for p in range(chips)] for c in range(2)]
         whole = jnp.concatenate(chunks, axis=0)
         return [
@@ -400,19 +412,25 @@
     resid, sent = attend(
         permuted, cache_len, ids, queries, fresh, kv_cache, hidden_state, norm_gain
     )
-    gu, dn, mixes = stage(permuted, chips, ids, weights, gate_up, down, resid)
+    gu, dn, mixes = stage(permuted, chips, ids, weights, gate_up, down)
     backs = []
     for batch, chunks in zip(BATCHES, sent):
-        if not permuted:
-            chunks = [jnp.repeat(chunk, chips_per_expert, axis=0) for chunk in chunks]
-        own = to_chips(chunks)
+        if permuted:
+            *late, gu, dn = lax.optimization_barrier((*chunks[STAGED:], gu, dn))
+            chunks = [*chunks[:STAGED], *late]
+            own = [chunks[0]] + [trade(chunks[n], n) for n in range(1, chips)]
+        else:
+            own = to_chips([jnp.repeat(chunk, chips_per_expert, axis=0) for chunk in chunks])
         other = [lax.ppermute(x, "afd", swap) for x in own]
         mine, theirs = experts(own, other, gu, dn, len(batch) * CAP)
         summed = [
             (a.astype(F32) + lax.ppermute(b, "afd", swap).astype(F32)).astype(BF16)
             for a, b in zip(mine, theirs)
         ]
-        backs.append(to_chips(summed))
+        if permuted:
+            backs.append([summed[0]] + [trade(summed[n], n) for n in range(1, chips)])
+        else:
+            backs.append(to_chips(summed))
     return combine(queries.shape, resid, mixes, backs)
 
 

time: 59.7 us -> 48.7 us (0.82)
  local copies, waits for them, and re-layouts: 11.4 us -> 0 us
  Pallas kernels: 9.85 us -> 11.3 us
  waiting for transfers between devices: 9.67 us -> 8.29 us
  starting transfers between devices: 28 us -> 28.7 us
    unnamed x20 -> x0, local copies, waits for them, and re-layouts: 11.4 us -> none
    ppermute x14, waiting for transfers between devices: 9.29 us -> 7.23 us  [trade(): return lax.ppermute(chunk, 'afd', turns)]
    pallas_call x1, Pallas kernels: 2.97 us -> 4.26 us  [stage(): pl.pallas_call(functools.partial(stage_kernel, permuted, chips, steps, ro...]
    ppermute x14, starting transfers between devices: 24 us -> 24.9 us  [trade(): return lax.ppermute(chunk, 'afd', turns)]
    ppermute x8, waiting for transfers between devices: 0.02 us -> 0.9 us  [per_device(): other = [lax.ppermute(x, 'afd', swap) for x in own]]
  transfers between devices with their start and end apart: 30 -> 30, of which waited for: 5 -> 10; matrix products, arithmetic and copies ran while one was open for 0% -> 0% of each run, Pallas kernels for 5% -> 9%
where the time goes in v5:
time: 48.7 us; the launch traced here: 48.5 us
  starting transfers between devices  28.7 us (59%)
  Pallas kernels  11.3 us (23%)
  waiting for transfers between devices  8.29 us (17%)
    ppermute x14, starting transfers between devices, trade(): return lax.ppermute(chunk, 'afd', turns)  24.9 us
    ppermute x14, waiting for transfers between devices, trade(): return lax.ppermute(chunk, 'afd', turns)  7.23 us
    pallas_call x1, Pallas kernels, stage(): pl.pallas_call(functools.partial(stage_kernel, permuted, chips, steps, ro...  4.26 us
    pallas_call x1, Pallas kernels, experts(): pl.pallas_call(functools.partial(expert_kernel, count, per), out_shape=sh...  3.61 us
    pallas_call x1, Pallas kernels, attend(): pl.pallas_call(functools.partial(attend_kernel, permuted), out_shape=(jax...  2.49 us
    ppermute x8, starting transfers between devices, per_device(): lax.ppermute(b, 'afd', swap).astype(F32)  2.23 us
    ppermute x8, starting transfers between devices, per_device(): other = [lax.ppermute(x, 'afd', swap) for x in own]  1.54 us
  transfers between devices with their start and end apart: 30, of which 10 were waited for; matrix products, arithmetic and copies ran while one was open for 0% of the time, Pallas kernels for 9%

profile of v5, /device:TPU:0, one launch (start us, length us, event | category | flops | bytes accessed | tf_op | source)
XLA Modules:
  0.0 48.5 jit_solution(11459096192698526102)
XLA Ops:
  0.0 2.5 %attend.1 = (f32[8,7168]{1,0:T(8,128)S(1)}, bf16[1,16,1792]{2,1,0:T(8,128)(2,1)S(1)}, bf16[1,16,1792]{2,1,0:T(8,128)(2,1)S(1)}, bf16[1,16,1792]{2,1,0:T(8,128)(2...) custom-call(s32[4]{0:T(128)} %len_hbm.1, ...), custom_call_target="tpu_custom_call" | custom-call | flops 300000000 | bytes 2000000 | tf_op jit(solution)/shard_map/attend/pallas_call | solution.py:170
  2.5 6.0 %collective-permute-start = (bf16[1,16,1792]{2,1,0:T(8,128)(2,1)S(1)}, bf16[1,16,1792]{2,1,0:T(8,128)(2,1)S(1)}, u32[]{:S(2)}, u32[]{:S(2)}) collective-permute-start(bf16[1,16,1792]{2,1,0:T(8,128)(2,1)S(1)} %get-tuple-element.41), channel_id=1, source_target_pairs={{0,14},{1,9},{2,12},{3,11},{4,10},{5,13},{6,8},{7,15},{8,6},{9,1},... | collective-permute-start | bytes 172040 | tf_op jit(solution)/shard_map/ppermute | solution.py:399
  8.5 0.5 %collective-permute-start.1 = (bf16[1,16,1792]{2,1,0:T(8,128)(2,1)S(1)}, bf16[1,16,1792]{2,1,0:T(8,128)(2,1)S(1)}, u32[]{:S(2)}, u32[]{:S(2)}) collective-permute-start(bf16[1,16,1792]{2,1,0:T(8,128)(2,1)S(1)} %get-tuple-element.42), channel_id=1, source_target_pairs={{0,2},{1,13},{2,0},{3,15},{4,6},{5,9},{6,4},{7,11},{8,10},{9,5},{1... | collective-permute-start | bytes 172040 | tf_op jit(solution)/shard_map/ppermute | solution.py:399
  9.4 1.3 %collective-permute-start.3 = (bf16[1,16,1792]{2,1,0:T(8,128)(2,1)S(1)}, bf16[1,16,1792]{2,1,0:T(8,128)(2,1)S(1)}, u32[]{:S(2)}, u32[]{:S(2)}) collective-permute-start(bf16[1,16,1792]{2,1,0:T(8,128)(2,1)S(1)} %get-tuple-element.44), channel_id=1, source_target_pairs={{0,4},{1,15},{2,6},{3,13},{4,0},{5,11},{6,2},{7,9},{8,12},{9,7},{1... | collective-permute-start | bytes 172040 | tf_op jit(solution)/shard_map/ppermute | solution.py:399
  10.8 4.3 %stage.1 = (bf16[2,256,7168]{2,1,0:T(8,128)(2,1)S(1)}, bf16[256,7168]{1,0:T(8,128)(2,1)S(1)}, bf16[96,128]{1,0:T(8,128)(2,1)S(1)}) custom-call(s32[3,2,4]{2,1,0:T(2,128)} %bitcast.5, f32[3,2,4]{2,1,0:T(2,128)} %bitcast.6, bf16[1,2,256,7168]{3,2,1,0:T(8,128)(2,1)} %gu_hbm.1, bf16[1,256,7168]{2,1,0:T(8,128)(2,1)} %dn_hbm.1), custom_call_target="tpu_custom_call" | custom-call | flops 1000000 | bytes 22000000 | tf_op jit(solution)/shard_map/stage/pallas_call | solution.py:259
  15.1 3.7 %collective-permute-start.4 = (bf16[1,16,1792]{2,1,0:T(8,128)(2,1)S(1)}, bf16[1,16,1792]{2,1,0:T(8,128)(2,1)S(1)}, u32[]{:S(2)}, u32[]{:S(2)}) collective-permute-start(bf16[1,16,1792]{2,1,0:T(8,128)(2,1)S(1)} %get-tuple-element.50), channel_id=1, source_target_pairs={{0,12},{1,5},{2,14},{3,7},{4,8},{5,1},{6,10},{7,3},{8,4},{9,13},{1... | collective-permute-start | bytes 172040 | tf_op jit(solution)/shard_map/ppermute | solution.py:399
  18.8 1.5 %collective-permute-start.6 = (bf16[1,16,1792]{2,1,0:T(8,128)(2,1)S(1)}, bf16[1,16,1792]{2,1,0:T(8,128)(2,1)S(1)}, u32[]{:S(2)}, u32[]{:S(2)}) collective-permute-start(bf16[1,16,1792]{2,1,0:T(8,128)(2,1)S(1)} %get-tuple-element.52), channel_id=1, source_target_pairs={{0,8},{1,7},{2,10},{3,5},{4,12},{5,3},{6,14},{7,1},{8,0},{9,15},{1... | collective-permute-start | bytes 172040 | tf_op jit(solution)/shard_map/ppermute | solution.py:399
  20.3 0.5 %collective-permute-start.9 = (bf16[1,16,1792]{2,1,0:T(8,128)(2,1)S(1)}, bf16[1,16,1792]{2,1,0:T(8,128)(2,1)S(1)}, u32[]{:S(2)}, u32[]{:S(2)}) collective-permute-start(bf16[1,16,1792]{2,1,0:T(8,128)(2,1)S(1)} %collective-permute-done.1.refs_2_), channel_id=1, source_target_pairs={{0,1},{1,0},{2,3},{3,2},{4,5},{5,4},{6,7},{7,6},{8,9},{9,8},{10,11... | collective-permute-start | bytes 172040 | tf_op jit(solution)/shard_map/ppermute | solution.py:424
  20.8 0.8 %collective-permute-done.4.refs_5_ = bf16[1,16,1792]{2,1,0:T(8,128)(2,1)S(1)} collective-permute-done((bf16[1,16,1792]{2,1,0:T(8,128)(2,1)S(1)}, bf16[1,16,1792]{2,1,0:T(8,128)(2,1)S(1)}, u32[]{:S(2)}, u32[]{:S(2)}) %collective-permute-start.4) | collective-permute-done | bytes 57376 | tf_op jit(solution)/shard_map/ppermute | solution.py:399
  21.6 2.9 %collective-permute-done.5.refs_6_ = bf16[1,16,1792]{2,1,0:T(8,128)(2,1)S(1)} collective-permute-done((bf16[1,16,1792]{2,1,0:T(8,128)(2,1)S(1)}, bf16[1,16,1792]{2,1,0:T(8,128)(2,1)S(1)}, u32[]{:S(2)}, u32[]{:S(2)}) %collective-permute-start.5) | collective-permute-done | bytes 57376 | tf_op jit(solution)/shard_map/ppermute | solution.py:399
  24.6 0.5 %collective-permute-start.12 = (bf16[1,16,1792]{2,1,0:T(8,128)(2,1)S(1)}, bf16[1,16,1792]{2,1,0:T(8,128)(2,1)S(1)}, u32[]{:S(2)}, u32[]{:S(2)}) collective-permute-start(bf16[1,16,1792]{2,1,0:T(8,128)(2,1)S(1)} %collective-permute-done.4.refs_5_), channel_id=1, source_target_pairs={{0,1},{1,0},{2,3},{3,2},{4,5},{5,4},{6,7},{7,6},{8,9},{9,8},{10,11... | collective-permute-start | bytes 172040 | tf_op jit(solution)/shard_map/ppermute | solution.py:424
  25.2 0.4 collective-permute-start.14
  26.5 3.6 %experts.1 = (bf16[1,16,1792]{2,1,0:T(8,128)(2,1)S(1)}, bf16[1,16,1792]{2,1,0:T(8,128)(2,1)S(1)}, bf16[1,16,1792]{2,1,0:T(8,128)(2,1)S(1)}, bf16[1,16,1792]{2,1,...) custom-call(bf16[1,16,1792]{2,1,0:T(8,128)(2,1)S(1)} %get-tuple-elem, ...), custom_call_target="tpu_custom_call" | custom-call | flops 800000000 | bytes 12000000 | tf_op jit(solution)/shard_map/experts/pallas_call | solution.py:326
  30.1 0.4 collective-permute-start.16
  32.6 2.3 %collective-permute-start.17 = (bf16[1,16,1792]{2,1,0:T(8,128)(2,1)S(1)}, bf16[1,16,1792]{2,1,0:T(8,128)(2,1)S(1)}, u32[]{:S(2)}, u32[]{:S(2)}) collective-permute-start(bf16[1,16,1792]{2,1,0:T(8,128)(2,1)S(1)} %add_convert_fusion.6), channel_id=1, source_target_pairs={{0,14},{1,9},{2,12},{3,11},{4,10},{5,13},{6,8},{7,15},{8,6},{9,1},... | collective-permute-start | bytes 172040 | tf_op jit(solution)/shard_map/ppermute | solution.py:399
  34.9 0.4 collective-permute-start.19
  35.4 2.4 %collective-permute-start.21 = (bf16[1,16,1792]{2,1,0:T(8,128)(2,1)S(1)}, bf16[1,16,1792]{2,1,0:T(8,128)(2,1)S(1)}, u32[]{:S(2)}, u32[]{:S(2)}) collective-permute-start(bf16[1,16,1792]{2,1,0:T(8,128)(2,1)S(1)} %add_convert_fusion.4), channel_id=1, source_target_pairs={{0,10},{1,3},{2,8},{3,1},{4,14},{5,7},{6,12},{7,5},{8,2},{9,11},{1... | collective-permute-start | bytes 172040 | tf_op jit(solution)/shard_map/ppermute | solution.py:399
  37.8 0.7 %collective-permute-start.23 = (bf16[1,16,1792]{2,1,0:T(8,128)(2,1)S(1)}, bf16[1,16,1792]{2,1,0:T(8,128)(2,1)S(1)}, u32[]{:S(2)}, u32[]{:S(2)}) collective-permute-start(bf16[1,16,1792]{2,1,0:T(8,128)(2,1)S(1)} %add_convert_fusion.3), channel_id=1, source_target_pairs={{0,4},{1,15},{2,6},{3,13},{4,0},{5,11},{6,2},{7,9},{8,12},{9,7},{1... | collective-permute-start | bytes 172040 | tf_op jit(solution)/shard_map/ppermute | solution.py:399
  38.6 2.6 %collective-permute-start.25 = (bf16[1,16,1792]{2,1,0:T(8,128)(2,1)S(1)}, bf16[1,16,1792]{2,1,0:T(8,128)(2,1)S(1)}, u32[]{:S(2)}, u32[]{:S(2)}) collective-permute-start(bf16[1,16,1792]{2,1,0:T(8,128)(2,1)S(1)} %add_convert_fusion.2), channel_id=1, source_target_pairs={{0,12},{1,5},{2,14},{3,7},{4,8},{5,1},{6,10},{7,3},{8,4},{9,13},{1... | collective-permute-start | bytes 172040 | tf_op jit(solution)/shard_map/ppermute | solution.py:399
  41.1 0.5 collective-permute-start.27
  41.6 2.6 %collective-permute-start.29 = (bf16[1,16,1792]{2,1,0:T(8,128)(2,1)S(1)}, bf16[1,16,1792]{2,1,0:T(8,128)(2,1)S(1)}, u32[]{:S(2)}, u32[]{:S(2)}) collective-permute-start(bf16[1,16,1792]{2,1,0:T(8,128)(2,1)S(1)} %add_convert_fusion), channel_id=1, source_target_pairs={{0,8},{1,7},{2,10},{3,5},{4,12},{5,3},{6,14},{7,1},{8,0},{9,15},{1... | collective-permute-start | bytes 172040 | tf_op jit(solution)/shard_map/ppermute | solution.py:399
  44.2 0.6 %collective-permute-done.23.refs_5_ = bf16[1,16,1792]{2,1,0:T(8,128)(2,1)S(1)} collective-permute-done((bf16[1,16,1792]{2,1,0:T(8,128)(2,1)S(1)}, bf16[1,16,1792]{2,1,0:T(8,128)(2,1)S(1)}, u32[]{:S(2)}, u32[]{:S(2)}) %collective-permute-start.23) | collective-permute-done | bytes 57376 | tf_op jit(solution)/shard_map/ppermute | solution.py:399
  45.0 2.7 %collective-permute-done.27.refs_7_ = bf16[1,16,1792]{2,1,0:T(8,128)(2,1)S(1)} collective-permute-done((bf16[1,16,1792]{2,1,0:T(8,128)(2,1)S(1)}, bf16[1,16,1792]{2,1,0:T(8,128)(2,1)S(1)}, u32[]{:S(2)}, u32[]{:S(2)}) %collective-permute-start.27) | collective-permute-done | bytes 57376 | tf_op jit(solution)/shard_map/ppermute | solution.py:399
  47.6 0.9 %combine.1 = bf16[2,4,7168]{2,1,0:T(4,128)(2,1)} custom-call(f32[8,7168]{1,0:T(8,128)S(1)} %get-tuple-element.38.resid_ref, bf16[96,128]{1,0:T(8,128)(2,1)S(1)} %get-tuple-element.39.refs_0_, bf16[1,16,1792]{2,1,0:T(8,128)(2,1)S(1)} %add_convert_fusion.7.refs_1_, bf16[1,16,1792]{2,1,0:T(8,128)(2,1)S(1)} %collective-permute-done.17.refs_2_, ...), custom_call_target="tpu_custom_call" | custom-call | flops 100000000 | bytes 1000000 | tf_op jit(solution)/shard_map/combine/pallas_call | solution.py:366
  (48 shorter events, 3.7 us)
Async XLA Ops:
  2.5 12.6 %collective-permute-start = (bf16[1,16,1792]{2,1,0:T(8,128)(2,1)S(1)}, bf16[1,16,1792]{2,1,0:T(8,128)(2,1)S(1)}, u32[]{:S(2)}, u32[]{:S(2)}) collective-permute-start(bf16[1,16,1792]{2,1,0:T(8,128)(2,1)S(1)} %get-tuple-element.41), channel_id=1, source_target_pairs={{0,14},{1,9},{2,12},{3,11},{4,10},{5,13},{6,8},{7,15},{8,6},{9,1},... | collective-permute-start | bytes 172040 | tf_op jit(solution)/shard_map/ppermute | solution.py:399
  8.5 10.2 %collective-permute-start.1 = (bf16[1,16,1792]{2,1,0:T(8,128)(2,1)S(1)}, bf16[1,16,1792]{2,1,0:T(8,128)(2,1)S(1)}, u32[]{:S(2)}, u32[]{:S(2)}) collective-permute-start(bf16[1,16,1792]{2,1,0:T(8,128)(2,1)S(1)} %get-tuple-element.42), channel_id=1, source_target_pairs={{0,2},{1,13},{2,0},{3,15},{4,6},{5,9},{6,4},{7,11},{8,10},{9,5},{1... | collective-permute-start | bytes 172040 | tf_op jit(solution)/shard_map/ppermute | solution.py:399
  9.1 9.7 %collective-permute-start.2 = (bf16[1,16,1792]{2,1,0:T(8,128)(2,1)S(1)}, bf16[1,16,1792]{2,1,0:T(8,128)(2,1)S(1)}, u32[]{:S(2)}, u32[]{:S(2)}) collective-permute-start(bf16[1,16,1792]{2,1,0:T(8,128)(2,1)S(1)} %get-tuple-element.43), channel_id=1, source_target_pairs={{0,10},{1,3},{2,8},{3,1},{4,14},{5,7},{6,12},{7,5},{8,2},{9,11},{1... | collective-permute-start | bytes 172040 | tf_op jit(solution)/shard_map/ppermute | solution.py:399
  9.4 10.8 %collective-permute-start.3 = (bf16[1,16,1792]{2,1,0:T(8,128)(2,1)S(1)}, bf16[1,16,1792]{2,1,0:T(8,128)(2,1)S(1)}, u32[]{:S(2)}, u32[]{:S(2)}) collective-permute-start(bf16[1,16,1792]{2,1,0:T(8,128)(2,1)S(1)} %get-tuple-element.44), channel_id=1, source_target_pairs={{0,4},{1,15},{2,6},{3,13},{4,0},{5,11},{6,2},{7,9},{8,12},{9,7},{1... | collective-permute-start | bytes 172040 | tf_op jit(solution)/shard_map/ppermute | solution.py:399
  10.8 9.5 %collective-permute-start.7 = (bf16[1,16,1792]{2,1,0:T(8,128)(2,1)S(1)}, bf16[1,16,1792]{2,1,0:T(8,128)(2,1)S(1)}, u32[]{:S(2)}, u32[]{:S(2)}) collective-permute-start(bf16[1,16,1792]{2,1,0:T(8,128)(2,1)S(1)} %get-tuple-element.40.refs_0_), channel_id=1, source_target_pairs={{0,1},{1,0},{2,3},{3,2},{4,5},{5,4},{6,7},{7,6},{8,9},{9,8},{10,11... | collective-permute-start | bytes 172040 | tf_op jit(solution)/shard_map/ppermute | solution.py:424
  15.1 6.6 %collective-permute-start.4 = (bf16[1,16,1792]{2,1,0:T(8,128)(2,1)S(1)}, bf16[1,16,1792]{2,1,0:T(8,128)(2,1)S(1)}, u32[]{:S(2)}, u32[]{:S(2)}) collective-permute-start(bf16[1,16,1792]{2,1,0:T(8,128)(2,1)S(1)} %get-tuple-element.50), channel_id=1, source_target_pairs={{0,12},{1,5},{2,14},{3,7},{4,8},{5,1},{6,10},{7,3},{8,4},{9,13},{1... | collective-permute-start | bytes 172040 | tf_op jit(solution)/shard_map/ppermute | solution.py:399
  18.7 5.8 %collective-permute-start.5 = (bf16[1,16,1792]{2,1,0:T(8,128)(2,1)S(1)}, bf16[1,16,1792]{2,1,0:T(8,128)(2,1)S(1)}, u32[]{:S(2)}, u32[]{:S(2)}) collective-permute-start(bf16[1,16,1792]{2,1,0:T(8,128)(2,1)S(1)} %get-tuple-element.51), channel_id=1, source_target_pairs={{0,6},{1,11},{2,4},{3,9},{4,2},{5,15},{6,0},{7,13},{8,14},{9,3},{1... | collective-permute-start | bytes 172040 | tf_op jit(solution)/shard_map/ppermute | solution.py:399
  18.8 5.8 %collective-permute-start.6 = (bf16[1,16,1792]{2,1,0:T(8,128)(2,1)S(1)}, bf16[1,16,1792]{2,1,0:T(8,128)(2,1)S(1)}, u32[]{:S(2)}, u32[]{:S(2)}) collective-permute-start(bf16[1,16,1792]{2,1,0:T(8,128)(2,1)S(1)} %get-tuple-element.52), channel_id=1, source_target_pairs={{0,8},{1,7},{2,10},{3,5},{4,12},{5,3},{6,14},{7,1},{8,0},{9,15},{1... | collective-permute-start | bytes 172040 | tf_op jit(solution)/shard_map/ppermute | solution.py:399
  20.3 4.8 %collective-permute-start.8 = (bf16[1,16,1792]{2,1,0:T(8,128)(2,1)S(1)}, bf16[1,16,1792]{2,1,0:T(8,128)(2,1)S(1)}, u32[]{:S(2)}, u32[]{:S(2)}) collective-permute-start(bf16[1,16,1792]{2,1,0:T(8,128)(2,1)S(1)} %collective-permute-done.refs_1_), channel_id=1, source_target_pairs={{0,1},{1,0},{2,3},{3,2},{4,5},{5,4},{6,7},{7,6},{8,9},{9,8},{10,11... | collective-permute-start | bytes 172040 | tf_op jit(solution)/shard_map/ppermute | solution.py:424
  20.3 4.9 %collective-permute-start.9 = (bf16[1,16,1792]{2,1,0:T(8,128)(2,1)S(1)}, bf16[1,16,1792]{2,1,0:T(8,128)(2,1)S(1)}, u32[]{:S(2)}, u32[]{:S(2)}) collective-permute-start(bf16[1,16,1792]{2,1,0:T(8,128)(2,1)S(1)} %collective-permute-done.1.refs_2_), channel_id=1, source_target_pairs={{0,1},{1,0},{2,3},{3,2},{4,5},{5,4},{6,7},{7,6},{8,9},{9,8},{10,11... | collective-permute-start | bytes 172040 | tf_op jit(solution)/shard_map/ppermute | solution.py:424
  21.6 4.0 %collective-permute-start.10 = (bf16[1,16,1792]{2,1,0:T(8,128)(2,1)S(1)}, bf16[1,16,1792]{2,1,0:T(8,128)(2,1)S(1)}, u32[]{:S(2)}, u32[]{:S(2)}) collective-permute-start(bf16[1,16,1792]{2,1,0:T(8,128)(2,1)S(1)} %collective-permute-done.2.refs_3_), channel_id=1, source_target_pairs={{0,1},{1,0},{2,3},{3,2},{4,5},{5,4},{6,7},{7,6},{8,9},{9,8},{10,11... | collective-permute-start | bytes 172040 | tf_op jit(solution)/shard_map/ppermute | solution.py:424
  24.6 1.4 %collective-permute-start.12 = (bf16[1,16,1792]{2,1,0:T(8,128)(2,1)S(1)}, bf16[1,16,1792]{2,1,0:T(8,128)(2,1)S(1)}, u32[]{:S(2)}, u32[]{:S(2)}) collective-permute-start(bf16[1,16,1792]{2,1,0:T(8,128)(2,1)S(1)} %collective-permute-done.4.refs_5_), channel_id=1, source_target_pairs={{0,1},{1,0},{2,3},{3,2},{4,5},{5,4},{6,7},{7,6},{8,9},{9,8},{10,11... | collective-permute-start | bytes 172040 | tf_op jit(solution)/shard_map/ppermute | solution.py:424
  30.1 1.4 %collective-permute-start.16 = (bf16[1,16,1792]{2,1,0:T(8,128)(2,1)S(1)}, bf16[1,16,1792]{2,1,0:T(8,128)(2,1)S(1)}, u32[]{:S(2)}, u32[]{:S(2)}) collective-permute-start(bf16[1,16,1792]{2,1,0:T(8,128)(2,1)S(1)} %get-tuple-element.58), channel_id=1, source_target_pairs={{0,1},{1,0},{2,3},{3,2},{4,5},{5,4},{6,7},{7,6},{8,9},{9,8},{10,11... | collective-permute-start | bytes 172040 | tf_op jit(solution)/shard_map/ppermute | solution.py:427
  30.5 8.0 %collective-permute-start.15 = (bf16[1,16,1792]{2,1,0:T(8,128)(2,1)S(1)}, bf16[1,16,1792]{2,1,0:T(8,128)(2,1)S(1)}, u32[]{:S(2)}, u32[]{:S(2)}) collective-permute-start(bf16[1,16,1792]{2,1,0:T(8,128)(2,1)S(1)} %get-tuple-element.56), channel_id=1, source_target_pairs={{0,1},{1,0},{2,3},{3,2},{4,5},{5,4},{6,7},{7,6},{8,9},{9,8},{10,11... | collective-permute-start | bytes 172040 | tf_op jit(solution)/shard_map/ppermute | solution.py:427
  31.6 3.4 %collective-permute-start.24 = (bf16[1,16,1792]{2,1,0:T(8,128)(2,1)S(1)}, bf16[1,16,1792]{2,1,0:T(8,128)(2,1)S(1)}, u32[]{:S(2)}, u32[]{:S(2)}) collective-permute-start(bf16[1,16,1792]{2,1,0:T(8,128)(2,1)S(1)} %get-tuple-element.66), channel_id=1, source_target_pairs={{0,1},{1,0},{2,3},{3,2},{4,5},{5,4},{6,7},{7,6},{8,9},{9,8},{10,11... | collective-permute-start | bytes 172040 | tf_op jit(solution)/shard_map/ppermute | solution.py:427
  31.9 3.5 %collective-permute-start.26 = (bf16[1,16,1792]{2,1,0:T(8,128)(2,1)S(1)}, bf16[1,16,1792]{2,1,0:T(8,128)(2,1)S(1)}, u32[]{:S(2)}, u32[]{:S(2)}) collective-permute-start(bf16[1,16,1792]{2,1,0:T(8,128)(2,1)S(1)} %get-tuple-element.68), channel_id=1, source_target_pairs={{0,1},{1,0},{2,3},{3,2},{4,5},{5,4},{6,7},{7,6},{8,9},{9,8},{10,11... | collective-permute-start | bytes 172040 | tf_op jit(solution)/shard_map/ppermute | solution.py:427
  32.3 5.5 %collective-permute-start.28 = (bf16[1,16,1792]{2,1,0:T(8,128)(2,1)S(1)}, bf16[1,16,1792]{2,1,0:T(8,128)(2,1)S(1)}, u32[]{:S(2)}, u32[]{:S(2)}) collective-permute-start(bf16[1,16,1792]{2,1,0:T(8,128)(2,1)S(1)} %get-tuple-element.70), channel_id=1, source_target_pairs={{0,1},{1,0},{2,3},{3,2},{4,5},{5,4},{6,7},{7,6},{8,9},{9,8},{10,11... | collective-permute-start | bytes 172040 | tf_op jit(solution)/shard_map/ppermute | solution.py:427
  32.6 8.6 %collective-permute-start.17 = (bf16[1,16,1792]{2,1,0:T(8,128)(2,1)S(1)}, bf16[1,16,1792]{2,1,0:T(8,128)(2,1)S(1)}, u32[]{:S(2)}, u32[]{:S(2)}) collective-permute-start(bf16[1,16,1792]{2,1,0:T(8,128)(2,1)S(1)} %add_convert_fusion.6), channel_id=1, source_target_pairs={{0,14},{1,9},{2,12},{3,11},{4,10},{5,13},{6,8},{7,15},{8,6},{9,1},... | collective-permute-start | bytes 172040 | tf_op jit(solution)/shard_map/ppermute | solution.py:399
  34.9 6.7 %collective-permute-start.19 = (bf16[1,16,1792]{2,1,0:T(8,128)(2,1)S(1)}, bf16[1,16,1792]{2,1,0:T(8,128)(2,1)S(1)}, u32[]{:S(2)}, u32[]{:S(2)}) collective-permute-start(bf16[1,16,1792]{2,1,0:T(8,128)(2,1)S(1)} %add_convert_fusion.5), channel_id=1, source_target_pairs={{0,2},{1,13},{2,0},{3,15},{4,6},{5,9},{6,4},{7,11},{8,10},{9,5},{1... | collective-permute-start | bytes 172040 | tf_op jit(solution)/shard_map/ppermute | solution.py:399
  35.4 8.8 %collective-permute-start.21 = (bf16[1,16,1792]{2,1,0:T(8,128)(2,1)S(1)}, bf16[1,16,1792]{2,1,0:T(8,128)(2,1)S(1)}, u32[]{:S(2)}, u32[]{:S(2)}) collective-permute-start(bf16[1,16,1792]{2,1,0:T(8,128)(2,1)S(1)} %add_convert_fusion.4), channel_id=1, source_target_pairs={{0,10},{1,3},{2,8},{3,1},{4,14},{5,7},{6,12},{7,5},{8,2},{9,11},{1... | collective-permute-start | bytes 172040 | tf_op jit(solution)/shard_map/ppermute | solution.py:399
  37.8 7.0 %collective-permute-start.23 = (bf16[1,16,1792]{2,1,0:T(8,128)(2,1)S(1)}, bf16[1,16,1792]{2,1,0:T(8,128)(2,1)S(1)}, u32[]{:S(2)}, u32[]{:S(2)}) collective-permute-start(bf16[1,16,1792]{2,1,0:T(8,128)(2,1)S(1)} %add_convert_fusion.3), channel_id=1, source_target_pairs={{0,4},{1,15},{2,6},{3,13},{4,0},{5,11},{6,2},{7,9},{8,12},{9,7},{1... | collective-permute-start | bytes 172040 | tf_op jit(solution)/shard_map/ppermute | solution.py:399
  38.6 6.4 %collective-permute-start.25 = (bf16[1,16,1792]{2,1,0:T(8,128)(2,1)S(1)}, bf16[1,16,1792]{2,1,0:T(8,128)(2,1)S(1)}, u32[]{:S(2)}, u32[]{:S(2)}) collective-permute-start(bf16[1,16,1792]{2,1,0:T(8,128)(2,1)S(1)} %add_convert_fusion.2), channel_id=1, source_target_pairs={{0,12},{1,5},{2,14},{3,7},{4,8},{5,1},{6,10},{7,3},{8,4},{9,13},{1... | collective-permute-start | bytes 172040 | tf_op jit(solution)/shard_map/ppermute | solution.py:399
  41.1 6.5 %collective-permute-start.27 = (bf16[1,16,1792]{2,1,0:T(8,128)(2,1)S(1)}, bf16[1,16,1792]{2,1,0:T(8,128)(2,1)S(1)}, u32[]{:S(2)}, u32[]{:S(2)}) collective-permute-start(bf16[1,16,1792]{2,1,0:T(8,128)(2,1)S(1)} %add_convert_fusion.1), channel_id=1, source_target_pairs={{0,6},{1,11},{2,4},{3,9},{4,2},{5,15},{6,0},{7,13},{8,14},{9,3},{1... | collective-permute-start | bytes 172040 | tf_op jit(solution)/shard_map/ppermute | solution.py:399
  41.6 6.0 %collective-permute-start.29 = (bf16[1,16,1792]{2,1,0:T(8,128)(2,1)S(1)}, bf16[1,16,1792]{2,1,0:T(8,128)(2,1)S(1)}, u32[]{:S(2)}, u32[]{:S(2)}) collective-permute-start(bf16[1,16,1792]{2,1,0:T(8,128)(2,1)S(1)} %add_convert_fusion), channel_id=1, source_target_pairs={{0,8},{1,7},{2,10},{3,5},{4,12},{5,3},{6,14},{7,1},{8,0},{9,15},{1... | collective-permute-start | bytes 172040 | tf_op jit(solution)/shard_map/ppermute | solution.py:399
  (6 other events, 7.7 us)

commit v6 on v3

--- a/solution.py
+++ b/solution.py
@@ -10,6 +10,8 @@
 HEAD = 224
 EXPERTS = 8
 TOP = 3
+CAP = 2
+PIECES = 4
 LANES = 128
 PARTS = 3
 F32 = jnp.float32
@@ -17,12 +19,17 @@
 MIB = 1 << 20
 VMEM = pl.BlockSpec(memory_space=pltpu.VMEM)
 HBM = pl.BlockSpec(memory_space=pltpu.HBM)
+TOGETHER = 4
 
 
 def iota(shape, dim):
     return lax.broadcasted_iota(jnp.int32, shape, dim)
 
 
+def in_hbm(*arrays):
+    return [pltpu.with_memory_space_constraint(x, pltpu.HBM) for x in arrays]
+
+
 def nt_dot(a, b):
     return lax.dot_general(a, b, (((1,), (1,)), ((), ())), preferred_element_type=F32)
 
@@ -33,6 +40,15 @@
 
 def one_hot(mask):
     return jnp.where(mask, 1.0, 0.0).astype(BF16)
+
+
+def distance(turn, core, chips):
+    return (2 * turn) ^ (core * (chips - 1))
+
+
+def expert_at(turn, chips):
+    place = lax.axis_index("afd")
+    return (distance(turn, place % 2, chips) ^ (place // 2)) // (chips // EXPERTS)
 
 
 def spread(ref, k, where, steps, rows, empty):
@@ -48,10 +64,12 @@
     lane = iota((both, LANES), 1)
     where = iota((both, 1), 0)
     mix = jnp.zeros((both, LANES), F32)
+    named = jnp.zeros((both, LANES), F32)
     for k in range(TOP):
         hit = spread(ids_ref, k, where, steps, rows, -1) == lane % EXPERTS
         mix = mix + jnp.where(hit, spread(weight_ref, k, where, steps, rows, 0.0), 0.0)
-    out = jnp.zeros((both, LANES), F32)
+        named = named + jnp.where(hit, 1.0, 0.0)
+    out = jnp.where(lane // EXPERTS == PARTS, named, 0.0)
     for part in range(PARTS):
         term = mix.astype(BF16).astype(F32)
         out = jnp.where(lane // EXPERTS == part, term, out)
@@ -175,10 +193,85 @@
             flops=300_000_000, bytes_accessed=2_000_000, transcendentals=131072
         ),
         name="attend",
-    )(cache_len, ids, weights, queries, fresh, kv, hidden_state, gain)
-
-
-def stage_kernel(gu_hbm, dn_hbm, after, gu, dn, sems):
+    )(*in_hbm(cache_len, ids, weights, queries, fresh, kv, hidden_state, gain))
+
+
+def pack_kernel(steps, chips, own_ref, other_ref, *outs):
+    both, width = own_ref.shape
+    width -= LANES
+    rows = both // steps
+    piece = width // PIECES
+    side_lines = steps * CAP
+    lines = PIECES * 2 * side_lines
+    tails = [ref[:, width:].astype(F32) for ref in (own_ref, other_ref)]
+    tails = jnp.concatenate(tails * PIECES, axis=0).astype(BF16)
+    count = 2 * both * PIECES
+    row = iota((len(outs) * lines, LANES), 0)
+    lane = iota((len(outs) * lines, LANES), 1)
+    wanted = one_hot(lane == PARTS * EXPERTS + expert_at(row // lines, chips))
+    named = nt_dot(wanted, tails)
+    at = iota((count, count), 0)
+    to = iota((count, count), 1)
+    before = one_hot((at // rows == to // rows) & (at < to))
+    rank = dot(named.astype(BF16), before)
+    line = iota(named.shape, 0)
+    col = iota(named.shape, 1)
+    same = (line // CAP) % (lines // CAP) == col // rows
+    picks = one_hot(same & (named > 0.5) & (rank == (line % CAP).astype(F32)))
+    parts = [ref[:, :width].astype(F32) for ref in (own_ref, other_ref)]
+    stacked = jnp.concatenate(
+        [part[:, k * piece : (k + 1) * piece] for k in range(PIECES) for part in parts], axis=0
+    ).astype(BF16)
+    sent = dot(picks, stacked).astype(BF16)
+    for t, out in enumerate(outs):
+        out[...] = sent[t * lines : (t + 1) * lines]
+
+
+def pack(steps, chips, own, other):
+    both, width = own.shape
+    shape = (PIECES * 2 * steps * CAP, (width - LANES) // PIECES)
+    turns = chips // 2
+    return pl.pallas_call(
+        functools.partial(pack_kernel, steps, chips),
+        out_shape=[jax.ShapeDtypeStruct(shape, BF16)] * turns,
+        in_specs=[VMEM] * 2,
+        out_specs=[VMEM] * turns,
+        compiler_params=pltpu.CompilerParams(vmem_limit_bytes=24 * MIB),
+        cost_estimate=pl.CostEstimate(
+            flops=50_000_000, bytes_accessed=2_000_000, transcendentals=0
+        ),
+        name="pack",
+    )(own, other)
+
+
+def mixing(steps, chips, own_ref, other_ref):
+    both, width = own_ref.shape
+    width -= LANES
+    rows = both // steps
+    lines = PIECES * 2 * steps * CAP
+    tails = [ref[:, width:].astype(F32) for ref in (own_ref, other_ref)]
+    tails = jnp.concatenate(tails, axis=0).astype(BF16)
+    count = chips // 2 * lines
+    lane = iota((LANES, count), 0)
+    expert = expert_at(iota((LANES, count), 1) // lines, chips)
+    found = [dot(tails, one_hot(lane == part * EXPERTS + expert)) for part in range(PARTS + 1)]
+    at = iota((2 * both, 2 * both), 1)
+    to = iota((2 * both, 2 * both), 0)
+    rank = dot(one_hot((at // rows == to // rows) & (at < to)), found[PARTS].astype(BF16))
+    line = iota((2 * both, count), 1)
+    row = iota((2 * both, count), 0)
+    same = (line // CAP) % (2 * steps) == row // rows
+    slot = same & (rank == (line % CAP).astype(F32))
+    k_of = line // (2 * steps * CAP) % PIECES
+    parts = [
+        jnp.where(slot & (k_of == k), found[part], 0.0)
+        for part in range(PARTS)
+        for k in range(PIECES)
+    ]
+    return jnp.concatenate(parts, axis=0).astype(BF16)
+
+
+def stage_kernel(steps, chips, own_ref, other_ref, gu_hbm, dn_hbm, gu, dn, mix_ref, sems):
     step = dn.shape[0] // 4
     pairs = []
     for i in range(4):
@@ -189,54 +282,132 @@
     copies = [pltpu.make_async_copy(a, b, sems.at[i]) for i, (a, b) in enumerate(pairs)]
     for copy in copies:
         copy.start()
+    mix_ref[...] = mixing(steps, chips, own_ref, other_ref)
     for copy in copies:
         copy.wait()
 
 
-def stage(gate_up, down, after):
+def stage(steps, chips, own, other, gate_up, down):
+    lines = PIECES * 2 * steps * CAP
     return pl.pallas_call(
-        stage_kernel,
+        functools.partial(stage_kernel, steps, chips),
         out_shape=(
             jax.ShapeDtypeStruct(gate_up.shape[1:], BF16),
             jax.ShapeDtypeStruct(down.shape[1:], BF16),
-        ),
-        in_specs=[HBM, HBM, VMEM],
-        out_specs=(VMEM, VMEM),
+            jax.ShapeDtypeStruct((PARTS * PIECES * 2 * own.shape[0], chips // 2 * lines), BF16),
+        ),
+        in_specs=[VMEM, VMEM, HBM, HBM],
+        out_specs=(VMEM,) * 3,
         scratch_shapes=[pltpu.SemaphoreType.DMA((12,))],
         compiler_params=pltpu.CompilerParams(vmem_limit_bytes=24 * MIB),
-        cost_estimate=pl.CostEstimate(flops=0, bytes_accessed=22_000_000, transcendentals=0),
+        cost_estimate=pl.CostEstimate(
+            flops=10_000_000, bytes_accessed=22_000_000, transcendentals=0
+        ),
         name="stage",
-    )(gate_up, down, after)
-
-
-def expert_kernel(rows_ref, gu, dn, out_ref):
-    width = out_ref.shape[1]
-    expert = lax.axis_index("afd") // (lax.axis_size("afd") // EXPERTS)
-    ends = rows_ref[:, width:].astype(F32)
-    lane = iota(ends.shape, 1)
-    mine = (lane % EXPERTS == expert) & (lane < PARTS * EXPERTS)
-    weight = jnp.sum(jnp.where(mine, ends, 0.0), axis=1, keepdims=True)
-    x = rows_ref[:, :width]
-    gate = nt_dot(x, gu[0])
-    upper = nt_dot(x, gu[1])
+    )(own, other, *in_hbm(gate_up, down))
+
+
+def expert_kernel(turns, *refs):
+    own_refs, other_refs = refs[:turns], refs[turns : 2 * turns]
+    gu, dn = refs[2 * turns : 2 * turns + 2]
+    mine_refs = refs[2 * turns + 2 : 3 * turns + 2]
+    theirs_refs = refs[3 * turns + 2 :]
+    lines, piece = own_refs[0].shape
+    per = lines // PIECES
+    half = turns * per
+    n = turns * lines
+    row = iota((n, n), 0)
+    col = iota((n, n), 1)
+    order = one_hot(col == row // per % turns * lines + row // half * per + row % per)
+    sides = [
+        dot(order, jnp.concatenate([ref[...] for ref in now], axis=0)).astype(BF16)
+        for now in (own_refs, other_refs)
+    ]
+    gate = upper = None
+    for k in range(PIECES):
+        x = jnp.concatenate([side[k * half : (k + 1) * half] for side in sides], axis=0)
+        cols = pl.ds(k * piece, piece)
+        g, u = nt_dot(x, gu[0, :, cols]), nt_dot(x, gu[1, :, cols])
+        gate, upper = (g, u) if k == 0 else (gate + g, upper + u)
     act = (gate / (1.0 + jnp.exp(-gate)) * upper).astype(BF16)
-    part = dot(act, dn[...]).astype(BF16).astype(F32)
-    out_ref[...] = (part * weight).astype(BF16)
-
-
-def experts(rows, gu, dn):
-    count, width = rows.shape[0], dn.shape[1]
-    return pl.pallas_call(
-        expert_kernel,
-        out_shape=jax.ShapeDtypeStruct((count, width), BF16),
-        in_specs=[VMEM] * 3,
-        out_specs=VMEM,
+    mine = []
+    theirs = []
+    for k in range(PIECES):
+        part = dot(act, dn[:, k * piece : (k + 1) * piece]).astype(BF16)
+        mine.append(part[:half])
+        theirs.append(part[half:])
+    back = one_hot(row == col // per % turns * lines + col // half * per + col % per)
+    for parts, now in ((theirs, theirs_refs), (mine, mine_refs)):
+        out = dot(back, jnp.concatenate(parts, axis=0)).astype(BF16)
+        for t, ref in enumerate(now):
+            ref[...] = out[t * lines : (t + 1) * lines]
+
+
+def experts(own, other, gu, dn):
+    turns = len(own)
+    shape = jax.ShapeDtypeStruct(own[0].shape, BF16)
+    results = pl.pallas_call(
+        functools.partial(expert_kernel, turns),
+        out_shape=[shape] * (2 * turns),
+        in_specs=[VMEM] * (2 * turns + 2),
+        out_specs=[VMEM] * (2 * turns),
         compiler_params=pltpu.CompilerParams(vmem_limit_bytes=32 * MIB),
         cost_estimate=pl.CostEstimate(
-            flops=1_500_000_000, bytes_accessed=12_000_000, transcendentals=16384
+            flops=800_000_000, bytes_accessed=12_000_000, transcendentals=16384
         ),
         name="experts",
-    )(rows, gu, dn)
+    )(*own, *other, gu, dn)
+    return results[:turns], results[turns:]
+
+
+def combine_kernel(mix_ref, resid_ref, *refs):
+    back_refs, (kept_ref, sent_ref) = refs[:-2], refs[-2:]
+    both = resid_ref.shape[0]
+    piece = back_refs[0].shape[1]
+    product = dot(mix_ref[...], jnp.concatenate([ref[...] for ref in back_refs], axis=0))
+    n = PIECES * 2 * both
+    total = product[:n] + product[n : 2 * n] + product[2 * n :]
+    for k in range(PIECES):
+        cols = pl.ds(k * piece, piece)
+        first = k * 2 * both
+        kept_ref[:, cols] = resid_ref[:, cols] + total[first : first + both]
+        sent_ref[:, cols] = total[first + both : first + 2 * both].astype(BF16)
+
+
+def combine(mix, resid, backs):
+    return pl.pallas_call(
+        combine_kernel,
+        out_shape=(
+            jax.ShapeDtypeStruct(resid.shape, F32),
+            jax.ShapeDtypeStruct(resid.shape, BF16),
+        ),
+        in_specs=[VMEM] * (2 + len(backs)),
+        out_specs=(VMEM, VMEM),
+        compiler_params=pltpu.CompilerParams(vmem_limit_bytes=24 * MIB),
+        cost_estimate=pl.CostEstimate(
+            flops=100_000_000, bytes_accessed=1_000_000, transcendentals=0
+        ),
+        name="combine",
+    )(mix, resid, *backs)
+
+
+def finish_kernel(kept_ref, other_ref, out_ref):
+    steps, rows, _ = out_ref.shape
+    done = (kept_ref[...] + other_ref[...].astype(F32)).astype(BF16)
+    for s in range(steps):
+        out_ref[s] = done[s * rows : (s + 1) * rows]
+
+
+def finish(shape, kept, other):
+    return pl.pallas_call(
+        finish_kernel,
+        out_shape=jax.ShapeDtypeStruct(shape, BF16),
+        in_specs=[VMEM, VMEM],
+        out_specs=VMEM,
+        compiler_params=pltpu.CompilerParams(vmem_limit_bytes=24 * MIB),
+        cost_estimate=pl.CostEstimate(flops=100_000, bytes_accessed=500_000, transcendentals=0),
+        name="finish",
+    )(kept, other)
 
 
 def per_device(
@@ -251,16 +422,39 @@
     gate_up,
     down,
 ):
+    steps = queries.shape[0]
+    owners = lax.axis_size("afd")
+    chips = owners // 2
+    turns = chips // 2
+    cores = [(i, i ^ 1) for i in range(owners)]
+
+    def swap(x):
+        return lax.ppermute(x, "afd", cores)
+
+    def trade(x, t):
+        to = [(i, (i // 2 ^ distance(t, i % 2, chips)) * 2 + i % 2) for i in range(owners)]
+        return lax.ppermute(x, "afd", to)
+
     ids = expert_ids.transpose(2, 0, 1)
     weights = route_weight.transpose(2, 0, 1)
-    resid, packed = attend(
+    resid, normed = attend(
         cache_len, ids, weights, queries, fresh, kv_cache, hidden_state, norm_gain
     )
-    gathered = lax.all_gather(packed, "afd", axis=0, tiled=True)
-    gu, dn = stage(gate_up, down, resid)
-    weighted = experts(gathered, gu, dn)
-    combined = lax.psum_scatter(weighted, "afd", scatter_dimension=0, tiled=True)
-    return (resid + combined.astype(F32)).astype(BF16).reshape(queries.shape)
+    normed_other = swap(normed)
+    sent = pack(steps, chips, normed, normed_other)
+    own = [trade(sent[t], t) for t in range(turns)]
+    gu, dn, mix = stage(steps, chips, normed, normed_other, gate_up, down)
+    own[0], gu, dn = lax.optimization_barrier((own[0], gu, dn))
+    other = [swap(x) for x in own]
+    summed = []
+    for t in range(0, turns, TOGETHER):
+        mine, theirs = experts(own[t : t + TOGETHER], other[t : t + TOGETHER], gu, dn)
+        summed += [
+            (a.astype(F32) + swap(b).astype(F32)).astype(BF16) for a, b in zip(mine, theirs)
+        ]
+    backs = [trade(summed[t], t) for t in range(turns)]
+    kept, given = combine(mix, resid, backs)
+    return finish(queries.shape, kept, swap(given))
 
 
 def solution(mesh):

time: 139 us -> 45.6 us (0.33)
  waiting for transfers between devices: 90.1 us -> 11 us
  local copies, waits for them, and re-layouts: 23.6 us -> 0 us
  starting transfers between devices: 0.04 us -> 22.6 us
  between operations: 13.4 us -> 0.11 us
  Pallas kernels: 10 us -> 11.6 us
    reduce_scatter x1 -> x0, waiting for transfers between devices: 59.3 us -> none  [per_device(): lax.psum_scatter(weighted, 'afd', scatter_dimension=0, tiled=True)]
    all_gather x1 -> x0, waiting for transfers between devices: 30.8 us -> none  [per_device(): gathered = lax.all_gather(packed, 'afd', axis=0, tiled=True)]
    unnamed x30 -> x0, local copies, waits for them, and re-layouts: 22.9 us -> none
    ppermute x0 -> x18, starting transfers between devices: none -> 22.6 us  [the longest x8 11.5 us: trade(): return lax.ppermute(x, 'afd', to)]
    ppermute x0 -> x18, waiting for transfers between devices: none -> 11 us  [the longest x8 7.48 us: trade(): return lax.ppermute(x, 'afd', to)]
    pallas_call x2 -> x5, Pallas kernels: 7.2 us -> 9.36 us  [the longest x1 4.25 us: stage(): pl.pallas_call(functools.partial(stage_kernel, steps, chips), out_shape=(...]
  transfers between devices with their start and end apart: 2 -> 18, of which waited for: 2 -> 9; matrix products, arithmetic and copies ran while one was open for 0% -> 0% of each run, Pallas kernels for 2% -> 9%
where the time goes in v6:
time: 45.6 us; the launch traced here: 45.4 us
  starting transfers between devices  22.6 us (50%)
  Pallas kernels  11.6 us (25%)
  waiting for transfers between devices  11 us (24%)
    ppermute x8, starting transfers between devices, trade(): return lax.ppermute(x, 'afd', to)  11.5 us
    ppermute x10, starting transfers between devices, swap(): return lax.ppermute(x, 'afd', cores)  11.1 us
    ppermute x8, waiting for transfers between devices, trade(): return lax.ppermute(x, 'afd', to)  7.48 us
    pallas_call x1, Pallas kernels, stage(): pl.pallas_call(functools.partial(stage_kernel, steps, chips), out_shape=(...  4.25 us
    pallas_call x1, Pallas kernels, experts(): pl.pallas_call(functools.partial(expert_kernel, turns), out_shape=[shape]...  3.62 us
    ppermute x10, waiting for transfers between devices, swap(): return lax.ppermute(x, 'afd', cores)  3.5 us
    pallas_call x1, Pallas kernels, attend(): pl.pallas_call(attend_kernel, out_shape=(jax.ShapeDtypeStruct((steps * ro...  2.25 us
  transfers between devices with their start and end apart: 18, of which 9 were waited for; matrix products, arithmetic and copies ran while one was open for 0% of the time, Pallas kernels for 9%

profile of v6, /device:TPU:0, one launch (start us, length us, event | category | flops | bytes accessed | tf_op | source)
XLA Modules:
  0.0 45.4 jit_solution(8927558759151973889)
XLA Ops:
  0.0 2.3 %attend.1 = (f32[8,7168]{1,0:T(8,128)S(1)}, bf16[8,7296]{1,0:T(8,128)(2,1)S(1)}) custom-call(s32[4]{0:T(128)} %len_hbm.1, s32[3,2,4]{2,1,0:T(2,128)} %bitcast.6, f32[3,2,4]{2,1,0:T(2,128)} %bitcast.7, bf16[2,4,7168]{2,1,0:T(4,128)(2,1)} %q_hbm.1, bf16[2,4,448]{2,1,0:T(4,128)(2,1)} %fresh_hbm.1, bf16[4,448,128]{2,1,0:T(8,128)(2,1)} %bitcast.4, ...), custom_call_target="tpu_custom_call" | custom-call | flops 300000000 | bytes 2000000 | tf_op jit(solution)/shard_map/attend/pallas_call | solution.py:171
  2.3 0.5 %collective-permute-start = (bf16[8,7296]{1,0:T(8,128)(2,1)S(1)}, bf16[8,7296]{1,0:T(8,128)(2,1)S(1)}, u32[]{:S(2)}, u32[]{:S(2)}) collective-permute-start(bf16[8,7296]{1,0:T(8,128)(2,1)S(1)} %get-tuple-element.27.own_ref), channel_id=1, source_target_pairs={{0,1},{1,0},{2,3},{3,2},{4,5},{5,4},{6,7},{7,6},{8,9},{9,8},{10,11... | collective-permute-start | bytes 350216 | tf_op jit(solution)/shard_map/ppermute | solution.py:432
  2.8 1.0 %collective-permute-done.other_ref = bf16[8,7296]{1,0:T(8,128)(2,1)S(1)} collective-permute-done((bf16[8,7296]{1,0:T(8,128)(2,1)S(1)}, bf16[8,7296]{1,0:T(8,128)(2,1)S(1)}, u32[]{:S(2)}, u32[]{:S(2)}) %collective-permute-start) | collective-permute-done | bytes 116768 | tf_op jit(solution)/shard_map/ppermute | solution.py:432
  3.7 0.5 %pack.1 = (bf16[32,1792]{1,0:T(8,128)(2,1)S(1)}, bf16[32,1792]{1,0:T(8,128)(2,1)S(1)}, bf16[32,1792]{1,0:T(8,128)(2,1)S(1)}, bf16[32,1792]{1,0:T(8,128)(2,1)S(1)}) custom-call(bf16[8,7296]{1,0:T(8,128)(2,1)S(1)} %get-tuple-element.27.own_ref, bf16[8,7296]{1,0:T(8,128)(2,1)S(1)} %collective-permute-done.other_ref), custom_call_target="tpu_custom_call" | custom-call | flops 50000000 | bytes 2000000 | tf_op jit(solution)/shard_map/pack/pallas_call | solution.py:234
  4.3 0.7 %collective-permute-start.1 = (bf16[32,1792]{1,0:T(8,128)(2,1)S(1)}, bf16[32,1792]{1,0:T(8,128)(2,1)S(1)}, u32[]{:S(2)}, u32[]{:S(2)}) collective-permute-start(bf16[32,1792]{1,0:T(8,128)(2,1)S(1)} %get-tuple-element.30), channel_id=1, source_target_pairs={{0,0},{1,15},{2,2},{3,13},{4,4},{5,11},{6,6},{7,9},{8,8},{9,7},{10... | collective-permute-start | bytes 344072 | tf_op jit(solution)/shard_map/ppermute | solution.py:436
  4.9 3.0 %collective-permute-start.2 = (bf16[32,1792]{1,0:T(8,128)(2,1)S(1)}, bf16[32,1792]{1,0:T(8,128)(2,1)S(1)}, u32[]{:S(2)}, u32[]{:S(2)}) collective-permute-start(bf16[32,1792]{1,0:T(8,128)(2,1)S(1)} %get-tuple-element.34), channel_id=1, source_target_pairs={{0,4},{1,11},{2,6},{3,9},{4,0},{5,15},{6,2},{7,13},{8,12},{9,3},{1... | collective-permute-start | bytes 344072 | tf_op jit(solution)/shard_map/ppermute | solution.py:436
  7.9 2.6 %collective-permute-start.3 = (bf16[32,1792]{1,0:T(8,128)(2,1)S(1)}, bf16[32,1792]{1,0:T(8,128)(2,1)S(1)}, u32[]{:S(2)}, u32[]{:S(2)}) collective-permute-start(bf16[32,1792]{1,0:T(8,128)(2,1)S(1)} %get-tuple-element.35), channel_id=1, source_target_pairs={{0,8},{1,7},{2,10},{3,5},{4,12},{5,3},{6,14},{7,1},{8,0},{9,15},{1... | collective-permute-start | bytes 344072 | tf_op jit(solution)/shard_map/ppermute | solution.py:436
  10.5 4.2 %stage.1 = (bf16[2,256,7168]{2,1,0:T(8,128)(2,1)S(1)}, bf16[256,7168]{1,0:T(8,128)(2,1)S(1)}, bf16[192,128]{1,0:T(8,128)(2,1)S(1)}) custom-call(bf16[8,7296]{1,0:T(8,128)(2,1)S(1)} %get-tuple-element.27.own_ref, bf16[8,7296]{1,0:T(8,128)(2,1)S(1)} %collective-permute-done.other_ref, bf16[1,2,256,7168]{3,2,1,0:T(8,128)(2,1)} %gu_hbm.1, ...), custom_call_target="tpu_custom_call" | custom-call | flops 10000000 | bytes 22000000 | tf_op jit(solution)/shard_map/stage/pallas_call | solution.py:292
  14.8 6.7 %collective-permute-start.6 = (bf16[32,1792]{1,0:T(8,128)(2,1)S(1)}, bf16[32,1792]{1,0:T(8,128)(2,1)S(1)}, u32[]{:S(2)}, u32[]{:S(2)}) collective-permute-start(bf16[32,1792]{1,0:T(8,128)(2,1)S(1)} %collective-permute-done.2.refs_1_), channel_id=1, source_target_pairs={{0,1},{1,0},{2,3},{3,2},{4,5},{5,4},{6,7},{7,6},{8,9},{9,8},{10,11... | collective-permute-start | bytes 344072 | tf_op jit(solution)/shard_map/ppermute | solution.py:432
  21.5 0.5 %collective-permute-start.8 = (bf16[32,1792]{1,0:T(8,128)(2,1)S(1)}, bf16[32,1792]{1,0:T(8,128)(2,1)S(1)}, u32[]{:S(2)}, u32[]{:S(2)}) collective-permute-start(bf16[32,1792]{1,0:T(8,128)(2,1)S(1)} %collective-permute-done.4.refs_3_), channel_id=1, source_target_pairs={{0,1},{1,0},{2,3},{3,2},{4,5},{5,4},{6,7},{7,6},{8,9},{9,8},{10,11... | collective-permute-start | bytes 344072 | tf_op jit(solution)/shard_map/ppermute | solution.py:432
  22.0 0.4 collective-permute-done.6.refs_5_
  22.4 0.4 collective-permute-done.7.refs_6_
  22.9 0.3 collective-permute-done.5.refs_4_
  23.3 3.6 %experts.1 = (bf16[32,1792]{1,0:T(8,128)(2,1)S(1)}, bf16[32,1792]{1,0:T(8,128)(2,1)S(1)}, bf16[32,1792]{1,0:T(8,128)(2,1)S(1)}, bf16[32,1792]{1,0:T(8,128)(2,1)S...) custom-call(bf16[32,1792]{1,0:T(8,128)(2,1)S(1)} %collective-permute, ...), custom_call_target="tpu_custom_call" | custom-call | flops 800000000 | bytes 12000000 | tf_op jit(solution)/shard_map/experts/pallas_call | solution.py:349
  27.1 0.3 collective-permute-start.11
  27.7 0.3 collective-permute-start.15
  28.3 0.7 %collective-permute-start.10 = (bf16[32,1792]{1,0:T(8,128)(2,1)S(1)}, bf16[32,1792]{1,0:T(8,128)(2,1)S(1)}, u32[]{:S(2)}, u32[]{:S(2)}) collective-permute-start(bf16[32,1792]{1,0:T(8,128)(2,1)S(1)} %add_convert_fusion.3), channel_id=1, source_target_pairs={{0,0},{1,15},{2,2},{3,13},{4,4},{5,11},{6,6},{7,9},{8,8},{9,7},{10... | collective-permute-start | bytes 344072 | tf_op jit(solution)/shard_map/ppermute | solution.py:436
  29.1 0.8 %collective-permute-start.12 = (bf16[32,1792]{1,0:T(8,128)(2,1)S(1)}, bf16[32,1792]{1,0:T(8,128)(2,1)S(1)}, u32[]{:S(2)}, u32[]{:S(2)}) collective-permute-start(bf16[32,1792]{1,0:T(8,128)(2,1)S(1)} %add_convert_fusion.2), channel_id=1, source_target_pairs={{0,4},{1,11},{2,6},{3,9},{4,0},{5,15},{6,2},{7,13},{8,12},{9,3},{1... | collective-permute-start | bytes 344072 | tf_op jit(solution)/shard_map/ppermute | solution.py:436
  30.0 2.2 %collective-permute-start.14 = (bf16[32,1792]{1,0:T(8,128)(2,1)S(1)}, bf16[32,1792]{1,0:T(8,128)(2,1)S(1)}, u32[]{:S(2)}, u32[]{:S(2)}) collective-permute-start(bf16[32,1792]{1,0:T(8,128)(2,1)S(1)} %add_convert_fusion.1), channel_id=1, source_target_pairs={{0,8},{1,7},{2,10},{3,5},{4,12},{5,3},{6,14},{7,1},{8,0},{9,15},{1... | collective-permute-start | bytes 344072 | tf_op jit(solution)/shard_map/ppermute | solution.py:436
  32.1 1.6 %collective-permute-start.16 = (bf16[32,1792]{1,0:T(8,128)(2,1)S(1)}, bf16[32,1792]{1,0:T(8,128)(2,1)S(1)}, u32[]{:S(2)}, u32[]{:S(2)}) collective-permute-start(bf16[32,1792]{1,0:T(8,128)(2,1)S(1)} %add_convert_fusion), channel_id=1, source_target_pairs={{0,12},{1,3},{2,14},{3,1},{4,8},{5,7},{6,10},{7,5},{8,4},{9,11},{1... | collective-permute-start | bytes 344072 | tf_op jit(solution)/shard_map/ppermute | solution.py:436
  33.9 7.3 %collective-permute-done.14.refs_2_ = bf16[32,1792]{1,0:T(8,128)(2,1)S(1)} collective-permute-done((bf16[32,1792]{1,0:T(8,128)(2,1)S(1)}, bf16[32,1792]{1,0:T(8,128)(2,1)S(1)}, u32[]{:S(2)}, u32[]{:S(2)}) %collective-permute-start.14) | collective-permute-done | bytes 114720 | tf_op jit(solution)/shard_map/ppermute | solution.py:436
  41.5 2.2 %collective-permute-start.17 = (bf16[8,7168]{1,0:T(8,128)(2,1)S(1)}, bf16[8,7168]{1,0:T(8,128)(2,1)S(1)}, u32[]{:S(2)}, u32[]{:S(2)}) collective-permute-start(bf16[8,7168]{1,0:T(8,128)(2,1)S(1)} %get-tuple-element.48), channel_id=1, source_target_pairs={{0,1},{1,0},{2,3},{3,2},{4,5},{5,4},{6,7},{7,6},{8,9},{9,8},{10,11... | collective-permute-start | bytes 344072 | tf_op jit(solution)/shard_map/ppermute | solution.py:432
  43.8 1.0 %collective-permute-done.17.other_ref = bf16[8,7168]{1,0:T(8,128)(2,1)S(1)} collective-permute-done((bf16[8,7168]{1,0:T(8,128)(2,1)S(1)}, bf16[8,7168]{1,0:T(8,128)(2,1)S(1)}, u32[]{:S(2)}, u32[]{:S(2)}) %collective-permute-start.17) | collective-permute-done | bytes 114720 | tf_op jit(solution)/shard_map/ppermute | solution.py:432
  44.7 0.7 %finish.1 = bf16[2,4,7168]{2,1,0:T(4,128)(2,1)} custom-call(f32[8,7168]{1,0:T(8,128)S(1)} %get-tuple-element.47.kept_ref, bf16[8,7168]{1,0:T(8,128)(2,1)S(1)} %collective-permute-done.17.other_ref), custom_call_target="tpu_custom_call" | custom-call | flops 100000 | bytes 500000 | tf_op jit(solution)/shard_map/finish/pallas_call | solution.py:402
  (22 shorter events, 1.6 us)
Async XLA Ops:
  2.3 1.5 %collective-permute-start = (bf16[8,7296]{1,0:T(8,128)(2,1)S(1)}, bf16[8,7296]{1,0:T(8,128)(2,1)S(1)}, u32[]{:S(2)}, u32[]{:S(2)}) collective-permute-start(bf16[8,7296]{1,0:T(8,128)(2,1)S(1)} %get-tuple-element.27.own_ref), channel_id=1, source_target_pairs={{0,1},{1,0},{2,3},{3,2},{4,5},{5,4},{6,7},{7,6},{8,9},{9,8},{10,11... | collective-permute-start | bytes 350216 | tf_op jit(solution)/shard_map/ppermute | solution.py:432
  4.3 10.5 %collective-permute-start.1 = (bf16[32,1792]{1,0:T(8,128)(2,1)S(1)}, bf16[32,1792]{1,0:T(8,128)(2,1)S(1)}, u32[]{:S(2)}, u32[]{:S(2)}) collective-permute-start(bf16[32,1792]{1,0:T(8,128)(2,1)S(1)} %get-tuple-element.30), channel_id=1, source_target_pairs={{0,0},{1,15},{2,2},{3,13},{4,4},{5,11},{6,6},{7,9},{8,8},{9,7},{10... | collective-permute-start | bytes 344072 | tf_op jit(solution)/shard_map/ppermute | solution.py:436
  4.9 9.9 %collective-permute-start.2 = (bf16[32,1792]{1,0:T(8,128)(2,1)S(1)}, bf16[32,1792]{1,0:T(8,128)(2,1)S(1)}, u32[]{:S(2)}, u32[]{:S(2)}) collective-permute-start(bf16[32,1792]{1,0:T(8,128)(2,1)S(1)} %get-tuple-element.34), channel_id=1, source_target_pairs={{0,4},{1,11},{2,6},{3,9},{4,0},{5,15},{6,2},{7,13},{8,12},{9,3},{1... | collective-permute-start | bytes 344072 | tf_op jit(solution)/shard_map/ppermute | solution.py:436
  7.9 13.5 %collective-permute-start.3 = (bf16[32,1792]{1,0:T(8,128)(2,1)S(1)}, bf16[32,1792]{1,0:T(8,128)(2,1)S(1)}, u32[]{:S(2)}, u32[]{:S(2)}) collective-permute-start(bf16[32,1792]{1,0:T(8,128)(2,1)S(1)} %get-tuple-element.35), channel_id=1, source_target_pairs={{0,8},{1,7},{2,10},{3,5},{4,12},{5,3},{6,14},{7,1},{8,0},{9,15},{1... | collective-permute-start | bytes 344072 | tf_op jit(solution)/shard_map/ppermute | solution.py:436
  10.5 10.9 %collective-permute-start.4 = (bf16[32,1792]{1,0:T(8,128)(2,1)S(1)}, bf16[32,1792]{1,0:T(8,128)(2,1)S(1)}, u32[]{:S(2)}, u32[]{:S(2)}) collective-permute-start(bf16[32,1792]{1,0:T(8,128)(2,1)S(1)} %get-tuple-element.36), channel_id=1, source_target_pairs={{0,12},{1,3},{2,14},{3,1},{4,8},{5,7},{6,10},{7,5},{8,4},{9,11},{1... | collective-permute-start | bytes 344072 | tf_op jit(solution)/shard_map/ppermute | solution.py:436
  14.8 7.6 %collective-permute-start.6 = (bf16[32,1792]{1,0:T(8,128)(2,1)S(1)}, bf16[32,1792]{1,0:T(8,128)(2,1)S(1)}, u32[]{:S(2)}, u32[]{:S(2)}) collective-permute-start(bf16[32,1792]{1,0:T(8,128)(2,1)S(1)} %collective-permute-done.2.refs_1_), channel_id=1, source_target_pairs={{0,1},{1,0},{2,3},{3,2},{4,5},{5,4},{6,7},{7,6},{8,9},{9,8},{10,11... | collective-permute-start | bytes 344072 | tf_op jit(solution)/shard_map/ppermute | solution.py:432
  21.5 1.3 %collective-permute-start.7 = (bf16[32,1792]{1,0:T(8,128)(2,1)S(1)}, bf16[32,1792]{1,0:T(8,128)(2,1)S(1)}, u32[]{:S(2)}, u32[]{:S(2)}) collective-permute-start(bf16[32,1792]{1,0:T(8,128)(2,1)S(1)} %collective-permute-done.3.refs_2_), channel_id=1, source_target_pairs={{0,1},{1,0},{2,3},{3,2},{4,5},{5,4},{6,7},{7,6},{8,9},{9,8},{10,11... | collective-permute-start | bytes 344072 | tf_op jit(solution)/shard_map/ppermute | solution.py:432
  21.5 1.5 %collective-permute-start.8 = (bf16[32,1792]{1,0:T(8,128)(2,1)S(1)}, bf16[32,1792]{1,0:T(8,128)(2,1)S(1)}, u32[]{:S(2)}, u32[]{:S(2)}) collective-permute-start(bf16[32,1792]{1,0:T(8,128)(2,1)S(1)} %collective-permute-done.4.refs_3_), channel_id=1, source_target_pairs={{0,1},{1,0},{2,3},{3,2},{4,5},{5,4},{6,7},{7,6},{8,9},{9,8},{10,11... | collective-permute-start | bytes 344072 | tf_op jit(solution)/shard_map/ppermute | solution.py:432
  22.0 1.3 %collective-permute-start.5 = (bf16[32,1792]{1,0:T(8,128)(2,1)S(1)}, bf16[32,1792]{1,0:T(8,128)(2,1)S(1)}, u32[]{:S(2)}, u32[]{:S(2)}) collective-permute-start(bf16[32,1792]{1,0:T(8,128)(2,1)S(1)} %collective-permute-done.1.refs_0_), channel_id=1, source_target_pairs={{0,1},{1,0},{2,3},{3,2},{4,5},{5,4},{6,7},{7,6},{8,9},{9,8},{10,11... | collective-permute-start | bytes 344072 | tf_op jit(solution)/shard_map/ppermute | solution.py:432
  26.9 1.4 %collective-permute-start.9 = (bf16[32,1792]{1,0:T(8,128)(2,1)S(1)}, bf16[32,1792]{1,0:T(8,128)(2,1)S(1)}, u32[]{:S(2)}, u32[]{:S(2)}) collective-permute-start(bf16[32,1792]{1,0:T(8,128)(2,1)S(1)} %get-tuple-element.40), channel_id=1, source_target_pairs={{0,1},{1,0},{2,3},{3,2},{4,5},{5,4},{6,7},{7,6},{8,9},{9,8},{10,11... | collective-permute-start | bytes 344072 | tf_op jit(solution)/shard_map/ppermute | solution.py:432
  27.1 1.9 %collective-permute-start.11 = (bf16[32,1792]{1,0:T(8,128)(2,1)S(1)}, bf16[32,1792]{1,0:T(8,128)(2,1)S(1)}, u32[]{:S(2)}, u32[]{:S(2)}) collective-permute-start(bf16[32,1792]{1,0:T(8,128)(2,1)S(1)} %get-tuple-element.42), channel_id=1, source_target_pairs={{0,1},{1,0},{2,3},{3,2},{4,5},{5,4},{6,7},{7,6},{8,9},{9,8},{10,11... | collective-permute-start | bytes 344072 | tf_op jit(solution)/shard_map/ppermute | solution.py:432
  27.5 2.4 %collective-permute-start.13 = (bf16[32,1792]{1,0:T(8,128)(2,1)S(1)}, bf16[32,1792]{1,0:T(8,128)(2,1)S(1)}, u32[]{:S(2)}, u32[]{:S(2)}) collective-permute-start(bf16[32,1792]{1,0:T(8,128)(2,1)S(1)} %get-tuple-element.44), channel_id=1, source_target_pairs={{0,1},{1,0},{2,3},{3,2},{4,5},{5,4},{6,7},{7,6},{8,9},{9,8},{10,11... | collective-permute-start | bytes 344072 | tf_op jit(solution)/shard_map/ppermute | solution.py:432
  27.7 4.5 %collective-permute-start.15 = (bf16[32,1792]{1,0:T(8,128)(2,1)S(1)}, bf16[32,1792]{1,0:T(8,128)(2,1)S(1)}, u32[]{:S(2)}, u32[]{:S(2)}) collective-permute-start(bf16[32,1792]{1,0:T(8,128)(2,1)S(1)} %get-tuple-element.46), channel_id=1, source_target_pairs={{0,1},{1,0},{2,3},{3,2},{4,5},{5,4},{6,7},{7,6},{8,9},{9,8},{10,11... | collective-permute-start | bytes 344072 | tf_op jit(solution)/shard_map/ppermute | solution.py:432
  28.3 5.4 %collective-permute-start.10 = (bf16[32,1792]{1,0:T(8,128)(2,1)S(1)}, bf16[32,1792]{1,0:T(8,128)(2,1)S(1)}, u32[]{:S(2)}, u32[]{:S(2)}) collective-permute-start(bf16[32,1792]{1,0:T(8,128)(2,1)S(1)} %add_convert_fusion.3), channel_id=1, source_target_pairs={{0,0},{1,15},{2,2},{3,13},{4,4},{5,11},{6,6},{7,9},{8,8},{9,7},{10... | collective-permute-start | bytes 344072 | tf_op jit(solution)/shard_map/ppermute | solution.py:436
  29.1 4.9 %collective-permute-start.12 = (bf16[32,1792]{1,0:T(8,128)(2,1)S(1)}, bf16[32,1792]{1,0:T(8,128)(2,1)S(1)}, u32[]{:S(2)}, u32[]{:S(2)}) collective-permute-start(bf16[32,1792]{1,0:T(8,128)(2,1)S(1)} %add_convert_fusion.2), channel_id=1, source_target_pairs={{0,4},{1,11},{2,6},{3,9},{4,0},{5,15},{6,2},{7,13},{8,12},{9,3},{1... | collective-permute-start | bytes 344072 | tf_op jit(solution)/shard_map/ppermute | solution.py:436
  30.0 11.2 %collective-permute-start.14 = (bf16[32,1792]{1,0:T(8,128)(2,1)S(1)}, bf16[32,1792]{1,0:T(8,128)(2,1)S(1)}, u32[]{:S(2)}, u32[]{:S(2)}) collective-permute-start(bf16[32,1792]{1,0:T(8,128)(2,1)S(1)} %add_convert_fusion.1), channel_id=1, source_target_pairs={{0,8},{1,7},{2,10},{3,5},{4,12},{5,3},{6,14},{7,1},{8,0},{9,15},{1... | collective-permute-start | bytes 344072 | tf_op jit(solution)/shard_map/ppermute | solution.py:436
  32.1 9.0 %collective-permute-start.16 = (bf16[32,1792]{1,0:T(8,128)(2,1)S(1)}, bf16[32,1792]{1,0:T(8,128)(2,1)S(1)}, u32[]{:S(2)}, u32[]{:S(2)}) collective-permute-start(bf16[32,1792]{1,0:T(8,128)(2,1)S(1)} %add_convert_fusion), channel_id=1, source_target_pairs={{0,12},{1,3},{2,14},{3,1},{4,8},{5,7},{6,10},{7,5},{8,4},{9,11},{1... | collective-permute-start | bytes 344072 | tf_op jit(solution)/shard_map/ppermute | solution.py:436
  41.5 3.2 %collective-permute-start.17 = (bf16[8,7168]{1,0:T(8,128)(2,1)S(1)}, bf16[8,7168]{1,0:T(8,128)(2,1)S(1)}, u32[]{:S(2)}, u32[]{:S(2)}) collective-permute-start(bf16[8,7168]{1,0:T(8,128)(2,1)S(1)} %get-tuple-element.48), channel_id=1, source_target_pairs={{0,1},{1,0},{2,3},{3,2},{4,5},{5,4},{6,7},{7,6},{8,9},{9,8},{10,11... | collective-permute-start | bytes 344072 | tf_op jit(solution)/shard_map/ppermute | solution.py:432

commit v7 on v6

--- a/solution.py
+++ b/solution.py
@@ -431,9 +431,14 @@
     def swap(x):
         return lax.ppermute(x, "afd", cores)
 
-    def trade(x, t):
-        to = [(i, (i // 2 ^ distance(t, i % 2, chips)) * 2 + i % 2) for i in range(owners)]
-        return lax.ppermute(x, "afd", to)
+    def route(t):
+        return [(i, (i // 2 ^ distance(t, i % 2, chips)) * 2 + 1 - i % 2) for i in range(owners)]
+
+    def send(x, t):
+        return lax.ppermute(x, "afd", route(t))
+
+    def send_back(x, t):
+        return lax.ppermute(x, "afd", [(j, i) for i, j in route(t)])
 
     ids = expert_ids.transpose(2, 0, 1)
     weights = route_weight.transpose(2, 0, 1)
@@ -442,7 +447,7 @@
     )
     normed_other = swap(normed)
     sent = pack(steps, chips, normed, normed_other)
-    own = [trade(sent[t], t) for t in range(turns)]
+    own = [send(sent[t], t) for t in range(turns)]
     gu, dn, mix = stage(steps, chips, normed, normed_other, gate_up, down)
     own[0], gu, dn = lax.optimization_barrier((own[0], gu, dn))
     other = [swap(x) for x in own]
@@ -452,7 +457,7 @@
         summed += [
             (a.astype(F32) + swap(b).astype(F32)).astype(BF16) for a, b in zip(mine, theirs)
         ]
-    backs = [trade(summed[t], t) for t in range(turns)]
+    backs = [send_back(summed[t], t) for t in range(turns)]
     kept, given = combine(mix, resid, backs)
     return finish(queries.shape, kept, swap(given))
 

time: 45.6 us -> 41.6 us (0.912)
  starting transfers between devices: 22.6 us -> 14.3 us
  waiting for transfers between devices: 11 us -> 15.4 us
    ppermute x10, starting transfers between devices: 11.1 us -> 2.19 us  [swap(): return lax.ppermute(x, 'afd', cores)]
    ppermute x8, waiting for transfers between devices: 7.48 us -> 11.5 us  [the longest x4 8.1 us: send_back(): return lax.ppermute(x, 'afd', [(j, i) for i, j in route(t)])]
    ppermute x8, starting transfers between devices: 11.5 us -> 12.1 us  [the longest x4 7.5 us: send(): return lax.ppermute(x, 'afd', route(t))]
  transfers between devices with their start and end apart: 18 -> 18, of which waited for: 9 -> 11; matrix products, arithmetic and copies ran while one was open for 0% -> 0% of each run, Pallas kernels for 9% -> 10%
where the time goes in v7:
time: 41.6 us; the launch traced here: 41.5 us
  waiting for transfers between devices  15.4 us (37%)
  starting transfers between devices  14.3 us (34%)
  Pallas kernels  11.6 us (28%)
    ppermute x4, waiting for transfers between devices, send_back(): return lax.ppermute(x, 'afd', [(j, i) for i, j in route(t)])  8.1 us
    ppermute x4, starting transfers between devices, send(): return lax.ppermute(x, 'afd', route(t))  7.5 us
    ppermute x4, starting transfers between devices, send_back(): return lax.ppermute(x, 'afd', [(j, i) for i, j in route(t)])  4.58 us
    pallas_call x1, Pallas kernels, stage(): pl.pallas_call(functools.partial(stage_kernel, steps, chips), out_shape=(...  4.25 us
    ppermute x10, waiting for transfers between devices, swap(): return lax.ppermute(x, 'afd', cores)  3.91 us
    pallas_call x1, Pallas kernels, experts(): pl.pallas_call(functools.partial(expert_kernel, turns), out_shape=[shape]...  3.61 us
    ppermute x4, waiting for transfers between devices, send(): return lax.ppermute(x, 'afd', route(t))  3.37 us
    pallas_call x1, Pallas kernels, attend(): pl.pallas_call(attend_kernel, out_shape=(jax.ShapeDtypeStruct((steps * ro...  2.25 us
  transfers between devices with their start and end apart: 18, of which 11 were waited for; matrix products, arithmetic and copies ran while one was open for 0% of the time, Pallas kernels for 10%

profile of v7, /device:TPU:0, one launch (start us, length us, event | category | flops | bytes accessed | tf_op | source)
XLA Modules:
  0.0 41.5 jit_solution(206780709613684342)
XLA Ops:
  0.0 2.3 %attend.1 = (f32[8,7168]{1,0:T(8,128)S(1)}, bf16[8,7296]{1,0:T(8,128)(2,1)S(1)}) custom-call(s32[4]{0:T(128)} %len_hbm.1, s32[3,2,4]{2,1,0:T(2,128)} %bitcast.6, f32[3,2,4]{2,1,0:T(2,128)} %bitcast.7, bf16[2,4,7168]{2,1,0:T(4,128)(2,1)} %q_hbm.1, bf16[2,4,448]{2,1,0:T(4,128)(2,1)} %fresh_hbm.1, bf16[4,448,128]{2,1,0:T(8,128)(2,1)} %bitcast.4, ...), custom_call_target="tpu_custom_call" | custom-call | flops 300000000 | bytes 2000000 | tf_op jit(solution)/shard_map/attend/pallas_call | solution.py:171
  2.3 0.5 %collective-permute-start = (bf16[8,7296]{1,0:T(8,128)(2,1)S(1)}, bf16[8,7296]{1,0:T(8,128)(2,1)S(1)}, u32[]{:S(2)}, u32[]{:S(2)}) collective-permute-start(bf16[8,7296]{1,0:T(8,128)(2,1)S(1)} %get-tuple-element.27.own_ref), channel_id=1, source_target_pairs={{0,1},{1,0},{2,3},{3,2},{4,5},{5,4},{6,7},{7,6},{8,9},{9,8},{10,11... | collective-permute-start | bytes 350216 | tf_op jit(solution)/shard_map/ppermute | solution.py:432
  2.8 1.0 %collective-permute-done.other_ref = bf16[8,7296]{1,0:T(8,128)(2,1)S(1)} collective-permute-done((bf16[8,7296]{1,0:T(8,128)(2,1)S(1)}, bf16[8,7296]{1,0:T(8,128)(2,1)S(1)}, u32[]{:S(2)}, u32[]{:S(2)}) %collective-permute-start) | collective-permute-done | bytes 116768 | tf_op jit(solution)/shard_map/ppermute | solution.py:432
  3.7 0.5 %pack.1 = (bf16[32,1792]{1,0:T(8,128)(2,1)S(1)}, bf16[32,1792]{1,0:T(8,128)(2,1)S(1)}, bf16[32,1792]{1,0:T(8,128)(2,1)S(1)}, bf16[32,1792]{1,0:T(8,128)(2,1)S(1)}) custom-call(bf16[8,7296]{1,0:T(8,128)(2,1)S(1)} %get-tuple-element.27.own_ref, bf16[8,7296]{1,0:T(8,128)(2,1)S(1)} %collective-permute-done.other_ref), custom_call_target="tpu_custom_call" | custom-call | flops 50000000 | bytes 2000000 | tf_op jit(solution)/shard_map/pack/pallas_call | solution.py:234
  4.3 0.4 collective-permute-start.1
  4.7 4.8 %collective-permute-start.2 = (bf16[32,1792]{1,0:T(8,128)(2,1)S(1)}, bf16[32,1792]{1,0:T(8,128)(2,1)S(1)}, u32[]{:S(2)}, u32[]{:S(2)}) collective-permute-start(bf16[32,1792]{1,0:T(8,128)(2,1)S(1)} %get-tuple-element.34), channel_id=1, source_target_pairs={{0,5},{1,10},{2,7},{3,8},{4,1},{5,14},{6,3},{7,12},{8,13},{9,2},{1... | collective-permute-start | bytes 344072 | tf_op jit(solution)/shard_map/ppermute | solution.py:438
  9.5 2.3 %collective-permute-start.4 = (bf16[32,1792]{1,0:T(8,128)(2,1)S(1)}, bf16[32,1792]{1,0:T(8,128)(2,1)S(1)}, u32[]{:S(2)}, u32[]{:S(2)}) collective-permute-start(bf16[32,1792]{1,0:T(8,128)(2,1)S(1)} %get-tuple-element.36), channel_id=1, source_target_pairs={{0,13},{1,2},{2,15},{3,0},{4,9},{5,6},{6,11},{7,4},{8,5},{9,10},{1... | collective-permute-start | bytes 344072 | tf_op jit(solution)/shard_map/ppermute | solution.py:438
  11.8 4.2 %stage.1 = (bf16[2,256,7168]{2,1,0:T(8,128)(2,1)S(1)}, bf16[256,7168]{1,0:T(8,128)(2,1)S(1)}, bf16[192,128]{1,0:T(8,128)(2,1)S(1)}) custom-call(bf16[8,7296]{1,0:T(8,128)(2,1)S(1)} %get-tuple-element.27.own_ref, bf16[8,7296]{1,0:T(8,128)(2,1)S(1)} %collective-permute-done.other_ref, bf16[1,2,256,7168]{3,2,1,0:T(8,128)(2,1)} %gu_hbm.1, ...), custom_call_target="tpu_custom_call" | custom-call | flops 10000000 | bytes 22000000 | tf_op jit(solution)/shard_map/stage/pallas_call | solution.py:292
  16.0 1.5 %collective-permute-done.2.refs_1_ = bf16[32,1792]{1,0:T(8,128)(2,1)S(1)} collective-permute-done((bf16[32,1792]{1,0:T(8,128)(2,1)S(1)}, bf16[32,1792]{1,0:T(8,128)(2,1)S(1)}, u32[]{:S(2)}, u32[]{:S(2)}) %collective-permute-start.2) | collective-permute-done | bytes 114720 | tf_op jit(solution)/shard_map/ppermute | solution.py:438
  17.5 1.9 %collective-permute-done.3.refs_2_ = bf16[32,1792]{1,0:T(8,128)(2,1)S(1)} collective-permute-done((bf16[32,1792]{1,0:T(8,128)(2,1)S(1)}, bf16[32,1792]{1,0:T(8,128)(2,1)S(1)}, u32[]{:S(2)}, u32[]{:S(2)}) %collective-permute-start.3) | collective-permute-done | bytes 114720 | tf_op jit(solution)/shard_map/ppermute | solution.py:438
  19.4 0.5 %collective-permute-start.8 = (bf16[32,1792]{1,0:T(8,128)(2,1)S(1)}, bf16[32,1792]{1,0:T(8,128)(2,1)S(1)}, u32[]{:S(2)}, u32[]{:S(2)}) collective-permute-start(bf16[32,1792]{1,0:T(8,128)(2,1)S(1)} %collective-permute-done.4.refs_3_), channel_id=1, source_target_pairs={{0,1},{1,0},{2,3},{3,2},{4,5},{5,4},{6,7},{7,6},{8,9},{9,8},{10,11... | collective-permute-start | bytes 344072 | tf_op jit(solution)/shard_map/ppermute | solution.py:432
  19.9 0.8 %collective-permute-done.7.refs_6_ = bf16[32,1792]{1,0:T(8,128)(2,1)S(1)} collective-permute-done((bf16[32,1792]{1,0:T(8,128)(2,1)S(1)}, bf16[32,1792]{1,0:T(8,128)(2,1)S(1)}, u32[]{:S(2)}, u32[]{:S(2)}) %collective-permute-start.7) | collective-permute-done | bytes 114720 | tf_op jit(solution)/shard_map/ppermute | solution.py:432
  20.9 0.3 collective-permute-done.5.refs_4_
  21.2 3.6 %experts.1 = (bf16[32,1792]{1,0:T(8,128)(2,1)S(1)}, bf16[32,1792]{1,0:T(8,128)(2,1)S(1)}, bf16[32,1792]{1,0:T(8,128)(2,1)S(1)}, bf16[32,1792]{1,0:T(8,128)(2,1)S...) custom-call(bf16[32,1792]{1,0:T(8,128)(2,1)S(1)} %collective-permute, ...), custom_call_target="tpu_custom_call" | custom-call | flops 800000000 | bytes 12000000 | tf_op jit(solution)/shard_map/experts/pallas_call | solution.py:349
  25.1 0.3 collective-permute-start.11
  25.6 0.3 collective-permute-start.15
  26.3 1.8 %collective-permute-start.10 = (bf16[32,1792]{1,0:T(8,128)(2,1)S(1)}, bf16[32,1792]{1,0:T(8,128)(2,1)S(1)}, u32[]{:S(2)}, u32[]{:S(2)}) collective-permute-start(bf16[32,1792]{1,0:T(8,128)(2,1)S(1)} %add_convert_fusion.3), channel_id=1, source_target_pairs={{1,0},{14,1},{3,2},{12,3},{5,4},{10,5},{7,6},{8,7},{9,8},{6,9},{11... | collective-permute-start | bytes 344072 | tf_op jit(solution)/shard_map/ppermute | solution.py:441
  28.1 0.4 collective-permute-start.12
  28.5 2.4 %collective-permute-start.14 = (bf16[32,1792]{1,0:T(8,128)(2,1)S(1)}, bf16[32,1792]{1,0:T(8,128)(2,1)S(1)}, u32[]{:S(2)}, u32[]{:S(2)}) collective-permute-start(bf16[32,1792]{1,0:T(8,128)(2,1)S(1)} %add_convert_fusion.1), channel_id=1, source_target_pairs={{9,0},{6,1},{11,2},{4,3},{13,4},{2,5},{15,6},{0,7},{1,8},{14,9},{3... | collective-permute-start | bytes 344072 | tf_op jit(solution)/shard_map/ppermute | solution.py:441
  31.0 0.5 %collective-permute-done.10.refs_0_ = bf16[32,1792]{1,0:T(8,128)(2,1)S(1)} collective-permute-done((bf16[32,1792]{1,0:T(8,128)(2,1)S(1)}, bf16[32,1792]{1,0:T(8,128)(2,1)S(1)}, u32[]{:S(2)}, u32[]{:S(2)}) %collective-permute-start.10) | collective-permute-done | bytes 114720 | tf_op jit(solution)/shard_map/ppermute | solution.py:441
  31.5 3.0 %collective-permute-done.12.refs_1_ = bf16[32,1792]{1,0:T(8,128)(2,1)S(1)} collective-permute-done((bf16[32,1792]{1,0:T(8,128)(2,1)S(1)}, bf16[32,1792]{1,0:T(8,128)(2,1)S(1)}, u32[]{:S(2)}, u32[]{:S(2)}) %collective-permute-start.12) | collective-permute-done | bytes 114720 | tf_op jit(solution)/shard_map/ppermute | solution.py:441
  34.5 4.6 %collective-permute-done.14.refs_2_ = bf16[32,1792]{1,0:T(8,128)(2,1)S(1)} collective-permute-done((bf16[32,1792]{1,0:T(8,128)(2,1)S(1)}, bf16[32,1792]{1,0:T(8,128)(2,1)S(1)}, u32[]{:S(2)}, u32[]{:S(2)}) %collective-permute-start.14) | collective-permute-done | bytes 114720 | tf_op jit(solution)/shard_map/ppermute | solution.py:441
  39.5 1.3 %collective-permute-done.17.other_ref = bf16[8,7168]{1,0:T(8,128)(2,1)S(1)} collective-permute-done((bf16[8,7168]{1,0:T(8,128)(2,1)S(1)}, bf16[8,7168]{1,0:T(8,128)(2,1)S(1)}, u32[]{:S(2)}, u32[]{:S(2)}) %collective-permute-start.17) | collective-permute-done | bytes 114720 | tf_op jit(solution)/shard_map/ppermute | solution.py:432
  40.8 0.7 %finish.1 = bf16[2,4,7168]{2,1,0:T(4,128)(2,1)} custom-call(f32[8,7168]{1,0:T(8,128)S(1)} %get-tuple-element.47.kept_ref, bf16[8,7168]{1,0:T(8,128)(2,1)S(1)} %collective-permute-done.17.other_ref), custom_call_target="tpu_custom_call" | custom-call | flops 100000 | bytes 500000 | tf_op jit(solution)/shard_map/finish/pallas_call | solution.py:402
  (22 shorter events, 1.5 us)
Async XLA Ops:
  2.3 1.5 %collective-permute-start = (bf16[8,7296]{1,0:T(8,128)(2,1)S(1)}, bf16[8,7296]{1,0:T(8,128)(2,1)S(1)}, u32[]{:S(2)}, u32[]{:S(2)}) collective-permute-start(bf16[8,7296]{1,0:T(8,128)(2,1)S(1)} %get-tuple-element.27.own_ref), channel_id=1, source_target_pairs={{0,1},{1,0},{2,3},{3,2},{4,5},{5,4},{6,7},{7,6},{8,9},{9,8},{10,11... | collective-permute-start | bytes 350216 | tf_op jit(solution)/shard_map/ppermute | solution.py:432
  4.3 11.8 %collective-permute-start.1 = (bf16[32,1792]{1,0:T(8,128)(2,1)S(1)}, bf16[32,1792]{1,0:T(8,128)(2,1)S(1)}, u32[]{:S(2)}, u32[]{:S(2)}) collective-permute-start(bf16[32,1792]{1,0:T(8,128)(2,1)S(1)} %get-tuple-element.30), channel_id=1, source_target_pairs={{0,1},{1,14},{2,3},{3,12},{4,5},{5,10},{6,7},{7,8},{8,9},{9,6},{10... | collective-permute-start | bytes 344072 | tf_op jit(solution)/shard_map/ppermute | solution.py:438
  4.7 12.9 %collective-permute-start.2 = (bf16[32,1792]{1,0:T(8,128)(2,1)S(1)}, bf16[32,1792]{1,0:T(8,128)(2,1)S(1)}, u32[]{:S(2)}, u32[]{:S(2)}) collective-permute-start(bf16[32,1792]{1,0:T(8,128)(2,1)S(1)} %get-tuple-element.34), channel_id=1, source_target_pairs={{0,5},{1,10},{2,7},{3,8},{4,1},{5,14},{6,3},{7,12},{8,13},{9,2},{1... | collective-permute-start | bytes 344072 | tf_op jit(solution)/shard_map/ppermute | solution.py:438
  9.5 9.9 %collective-permute-start.3 = (bf16[32,1792]{1,0:T(8,128)(2,1)S(1)}, bf16[32,1792]{1,0:T(8,128)(2,1)S(1)}, u32[]{:S(2)}, u32[]{:S(2)}) collective-permute-start(bf16[32,1792]{1,0:T(8,128)(2,1)S(1)} %get-tuple-element.35), channel_id=1, source_target_pairs={{0,9},{1,6},{2,11},{3,4},{4,13},{5,2},{6,15},{7,0},{8,1},{9,14},{1... | collective-permute-start | bytes 344072 | tf_op jit(solution)/shard_map/ppermute | solution.py:438
  9.5 9.9 %collective-permute-start.4 = (bf16[32,1792]{1,0:T(8,128)(2,1)S(1)}, bf16[32,1792]{1,0:T(8,128)(2,1)S(1)}, u32[]{:S(2)}, u32[]{:S(2)}) collective-permute-start(bf16[32,1792]{1,0:T(8,128)(2,1)S(1)} %get-tuple-element.36), channel_id=1, source_target_pairs={{0,13},{1,2},{2,15},{3,0},{4,9},{5,6},{6,11},{7,4},{8,5},{9,10},{1... | collective-permute-start | bytes 344072 | tf_op jit(solution)/shard_map/ppermute | solution.py:438
  17.5 2.4 %collective-permute-start.6 = (bf16[32,1792]{1,0:T(8,128)(2,1)S(1)}, bf16[32,1792]{1,0:T(8,128)(2,1)S(1)}, u32[]{:S(2)}, u32[]{:S(2)}) collective-permute-start(bf16[32,1792]{1,0:T(8,128)(2,1)S(1)} %collective-permute-done.2.refs_1_), channel_id=1, source_target_pairs={{0,1},{1,0},{2,3},{3,2},{4,5},{5,4},{6,7},{7,6},{8,9},{9,8},{10,11... | collective-permute-start | bytes 344072 | tf_op jit(solution)/shard_map/ppermute | solution.py:432
  19.4 1.3 %collective-permute-start.7 = (bf16[32,1792]{1,0:T(8,128)(2,1)S(1)}, bf16[32,1792]{1,0:T(8,128)(2,1)S(1)}, u32[]{:S(2)}, u32[]{:S(2)}) collective-permute-start(bf16[32,1792]{1,0:T(8,128)(2,1)S(1)} %collective-permute-done.3.refs_2_), channel_id=1, source_target_pairs={{0,1},{1,0},{2,3},{3,2},{4,5},{5,4},{6,7},{7,6},{8,9},{9,8},{10,11... | collective-permute-start | bytes 344072 | tf_op jit(solution)/shard_map/ppermute | solution.py:432
  19.4 1.5 %collective-permute-start.8 = (bf16[32,1792]{1,0:T(8,128)(2,1)S(1)}, bf16[32,1792]{1,0:T(8,128)(2,1)S(1)}, u32[]{:S(2)}, u32[]{:S(2)}) collective-permute-start(bf16[32,1792]{1,0:T(8,128)(2,1)S(1)} %collective-permute-done.4.refs_3_), channel_id=1, source_target_pairs={{0,1},{1,0},{2,3},{3,2},{4,5},{5,4},{6,7},{7,6},{8,9},{9,8},{10,11... | collective-permute-start | bytes 344072 | tf_op jit(solution)/shard_map/ppermute | solution.py:432
  19.9 1.3 %collective-permute-start.5 = (bf16[32,1792]{1,0:T(8,128)(2,1)S(1)}, bf16[32,1792]{1,0:T(8,128)(2,1)S(1)}, u32[]{:S(2)}, u32[]{:S(2)}) collective-permute-start(bf16[32,1792]{1,0:T(8,128)(2,1)S(1)} %collective-permute-done.1.refs_0_), channel_id=1, source_target_pairs={{0,1},{1,0},{2,3},{3,2},{4,5},{5,4},{6,7},{7,6},{8,9},{9,8},{10,11... | collective-permute-start | bytes 344072 | tf_op jit(solution)/shard_map/ppermute | solution.py:432
  24.9 1.4 %collective-permute-start.9 = (bf16[32,1792]{1,0:T(8,128)(2,1)S(1)}, bf16[32,1792]{1,0:T(8,128)(2,1)S(1)}, u32[]{:S(2)}, u32[]{:S(2)}) collective-permute-start(bf16[32,1792]{1,0:T(8,128)(2,1)S(1)} %get-tuple-element.40), channel_id=1, source_target_pairs={{0,1},{1,0},{2,3},{3,2},{4,5},{5,4},{6,7},{7,6},{8,9},{9,8},{10,11... | collective-permute-start | bytes 344072 | tf_op jit(solution)/shard_map/ppermute | solution.py:432
  25.1 3.0 %collective-permute-start.11 = (bf16[32,1792]{1,0:T(8,128)(2,1)S(1)}, bf16[32,1792]{1,0:T(8,128)(2,1)S(1)}, u32[]{:S(2)}, u32[]{:S(2)}) collective-permute-start(bf16[32,1792]{1,0:T(8,128)(2,1)S(1)} %get-tuple-element.42), channel_id=1, source_target_pairs={{0,1},{1,0},{2,3},{3,2},{4,5},{5,4},{6,7},{7,6},{8,9},{9,8},{10,11... | collective-permute-start | bytes 344072 | tf_op jit(solution)/shard_map/ppermute | solution.py:432
  25.4 3.0 %collective-permute-start.13 = (bf16[32,1792]{1,0:T(8,128)(2,1)S(1)}, bf16[32,1792]{1,0:T(8,128)(2,1)S(1)}, u32[]{:S(2)}, u32[]{:S(2)}) collective-permute-start(bf16[32,1792]{1,0:T(8,128)(2,1)S(1)} %get-tuple-element.44), channel_id=1, source_target_pairs={{0,1},{1,0},{2,3},{3,2},{4,5},{5,4},{6,7},{7,6},{8,9},{9,8},{10,11... | collective-permute-start | bytes 344072 | tf_op jit(solution)/shard_map/ppermute | solution.py:432
  25.6 5.3 %collective-permute-start.15 = (bf16[32,1792]{1,0:T(8,128)(2,1)S(1)}, bf16[32,1792]{1,0:T(8,128)(2,1)S(1)}, u32[]{:S(2)}, u32[]{:S(2)}) collective-permute-start(bf16[32,1792]{1,0:T(8,128)(2,1)S(1)} %get-tuple-element.46), channel_id=1, source_target_pairs={{0,1},{1,0},{2,3},{3,2},{4,5},{5,4},{6,7},{7,6},{8,9},{9,8},{10,11... | collective-permute-start | bytes 344072 | tf_op jit(solution)/shard_map/ppermute | solution.py:432
  26.3 5.2 %collective-permute-start.10 = (bf16[32,1792]{1,0:T(8,128)(2,1)S(1)}, bf16[32,1792]{1,0:T(8,128)(2,1)S(1)}, u32[]{:S(2)}, u32[]{:S(2)}) collective-permute-start(bf16[32,1792]{1,0:T(8,128)(2,1)S(1)} %add_convert_fusion.3), channel_id=1, source_target_pairs={{1,0},{14,1},{3,2},{12,3},{5,4},{10,5},{7,6},{8,7},{9,8},{6,9},{11... | collective-permute-start | bytes 344072 | tf_op jit(solution)/shard_map/ppermute | solution.py:441
  28.1 6.4 %collective-permute-start.12 = (bf16[32,1792]{1,0:T(8,128)(2,1)S(1)}, bf16[32,1792]{1,0:T(8,128)(2,1)S(1)}, u32[]{:S(2)}, u32[]{:S(2)}) collective-permute-start(bf16[32,1792]{1,0:T(8,128)(2,1)S(1)} %add_convert_fusion.2), channel_id=1, source_target_pairs={{5,0},{10,1},{7,2},{8,3},{1,4},{14,5},{3,6},{12,7},{13,8},{2,9},{1... | collective-permute-start | bytes 344072 | tf_op jit(solution)/shard_map/ppermute | solution.py:441
  28.5 10.6 %collective-permute-start.14 = (bf16[32,1792]{1,0:T(8,128)(2,1)S(1)}, bf16[32,1792]{1,0:T(8,128)(2,1)S(1)}, u32[]{:S(2)}, u32[]{:S(2)}) collective-permute-start(bf16[32,1792]{1,0:T(8,128)(2,1)S(1)} %add_convert_fusion.1), channel_id=1, source_target_pairs={{9,0},{6,1},{11,2},{4,3},{13,4},{2,5},{15,6},{0,7},{1,8},{14,9},{3... | collective-permute-start | bytes 344072 | tf_op jit(solution)/shard_map/ppermute | solution.py:441
  30.9 8.2 %collective-permute-start.16 = (bf16[32,1792]{1,0:T(8,128)(2,1)S(1)}, bf16[32,1792]{1,0:T(8,128)(2,1)S(1)}, u32[]{:S(2)}, u32[]{:S(2)}) collective-permute-start(bf16[32,1792]{1,0:T(8,128)(2,1)S(1)} %add_convert_fusion), channel_id=1, source_target_pairs={{13,0},{2,1},{15,2},{0,3},{9,4},{6,5},{11,6},{4,7},{5,8},{10,9},{7... | collective-permute-start | bytes 344072 | tf_op jit(solution)/shard_map/ppermute | solution.py:441
  39.4 1.4 %collective-permute-start.17 = (bf16[8,7168]{1,0:T(8,128)(2,1)S(1)}, bf16[8,7168]{1,0:T(8,128)(2,1)S(1)}, u32[]{:S(2)}, u32[]{:S(2)}) collective-permute-start(bf16[8,7168]{1,0:T(8,128)(2,1)S(1)} %get-tuple-element.48), channel_id=1, source_target_pairs={{0,1},{1,0},{2,3},{3,2},{4,5},{5,4},{6,7},{7,6},{8,9},{9,8},{10,11... | collective-permute-start | bytes 344072 | tf_op jit(solution)/shard_map/ppermute | solution.py:432

commit v8 on v7

--- a/solution.py
+++ b/solution.py
@@ -20,6 +20,7 @@
 VMEM = pl.BlockSpec(memory_space=pltpu.VMEM)
 HBM = pl.BlockSpec(memory_space=pltpu.HBM)
 TOGETHER = 4
+STAGED = 2
 
 
 def iota(shape, dim):
@@ -43,7 +44,7 @@
 
 
 def distance(turn, core, chips):
-    return (2 * turn) ^ (core * (chips - 1))
+    return ((chips - 2 * turn) % chips) ^ core
 
 
 def expert_at(turn, chips):
@@ -447,9 +448,10 @@
     )
     normed_other = swap(normed)
     sent = pack(steps, chips, normed, normed_other)
+    gu, dn, mix = stage(steps, chips, normed, normed_other, gate_up, down)
+    *late, gu, dn = lax.optimization_barrier((*sent[STAGED:], gu, dn))
+    sent = [*sent[:STAGED], *late]
     own = [send(sent[t], t) for t in range(turns)]
-    gu, dn, mix = stage(steps, chips, normed, normed_other, gate_up, down)
-    own[0], gu, dn = lax.optimization_barrier((own[0], gu, dn))
     other = [swap(x) for x in own]
     summed = []
     for t in range(0, turns, TOGETHER):

time: 41.6 us -> 45.3 us (1.089)
  waiting for transfers between devices: 15.4 us -> 18.7 us
    ppermute x4, waiting for transfers between devices: 3.37 us -> 7.81 us  [send(): return lax.ppermute(x, 'afd', route(t))]
    ppermute x4, starting transfers between devices: 7.5 us -> 6.42 us  [send(): return lax.ppermute(x, 'afd', route(t))]
    ppermute x4, waiting for transfers between devices: 8.1 us -> 7.34 us  [send_back(): return lax.ppermute(x, 'afd', [(j, i) for i, j in route(t)])]
    ppermute x4, starting transfers between devices: 4.58 us -> 5.33 us  [send_back(): return lax.ppermute(x, 'afd', [(j, i) for i, j in route(t)])]
    ppermute x10, starting transfers between devices: 2.19 us -> 2.83 us  [swap(): return lax.ppermute(x, 'afd', cores)]
  transfers between devices with their start and end apart: 18 -> 18, of which waited for: 11 -> 9; matrix products, arithmetic and copies ran while one was open for 0% -> 0% of each run, Pallas kernels for 10% -> 9%
where the time goes in v8:
time: 45.3 us; the launch traced here: 45.1 us
  waiting for transfers between devices  18.7 us (41%)
  starting transfers between devices  14.6 us (32%)
  Pallas kernels  11.6 us (26%)
    ppermute x4, waiting for transfers between devices, send(): return lax.ppermute(x, 'afd', route(t))  7.81 us
    ppermute x4, waiting for transfers between devices, send_back(): return lax.ppermute(x, 'afd', [(j, i) for i, j in route(t)])  7.34 us
    ppermute x4, starting transfers between devices, send(): return lax.ppermute(x, 'afd', route(t))  6.42 us
    ppermute x4, starting transfers between devices, send_back(): return lax.ppermute(x, 'afd', [(j, i) for i, j in route(t)])  5.33 us
    pallas_call x1, Pallas kernels, stage(): pl.pallas_call(functools.partial(stage_kernel, steps, chips), out_shape=(...  4.25 us
    pallas_call x1, Pallas kernels, experts(): pl.pallas_call(functools.partial(expert_kernel, turns), out_shape=[shape]...  3.62 us
    ppermute x10, waiting for transfers between devices, swap(): return lax.ppermute(x, 'afd', cores)  3.56 us
    ppermute x10, starting transfers between devices, swap(): return lax.ppermute(x, 'afd', cores)  2.83 us
  transfers between devices with their start and end apart: 18, of which 9 were waited for; matrix products, arithmetic and copies ran while one was open for 0% of the time, Pallas kernels for 9%

profile of v8, /device:TPU:0, one launch (start us, length us, event | category | flops | bytes accessed | tf_op | source)
XLA Modules:
  0.0 45.1 jit_solution(10372330911348750026)
XLA Ops:
  0.0 2.3 %attend.1 = (f32[8,7168]{1,0:T(8,128)S(1)}, bf16[8,7296]{1,0:T(8,128)(2,1)S(1)}) custom-call(s32[4]{0:T(128)} %len_hbm.1, s32[3,2,4]{2,1,0:T(2,128)} %bitcast.6, f32[3,2,4]{2,1,0:T(2,128)} %bitcast.7, bf16[2,4,7168]{2,1,0:T(4,128)(2,1)} %q_hbm.1, bf16[2,4,448]{2,1,0:T(4,128)(2,1)} %fresh_hbm.1, bf16[4,448,128]{2,1,0:T(8,128)(2,1)} %bitcast.4, ...), custom_call_target="tpu_custom_call" | custom-call | flops 300000000 | bytes 2000000 | tf_op jit(solution)/shard_map/attend/pallas_call | solution.py:172
  2.3 0.5 %collective-permute-start = (bf16[8,7296]{1,0:T(8,128)(2,1)S(1)}, bf16[8,7296]{1,0:T(8,128)(2,1)S(1)}, u32[]{:S(2)}, u32[]{:S(2)}) collective-permute-start(bf16[8,7296]{1,0:T(8,128)(2,1)S(1)} %get-tuple-element.28.own_ref), channel_id=1, source_target_pairs={{0,1},{1,0},{2,3},{3,2},{4,5},{5,4},{6,7},{7,6},{8,9},{9,8},{10,11... | collective-permute-start | bytes 350216 | tf_op jit(solution)/shard_map/ppermute | solution.py:433
  2.8 1.0 %collective-permute-done.other_ref = bf16[8,7296]{1,0:T(8,128)(2,1)S(1)} collective-permute-done((bf16[8,7296]{1,0:T(8,128)(2,1)S(1)}, bf16[8,7296]{1,0:T(8,128)(2,1)S(1)}, u32[]{:S(2)}, u32[]{:S(2)}) %collective-permute-start) | collective-permute-done | bytes 116768 | tf_op jit(solution)/shard_map/ppermute | solution.py:433
  3.7 0.5 %pack.1 = (bf16[32,1792]{1,0:T(8,128)(2,1)S(1)}, bf16[32,1792]{1,0:T(8,128)(2,1)S(1)}, bf16[32,1792]{1,0:T(8,128)(2,1)S(1)}, bf16[32,1792]{1,0:T(8,128)(2,1)S(1)}) custom-call(bf16[8,7296]{1,0:T(8,128)(2,1)S(1)} %get-tuple-element.28.own_ref, bf16[8,7296]{1,0:T(8,128)(2,1)S(1)} %collective-permute-done.other_ref), custom_call_target="tpu_custom_call" | custom-call | flops 50000000 | bytes 2000000 | tf_op jit(solution)/shard_map/pack/pallas_call | solution.py:235
  4.3 0.4 collective-permute-start.1
  4.7 5.8 %collective-permute-start.2 = (bf16[32,1792]{1,0:T(8,128)(2,1)S(1)}, bf16[32,1792]{1,0:T(8,128)(2,1)S(1)}, u32[]{:S(2)}, u32[]{:S(2)}) collective-permute-start(bf16[32,1792]{1,0:T(8,128)(2,1)S(1)} %get-tuple-element.32), channel_id=1, source_target_pairs={{0,13},{1,14},{2,15},{3,12},{4,9},{5,10},{6,11},{7,8},{8,5},{9,6},... | collective-permute-start | bytes 344072 | tf_op jit(solution)/shard_map/ppermute | solution.py:439
  10.5 4.2 %stage.1 = (bf16[2,256,7168]{2,1,0:T(8,128)(2,1)S(1)}, bf16[256,7168]{1,0:T(8,128)(2,1)S(1)}, bf16[192,128]{1,0:T(8,128)(2,1)S(1)}) custom-call(bf16[8,7296]{1,0:T(8,128)(2,1)S(1)} %get-tuple-element.28.own_ref, bf16[8,7296]{1,0:T(8,128)(2,1)S(1)} %collective-permute-done.other_ref, bf16[1,2,256,7168]{3,2,1,0:T(8,128)(2,1)} %gu_hbm.1, ...), custom_call_target="tpu_custom_call" | custom-call | flops 10000000 | bytes 22000000 | tf_op jit(solution)/shard_map/stage/pallas_call | solution.py:293
  15.0 0.5 %collective-permute-start.5 = (bf16[32,1792]{1,0:T(8,128)(2,1)S(1)}, bf16[32,1792]{1,0:T(8,128)(2,1)S(1)}, u32[]{:S(2)}, u32[]{:S(2)}) collective-permute-start(bf16[32,1792]{1,0:T(8,128)(2,1)S(1)} %collective-permute-done.1.refs_0_), channel_id=1, source_target_pairs={{0,1},{1,0},{2,3},{3,2},{4,5},{5,4},{6,7},{7,6},{8,9},{9,8},{10,11... | collective-permute-start | bytes 344072 | tf_op jit(solution)/shard_map/ppermute | solution.py:433
  15.5 7.3 %collective-permute-done.3.refs_2_ = bf16[32,1792]{1,0:T(8,128)(2,1)S(1)} collective-permute-done((bf16[32,1792]{1,0:T(8,128)(2,1)S(1)}, bf16[32,1792]{1,0:T(8,128)(2,1)S(1)}, u32[]{:S(2)}, u32[]{:S(2)}) %collective-permute-start.3) | collective-permute-done | bytes 114720 | tf_op jit(solution)/shard_map/ppermute | solution.py:439
  22.8 0.5 %collective-permute-done.4.refs_3_ = bf16[32,1792]{1,0:T(8,128)(2,1)S(1)} collective-permute-done((bf16[32,1792]{1,0:T(8,128)(2,1)S(1)}, bf16[32,1792]{1,0:T(8,128)(2,1)S(1)}, u32[]{:S(2)}, u32[]{:S(2)}) %collective-permute-start.4) | collective-permute-done | bytes 114720 | tf_op jit(solution)/shard_map/ppermute | solution.py:439
  23.3 0.8 %collective-permute-done.7.refs_6_ = bf16[32,1792]{1,0:T(8,128)(2,1)S(1)} collective-permute-done((bf16[32,1792]{1,0:T(8,128)(2,1)S(1)}, bf16[32,1792]{1,0:T(8,128)(2,1)S(1)}, u32[]{:S(2)}, u32[]{:S(2)}) %collective-permute-start.7) | collective-permute-done | bytes 114720 | tf_op jit(solution)/shard_map/ppermute | solution.py:433
  24.1 0.5 %collective-permute-done.8.refs_7_ = bf16[32,1792]{1,0:T(8,128)(2,1)S(1)} collective-permute-done((bf16[32,1792]{1,0:T(8,128)(2,1)S(1)}, bf16[32,1792]{1,0:T(8,128)(2,1)S(1)}, u32[]{:S(2)}, u32[]{:S(2)}) %collective-permute-start.8) | collective-permute-done | bytes 114720 | tf_op jit(solution)/shard_map/ppermute | solution.py:433
  24.7 3.6 %experts.1 = (bf16[32,1792]{1,0:T(8,128)(2,1)S(1)}, bf16[32,1792]{1,0:T(8,128)(2,1)S(1)}, bf16[32,1792]{1,0:T(8,128)(2,1)S(1)}, bf16[32,1792]{1,0:T(8,128)(2,1)S...) custom-call(bf16[32,1792]{1,0:T(8,128)(2,1)S(1)} %collective-permute, ...), custom_call_target="tpu_custom_call" | custom-call | flops 800000000 | bytes 12000000 | tf_op jit(solution)/shard_map/experts/pallas_call | solution.py:350
  28.5 0.4 collective-permute-start.11
  29.0 0.4 collective-permute-start.15
  29.7 0.9 %collective-permute-start.10 = (bf16[32,1792]{1,0:T(8,128)(2,1)S(1)}, bf16[32,1792]{1,0:T(8,128)(2,1)S(1)}, u32[]{:S(2)}, u32[]{:S(2)}) collective-permute-start(bf16[32,1792]{1,0:T(8,128)(2,1)S(1)} %add_convert_fusion.3), channel_id=1, source_target_pairs={{1,0},{2,1},{3,2},{0,3},{5,4},{6,5},{7,6},{4,7},{9,8},{10,9},{11,1... | collective-permute-start | bytes 344072 | tf_op jit(solution)/shard_map/ppermute | solution.py:442
  30.7 0.7 %collective-permute-start.12 = (bf16[32,1792]{1,0:T(8,128)(2,1)S(1)}, bf16[32,1792]{1,0:T(8,128)(2,1)S(1)}, u32[]{:S(2)}, u32[]{:S(2)}) collective-permute-start(bf16[32,1792]{1,0:T(8,128)(2,1)S(1)} %add_convert_fusion.2), channel_id=1, source_target_pairs={{13,0},{14,1},{15,2},{12,3},{9,4},{10,5},{11,6},{8,7},{5,8},{6,9},... | collective-permute-start | bytes 344072 | tf_op jit(solution)/shard_map/ppermute | solution.py:442
  31.4 0.5 %collective-permute-start.14 = (bf16[32,1792]{1,0:T(8,128)(2,1)S(1)}, bf16[32,1792]{1,0:T(8,128)(2,1)S(1)}, u32[]{:S(2)}, u32[]{:S(2)}) collective-permute-start(bf16[32,1792]{1,0:T(8,128)(2,1)S(1)} %add_convert_fusion.1), channel_id=1, source_target_pairs={{9,0},{10,1},{11,2},{8,3},{13,4},{14,5},{15,6},{12,7},{1,8},{2,9},... | collective-permute-start | bytes 344072 | tf_op jit(solution)/shard_map/ppermute | solution.py:442
  31.9 3.2 %collective-permute-start.16 = (bf16[32,1792]{1,0:T(8,128)(2,1)S(1)}, bf16[32,1792]{1,0:T(8,128)(2,1)S(1)}, u32[]{:S(2)}, u32[]{:S(2)}) collective-permute-start(bf16[32,1792]{1,0:T(8,128)(2,1)S(1)} %add_convert_fusion), channel_id=1, source_target_pairs={{5,0},{6,1},{7,2},{4,3},{1,4},{2,5},{3,6},{0,7},{13,8},{14,9},{15,... | collective-permute-start | bytes 344072 | tf_op jit(solution)/shard_map/ppermute | solution.py:442
  35.1 2.9 %collective-permute-done.12.refs_1_ = bf16[32,1792]{1,0:T(8,128)(2,1)S(1)} collective-permute-done((bf16[32,1792]{1,0:T(8,128)(2,1)S(1)}, bf16[32,1792]{1,0:T(8,128)(2,1)S(1)}, u32[]{:S(2)}, u32[]{:S(2)}) %collective-permute-start.12) | collective-permute-done | bytes 114720 | tf_op jit(solution)/shard_map/ppermute | solution.py:442
  38.0 4.5 %collective-permute-done.14.refs_2_ = bf16[32,1792]{1,0:T(8,128)(2,1)S(1)} collective-permute-done((bf16[32,1792]{1,0:T(8,128)(2,1)S(1)}, bf16[32,1792]{1,0:T(8,128)(2,1)S(1)}, u32[]{:S(2)}, u32[]{:S(2)}) %collective-permute-start.14) | collective-permute-done | bytes 114720 | tf_op jit(solution)/shard_map/ppermute | solution.py:442
  42.8 0.7 %collective-permute-start.17 = (bf16[8,7168]{1,0:T(8,128)(2,1)S(1)}, bf16[8,7168]{1,0:T(8,128)(2,1)S(1)}, u32[]{:S(2)}, u32[]{:S(2)}) collective-permute-start(bf16[8,7168]{1,0:T(8,128)(2,1)S(1)} %get-tuple-element.50), channel_id=1, source_target_pairs={{0,1},{1,0},{2,3},{3,2},{4,5},{5,4},{6,7},{7,6},{8,9},{9,8},{10,11... | collective-permute-start | bytes 344072 | tf_op jit(solution)/shard_map/ppermute | solution.py:433
  43.5 1.0 %collective-permute-done.17.other_ref = bf16[8,7168]{1,0:T(8,128)(2,1)S(1)} collective-permute-done((bf16[8,7168]{1,0:T(8,128)(2,1)S(1)}, bf16[8,7168]{1,0:T(8,128)(2,1)S(1)}, u32[]{:S(2)}, u32[]{:S(2)}) %collective-permute-start.17) | collective-permute-done | bytes 114720 | tf_op jit(solution)/shard_map/ppermute | solution.py:433
  44.4 0.7 %finish.1 = bf16[2,4,7168]{2,1,0:T(4,128)(2,1)} custom-call(f32[8,7168]{1,0:T(8,128)S(1)} %get-tuple-element.49.kept_ref, bf16[8,7168]{1,0:T(8,128)(2,1)S(1)} %collective-permute-done.17.other_ref), custom_call_target="tpu_custom_call" | custom-call | flops 100000 | bytes 500000 | tf_op jit(solution)/shard_map/finish/pallas_call | solution.py:403
  (22 shorter events, 1.4 us)
Async XLA Ops:
  2.3 1.5 %collective-permute-start = (bf16[8,7296]{1,0:T(8,128)(2,1)S(1)}, bf16[8,7296]{1,0:T(8,128)(2,1)S(1)}, u32[]{:S(2)}, u32[]{:S(2)}) collective-permute-start(bf16[8,7296]{1,0:T(8,128)(2,1)S(1)} %get-tuple-element.28.own_ref), channel_id=1, source_target_pairs={{0,1},{1,0},{2,3},{3,2},{4,5},{5,4},{6,7},{7,6},{8,9},{9,8},{10,11... | collective-permute-start | bytes 350216 | tf_op jit(solution)/shard_map/ppermute | solution.py:433
  4.3 10.7 %collective-permute-start.1 = (bf16[32,1792]{1,0:T(8,128)(2,1)S(1)}, bf16[32,1792]{1,0:T(8,128)(2,1)S(1)}, u32[]{:S(2)}, u32[]{:S(2)}) collective-permute-start(bf16[32,1792]{1,0:T(8,128)(2,1)S(1)} %get-tuple-element.31), channel_id=1, source_target_pairs={{0,1},{1,2},{2,3},{3,0},{4,5},{5,6},{6,7},{7,4},{8,9},{9,10},{10,1... | collective-permute-start | bytes 344072 | tf_op jit(solution)/shard_map/ppermute | solution.py:439
  4.7 10.8 %collective-permute-start.2 = (bf16[32,1792]{1,0:T(8,128)(2,1)S(1)}, bf16[32,1792]{1,0:T(8,128)(2,1)S(1)}, u32[]{:S(2)}, u32[]{:S(2)}) collective-permute-start(bf16[32,1792]{1,0:T(8,128)(2,1)S(1)} %get-tuple-element.32), channel_id=1, source_target_pairs={{0,13},{1,14},{2,15},{3,12},{4,9},{5,10},{6,11},{7,8},{8,5},{9,6},... | collective-permute-start | bytes 344072 | tf_op jit(solution)/shard_map/ppermute | solution.py:439
  14.7 8.1 %collective-permute-start.3 = (bf16[32,1792]{1,0:T(8,128)(2,1)S(1)}, bf16[32,1792]{1,0:T(8,128)(2,1)S(1)}, u32[]{:S(2)}, u32[]{:S(2)}) collective-permute-start(bf16[32,1792]{1,0:T(8,128)(2,1)S(1)} %get-tuple-element.37), channel_id=1, source_target_pairs={{0,9},{1,10},{2,11},{3,8},{4,13},{5,14},{6,15},{7,12},{8,1},{9,2},... | collective-permute-start | bytes 344072 | tf_op jit(solution)/shard_map/ppermute | solution.py:439
  14.8 8.5 %collective-permute-start.4 = (bf16[32,1792]{1,0:T(8,128)(2,1)S(1)}, bf16[32,1792]{1,0:T(8,128)(2,1)S(1)}, u32[]{:S(2)}, u32[]{:S(2)}) collective-permute-start(bf16[32,1792]{1,0:T(8,128)(2,1)S(1)} %get-tuple-element.38), channel_id=1, source_target_pairs={{0,5},{1,6},{2,7},{3,4},{4,1},{5,2},{6,3},{7,0},{8,13},{9,14},{10,... | collective-permute-start | bytes 344072 | tf_op jit(solution)/shard_map/ppermute | solution.py:439
  15.0 8.4 %collective-permute-start.5 = (bf16[32,1792]{1,0:T(8,128)(2,1)S(1)}, bf16[32,1792]{1,0:T(8,128)(2,1)S(1)}, u32[]{:S(2)}, u32[]{:S(2)}) collective-permute-start(bf16[32,1792]{1,0:T(8,128)(2,1)S(1)} %collective-permute-done.1.refs_0_), channel_id=1, source_target_pairs={{0,1},{1,0},{2,3},{3,2},{4,5},{5,4},{6,7},{7,6},{8,9},{9,8},{10,11... | collective-permute-start | bytes 344072 | tf_op jit(solution)/shard_map/ppermute | solution.py:433
  15.5 7.9 %collective-permute-start.6 = (bf16[32,1792]{1,0:T(8,128)(2,1)S(1)}, bf16[32,1792]{1,0:T(8,128)(2,1)S(1)}, u32[]{:S(2)}, u32[]{:S(2)}) collective-permute-start(bf16[32,1792]{1,0:T(8,128)(2,1)S(1)} %collective-permute-done.2.refs_1_), channel_id=1, source_target_pairs={{0,1},{1,0},{2,3},{3,2},{4,5},{5,4},{6,7},{7,6},{8,9},{9,8},{10,11... | collective-permute-start | bytes 344072 | tf_op jit(solution)/shard_map/ppermute | solution.py:433
  22.8 1.3 %collective-permute-start.7 = (bf16[32,1792]{1,0:T(8,128)(2,1)S(1)}, bf16[32,1792]{1,0:T(8,128)(2,1)S(1)}, u32[]{:S(2)}, u32[]{:S(2)}) collective-permute-start(bf16[32,1792]{1,0:T(8,128)(2,1)S(1)} %collective-permute-done.3.refs_2_), channel_id=1, source_target_pairs={{0,1},{1,0},{2,3},{3,2},{4,5},{5,4},{6,7},{7,6},{8,9},{9,8},{10,11... | collective-permute-start | bytes 344072 | tf_op jit(solution)/shard_map/ppermute | solution.py:433
  23.3 1.3 %collective-permute-start.8 = (bf16[32,1792]{1,0:T(8,128)(2,1)S(1)}, bf16[32,1792]{1,0:T(8,128)(2,1)S(1)}, u32[]{:S(2)}, u32[]{:S(2)}) collective-permute-start(bf16[32,1792]{1,0:T(8,128)(2,1)S(1)} %collective-permute-done.4.refs_3_), channel_id=1, source_target_pairs={{0,1},{1,0},{2,3},{3,2},{4,5},{5,4},{6,7},{7,6},{8,9},{9,8},{10,11... | collective-permute-start | bytes 344072 | tf_op jit(solution)/shard_map/ppermute | solution.py:433
  28.3 1.4 %collective-permute-start.9 = (bf16[32,1792]{1,0:T(8,128)(2,1)S(1)}, bf16[32,1792]{1,0:T(8,128)(2,1)S(1)}, u32[]{:S(2)}, u32[]{:S(2)}) collective-permute-start(bf16[32,1792]{1,0:T(8,128)(2,1)S(1)} %get-tuple-element.42), channel_id=1, source_target_pairs={{0,1},{1,0},{2,3},{3,2},{4,5},{5,4},{6,7},{7,6},{8,9},{9,8},{10,11... | collective-permute-start | bytes 344072 | tf_op jit(solution)/shard_map/ppermute | solution.py:433
  28.5 2.2 %collective-permute-start.11 = (bf16[32,1792]{1,0:T(8,128)(2,1)S(1)}, bf16[32,1792]{1,0:T(8,128)(2,1)S(1)}, u32[]{:S(2)}, u32[]{:S(2)}) collective-permute-start(bf16[32,1792]{1,0:T(8,128)(2,1)S(1)} %get-tuple-element.44), channel_id=1, source_target_pairs={{0,1},{1,0},{2,3},{3,2},{4,5},{5,4},{6,7},{7,6},{8,9},{9,8},{10,11... | collective-permute-start | bytes 344072 | tf_op jit(solution)/shard_map/ppermute | solution.py:433
  28.9 2.5 %collective-permute-start.13 = (bf16[32,1792]{1,0:T(8,128)(2,1)S(1)}, bf16[32,1792]{1,0:T(8,128)(2,1)S(1)}, u32[]{:S(2)}, u32[]{:S(2)}) collective-permute-start(bf16[32,1792]{1,0:T(8,128)(2,1)S(1)} %get-tuple-element.46), channel_id=1, source_target_pairs={{0,1},{1,0},{2,3},{3,2},{4,5},{5,4},{6,7},{7,6},{8,9},{9,8},{10,11... | collective-permute-start | bytes 344072 | tf_op jit(solution)/shard_map/ppermute | solution.py:433
  29.0 2.9 %collective-permute-start.15 = (bf16[32,1792]{1,0:T(8,128)(2,1)S(1)}, bf16[32,1792]{1,0:T(8,128)(2,1)S(1)}, u32[]{:S(2)}, u32[]{:S(2)}) collective-permute-start(bf16[32,1792]{1,0:T(8,128)(2,1)S(1)} %get-tuple-element.48), channel_id=1, source_target_pairs={{0,1},{1,0},{2,3},{3,2},{4,5},{5,4},{6,7},{7,6},{8,9},{9,8},{10,11... | collective-permute-start | bytes 344072 | tf_op jit(solution)/shard_map/ppermute | solution.py:433
  29.7 5.4 %collective-permute-start.10 = (bf16[32,1792]{1,0:T(8,128)(2,1)S(1)}, bf16[32,1792]{1,0:T(8,128)(2,1)S(1)}, u32[]{:S(2)}, u32[]{:S(2)}) collective-permute-start(bf16[32,1792]{1,0:T(8,128)(2,1)S(1)} %add_convert_fusion.3), channel_id=1, source_target_pairs={{1,0},{2,1},{3,2},{0,3},{5,4},{6,5},{7,6},{4,7},{9,8},{10,9},{11,1... | collective-permute-start | bytes 344072 | tf_op jit(solution)/shard_map/ppermute | solution.py:442
  30.7 7.3 %collective-permute-start.12 = (bf16[32,1792]{1,0:T(8,128)(2,1)S(1)}, bf16[32,1792]{1,0:T(8,128)(2,1)S(1)}, u32[]{:S(2)}, u32[]{:S(2)}) collective-permute-start(bf16[32,1792]{1,0:T(8,128)(2,1)S(1)} %add_convert_fusion.2), channel_id=1, source_target_pairs={{13,0},{14,1},{15,2},{12,3},{9,4},{10,5},{11,6},{8,7},{5,8},{6,9},... | collective-permute-start | bytes 344072 | tf_op jit(solution)/shard_map/ppermute | solution.py:442
  31.4 11.1 %collective-permute-start.14 = (bf16[32,1792]{1,0:T(8,128)(2,1)S(1)}, bf16[32,1792]{1,0:T(8,128)(2,1)S(1)}, u32[]{:S(2)}, u32[]{:S(2)}) collective-permute-start(bf16[32,1792]{1,0:T(8,128)(2,1)S(1)} %add_convert_fusion.1), channel_id=1, source_target_pairs={{9,0},{10,1},{11,2},{8,3},{13,4},{14,5},{15,6},{12,7},{1,8},{2,9},... | collective-permute-start | bytes 344072 | tf_op jit(solution)/shard_map/ppermute | solution.py:442
  31.9 10.6 %collective-permute-start.16 = (bf16[32,1792]{1,0:T(8,128)(2,1)S(1)}, bf16[32,1792]{1,0:T(8,128)(2,1)S(1)}, u32[]{:S(2)}, u32[]{:S(2)}) collective-permute-start(bf16[32,1792]{1,0:T(8,128)(2,1)S(1)} %add_convert_fusion), channel_id=1, source_target_pairs={{5,0},{6,1},{7,2},{4,3},{1,4},{2,5},{3,6},{0,7},{13,8},{14,9},{15,... | collective-permute-start | bytes 344072 | tf_op jit(solution)/shard_map/ppermute | solution.py:442
  42.8 1.6 %collective-permute-start.17 = (bf16[8,7168]{1,0:T(8,128)(2,1)S(1)}, bf16[8,7168]{1,0:T(8,128)(2,1)S(1)}, u32[]{:S(2)}, u32[]{:S(2)}) collective-permute-start(bf16[8,7168]{1,0:T(8,128)(2,1)S(1)} %get-tuple-element.50), channel_id=1, source_target_pairs={{0,1},{1,0},{2,3},{3,2},{4,5},{5,4},{6,7},{7,6},{8,9},{9,8},{10,11... | collective-permute-start | bytes 344072 | tf_op jit(solution)/shard_map/ppermute | solution.py:433

commit v9 on v7

--- a/solution.py
+++ b/solution.py
@@ -17,9 +17,10 @@
 F32 = jnp.float32
 BF16 = jnp.bfloat16
 MIB = 1 << 20
+LIGHT = pl.CostEstimate(flops=1, bytes_accessed=1, transcendentals=0)
 VMEM = pl.BlockSpec(memory_space=pltpu.VMEM)
 HBM = pl.BlockSpec(memory_space=pltpu.HBM)
-TOGETHER = 4
+TOGETHER = 2
 
 
 def iota(shape, dim):
@@ -237,9 +238,7 @@
         in_specs=[VMEM] * 2,
         out_specs=[VMEM] * turns,
         compiler_params=pltpu.CompilerParams(vmem_limit_bytes=24 * MIB),
-        cost_estimate=pl.CostEstimate(
-            flops=50_000_000, bytes_accessed=2_000_000, transcendentals=0
-        ),
+        cost_estimate=LIGHT,
         name="pack",
     )(own, other)
 
@@ -300,9 +299,7 @@
         out_specs=(VMEM,) * 3,
         scratch_shapes=[pltpu.SemaphoreType.DMA((12,))],
         compiler_params=pltpu.CompilerParams(vmem_limit_bytes=24 * MIB),
-        cost_estimate=pl.CostEstimate(
-            flops=10_000_000, bytes_accessed=22_000_000, transcendentals=0
-        ),
+        cost_estimate=LIGHT,
         name="stage",
     )(own, other, *in_hbm(gate_up, down))
 
@@ -352,9 +349,7 @@
         in_specs=[VMEM] * (2 * turns + 2),
         out_specs=[VMEM] * (2 * turns),
         compiler_params=pltpu.CompilerParams(vmem_limit_bytes=32 * MIB),
-        cost_estimate=pl.CostEstimate(
-            flops=800_000_000, bytes_accessed=12_000_000, transcendentals=16384
-        ),
+        cost_estimate=LIGHT,
         name="experts",
     )(*own, *other, gu, dn)
     return results[:turns], results[turns:]
@@ -447,17 +442,22 @@
     )
     normed_other = swap(normed)
     sent = pack(steps, chips, normed, normed_other)
+    gu, dn, mix = stage(steps, chips, normed, normed_other, gate_up, down)
+    *late, gu, dn = lax.optimization_barrier((*sent[TOGETHER:], gu, dn))
+    sent = [*sent[:TOGETHER], *late]
     own = [send(sent[t], t) for t in range(turns)]
-    gu, dn, mix = stage(steps, chips, normed, normed_other, gate_up, down)
-    own[0], gu, dn = lax.optimization_barrier((own[0], gu, dn))
-    other = [swap(x) for x in own]
-    summed = []
-    for t in range(0, turns, TOGETHER):
-        mine, theirs = experts(own[t : t + TOGETHER], other[t : t + TOGETHER], gu, dn)
-        summed += [
+    own[:TOGETHER], gu, dn = lax.optimization_barrier((own[:TOGETHER], gu, dn))
+    backs = []
+    for first in range(0, turns, TOGETHER):
+        now = own[first : first + TOGETHER]
+        mine, theirs = experts(now, [swap(x) for x in now], gu, dn)
+        theirs, backs = lax.optimization_barrier((theirs, backs))
+        rest = own[first + TOGETHER :]
+        mine, own[first + TOGETHER :] = lax.optimization_barrier((mine, rest))
+        summed = [
             (a.astype(F32) + swap(b).astype(F32)).astype(BF16) for a, b in zip(mine, theirs)
         ]
-    backs = [send_back(summed[t], t) for t in range(turns)]
+        backs = backs + [send_back(x, first + i) for i, x in enumerate(summed)]
     kept, given = combine(mix, resid, backs)
     return finish(queries.shape, kept, swap(given))
 

time: 41.6 us -> 46.2 us (1.11)
  starting transfers between devices: 14.3 us -> 19.5 us
  waiting for transfers between devices: 15.4 us -> 11.5 us
  Pallas kernels: 11.6 us -> 14.8 us
    pallas_call x1 -> x2, Pallas kernels: 3.61 us -> 6.76 us  [experts(): pl.pallas_call(functools.partial(expert_kernel, turns), out_shape=[shape]...]
    ppermute x10, starting transfers between devices: 2.19 us -> 4.43 us  [swap(): return lax.ppermute(x, 'afd', cores)]
    ppermute x4, waiting for transfers between devices: 8.1 us -> 6.13 us  [send_back(): return lax.ppermute(x, 'afd', [(j, i) for i, j in route(t)])]
    ppermute x4, starting transfers between devices: 7.5 us -> 9.31 us  [send(): return lax.ppermute(x, 'afd', route(t))]
    ppermute x4, waiting for transfers between devices: 3.37 us -> 1.87 us  [send(): return lax.ppermute(x, 'afd', route(t))]
    ppermute x4, starting transfers between devices: 4.58 us -> 5.72 us  [send_back(): return lax.ppermute(x, 'afd', [(j, i) for i, j in route(t)])]
  transfers between devices with their start and end apart: 18 -> 18, of which waited for: 11 -> 7; matrix products, arithmetic and copies ran while one was open for 0% -> 0% of each run, Pallas kernels for 10% -> 24%
where the time goes in v9:
time: 46.2 us; the launch traced here: 46 us
  starting transfers between devices  19.5 us (42%)
  Pallas kernels  14.8 us (32%)
  waiting for transfers between devices  11.5 us (25%)
    ppermute x4, starting transfers between devices, send(): return lax.ppermute(x, 'afd', route(t))  9.31 us
    pallas_call x2, Pallas kernels, experts(): pl.pallas_call(functools.partial(expert_kernel, turns), out_shape=[shape]...  6.76 us
    ppermute x4, waiting for transfers between devices, send_back(): return lax.ppermute(x, 'afd', [(j, i) for i, j in route(t)])  6.13 us
    ppermute x4, starting transfers between devices, send_back(): return lax.ppermute(x, 'afd', [(j, i) for i, j in route(t)])  5.72 us
    ppermute x10, starting transfers between devices, swap(): return lax.ppermute(x, 'afd', cores)  4.43 us
    pallas_call x1, Pallas kernels, stage(): pl.pallas_call(functools.partial(stage_kernel, steps, chips), out_shape=(...  4.25 us
    ppermute x10, waiting for transfers between devices, swap(): return lax.ppermute(x, 'afd', cores)  3.55 us
    pallas_call x1, Pallas kernels, attend(): pl.pallas_call(attend_kernel, out_shape=(jax.ShapeDtypeStruct((steps * ro...  2.25 us
  transfers between devices with their start and end apart: 18, of which 7 were waited for; matrix products, arithmetic and copies ran while one was open for 0% of the time, Pallas kernels for 24%

profile of v9, /device:TPU:0, one launch (start us, length us, event | category | flops | bytes accessed | tf_op | source)
XLA Modules:
  0.0 46.0 jit_solution(1946640242020482688)
XLA Ops:
  0.0 2.3 %attend.1 = (f32[8,7168]{1,0:T(8,128)S(1)}, bf16[8,7296]{1,0:T(8,128)(2,1)S(1)}) custom-call(s32[4]{0:T(128)} %len_hbm.1, s32[3,2,4]{2,1,0:T(2,128)} %bitcast.6, f32[3,2,4]{2,1,0:T(2,128)} %bitcast.7, bf16[2,4,7168]{2,1,0:T(4,128)(2,1)} %q_hbm.1, bf16[2,4,448]{2,1,0:T(4,128)(2,1)} %fresh_hbm.1, bf16[4,448,128]{2,1,0:T(8,128)(2,1)} %bitcast.4, ...), custom_call_target="tpu_custom_call" | custom-call | flops 300000000 | bytes 2000000 | tf_op jit(solution)/shard_map/attend/pallas_call | solution.py:172
  2.3 0.5 %collective-permute-start = (bf16[8,7296]{1,0:T(8,128)(2,1)S(1)}, bf16[8,7296]{1,0:T(8,128)(2,1)S(1)}, u32[]{:S(2)}, u32[]{:S(2)}) collective-permute-start(bf16[8,7296]{1,0:T(8,128)(2,1)S(1)} %get-tuple-element.44.own_ref), channel_id=1, source_target_pairs={{0,1},{1,0},{2,3},{3,2},{4,5},{5,4},{6,7},{7,6},{8,9},{9,8},{10,11... | collective-permute-start | bytes 350216 | tf_op jit(solution)/shard_map/ppermute | solution.py:427
  2.8 1.0 %collective-permute-done.other_ref = bf16[8,7296]{1,0:T(8,128)(2,1)S(1)} collective-permute-done((bf16[8,7296]{1,0:T(8,128)(2,1)S(1)}, bf16[8,7296]{1,0:T(8,128)(2,1)S(1)}, u32[]{:S(2)}, u32[]{:S(2)}) %collective-permute-start) | collective-permute-done | bytes 116768 | tf_op jit(solution)/shard_map/ppermute | solution.py:427
  3.7 0.5 %pack.1 = (bf16[32,1792]{1,0:T(8,128)(2,1)S(1)}, bf16[32,1792]{1,0:T(8,128)(2,1)S(1)}, bf16[32,1792]{1,0:T(8,128)(2,1)S(1)}, bf16[32,1792]{1,0:T(8,128)(2,1)S(1)}) custom-call(bf16[8,7296]{1,0:T(8,128)(2,1)S(1)} %get-tuple-element.44.own_ref, bf16[8,7296]{1,0:T(8,128)(2,1)S(1)} %collective-permute-done.other_ref), custom_call_target="tpu_custom_call" | custom-call | flops 1 | bytes 1 | tf_op jit(solution)/shard_map/pack/pallas_call | solution.py:235
  4.7 4.8 %collective-permute-start.2 = (bf16[32,1792]{1,0:T(8,128)(2,1)S(1)}, bf16[32,1792]{1,0:T(8,128)(2,1)S(1)}, u32[]{:S(2)}, u32[]{:S(2)}) collective-permute-start(bf16[32,1792]{1,0:T(8,128)(2,1)S(1)} %get-tuple-element.48), channel_id=1, source_target_pairs={{0,5},{1,10},{2,7},{3,8},{4,1},{5,14},{6,3},{7,12},{8,13},{9,2},{1... | collective-permute-start | bytes 344072 | tf_op jit(solution)/shard_map/ppermute | solution.py:433
  9.5 4.2 %stage.1 = (bf16[2,256,7168]{2,1,0:T(8,128)(2,1)S(1)}, bf16[256,7168]{1,0:T(8,128)(2,1)S(1)}, bf16[192,128]{1,0:T(8,128)(2,1)S(1)}) custom-call(bf16[8,7296]{1,0:T(8,128)(2,1)S(1)} %get-tuple-element.44.own_ref, bf16[8,7296]{1,0:T(8,128)(2,1)S(1)} %collective-permute-done.other_ref, bf16[1,2,256,7168]{3,2,1,0:T(8,128)(2,1)} %gu_hbm.1, ...), custom_call_target="tpu_custom_call" | custom-call | flops 1 | bytes 1 | tf_op jit(solution)/shard_map/stage/pallas_call | solution.py:291
  13.7 1.9 %collective-permute-done.2.refs_1_ = bf16[32,1792]{1,0:T(8,128)(2,1)S(1)} collective-permute-done((bf16[32,1792]{1,0:T(8,128)(2,1)S(1)}, bf16[32,1792]{1,0:T(8,128)(2,1)S(1)}, u32[]{:S(2)}, u32[]{:S(2)}) %collective-permute-start.2) | collective-permute-done | bytes 114720 | tf_op jit(solution)/shard_map/ppermute | solution.py:433
  15.6 0.5 %collective-permute-start.4 = (bf16[32,1792]{1,0:T(8,128)(2,1)S(1)}, bf16[32,1792]{1,0:T(8,128)(2,1)S(1)}, u32[]{:S(2)}, u32[]{:S(2)}) collective-permute-start(bf16[32,1792]{1,0:T(8,128)(2,1)S(1)} %collective-permute-done.2.refs_1_), channel_id=1, source_target_pairs={{0,1},{1,0},{2,3},{3,2},{4,5},{5,4},{6,7},{7,6},{8,9},{9,8},{10,11... | collective-permute-start | bytes 344072 | tf_op jit(solution)/shard_map/ppermute | solution.py:427
  16.1 1.6 %collective-permute-start.5 = (bf16[32,1792]{1,0:T(8,128)(2,1)S(1)}, bf16[32,1792]{1,0:T(8,128)(2,1)S(1)}, u32[]{:S(2)}, u32[]{:S(2)}) collective-permute-start(bf16[32,1792]{1,0:T(8,128)(2,1)S(1)} %get-tuple-element.61), channel_id=1, source_target_pairs={{0,9},{1,6},{2,11},{3,4},{4,13},{5,2},{6,15},{7,0},{8,1},{9,14},{1... | collective-permute-start | bytes 344072 | tf_op jit(solution)/shard_map/ppermute | solution.py:433
  17.7 2.5 %collective-permute-start.6 = (bf16[32,1792]{1,0:T(8,128)(2,1)S(1)}, bf16[32,1792]{1,0:T(8,128)(2,1)S(1)}, u32[]{:S(2)}, u32[]{:S(2)}) collective-permute-start(bf16[32,1792]{1,0:T(8,128)(2,1)S(1)} %get-tuple-element.62), channel_id=1, source_target_pairs={{0,13},{1,2},{2,15},{3,0},{4,9},{5,6},{6,11},{7,4},{8,5},{9,10},{1... | collective-permute-start | bytes 344072 | tf_op jit(solution)/shard_map/ppermute | solution.py:433
  20.2 3.4 %experts.2 = (bf16[32,1792]{1,0:T(8,128)(2,1)S(1)}, bf16[32,1792]{1,0:T(8,128)(2,1)S(1)}, bf16[32,1792]{1,0:T(8,128)(2,1)S(1)}, bf16[32,1792]{1,0:T(8,128)(2,1)S(1)}) custom-call(bf16[32,1792]{1,0:T(8,128)(2,1)S(1)} %collective-permute-done.1.refs_0_, bf16[32,1792]{1,0:T(8,128)(2,1)S(1)} %collective-permute-done.2.refs_1_, ...), custom_call_target="tpu_custom_call" | custom-call | flops 1 | bytes 1 | tf_op jit(solution)/shard_map/experts/pallas_call | solution.py:346
  23.7 0.5 %collective-permute-start.9 = (bf16[32,1792]{1,0:T(8,128)(2,1)S(1)}, bf16[32,1792]{1,0:T(8,128)(2,1)S(1)}, u32[]{:S(2)}, u32[]{:S(2)}) collective-permute-start(bf16[32,1792]{1,0:T(8,128)(2,1)S(1)} %get-tuple-element.70), channel_id=1, source_target_pairs={{0,1},{1,0},{2,3},{3,2},{4,5},{5,4},{6,7},{7,6},{8,9},{9,8},{10,11... | collective-permute-start | bytes 344072 | tf_op jit(solution)/shard_map/ppermute | solution.py:427
  24.3 0.4 collective-permute-start.8
  25.0 1.9 %collective-permute-start.12 = (bf16[32,1792]{1,0:T(8,128)(2,1)S(1)}, bf16[32,1792]{1,0:T(8,128)(2,1)S(1)}, u32[]{:S(2)}, u32[]{:S(2)}) collective-permute-start(bf16[32,1792]{1,0:T(8,128)(2,1)S(1)} %add_convert_fusion.2), channel_id=1, source_target_pairs={{5,0},{10,1},{7,2},{8,3},{1,4},{14,5},{3,6},{12,7},{13,8},{2,9},{1... | collective-permute-start | bytes 344072 | tf_op jit(solution)/shard_map/ppermute | solution.py:436
  26.9 1.1 %collective-permute-start.10 = (bf16[32,1792]{1,0:T(8,128)(2,1)S(1)}, bf16[32,1792]{1,0:T(8,128)(2,1)S(1)}, u32[]{:S(2)}, u32[]{:S(2)}) collective-permute-start(bf16[32,1792]{1,0:T(8,128)(2,1)S(1)} %add_convert_fusion.3), channel_id=1, source_target_pairs={{1,0},{14,1},{3,2},{12,3},{5,4},{10,5},{7,6},{8,7},{9,8},{6,9},{11... | collective-permute-start | bytes 344072 | tf_op jit(solution)/shard_map/ppermute | solution.py:436
  28.0 3.4 %experts.3 = (bf16[32,1792]{1,0:T(8,128)(2,1)S(1)}, bf16[32,1792]{1,0:T(8,128)(2,1)S(1)}, bf16[32,1792]{1,0:T(8,128)(2,1)S(1)}, bf16[32,1792]{1,0:T(8,128)(2,1)S(1)}) custom-call(bf16[32,1792]{1,0:T(8,128)(2,1)S(1)} %collective-permute-done.5.refs_0_, bf16[32,1792]{1,0:T(8,128)(2,1)S(1)} %collective-permute-done.6.refs_1_, ...), custom_call_target="tpu_custom_call" | custom-call | flops 1 | bytes 1 | tf_op jit(solution)/shard_map/experts/pallas_call | solution.py:346
  31.5 2.3 %collective-permute-start.13 = (bf16[32,1792]{1,0:T(8,128)(2,1)S(1)}, bf16[32,1792]{1,0:T(8,128)(2,1)S(1)}, u32[]{:S(2)}, u32[]{:S(2)}) collective-permute-start(bf16[32,1792]{1,0:T(8,128)(2,1)S(1)} %get-tuple-element.78), channel_id=1, source_target_pairs={{0,1},{1,0},{2,3},{3,2},{4,5},{5,4},{6,7},{7,6},{8,9},{9,8},{10,11... | collective-permute-start | bytes 344072 | tf_op jit(solution)/shard_map/ppermute | solution.py:427
  33.7 1.0 %collective-permute-done.13 = bf16[32,1792]{1,0:T(8,128)(2,1)S(1)} collective-permute-done((bf16[32,1792]{1,0:T(8,128)(2,1)S(1)}, bf16[32,1792]{1,0:T(8,128)(2,1)S(1)}, u32[]{:S(2)}, u32[]{:S(2)}) %collective-permute-start.13) | collective-permute-done | bytes 114720 | tf_op jit(solution)/shard_map/ppermute | solution.py:427
  34.7 1.8 %collective-permute-start.14 = (bf16[32,1792]{1,0:T(8,128)(2,1)S(1)}, bf16[32,1792]{1,0:T(8,128)(2,1)S(1)}, u32[]{:S(2)}, u32[]{:S(2)}) collective-permute-start(bf16[32,1792]{1,0:T(8,128)(2,1)S(1)} %add_convert_fusion.1), channel_id=1, source_target_pairs={{9,0},{6,1},{11,2},{4,3},{13,4},{2,5},{15,6},{0,7},{1,8},{14,9},{3... | collective-permute-start | bytes 344072 | tf_op jit(solution)/shard_map/ppermute | solution.py:436
  36.5 1.0 %collective-permute-start.16 = (bf16[32,1792]{1,0:T(8,128)(2,1)S(1)}, bf16[32,1792]{1,0:T(8,128)(2,1)S(1)}, u32[]{:S(2)}, u32[]{:S(2)}) collective-permute-start(bf16[32,1792]{1,0:T(8,128)(2,1)S(1)} %add_convert_fusion), channel_id=1, source_target_pairs={{13,0},{2,1},{15,2},{0,3},{9,4},{6,5},{11,6},{4,7},{5,8},{10,9},{7... | collective-permute-start | bytes 344072 | tf_op jit(solution)/shard_map/ppermute | solution.py:436
  37.5 2.5 %collective-permute-done.14.refs_2_ = bf16[32,1792]{1,0:T(8,128)(2,1)S(1)} collective-permute-done((bf16[32,1792]{1,0:T(8,128)(2,1)S(1)}, bf16[32,1792]{1,0:T(8,128)(2,1)S(1)}, u32[]{:S(2)}, u32[]{:S(2)}) %collective-permute-start.14) | collective-permute-done | bytes 114720 | tf_op jit(solution)/shard_map/ppermute | solution.py:436
  40.0 3.6 %collective-permute-done.16.refs_3_ = bf16[32,1792]{1,0:T(8,128)(2,1)S(1)} collective-permute-done((bf16[32,1792]{1,0:T(8,128)(2,1)S(1)}, bf16[32,1792]{1,0:T(8,128)(2,1)S(1)}, u32[]{:S(2)}, u32[]{:S(2)}) %collective-permute-start.16) | collective-permute-done | bytes 114720 | tf_op jit(solution)/shard_map/ppermute | solution.py:436
  44.0 1.3 %collective-permute-done.17.other_ref = bf16[8,7168]{1,0:T(8,128)(2,1)S(1)} collective-permute-done((bf16[8,7168]{1,0:T(8,128)(2,1)S(1)}, bf16[8,7168]{1,0:T(8,128)(2,1)S(1)}, u32[]{:S(2)}, u32[]{:S(2)}) %collective-permute-start.17) | collective-permute-done | bytes 114720 | tf_op jit(solution)/shard_map/ppermute | solution.py:427
  45.3 0.7 %finish.1 = bf16[2,4,7168]{2,1,0:T(4,128)(2,1)} custom-call(f32[8,7168]{1,0:T(8,128)S(1)} %get-tuple-element.81.kept_ref, bf16[8,7168]{1,0:T(8,128)(2,1)S(1)} %collective-permute-done.17.other_ref), custom_call_target="tpu_custom_call" | custom-call | flops 100000 | bytes 500000 | tf_op jit(solution)/shard_map/finish/pallas_call | solution.py:397
  (23 shorter events, 1.4 us)
Async XLA Ops:
  2.3 1.5 %collective-permute-start = (bf16[8,7296]{1,0:T(8,128)(2,1)S(1)}, bf16[8,7296]{1,0:T(8,128)(2,1)S(1)}, u32[]{:S(2)}, u32[]{:S(2)}) collective-permute-start(bf16[8,7296]{1,0:T(8,128)(2,1)S(1)} %get-tuple-element.44.own_ref), channel_id=1, source_target_pairs={{0,1},{1,0},{2,3},{3,2},{4,5},{5,4},{6,7},{7,6},{8,9},{9,8},{10,11... | collective-permute-start | bytes 350216 | tf_op jit(solution)/shard_map/ppermute | solution.py:427
  4.3 9.5 %collective-permute-start.1 = (bf16[32,1792]{1,0:T(8,128)(2,1)S(1)}, bf16[32,1792]{1,0:T(8,128)(2,1)S(1)}, u32[]{:S(2)}, u32[]{:S(2)}) collective-permute-start(bf16[32,1792]{1,0:T(8,128)(2,1)S(1)} %get-tuple-element.47), channel_id=1, source_target_pairs={{0,1},{1,14},{2,3},{3,12},{4,5},{5,10},{6,7},{7,8},{8,9},{9,6},{10... | collective-permute-start | bytes 344072 | tf_op jit(solution)/shard_map/ppermute | solution.py:433
  4.7 10.9 %collective-permute-start.2 = (bf16[32,1792]{1,0:T(8,128)(2,1)S(1)}, bf16[32,1792]{1,0:T(8,128)(2,1)S(1)}, u32[]{:S(2)}, u32[]{:S(2)}) collective-permute-start(bf16[32,1792]{1,0:T(8,128)(2,1)S(1)} %get-tuple-element.48), channel_id=1, source_target_pairs={{0,5},{1,10},{2,7},{3,8},{4,1},{5,14},{6,3},{7,12},{8,13},{9,2},{1... | collective-permute-start | bytes 344072 | tf_op jit(solution)/shard_map/ppermute | solution.py:433
  15.6 4.6 %collective-permute-start.3 = (bf16[32,1792]{1,0:T(8,128)(2,1)S(1)}, bf16[32,1792]{1,0:T(8,128)(2,1)S(1)}, u32[]{:S(2)}, u32[]{:S(2)}) collective-permute-start(bf16[32,1792]{1,0:T(8,128)(2,1)S(1)} %collective-permute-done.1.refs_0_), channel_id=1, source_target_pairs={{0,1},{1,0},{2,3},{3,2},{4,5},{5,4},{6,7},{7,6},{8,9},{9,8},{10,11... | collective-permute-start | bytes 344072 | tf_op jit(solution)/shard_map/ppermute | solution.py:427
  15.6 4.6 %collective-permute-start.4 = (bf16[32,1792]{1,0:T(8,128)(2,1)S(1)}, bf16[32,1792]{1,0:T(8,128)(2,1)S(1)}, u32[]{:S(2)}, u32[]{:S(2)}) collective-permute-start(bf16[32,1792]{1,0:T(8,128)(2,1)S(1)} %collective-permute-done.2.refs_1_), channel_id=1, source_target_pairs={{0,1},{1,0},{2,3},{3,2},{4,5},{5,4},{6,7},{7,6},{8,9},{9,8},{10,11... | collective-permute-start | bytes 344072 | tf_op jit(solution)/shard_map/ppermute | solution.py:427
  16.1 8.1 %collective-permute-start.5 = (bf16[32,1792]{1,0:T(8,128)(2,1)S(1)}, bf16[32,1792]{1,0:T(8,128)(2,1)S(1)}, u32[]{:S(2)}, u32[]{:S(2)}) collective-permute-start(bf16[32,1792]{1,0:T(8,128)(2,1)S(1)} %get-tuple-element.61), channel_id=1, source_target_pairs={{0,9},{1,6},{2,11},{3,4},{4,13},{5,2},{6,15},{7,0},{8,1},{9,14},{1... | collective-permute-start | bytes 344072 | tf_op jit(solution)/shard_map/ppermute | solution.py:433
  17.7 6.5 %collective-permute-start.6 = (bf16[32,1792]{1,0:T(8,128)(2,1)S(1)}, bf16[32,1792]{1,0:T(8,128)(2,1)S(1)}, u32[]{:S(2)}, u32[]{:S(2)}) collective-permute-start(bf16[32,1792]{1,0:T(8,128)(2,1)S(1)} %get-tuple-element.62), channel_id=1, source_target_pairs={{0,13},{1,2},{2,15},{3,0},{4,9},{5,6},{6,11},{7,4},{8,5},{9,10},{1... | collective-permute-start | bytes 344072 | tf_op jit(solution)/shard_map/ppermute | solution.py:433
  23.6 1.4 %collective-permute-start.11 = (bf16[32,1792]{1,0:T(8,128)(2,1)S(1)}, bf16[32,1792]{1,0:T(8,128)(2,1)S(1)}, u32[]{:S(2)}, u32[]{:S(2)}) collective-permute-start(bf16[32,1792]{1,0:T(8,128)(2,1)S(1)} %get-tuple-element.72), channel_id=1, source_target_pairs={{0,1},{1,0},{2,3},{3,2},{4,5},{5,4},{6,7},{7,6},{8,9},{9,8},{10,11... | collective-permute-start | bytes 344072 | tf_op jit(solution)/shard_map/ppermute | solution.py:427
  23.7 3.2 %collective-permute-start.9 = (bf16[32,1792]{1,0:T(8,128)(2,1)S(1)}, bf16[32,1792]{1,0:T(8,128)(2,1)S(1)}, u32[]{:S(2)}, u32[]{:S(2)}) collective-permute-start(bf16[32,1792]{1,0:T(8,128)(2,1)S(1)} %get-tuple-element.70), channel_id=1, source_target_pairs={{0,1},{1,0},{2,3},{3,2},{4,5},{5,4},{6,7},{7,6},{8,9},{9,8},{10,11... | collective-permute-start | bytes 344072 | tf_op jit(solution)/shard_map/ppermute | solution.py:427
  24.2 3.9 %collective-permute-start.7 = (bf16[32,1792]{1,0:T(8,128)(2,1)S(1)}, bf16[32,1792]{1,0:T(8,128)(2,1)S(1)}, u32[]{:S(2)}, u32[]{:S(2)}) collective-permute-start(bf16[32,1792]{1,0:T(8,128)(2,1)S(1)} %collective-permute-done.5.refs_0_), channel_id=1, source_target_pairs={{0,1},{1,0},{2,3},{3,2},{4,5},{5,4},{6,7},{7,6},{8,9},{9,8},{10,11... | collective-permute-start | bytes 344072 | tf_op jit(solution)/shard_map/ppermute | solution.py:427
  24.3 3.8 %collective-permute-start.8 = (bf16[32,1792]{1,0:T(8,128)(2,1)S(1)}, bf16[32,1792]{1,0:T(8,128)(2,1)S(1)}, u32[]{:S(2)}, u32[]{:S(2)}) collective-permute-start(bf16[32,1792]{1,0:T(8,128)(2,1)S(1)} %collective-permute-done.6.refs_1_), channel_id=1, source_target_pairs={{0,1},{1,0},{2,3},{3,2},{4,5},{5,4},{6,7},{7,6},{8,9},{9,8},{10,11... | collective-permute-start | bytes 344072 | tf_op jit(solution)/shard_map/ppermute | solution.py:427
  25.0 6.4 %collective-permute-start.12 = (bf16[32,1792]{1,0:T(8,128)(2,1)S(1)}, bf16[32,1792]{1,0:T(8,128)(2,1)S(1)}, u32[]{:S(2)}, u32[]{:S(2)}) collective-permute-start(bf16[32,1792]{1,0:T(8,128)(2,1)S(1)} %add_convert_fusion.2), channel_id=1, source_target_pairs={{5,0},{10,1},{7,2},{8,3},{1,4},{14,5},{3,6},{12,7},{13,8},{2,9},{1... | collective-permute-start | bytes 344072 | tf_op jit(solution)/shard_map/ppermute | solution.py:436
  26.9 4.5 %collective-permute-start.10 = (bf16[32,1792]{1,0:T(8,128)(2,1)S(1)}, bf16[32,1792]{1,0:T(8,128)(2,1)S(1)}, u32[]{:S(2)}, u32[]{:S(2)}) collective-permute-start(bf16[32,1792]{1,0:T(8,128)(2,1)S(1)} %add_convert_fusion.3), channel_id=1, source_target_pairs={{1,0},{14,1},{3,2},{12,3},{5,4},{10,5},{7,6},{8,7},{9,8},{6,9},{11... | collective-permute-start | bytes 344072 | tf_op jit(solution)/shard_map/ppermute | solution.py:436
  31.5 3.2 %collective-permute-start.13 = (bf16[32,1792]{1,0:T(8,128)(2,1)S(1)}, bf16[32,1792]{1,0:T(8,128)(2,1)S(1)}, u32[]{:S(2)}, u32[]{:S(2)}) collective-permute-start(bf16[32,1792]{1,0:T(8,128)(2,1)S(1)} %get-tuple-element.78), channel_id=1, source_target_pairs={{0,1},{1,0},{2,3},{3,2},{4,5},{5,4},{6,7},{7,6},{8,9},{9,8},{10,11... | collective-permute-start | bytes 344072 | tf_op jit(solution)/shard_map/ppermute | solution.py:427
  33.7 2.8 %collective-permute-start.15 = (bf16[32,1792]{1,0:T(8,128)(2,1)S(1)}, bf16[32,1792]{1,0:T(8,128)(2,1)S(1)}, u32[]{:S(2)}, u32[]{:S(2)}) collective-permute-start(bf16[32,1792]{1,0:T(8,128)(2,1)S(1)} %get-tuple-element.80), channel_id=1, source_target_pairs={{0,1},{1,0},{2,3},{3,2},{4,5},{5,4},{6,7},{7,6},{8,9},{9,8},{10,11... | collective-permute-start | bytes 344072 | tf_op jit(solution)/shard_map/ppermute | solution.py:427
  34.7 5.3 %collective-permute-start.14 = (bf16[32,1792]{1,0:T(8,128)(2,1)S(1)}, bf16[32,1792]{1,0:T(8,128)(2,1)S(1)}, u32[]{:S(2)}, u32[]{:S(2)}) collective-permute-start(bf16[32,1792]{1,0:T(8,128)(2,1)S(1)} %add_convert_fusion.1), channel_id=1, source_target_pairs={{9,0},{6,1},{11,2},{4,3},{13,4},{2,5},{15,6},{0,7},{1,8},{14,9},{3... | collective-permute-start | bytes 344072 | tf_op jit(solution)/shard_map/ppermute | solution.py:436
  36.5 7.1 %collective-permute-start.16 = (bf16[32,1792]{1,0:T(8,128)(2,1)S(1)}, bf16[32,1792]{1,0:T(8,128)(2,1)S(1)}, u32[]{:S(2)}, u32[]{:S(2)}) collective-permute-start(bf16[32,1792]{1,0:T(8,128)(2,1)S(1)} %add_convert_fusion), channel_id=1, source_target_pairs={{13,0},{2,1},{15,2},{0,3},{9,4},{6,5},{11,6},{4,7},{5,8},{10,9},{7... | collective-permute-start | bytes 344072 | tf_op jit(solution)/shard_map/ppermute | solution.py:436
  43.9 1.4 %collective-permute-start.17 = (bf16[8,7168]{1,0:T(8,128)(2,1)S(1)}, bf16[8,7168]{1,0:T(8,128)(2,1)S(1)}, u32[]{:S(2)}, u32[]{:S(2)}) collective-permute-start(bf16[8,7168]{1,0:T(8,128)(2,1)S(1)} %get-tuple-element.82), channel_id=1, source_target_pairs={{0,1},{1,0},{2,3},{3,2},{4,5},{5,4},{6,7},{7,6},{8,9},{9,8},{10,11... | collective-permute-start | bytes 344072 | tf_op jit(solution)/shard_map/ppermute | solution.py:427

commit v10 on v5

--- a/solution.py
+++ b/solution.py
@@ -394,9 +394,14 @@
     permuted = chips == EXPERTS
     swap = [(i, i ^ 1) for i in range(owners)]
 
-    def trade(chunk, n):
-        turns = [(i, ((i // 2) ^ TURNS[i % 2][n]) * 2 + i % 2) for i in range(owners)]
-        return lax.ppermute(chunk, "afd", turns)
+    def route(n):
+        return [(i, (i // 2 ^ TURNS[i % 2][n]) * 2 + 1 - i % 2) for i in range(owners)]
+
+    def send(chunk, n):
+        return lax.ppermute(chunk, "afd", route(n))
+
+    def send_back(chunk, n):
+        return lax.ppermute(chunk, "afd", [(j, i) for i, j in route(n)])
 
     def to_chips(chunks):
         same_core = [[2 * p + c for p in range(chips)] for c in range(2)]
@@ -418,7 +423,7 @@
         if permuted:
             *late, gu, dn = lax.optimization_barrier((*chunks[STAGED:], gu, dn))
             chunks = [*chunks[:STAGED], *late]
-            own = [chunks[0]] + [trade(chunks[n], n) for n in range(1, chips)]
+            own = [chunks[0]] + [send(chunks[n], n) for n in range(1, chips)]
         else:
             own = to_chips([jnp.repeat(chunk, chips_per_expert, axis=0) for chunk in chunks])
         other = [lax.ppermute(x, "afd", swap) for x in own]
@@ -428,7 +433,7 @@
             for a, b in zip(mine, theirs)
         ]
         if permuted:
-            backs.append([summed[0]] + [trade(summed[n], n) for n in range(1, chips)])
+            backs.append([summed[0]] + [send_back(summed[n], n) for n in range(1, chips)])
         else:
             backs.append(to_chips(summed))
     return combine(queries.shape, resid, mixes, backs)

time: 48.7 us -> 48.3 us (level)
  starting transfers between devices: 28.7 us -> 27.3 us
  waiting for transfers between devices: 8.29 us -> 9.29 us
    ppermute x14, starting transfers between devices: 24.9 us -> 21.9 us  [the longest x7 11.7 us: send(): return lax.ppermute(chunk, 'afd', route(n))]
    ppermute x8, starting transfers between devices: 1.54 us -> 3.35 us  [per_device(): other = [lax.ppermute(x, 'afd', swap) for x in own]]
    ppermute x14, waiting for transfers between devices: 7.23 us -> 7.88 us  [the longest x7 5.41 us: send_back(): return lax.ppermute(chunk, 'afd', [(j, i) for i, j in route(n)])]
  transfers between devices with their start and end apart: 30 -> 30, of which waited for: 10 -> 11; matrix products, arithmetic and copies ran while one was open for 0% -> 0% of each run, Pallas kernels for 9% -> 9%
where the time goes in v10:
time: 48.3 us; the launch traced here: 48.2 us
  starting transfers between devices  27.3 us (57%)
  Pallas kernels  11.3 us (23%)
  waiting for transfers between devices  9.29 us (19%)
    ppermute x7, starting transfers between devices, send(): return lax.ppermute(chunk, 'afd', route(n))  11.7 us
    ppermute x7, starting transfers between devices, send_back(): return lax.ppermute(chunk, 'afd', [(j, i) for i, j in route(n)])  10.2 us
    ppermute x7, waiting for transfers between devices, send_back(): return lax.ppermute(chunk, 'afd', [(j, i) for i, j in route(n)])  5.41 us
    pallas_call x1, Pallas kernels, stage(): pl.pallas_call(functools.partial(stage_kernel, permuted, chips, steps, ro...  4.26 us
    pallas_call x1, Pallas kernels, experts(): pl.pallas_call(functools.partial(expert_kernel, count, per), out_shape=sh...  3.61 us
    ppermute x8, starting transfers between devices, per_device(): other = [lax.ppermute(x, 'afd', swap) for x in own]  3.35 us
    pallas_call x1, Pallas kernels, attend(): pl.pallas_call(functools.partial(attend_kernel, permuted), out_shape=(jax...  2.49 us
    ppermute x7, waiting for transfers between devices, send(): return lax.ppermute(chunk, 'afd', route(n))  2.48 us
  transfers between devices with their start and end apart: 30, of which 11 were waited for; matrix products, arithmetic and copies ran while one was open for 0% of the time, Pallas kernels for 9%

profile of v10, /device:TPU:0, one launch (start us, length us, event | category | flops | bytes accessed | tf_op | source)
XLA Modules:
  0.0 48.2 jit_solution(635986327904454905)
XLA Ops:
  0.0 2.5 %attend.1 = (f32[8,7168]{1,0:T(8,128)S(1)}, bf16[1,16,1792]{2,1,0:T(8,128)(2,1)S(1)}, bf16[1,16,1792]{2,1,0:T(8,128)(2,1)S(1)}, bf16[1,16,1792]{2,1,0:T(8,128)(2...) custom-call(s32[4]{0:T(128)} %len_hbm.1, ...), custom_call_target="tpu_custom_call" | custom-call | flops 300000000 | bytes 2000000 | tf_op jit(solution)/shard_map/attend/pallas_call | solution.py:170
  2.5 5.5 %collective-permute-start = (bf16[1,16,1792]{2,1,0:T(8,128)(2,1)S(1)}, bf16[1,16,1792]{2,1,0:T(8,128)(2,1)S(1)}, u32[]{:S(2)}, u32[]{:S(2)}) collective-permute-start(bf16[1,16,1792]{2,1,0:T(8,128)(2,1)S(1)} %get-tuple-element.41), channel_id=1, source_target_pairs={{0,15},{1,8},{2,13},{3,10},{4,11},{5,12},{6,9},{7,14},{8,7},{9,0},... | collective-permute-start | bytes 172040 | tf_op jit(solution)/shard_map/ppermute | solution.py:401
  8.0 0.7 %collective-permute-start.2 = (bf16[1,16,1792]{2,1,0:T(8,128)(2,1)S(1)}, bf16[1,16,1792]{2,1,0:T(8,128)(2,1)S(1)}, u32[]{:S(2)}, u32[]{:S(2)}) collective-permute-start(bf16[1,16,1792]{2,1,0:T(8,128)(2,1)S(1)} %get-tuple-element.43), channel_id=1, source_target_pairs={{0,11},{1,2},{2,9},{3,0},{4,15},{5,6},{6,13},{7,4},{8,3},{9,10},{1... | collective-permute-start | bytes 172040 | tf_op jit(solution)/shard_map/ppermute | solution.py:401
  8.7 1.0 %collective-permute-start.3 = (bf16[1,16,1792]{2,1,0:T(8,128)(2,1)S(1)}, bf16[1,16,1792]{2,1,0:T(8,128)(2,1)S(1)}, u32[]{:S(2)}, u32[]{:S(2)}) collective-permute-start(bf16[1,16,1792]{2,1,0:T(8,128)(2,1)S(1)} %get-tuple-element.44), channel_id=1, source_target_pairs={{0,5},{1,14},{2,7},{3,12},{4,1},{5,10},{6,3},{7,8},{8,13},{9,6},{1... | collective-permute-start | bytes 172040 | tf_op jit(solution)/shard_map/ppermute | solution.py:401
  9.6 1.6 %collective-permute-start.7 = (bf16[1,16,1792]{2,1,0:T(8,128)(2,1)S(1)}, bf16[1,16,1792]{2,1,0:T(8,128)(2,1)S(1)}, u32[]{:S(2)}, u32[]{:S(2)}) collective-permute-start(bf16[1,16,1792]{2,1,0:T(8,128)(2,1)S(1)} %get-tuple-element.40.refs_0_), channel_id=1, source_target_pairs={{0,1},{1,0},{2,3},{3,2},{4,5},{5,4},{6,7},{7,6},{8,9},{9,8},{10,11... | collective-permute-start | bytes 172040 | tf_op jit(solution)/shard_map/ppermute | solution.py:429
  11.3 4.3 %stage.1 = (bf16[2,256,7168]{2,1,0:T(8,128)(2,1)S(1)}, bf16[256,7168]{1,0:T(8,128)(2,1)S(1)}, bf16[96,128]{1,0:T(8,128)(2,1)S(1)}) custom-call(s32[3,2,4]{2,1,0:T(2,128)} %bitcast.5, f32[3,2,4]{2,1,0:T(2,128)} %bitcast.6, bf16[1,2,256,7168]{3,2,1,0:T(8,128)(2,1)} %gu_hbm.1, bf16[1,256,7168]{2,1,0:T(8,128)(2,1)} %dn_hbm.1), custom_call_target="tpu_custom_call" | custom-call | flops 1000000 | bytes 22000000 | tf_op jit(solution)/shard_map/stage/pallas_call | solution.py:259
  15.5 1.9 %collective-permute-start.4 = (bf16[1,16,1792]{2,1,0:T(8,128)(2,1)S(1)}, bf16[1,16,1792]{2,1,0:T(8,128)(2,1)S(1)}, u32[]{:S(2)}, u32[]{:S(2)}) collective-permute-start(bf16[1,16,1792]{2,1,0:T(8,128)(2,1)S(1)} %get-tuple-element.50), channel_id=1, source_target_pairs={{0,13},{1,4},{2,15},{3,6},{4,9},{5,0},{6,11},{7,2},{8,5},{9,12},{1... | collective-permute-start | bytes 172040 | tf_op jit(solution)/shard_map/ppermute | solution.py:401
  17.5 0.8 %collective-permute-start.5 = (bf16[1,16,1792]{2,1,0:T(8,128)(2,1)S(1)}, bf16[1,16,1792]{2,1,0:T(8,128)(2,1)S(1)}, u32[]{:S(2)}, u32[]{:S(2)}) collective-permute-start(bf16[1,16,1792]{2,1,0:T(8,128)(2,1)S(1)} %get-tuple-element.51), channel_id=1, source_target_pairs={{0,7},{1,10},{2,5},{3,8},{4,3},{5,14},{6,1},{7,12},{8,15},{9,2},{1... | collective-permute-start | bytes 172040 | tf_op jit(solution)/shard_map/ppermute | solution.py:401
  18.3 1.8 %collective-permute-start.6 = (bf16[1,16,1792]{2,1,0:T(8,128)(2,1)S(1)}, bf16[1,16,1792]{2,1,0:T(8,128)(2,1)S(1)}, u32[]{:S(2)}, u32[]{:S(2)}) collective-permute-start(bf16[1,16,1792]{2,1,0:T(8,128)(2,1)S(1)} %get-tuple-element.52), channel_id=1, source_target_pairs={{0,9},{1,6},{2,11},{3,4},{4,13},{5,2},{6,15},{7,0},{8,1},{9,14},{1... | collective-permute-start | bytes 172040 | tf_op jit(solution)/shard_map/ppermute | solution.py:401
  20.1 0.5 %collective-permute-start.9 = (bf16[1,16,1792]{2,1,0:T(8,128)(2,1)S(1)}, bf16[1,16,1792]{2,1,0:T(8,128)(2,1)S(1)}, u32[]{:S(2)}, u32[]{:S(2)}) collective-permute-start(bf16[1,16,1792]{2,1,0:T(8,128)(2,1)S(1)} %collective-permute-done.1.refs_2_), channel_id=1, source_target_pairs={{0,1},{1,0},{2,3},{3,2},{4,5},{5,4},{6,7},{7,6},{8,9},{9,8},{10,11... | collective-permute-start | bytes 172040 | tf_op jit(solution)/shard_map/ppermute | solution.py:429
  20.6 0.6 %collective-permute-start.10 = (bf16[1,16,1792]{2,1,0:T(8,128)(2,1)S(1)}, bf16[1,16,1792]{2,1,0:T(8,128)(2,1)S(1)}, u32[]{:S(2)}, u32[]{:S(2)}) collective-permute-start(bf16[1,16,1792]{2,1,0:T(8,128)(2,1)S(1)} %collective-permute-done.2.refs_3_), channel_id=1, source_target_pairs={{0,1},{1,0},{2,3},{3,2},{4,5},{5,4},{6,7},{7,6},{8,9},{9,8},{10,11... | collective-permute-start | bytes 172040 | tf_op jit(solution)/shard_map/ppermute | solution.py:429
  21.2 2.0 %collective-permute-done.5.refs_6_ = bf16[1,16,1792]{2,1,0:T(8,128)(2,1)S(1)} collective-permute-done((bf16[1,16,1792]{2,1,0:T(8,128)(2,1)S(1)}, bf16[1,16,1792]{2,1,0:T(8,128)(2,1)S(1)}, u32[]{:S(2)}, u32[]{:S(2)}) %collective-permute-start.5) | collective-permute-done | bytes 57376 | tf_op jit(solution)/shard_map/ppermute | solution.py:401
  23.2 0.5 collective-permute-done.6.refs_7_
  24.5 0.5 collective-permute-done.12.refs_13_
  25.4 3.6 %experts.1 = (bf16[1,16,1792]{2,1,0:T(8,128)(2,1)S(1)}, bf16[1,16,1792]{2,1,0:T(8,128)(2,1)S(1)}, bf16[1,16,1792]{2,1,0:T(8,128)(2,1)S(1)}, bf16[1,16,1792]{2,1,...) custom-call(bf16[1,16,1792]{2,1,0:T(8,128)(2,1)S(1)} %get-tuple-elem, ...), custom_call_target="tpu_custom_call" | custom-call | flops 800000000 | bytes 12000000 | tf_op jit(solution)/shard_map/experts/pallas_call | solution.py:326
  31.5 1.7 %collective-permute-start.17 = (bf16[1,16,1792]{2,1,0:T(8,128)(2,1)S(1)}, bf16[1,16,1792]{2,1,0:T(8,128)(2,1)S(1)}, u32[]{:S(2)}, u32[]{:S(2)}) collective-permute-start(bf16[1,16,1792]{2,1,0:T(8,128)(2,1)S(1)} %add_convert_fusion.6), channel_id=1, source_target_pairs={{15,0},{8,1},{13,2},{10,3},{11,4},{12,5},{9,6},{14,7},{7,8},{0,9},... | collective-permute-start | bytes 172040 | tf_op jit(solution)/shard_map/ppermute | solution.py:404
  33.2 3.0 %collective-permute-start.19 = (bf16[1,16,1792]{2,1,0:T(8,128)(2,1)S(1)}, bf16[1,16,1792]{2,1,0:T(8,128)(2,1)S(1)}, u32[]{:S(2)}, u32[]{:S(2)}) collective-permute-start(bf16[1,16,1792]{2,1,0:T(8,128)(2,1)S(1)} %add_convert_fusion.5), channel_id=1, source_target_pairs={{3,0},{12,1},{1,2},{14,3},{7,4},{8,5},{5,6},{10,7},{11,8},{4,9},{9... | collective-permute-start | bytes 172040 | tf_op jit(solution)/shard_map/ppermute | solution.py:404
  36.4 1.8 %collective-permute-start.23 = (bf16[1,16,1792]{2,1,0:T(8,128)(2,1)S(1)}, bf16[1,16,1792]{2,1,0:T(8,128)(2,1)S(1)}, u32[]{:S(2)}, u32[]{:S(2)}) collective-permute-start(bf16[1,16,1792]{2,1,0:T(8,128)(2,1)S(1)} %add_convert_fusion.3), channel_id=1, source_target_pairs={{5,0},{14,1},{7,2},{12,3},{1,4},{10,5},{3,6},{8,7},{13,8},{6,9},{1... | collective-permute-start | bytes 172040 | tf_op jit(solution)/shard_map/ppermute | solution.py:404
  38.2 1.0 %collective-permute-start.25 = (bf16[1,16,1792]{2,1,0:T(8,128)(2,1)S(1)}, bf16[1,16,1792]{2,1,0:T(8,128)(2,1)S(1)}, u32[]{:S(2)}, u32[]{:S(2)}) collective-permute-start(bf16[1,16,1792]{2,1,0:T(8,128)(2,1)S(1)} %add_convert_fusion.2), channel_id=1, source_target_pairs={{13,0},{4,1},{15,2},{6,3},{9,4},{0,5},{11,6},{2,7},{5,8},{12,9},{7... | collective-permute-start | bytes 172040 | tf_op jit(solution)/shard_map/ppermute | solution.py:404
  39.1 2.5 %collective-permute-start.27 = (bf16[1,16,1792]{2,1,0:T(8,128)(2,1)S(1)}, bf16[1,16,1792]{2,1,0:T(8,128)(2,1)S(1)}, u32[]{:S(2)}, u32[]{:S(2)}) collective-permute-start(bf16[1,16,1792]{2,1,0:T(8,128)(2,1)S(1)} %add_convert_fusion.1), channel_id=1, source_target_pairs={{7,0},{10,1},{5,2},{8,3},{3,4},{14,5},{1,6},{12,7},{15,8},{2,9},{1... | collective-permute-start | bytes 172040 | tf_op jit(solution)/shard_map/ppermute | solution.py:404
  41.9 2.3 %collective-permute-done.25.refs_6_ = bf16[1,16,1792]{2,1,0:T(8,128)(2,1)S(1)} collective-permute-done((bf16[1,16,1792]{2,1,0:T(8,128)(2,1)S(1)}, bf16[1,16,1792]{2,1,0:T(8,128)(2,1)S(1)}, u32[]{:S(2)}, u32[]{:S(2)}) %collective-permute-start.25) | collective-permute-done | bytes 57376 | tf_op jit(solution)/shard_map/ppermute | solution.py:404
  44.2 0.7 %collective-permute-done.27.refs_7_ = bf16[1,16,1792]{2,1,0:T(8,128)(2,1)S(1)} collective-permute-done((bf16[1,16,1792]{2,1,0:T(8,128)(2,1)S(1)}, bf16[1,16,1792]{2,1,0:T(8,128)(2,1)S(1)}, u32[]{:S(2)}, u32[]{:S(2)}) %collective-permute-start.27) | collective-permute-done | bytes 57376 | tf_op jit(solution)/shard_map/ppermute | solution.py:404
  44.9 2.4 %collective-permute-done.29.refs_8_ = bf16[1,16,1792]{2,1,0:T(8,128)(2,1)S(1)} collective-permute-done((bf16[1,16,1792]{2,1,0:T(8,128)(2,1)S(1)}, bf16[1,16,1792]{2,1,0:T(8,128)(2,1)S(1)}, u32[]{:S(2)}, u32[]{:S(2)}) %collective-permute-start.29) | collective-permute-done | bytes 57376 | tf_op jit(solution)/shard_map/ppermute | solution.py:404
  47.3 0.9 %combine.1 = bf16[2,4,7168]{2,1,0:T(4,128)(2,1)} custom-call(f32[8,7168]{1,0:T(8,128)S(1)} %get-tuple-element.38.resid_ref, bf16[96,128]{1,0:T(8,128)(2,1)S(1)} %get-tuple-element.39.refs_0_, bf16[1,16,1792]{2,1,0:T(8,128)(2,1)S(1)} %add_convert_fusion.7.refs_1_, bf16[1,16,1792]{2,1,0:T(8,128)(2,1)S(1)} %collective-permute-done.17.refs_2_, ...), custom_call_target="tpu_custom_call" | custom-call | flops 100000000 | bytes 1000000 | tf_op jit(solution)/shard_map/combine/pallas_call | solution.py:366
  (48 shorter events, 4.1 us)
Async XLA Ops:
  2.5 13.0 %collective-permute-start = (bf16[1,16,1792]{2,1,0:T(8,128)(2,1)S(1)}, bf16[1,16,1792]{2,1,0:T(8,128)(2,1)S(1)}, u32[]{:S(2)}, u32[]{:S(2)}) collective-permute-start(bf16[1,16,1792]{2,1,0:T(8,128)(2,1)S(1)} %get-tuple-element.41), channel_id=1, source_target_pairs={{0,15},{1,8},{2,13},{3,10},{4,11},{5,12},{6,9},{7,14},{8,7},{9,0},... | collective-permute-start | bytes 172040 | tf_op jit(solution)/shard_map/ppermute | solution.py:401
  8.0 9.5 %collective-permute-start.1 = (bf16[1,16,1792]{2,1,0:T(8,128)(2,1)S(1)}, bf16[1,16,1792]{2,1,0:T(8,128)(2,1)S(1)}, u32[]{:S(2)}, u32[]{:S(2)}) collective-permute-start(bf16[1,16,1792]{2,1,0:T(8,128)(2,1)S(1)} %get-tuple-element.42), channel_id=1, source_target_pairs={{0,3},{1,12},{2,1},{3,14},{4,7},{5,8},{6,5},{7,10},{8,11},{9,4},{1... | collective-permute-start | bytes 172040 | tf_op jit(solution)/shard_map/ppermute | solution.py:401
  8.0 10.3 %collective-permute-start.2 = (bf16[1,16,1792]{2,1,0:T(8,128)(2,1)S(1)}, bf16[1,16,1792]{2,1,0:T(8,128)(2,1)S(1)}, u32[]{:S(2)}, u32[]{:S(2)}) collective-permute-start(bf16[1,16,1792]{2,1,0:T(8,128)(2,1)S(1)} %get-tuple-element.43), channel_id=1, source_target_pairs={{0,11},{1,2},{2,9},{3,0},{4,15},{5,6},{6,13},{7,4},{8,3},{9,10},{1... | collective-permute-start | bytes 172040 | tf_op jit(solution)/shard_map/ppermute | solution.py:401
  8.7 11.4 %collective-permute-start.3 = (bf16[1,16,1792]{2,1,0:T(8,128)(2,1)S(1)}, bf16[1,16,1792]{2,1,0:T(8,128)(2,1)S(1)}, u32[]{:S(2)}, u32[]{:S(2)}) collective-permute-start(bf16[1,16,1792]{2,1,0:T(8,128)(2,1)S(1)} %get-tuple-element.44), channel_id=1, source_target_pairs={{0,5},{1,14},{2,7},{3,12},{4,1},{5,10},{6,3},{7,8},{8,13},{9,6},{1... | collective-permute-start | bytes 172040 | tf_op jit(solution)/shard_map/ppermute | solution.py:401
  9.6 10.5 %collective-permute-start.7 = (bf16[1,16,1792]{2,1,0:T(8,128)(2,1)S(1)}, bf16[1,16,1792]{2,1,0:T(8,128)(2,1)S(1)}, u32[]{:S(2)}, u32[]{:S(2)}) collective-permute-start(bf16[1,16,1792]{2,1,0:T(8,128)(2,1)S(1)} %get-tuple-element.40.refs_0_), channel_id=1, source_target_pairs={{0,1},{1,0},{2,3},{3,2},{4,5},{5,4},{6,7},{7,6},{8,9},{9,8},{10,11... | collective-permute-start | bytes 172040 | tf_op jit(solution)/shard_map/ppermute | solution.py:429
  15.5 5.1 %collective-permute-start.4 = (bf16[1,16,1792]{2,1,0:T(8,128)(2,1)S(1)}, bf16[1,16,1792]{2,1,0:T(8,128)(2,1)S(1)}, u32[]{:S(2)}, u32[]{:S(2)}) collective-permute-start(bf16[1,16,1792]{2,1,0:T(8,128)(2,1)S(1)} %get-tuple-element.50), channel_id=1, source_target_pairs={{0,13},{1,4},{2,15},{3,6},{4,9},{5,0},{6,11},{7,2},{8,5},{9,12},{1... | collective-permute-start | bytes 172040 | tf_op jit(solution)/shard_map/ppermute | solution.py:401
  17.5 5.7 %collective-permute-start.5 = (bf16[1,16,1792]{2,1,0:T(8,128)(2,1)S(1)}, bf16[1,16,1792]{2,1,0:T(8,128)(2,1)S(1)}, u32[]{:S(2)}, u32[]{:S(2)}) collective-permute-start(bf16[1,16,1792]{2,1,0:T(8,128)(2,1)S(1)} %get-tuple-element.51), channel_id=1, source_target_pairs={{0,7},{1,10},{2,5},{3,8},{4,3},{5,14},{6,1},{7,12},{8,15},{9,2},{1... | collective-permute-start | bytes 172040 | tf_op jit(solution)/shard_map/ppermute | solution.py:401
  18.3 5.4 %collective-permute-start.6 = (bf16[1,16,1792]{2,1,0:T(8,128)(2,1)S(1)}, bf16[1,16,1792]{2,1,0:T(8,128)(2,1)S(1)}, u32[]{:S(2)}, u32[]{:S(2)}) collective-permute-start(bf16[1,16,1792]{2,1,0:T(8,128)(2,1)S(1)} %get-tuple-element.52), channel_id=1, source_target_pairs={{0,9},{1,6},{2,11},{3,4},{4,13},{5,2},{6,15},{7,0},{8,1},{9,14},{1... | collective-permute-start | bytes 172040 | tf_op jit(solution)/shard_map/ppermute | solution.py:401
  20.1 3.7 %collective-permute-start.8 = (bf16[1,16,1792]{2,1,0:T(8,128)(2,1)S(1)}, bf16[1,16,1792]{2,1,0:T(8,128)(2,1)S(1)}, u32[]{:S(2)}, u32[]{:S(2)}) collective-permute-start(bf16[1,16,1792]{2,1,0:T(8,128)(2,1)S(1)} %collective-permute-done.refs_1_), channel_id=1, source_target_pairs={{0,1},{1,0},{2,3},{3,2},{4,5},{5,4},{6,7},{7,6},{8,9},{9,8},{10,11... | collective-permute-start | bytes 172040 | tf_op jit(solution)/shard_map/ppermute | solution.py:429
  20.1 4.1 %collective-permute-start.9 = (bf16[1,16,1792]{2,1,0:T(8,128)(2,1)S(1)}, bf16[1,16,1792]{2,1,0:T(8,128)(2,1)S(1)}, u32[]{:S(2)}, u32[]{:S(2)}) collective-permute-start(bf16[1,16,1792]{2,1,0:T(8,128)(2,1)S(1)} %collective-permute-done.1.refs_2_), channel_id=1, source_target_pairs={{0,1},{1,0},{2,3},{3,2},{4,5},{5,4},{6,7},{7,6},{8,9},{9,8},{10,11... | collective-permute-start | bytes 172040 | tf_op jit(solution)/shard_map/ppermute | solution.py:429
  20.6 3.7 %collective-permute-start.10 = (bf16[1,16,1792]{2,1,0:T(8,128)(2,1)S(1)}, bf16[1,16,1792]{2,1,0:T(8,128)(2,1)S(1)}, u32[]{:S(2)}, u32[]{:S(2)}) collective-permute-start(bf16[1,16,1792]{2,1,0:T(8,128)(2,1)S(1)} %collective-permute-done.2.refs_3_), channel_id=1, source_target_pairs={{0,1},{1,0},{2,3},{3,2},{4,5},{5,4},{6,7},{7,6},{8,9},{9,8},{10,11... | collective-permute-start | bytes 172040 | tf_op jit(solution)/shard_map/ppermute | solution.py:429
  29.1 1.3 %collective-permute-start.16 = (bf16[1,16,1792]{2,1,0:T(8,128)(2,1)S(1)}, bf16[1,16,1792]{2,1,0:T(8,128)(2,1)S(1)}, u32[]{:S(2)}, u32[]{:S(2)}) collective-permute-start(bf16[1,16,1792]{2,1,0:T(8,128)(2,1)S(1)} %get-tuple-element.58), channel_id=1, source_target_pairs={{0,1},{1,0},{2,3},{3,2},{4,5},{5,4},{6,7},{7,6},{8,9},{9,8},{10,11... | collective-permute-start | bytes 172040 | tf_op jit(solution)/shard_map/ppermute | solution.py:432
  29.3 8.9 %collective-permute-start.15 = (bf16[1,16,1792]{2,1,0:T(8,128)(2,1)S(1)}, bf16[1,16,1792]{2,1,0:T(8,128)(2,1)S(1)}, u32[]{:S(2)}, u32[]{:S(2)}) collective-permute-start(bf16[1,16,1792]{2,1,0:T(8,128)(2,1)S(1)} %get-tuple-element.56), channel_id=1, source_target_pairs={{0,1},{1,0},{2,3},{3,2},{4,5},{5,4},{6,7},{7,6},{8,9},{9,8},{10,11... | collective-permute-start | bytes 172040 | tf_op jit(solution)/shard_map/ppermute | solution.py:432
  30.1 1.4 %collective-permute-start.22 = (bf16[1,16,1792]{2,1,0:T(8,128)(2,1)S(1)}, bf16[1,16,1792]{2,1,0:T(8,128)(2,1)S(1)}, u32[]{:S(2)}, u32[]{:S(2)}) collective-permute-start(bf16[1,16,1792]{2,1,0:T(8,128)(2,1)S(1)} %get-tuple-element.64), channel_id=1, source_target_pairs={{0,1},{1,0},{2,3},{3,2},{4,5},{5,4},{6,7},{7,6},{8,9},{9,8},{10,11... | collective-permute-start | bytes 172040 | tf_op jit(solution)/shard_map/ppermute | solution.py:432
  30.4 2.9 %collective-permute-start.24 = (bf16[1,16,1792]{2,1,0:T(8,128)(2,1)S(1)}, bf16[1,16,1792]{2,1,0:T(8,128)(2,1)S(1)}, u32[]{:S(2)}, u32[]{:S(2)}) collective-permute-start(bf16[1,16,1792]{2,1,0:T(8,128)(2,1)S(1)} %get-tuple-element.66), channel_id=1, source_target_pairs={{0,1},{1,0},{2,3},{3,2},{4,5},{5,4},{6,7},{7,6},{8,9},{9,8},{10,11... | collective-permute-start | bytes 172040 | tf_op jit(solution)/shard_map/ppermute | solution.py:432
  30.9 5.4 %collective-permute-start.26 = (bf16[1,16,1792]{2,1,0:T(8,128)(2,1)S(1)}, bf16[1,16,1792]{2,1,0:T(8,128)(2,1)S(1)}, u32[]{:S(2)}, u32[]{:S(2)}) collective-permute-start(bf16[1,16,1792]{2,1,0:T(8,128)(2,1)S(1)} %get-tuple-element.68), channel_id=1, source_target_pairs={{0,1},{1,0},{2,3},{3,2},{4,5},{5,4},{6,7},{7,6},{8,9},{9,8},{10,11... | collective-permute-start | bytes 172040 | tf_op jit(solution)/shard_map/ppermute | solution.py:432
  31.1 5.3 %collective-permute-start.28 = (bf16[1,16,1792]{2,1,0:T(8,128)(2,1)S(1)}, bf16[1,16,1792]{2,1,0:T(8,128)(2,1)S(1)}, u32[]{:S(2)}, u32[]{:S(2)}) collective-permute-start(bf16[1,16,1792]{2,1,0:T(8,128)(2,1)S(1)} %get-tuple-element.70), channel_id=1, source_target_pairs={{0,1},{1,0},{2,3},{3,2},{4,5},{5,4},{6,7},{7,6},{8,9},{9,8},{10,11... | collective-permute-start | bytes 172040 | tf_op jit(solution)/shard_map/ppermute | solution.py:432
  31.5 7.6 %collective-permute-start.17 = (bf16[1,16,1792]{2,1,0:T(8,128)(2,1)S(1)}, bf16[1,16,1792]{2,1,0:T(8,128)(2,1)S(1)}, u32[]{:S(2)}, u32[]{:S(2)}) collective-permute-start(bf16[1,16,1792]{2,1,0:T(8,128)(2,1)S(1)} %add_convert_fusion.6), channel_id=1, source_target_pairs={{15,0},{8,1},{13,2},{10,3},{11,4},{12,5},{9,6},{14,7},{7,8},{0,9},... | collective-permute-start | bytes 172040 | tf_op jit(solution)/shard_map/ppermute | solution.py:404
  33.2 8.4 %collective-permute-start.19 = (bf16[1,16,1792]{2,1,0:T(8,128)(2,1)S(1)}, bf16[1,16,1792]{2,1,0:T(8,128)(2,1)S(1)}, u32[]{:S(2)}, u32[]{:S(2)}) collective-permute-start(bf16[1,16,1792]{2,1,0:T(8,128)(2,1)S(1)} %add_convert_fusion.5), channel_id=1, source_target_pairs={{3,0},{12,1},{1,2},{14,3},{7,4},{8,5},{5,6},{10,7},{11,8},{4,9},{9... | collective-permute-start | bytes 172040 | tf_op jit(solution)/shard_map/ppermute | solution.py:404
  36.3 5.6 %collective-permute-start.21 = (bf16[1,16,1792]{2,1,0:T(8,128)(2,1)S(1)}, bf16[1,16,1792]{2,1,0:T(8,128)(2,1)S(1)}, u32[]{:S(2)}, u32[]{:S(2)}) collective-permute-start(bf16[1,16,1792]{2,1,0:T(8,128)(2,1)S(1)} %add_convert_fusion.4), channel_id=1, source_target_pairs={{11,0},{2,1},{9,2},{0,3},{15,4},{6,5},{13,6},{4,7},{3,8},{10,9},{1... | collective-permute-start | bytes 172040 | tf_op jit(solution)/shard_map/ppermute | solution.py:404
  36.4 5.5 %collective-permute-start.23 = (bf16[1,16,1792]{2,1,0:T(8,128)(2,1)S(1)}, bf16[1,16,1792]{2,1,0:T(8,128)(2,1)S(1)}, u32[]{:S(2)}, u32[]{:S(2)}) collective-permute-start(bf16[1,16,1792]{2,1,0:T(8,128)(2,1)S(1)} %add_convert_fusion.3), channel_id=1, source_target_pairs={{5,0},{14,1},{7,2},{12,3},{1,4},{10,5},{3,6},{8,7},{13,8},{6,9},{1... | collective-permute-start | bytes 172040 | tf_op jit(solution)/shard_map/ppermute | solution.py:404
  38.2 6.0 %collective-permute-start.25 = (bf16[1,16,1792]{2,1,0:T(8,128)(2,1)S(1)}, bf16[1,16,1792]{2,1,0:T(8,128)(2,1)S(1)}, u32[]{:S(2)}, u32[]{:S(2)}) collective-permute-start(bf16[1,16,1792]{2,1,0:T(8,128)(2,1)S(1)} %add_convert_fusion.2), channel_id=1, source_target_pairs={{13,0},{4,1},{15,2},{6,3},{9,4},{0,5},{11,6},{2,7},{5,8},{12,9},{7... | collective-permute-start | bytes 172040 | tf_op jit(solution)/shard_map/ppermute | solution.py:404
  39.1 5.7 %collective-permute-start.27 = (bf16[1,16,1792]{2,1,0:T(8,128)(2,1)S(1)}, bf16[1,16,1792]{2,1,0:T(8,128)(2,1)S(1)}, u32[]{:S(2)}, u32[]{:S(2)}) collective-permute-start(bf16[1,16,1792]{2,1,0:T(8,128)(2,1)S(1)} %add_convert_fusion.1), channel_id=1, source_target_pairs={{7,0},{10,1},{5,2},{8,3},{3,4},{14,5},{1,6},{12,7},{15,8},{2,9},{1... | collective-permute-start | bytes 172040 | tf_op jit(solution)/shard_map/ppermute | solution.py:404
  41.6 5.6 %collective-permute-start.29 = (bf16[1,16,1792]{2,1,0:T(8,128)(2,1)S(1)}, bf16[1,16,1792]{2,1,0:T(8,128)(2,1)S(1)}, u32[]{:S(2)}, u32[]{:S(2)}) collective-permute-start(bf16[1,16,1792]{2,1,0:T(8,128)(2,1)S(1)} %add_convert_fusion), channel_id=1, source_target_pairs={{9,0},{6,1},{11,2},{4,3},{13,4},{2,5},{15,6},{0,7},{1,8},{14,9},{3... | collective-permute-start | bytes 172040 | tf_op jit(solution)/shard_map/ppermute | solution.py:404
  (6 other events, 7.5 us)

commit v11 on v7

--- a/solution.py
+++ b/solution.py
@@ -86,8 +86,10 @@
     kv_hbm,
     hid_hbm,
     gain_hbm,
+    dn_hbm,
     resid_ref,
     out_ref,
+    dn_ref,
     len_ref,
     ids_ref,
     weight_ref,
@@ -114,7 +116,8 @@
             )
         )
     ]
-    for copy in copies:
+    down = pltpu.make_async_copy(dn_hbm.at[0], dn_ref, sems.at[len(copies)])
+    for copy in [*copies, down]:
         copy.start()
     steps, rows, width = q_ref.shape
     length = kv_ref.shape[2]
@@ -162,9 +165,10 @@
     normed = resid * lax.rsqrt(meansq + 1e-06) * gain
     out_ref[:, :width] = normed.astype(BF16)
     out_ref[:, width:] = tail(ids_ref, weight_ref, steps, rows)
-
-
-def attend(cache_len, ids, weights, queries, fresh, kv_cache, hidden_state, norm_gain):
+    down.wait()
+
+
+def attend(cache_len, ids, weights, queries, fresh, kv_cache, hidden_state, norm_gain, down):
     steps, rows, width = queries.shape
     kv = kv_cache.transpose(0, 2, 1)
     gain = norm_gain.reshape(width // LANES, LANES)
@@ -173,9 +177,10 @@
         out_shape=(
             jax.ShapeDtypeStruct((steps * rows, width), F32),
             jax.ShapeDtypeStruct((steps * rows, width + LANES), BF16),
-        ),
-        in_specs=[HBM] * 8,
-        out_specs=(VMEM, VMEM),
+            jax.ShapeDtypeStruct(down.shape[1:], BF16),
+        ),
+        in_specs=[HBM] * 9,
+        out_specs=(VMEM, VMEM, VMEM),
         scratch_shapes=[
             pltpu.SMEM(cache_len.shape, jnp.int32),
             pltpu.SMEM(ids.shape, jnp.int32),
@@ -186,14 +191,14 @@
             pltpu.VMEM(hidden_state.shape, BF16),
             pltpu.VMEM(gain.shape, BF16),
             pltpu.VMEM((steps * rows, width), F32),
-            pltpu.SemaphoreType.DMA((8,)),
+            pltpu.SemaphoreType.DMA((9,)),
         ],
         compiler_params=pltpu.CompilerParams(vmem_limit_bytes=24 * MIB),
         cost_estimate=pl.CostEstimate(
             flops=300_000_000, bytes_accessed=2_000_000, transcendentals=131072
         ),
         name="attend",
-    )(*in_hbm(cache_len, ids, weights, queries, fresh, kv, hidden_state, gain))
+    )(*in_hbm(cache_len, ids, weights, queries, fresh, kv, hidden_state, gain, down))
 
 
 def pack_kernel(steps, chips, own_ref, other_ref, *outs):
@@ -271,47 +276,56 @@
     return jnp.concatenate(parts, axis=0).astype(BF16)
 
 
-def stage_kernel(steps, chips, own_ref, other_ref, gu_hbm, dn_hbm, gu, dn, mix_ref, sems):
-    step = dn.shape[0] // 4
-    pairs = []
+def stage_kernel(which, gu_hbm, out, sems):
+    step = out.shape[0] // 4
+    copies = []
     for i in range(4):
         part = pl.ds(i * step, step)
-        pairs.append((gu_hbm.at[0, 0, part], gu.at[0, part]))
-        pairs.append((gu_hbm.at[0, 1, part], gu.at[1, part]))
-        pairs.append((dn_hbm.at[0, part], dn.at[part]))
-    copies = [pltpu.make_async_copy(a, b, sems.at[i]) for i, (a, b) in enumerate(pairs)]
+        copies.append(pltpu.make_async_copy(gu_hbm.at[0, which, part], out.at[part], sems.at[i]))
     for copy in copies:
         copy.start()
-    mix_ref[...] = mixing(steps, chips, own_ref, other_ref)
     for copy in copies:
         copy.wait()
 
 
-def stage(steps, chips, own, other, gate_up, down):
+def stage(which, gate_up):
+    return pl.pallas_call(
+        functools.partial(stage_kernel, which),
+        out_shape=jax.ShapeDtypeStruct(gate_up.shape[2:], BF16),
+        in_specs=[HBM],
+        out_specs=VMEM,
+        scratch_shapes=[pltpu.SemaphoreType.DMA((4,))],
+        compiler_params=pltpu.CompilerParams(vmem_limit_bytes=16 * MIB),
+        cost_estimate=pl.CostEstimate(flops=0, bytes_accessed=8_000_000, transcendentals=0),
+        name="stage",
+    )(*in_hbm(gate_up))
+
+
+def mix_kernel(steps, chips, own_ref, other_ref, mix_ref):
+    mix_ref[...] = mixing(steps, chips, own_ref, other_ref)
+
+
+def mixer(steps, chips, own, other):
     lines = PIECES * 2 * steps * CAP
+    shape = (PARTS * PIECES * 2 * own.shape[0], chips // 2 * lines)
     return pl.pallas_call(
-        functools.partial(stage_kernel, steps, chips),
-        out_shape=(
-            jax.ShapeDtypeStruct(gate_up.shape[1:], BF16),
-            jax.ShapeDtypeStruct(down.shape[1:], BF16),
-            jax.ShapeDtypeStruct((PARTS * PIECES * 2 * own.shape[0], chips // 2 * lines), BF16),
-        ),
-        in_specs=[VMEM, VMEM, HBM, HBM],
-        out_specs=(VMEM,) * 3,
-        scratch_shapes=[pltpu.SemaphoreType.DMA((12,))],
+        functools.partial(mix_kernel, steps, chips),
+        out_shape=jax.ShapeDtypeStruct(shape, BF16),
+        in_specs=[VMEM, VMEM],
+        out_specs=VMEM,
         compiler_params=pltpu.CompilerParams(vmem_limit_bytes=24 * MIB),
         cost_estimate=pl.CostEstimate(
-            flops=10_000_000, bytes_accessed=22_000_000, transcendentals=0
-        ),
-        name="stage",
-    )(own, other, *in_hbm(gate_up, down))
+            flops=10_000_000, bytes_accessed=1_000_000, transcendentals=0
+        ),
+        name="mixer",
+    )(own, other)
 
 
 def expert_kernel(turns, *refs):
     own_refs, other_refs = refs[:turns], refs[turns : 2 * turns]
-    gu, dn = refs[2 * turns : 2 * turns + 2]
-    mine_refs = refs[2 * turns + 2 : 3 * turns + 2]
-    theirs_refs = refs[3 * turns + 2 :]
+    w_gate, w_upper, w_down = refs[2 * turns : 2 * turns + 3]
+    mine_refs = refs[2 * turns + 3 : 3 * turns + 3]
+    theirs_refs = refs[3 * turns + 3 :]
     lines, piece = own_refs[0].shape
     per = lines // PIECES
     half = turns * per
@@ -327,13 +341,13 @@
     for k in range(PIECES):
         x = jnp.concatenate([side[k * half : (k + 1) * half] for side in sides], axis=0)
         cols = pl.ds(k * piece, piece)
-        g, u = nt_dot(x, gu[0, :, cols]), nt_dot(x, gu[1, :, cols])
+        g, u = nt_dot(x, w_gate[:, cols]), nt_dot(x, w_upper[:, cols])
         gate, upper = (g, u) if k == 0 else (gate + g, upper + u)
     act = (gate / (1.0 + jnp.exp(-gate)) * upper).astype(BF16)
     mine = []
     theirs = []
     for k in range(PIECES):
-        part = dot(act, dn[:, k * piece : (k + 1) * piece]).astype(BF16)
+        part = dot(act, w_down[:, k * piece : (k + 1) * piece]).astype(BF16)
         mine.append(part[:half])
         theirs.append(part[half:])
     back = one_hot(row == col // per % turns * lines + col // half * per + col % per)
@@ -343,20 +357,20 @@
             ref[...] = out[t * lines : (t + 1) * lines]
 
 
-def experts(own, other, gu, dn):
+def experts(own, other, gate, upper, down):
     turns = len(own)
     shape = jax.ShapeDtypeStruct(own[0].shape, BF16)
     results = pl.pallas_call(
         functools.partial(expert_kernel, turns),
         out_shape=[shape] * (2 * turns),
-        in_specs=[VMEM] * (2 * turns + 2),
+        in_specs=[VMEM] * (2 * turns + 3),
         out_specs=[VMEM] * (2 * turns),
         compiler_params=pltpu.CompilerParams(vmem_limit_bytes=32 * MIB),
         cost_estimate=pl.CostEstimate(
             flops=800_000_000, bytes_accessed=12_000_000, transcendentals=16384
         ),
         name="experts",
-    )(*own, *other, gu, dn)
+    )(*own, *other, gate, upper, down)
     return results[:turns], results[turns:]
 
 
@@ -442,18 +456,22 @@
 
     ids = expert_ids.transpose(2, 0, 1)
     weights = route_weight.transpose(2, 0, 1)
-    resid, normed = attend(
-        cache_len, ids, weights, queries, fresh, kv_cache, hidden_state, norm_gain
+    resid, normed, w_down = attend(
+        cache_len, ids, weights, queries, fresh, kv_cache, hidden_state, norm_gain, down
     )
     normed_other = swap(normed)
+    w_gate = stage(0, gate_up)
+    w_gate, normed_other = lax.optimization_barrier((w_gate, normed_other))
     sent = pack(steps, chips, normed, normed_other)
     own = [send(sent[t], t) for t in range(turns)]
-    gu, dn, mix = stage(steps, chips, normed, normed_other, gate_up, down)
-    own[0], gu, dn = lax.optimization_barrier((own[0], gu, dn))
+    w_upper = stage(1, gate_up)
+    mix = mixer(steps, chips, normed, normed_other)
+    own[0], w_upper = lax.optimization_barrier((own[0], w_upper))
     other = [swap(x) for x in own]
     summed = []
     for t in range(0, turns, TOGETHER):
-        mine, theirs = experts(own[t : t + TOGETHER], other[t : t + TOGETHER], gu, dn)
+        now = slice(t, t + TOGETHER)
+        mine, theirs = experts(own[now], other[now], w_gate, w_upper, w_down)
         summed += [
             (a.astype(F32) + swap(b).astype(F32)).astype(BF16) for a, b in zip(mine, theirs)
         ]

time: 41.6 us -> 42.1 us (1.012)
  starting transfers between devices: 14.3 us -> 16.8 us
  waiting for transfers between devices: 15.4 us -> 13 us
    ppermute x10, starting transfers between devices: 2.19 us -> 3.98 us  [swap(): return lax.ppermute(x, 'afd', cores)]
    ppermute x10, waiting for transfers between devices: 3.91 us -> 2.59 us  [swap(): return lax.ppermute(x, 'afd', cores)]
    ppermute x4, waiting for transfers between devices: 8.1 us -> 7.23 us  [send_back(): return lax.ppermute(x, 'afd', [(j, i) for i, j in route(t)])]
    ppermute x4, starting transfers between devices: 4.58 us -> 5.34 us  [send_back(): return lax.ppermute(x, 'afd', [(j, i) for i, j in route(t)])]
    pallas_call x1 -> x3, Pallas kernels: 4.25 us -> 4.37 us  [the longest x2 4.08 us: stage(): pl.pallas_call(functools.partial(stage_kernel, which), out_shape=jax.Shap...]
  transfers between devices with their start and end apart: 18 -> 18, of which waited for: 11 -> 8; matrix products, arithmetic and copies ran while one was open for 0% -> 0% of each run, Pallas kernels for 10% -> 10%
where the time goes in v11:
time: 42.1 us; the launch traced here: 41.9 us
  starting transfers between devices  16.8 us (40%)
  waiting for transfers between devices  13 us (31%)
  Pallas kernels  11.9 us (28%)
    ppermute x4, starting transfers between devices, send(): return lax.ppermute(x, 'afd', route(t))  7.5 us
    ppermute x4, waiting for transfers between devices, send_back(): return lax.ppermute(x, 'afd', [(j, i) for i, j in route(t)])  7.23 us
    ppermute x4, starting transfers between devices, send_back(): return lax.ppermute(x, 'afd', [(j, i) for i, j in route(t)])  5.34 us
    pallas_call x2, Pallas kernels, stage(): pl.pallas_call(functools.partial(stage_kernel, which), out_shape=jax.Shap...  4.08 us
    ppermute x10, starting transfers between devices, swap(): return lax.ppermute(x, 'afd', cores)  3.98 us
    pallas_call x1, Pallas kernels, experts(): pl.pallas_call(functools.partial(expert_kernel, turns), out_shape=[shape]...  3.62 us
    ppermute x4, waiting for transfers between devices, send(): return lax.ppermute(x, 'afd', route(t))  3.16 us
    ppermute x10, waiting for transfers between devices, swap(): return lax.ppermute(x, 'afd', cores)  2.59 us
  transfers between devices with their start and end apart: 18, of which 8 were waited for; matrix products, arithmetic and copies ran while one was open for 0% of the time, Pallas kernels for 10%

profile of v11, /device:TPU:0, one launch (start us, length us, event | category | flops | bytes accessed | tf_op | source)
XLA Modules:
  0.0 41.9 jit_solution(1498638053379487705)
XLA Ops:
  0.0 2.4 %attend.1 = (f32[8,7168]{1,0:T(8,128)S(1)}, bf16[8,7296]{1,0:T(8,128)(2,1)S(1)}, bf16[256,7168]{1,0:T(8,128)(2,1)S(1)}) custom-call(s32[4]{0:T(128)} %len_hbm.1, s32[3,2,4]{2,1,0:T(2,128)} %bitcast.6, f32[3,2,4]{2,1,0:T(2,128)} %bitcast.7, bf16[2,4,7168]{2,1,0:T(4,128)(2,1)} %q_hbm.1, bf16[2,4,448]{2,1,0:T(4,128)(2,1)} %fresh_hbm.1, ...), custom_call_target="tpu_custom_call" | custom-call | flops 300000000 | bytes 2000000 | tf_op jit(solution)/shard_map/attend/pallas_call | solution.py:175
  2.4 0.5 %collective-permute-start = (bf16[8,7296]{1,0:T(8,128)(2,1)S(1)}, bf16[8,7296]{1,0:T(8,128)(2,1)S(1)}, u32[]{:S(2)}, u32[]{:S(2)}) collective-permute-start(bf16[8,7296]{1,0:T(8,128)(2,1)S(1)} %get-tuple-element.26.own_ref), channel_id=1, source_target_pairs={{0,1},{1,0},{2,3},{3,2},{4,5},{5,4},{6,7},{7,6},{8,9},{9,8},{10,11... | collective-permute-start | bytes 350216 | tf_op jit(solution)/shard_map/ppermute | solution.py:446
  2.9 2.0 %stage.2.refs_8_ = bf16[256,7168]{1,0:T(8,128)(2,1)S(1)} custom-call(bf16[1,2,256,7168]{3,2,1,0:T(8,128)(2,1)} %gu_hbm.3), custom_call_target="tpu_custom_call" | custom-call | bytes 8000000 | tf_op jit(solution)/shard_map/stage/pallas_call | solution.py:292
  5.0 0.5 %pack.1 = (bf16[32,1792]{1,0:T(8,128)(2,1)S(1)}, bf16[32,1792]{1,0:T(8,128)(2,1)S(1)}, bf16[32,1792]{1,0:T(8,128)(2,1)S(1)}, bf16[32,1792]{1,0:T(8,128)(2,1)S(1)}) custom-call(bf16[8,7296]{1,0:T(8,128)(2,1)S(1)} %get-tuple-element.26.own_ref, bf16[8,7296]{1,0:T(8,128)(2,1)S(1)} %collective-permute-done.other_ref), custom_call_target="tpu_custom_call" | custom-call | flops 50000000 | bytes 2000000 | tf_op jit(solution)/shard_map/pack/pallas_call | solution.py:239
  5.6 4.8 %collective-permute-start.2 = (bf16[32,1792]{1,0:T(8,128)(2,1)S(1)}, bf16[32,1792]{1,0:T(8,128)(2,1)S(1)}, u32[]{:S(2)}, u32[]{:S(2)}) collective-permute-start(bf16[32,1792]{1,0:T(8,128)(2,1)S(1)} %get-tuple-element.31), channel_id=1, source_target_pairs={{0,5},{1,10},{2,7},{3,8},{4,1},{5,14},{6,3},{7,12},{8,13},{9,2},{1... | collective-permute-start | bytes 344072 | tf_op jit(solution)/shard_map/ppermute | solution.py:452
  10.6 2.4 %collective-permute-start.4 = (bf16[32,1792]{1,0:T(8,128)(2,1)S(1)}, bf16[32,1792]{1,0:T(8,128)(2,1)S(1)}, u32[]{:S(2)}, u32[]{:S(2)}) collective-permute-start(bf16[32,1792]{1,0:T(8,128)(2,1)S(1)} %get-tuple-element.33), channel_id=1, source_target_pairs={{0,13},{1,2},{2,15},{3,0},{4,9},{5,6},{6,11},{7,4},{8,5},{9,10},{1... | collective-permute-start | bytes 344072 | tf_op jit(solution)/shard_map/ppermute | solution.py:452
  13.0 2.0 %stage.3.refs_9_ = bf16[256,7168]{1,0:T(8,128)(2,1)S(1)} custom-call(bf16[1,2,256,7168]{3,2,1,0:T(8,128)(2,1)} %gu_hbm.3), custom_call_target="tpu_custom_call" | custom-call | bytes 8000000 | tf_op jit(solution)/shard_map/stage/pallas_call | solution.py:292
  15.1 2.6 %collective-permute-done.2.refs_1_ = bf16[32,1792]{1,0:T(8,128)(2,1)S(1)} collective-permute-done((bf16[32,1792]{1,0:T(8,128)(2,1)S(1)}, bf16[32,1792]{1,0:T(8,128)(2,1)S(1)}, u32[]{:S(2)}, u32[]{:S(2)}) %collective-permute-start.2) | collective-permute-done | bytes 114720 | tf_op jit(solution)/shard_map/ppermute | solution.py:452
  17.7 0.6 %collective-permute-done.3.refs_2_ = bf16[32,1792]{1,0:T(8,128)(2,1)S(1)} collective-permute-done((bf16[32,1792]{1,0:T(8,128)(2,1)S(1)}, bf16[32,1792]{1,0:T(8,128)(2,1)S(1)}, u32[]{:S(2)}, u32[]{:S(2)}) %collective-permute-start.3) | collective-permute-done | bytes 114720 | tf_op jit(solution)/shard_map/ppermute | solution.py:452
  18.3 1.6 %collective-permute-start.7 = (bf16[32,1792]{1,0:T(8,128)(2,1)S(1)}, bf16[32,1792]{1,0:T(8,128)(2,1)S(1)}, u32[]{:S(2)}, u32[]{:S(2)}) collective-permute-start(bf16[32,1792]{1,0:T(8,128)(2,1)S(1)} %collective-permute-done.3.refs_2_), channel_id=1, source_target_pairs={{0,1},{1,0},{2,3},{3,2},{4,5},{5,4},{6,7},{7,6},{8,9},{9,8},{10,11... | collective-permute-start | bytes 344072 | tf_op jit(solution)/shard_map/ppermute | solution.py:446
  19.9 0.9 %collective-permute-done.7.refs_6_ = bf16[32,1792]{1,0:T(8,128)(2,1)S(1)} collective-permute-done((bf16[32,1792]{1,0:T(8,128)(2,1)S(1)}, bf16[32,1792]{1,0:T(8,128)(2,1)S(1)}, u32[]{:S(2)}, u32[]{:S(2)}) %collective-permute-start.7) | collective-permute-done | bytes 114720 | tf_op jit(solution)/shard_map/ppermute | solution.py:446
  20.9 0.4 collective-permute-done.8.refs_7_
  21.2 3.6 %experts.1 = (bf16[32,1792]{1,0:T(8,128)(2,1)S(1)}, bf16[32,1792]{1,0:T(8,128)(2,1)S(1)}, bf16[32,1792]{1,0:T(8,128)(2,1)S(1)}, bf16[32,1792]{1,0:T(8,128)(2,1)S...) custom-call(bf16[32,1792]{1,0:T(8,128)(2,1)S(1)} %collective-permute, ...), custom_call_target="tpu_custom_call" | custom-call | flops 800000000 | bytes 12000000 | tf_op jit(solution)/shard_map/experts/pallas_call | solution.py:363
  25.1 0.4 collective-permute-start.11
  25.6 0.4 collective-permute-start.15
  26.3 2.5 %collective-permute-start.10 = (bf16[32,1792]{1,0:T(8,128)(2,1)S(1)}, bf16[32,1792]{1,0:T(8,128)(2,1)S(1)}, u32[]{:S(2)}, u32[]{:S(2)}) collective-permute-start(bf16[32,1792]{1,0:T(8,128)(2,1)S(1)} %add_convert_fusion.3), channel_id=1, source_target_pairs={{1,0},{14,1},{3,2},{12,3},{5,4},{10,5},{7,6},{8,7},{9,8},{6,9},{11... | collective-permute-start | bytes 344072 | tf_op jit(solution)/shard_map/ppermute | solution.py:455
  28.9 0.4 %collective-permute-start.12 = (bf16[32,1792]{1,0:T(8,128)(2,1)S(1)}, bf16[32,1792]{1,0:T(8,128)(2,1)S(1)}, u32[]{:S(2)}, u32[]{:S(2)}) collective-permute-start(bf16[32,1792]{1,0:T(8,128)(2,1)S(1)} %add_convert_fusion.2), channel_id=1, source_target_pairs={{5,0},{10,1},{7,2},{8,3},{1,4},{14,5},{3,6},{12,7},{13,8},{2,9},{1... | collective-permute-start | bytes 344072 | tf_op jit(solution)/shard_map/ppermute | solution.py:455
  29.3 2.3 %collective-permute-start.14 = (bf16[32,1792]{1,0:T(8,128)(2,1)S(1)}, bf16[32,1792]{1,0:T(8,128)(2,1)S(1)}, u32[]{:S(2)}, u32[]{:S(2)}) collective-permute-start(bf16[32,1792]{1,0:T(8,128)(2,1)S(1)} %add_convert_fusion.1), channel_id=1, source_target_pairs={{9,0},{6,1},{11,2},{4,3},{13,4},{2,5},{15,6},{0,7},{1,8},{14,9},{3... | collective-permute-start | bytes 344072 | tf_op jit(solution)/shard_map/ppermute | solution.py:455
  32.1 2.5 %collective-permute-done.12.refs_1_ = bf16[32,1792]{1,0:T(8,128)(2,1)S(1)} collective-permute-done((bf16[32,1792]{1,0:T(8,128)(2,1)S(1)}, bf16[32,1792]{1,0:T(8,128)(2,1)S(1)}, u32[]{:S(2)}, u32[]{:S(2)}) %collective-permute-start.12) | collective-permute-done | bytes 114720 | tf_op jit(solution)/shard_map/ppermute | solution.py:455
  34.5 4.8 %collective-permute-done.14.refs_2_ = bf16[32,1792]{1,0:T(8,128)(2,1)S(1)} collective-permute-done((bf16[32,1792]{1,0:T(8,128)(2,1)S(1)}, bf16[32,1792]{1,0:T(8,128)(2,1)S(1)}, u32[]{:S(2)}, u32[]{:S(2)}) %collective-permute-start.14) | collective-permute-done | bytes 114720 | tf_op jit(solution)/shard_map/ppermute | solution.py:455
  39.3 0.3 combine.1
  39.6 0.7 %collective-permute-start.17 = (bf16[8,7168]{1,0:T(8,128)(2,1)S(1)}, bf16[8,7168]{1,0:T(8,128)(2,1)S(1)}, u32[]{:S(2)}, u32[]{:S(2)}) collective-permute-start(bf16[8,7168]{1,0:T(8,128)(2,1)S(1)} %get-tuple-element.46), channel_id=1, source_target_pairs={{0,1},{1,0},{2,3},{3,2},{4,5},{5,4},{6,7},{7,6},{8,9},{9,8},{10,11... | collective-permute-start | bytes 344072 | tf_op jit(solution)/shard_map/ppermute | solution.py:446
  40.3 1.0 %collective-permute-done.17.other_ref = bf16[8,7168]{1,0:T(8,128)(2,1)S(1)} collective-permute-done((bf16[8,7168]{1,0:T(8,128)(2,1)S(1)}, bf16[8,7168]{1,0:T(8,128)(2,1)S(1)}, u32[]{:S(2)}, u32[]{:S(2)}) %collective-permute-start.17) | collective-permute-done | bytes 114720 | tf_op jit(solution)/shard_map/ppermute | solution.py:446
  41.2 0.7 %finish.1 = bf16[2,4,7168]{2,1,0:T(4,128)(2,1)} custom-call(f32[8,7168]{1,0:T(8,128)S(1)} %get-tuple-element.45.kept_ref, bf16[8,7168]{1,0:T(8,128)(2,1)S(1)} %collective-permute-done.17.other_ref), custom_call_target="tpu_custom_call" | custom-call | flops 100000 | bytes 500000 | tf_op jit(solution)/shard_map/finish/pallas_call | solution.py:416
  (24 shorter events, 1.6 us)
Async XLA Ops:
  2.4 2.6 %collective-permute-start = (bf16[8,7296]{1,0:T(8,128)(2,1)S(1)}, bf16[8,7296]{1,0:T(8,128)(2,1)S(1)}, u32[]{:S(2)}, u32[]{:S(2)}) collective-permute-start(bf16[8,7296]{1,0:T(8,128)(2,1)S(1)} %get-tuple-element.26.own_ref), channel_id=1, source_target_pairs={{0,1},{1,0},{2,3},{3,2},{4,5},{5,4},{6,7},{7,6},{8,9},{9,8},{10,11... | collective-permute-start | bytes 350216 | tf_op jit(solution)/shard_map/ppermute | solution.py:446
  5.5 9.6 %collective-permute-start.1 = (bf16[32,1792]{1,0:T(8,128)(2,1)S(1)}, bf16[32,1792]{1,0:T(8,128)(2,1)S(1)}, u32[]{:S(2)}, u32[]{:S(2)}) collective-permute-start(bf16[32,1792]{1,0:T(8,128)(2,1)S(1)} %get-tuple-element.29), channel_id=1, source_target_pairs={{0,1},{1,14},{2,3},{3,12},{4,5},{5,10},{6,7},{7,8},{8,9},{9,6},{10... | collective-permute-start | bytes 344072 | tf_op jit(solution)/shard_map/ppermute | solution.py:452
  5.6 12.1 %collective-permute-start.2 = (bf16[32,1792]{1,0:T(8,128)(2,1)S(1)}, bf16[32,1792]{1,0:T(8,128)(2,1)S(1)}, u32[]{:S(2)}, u32[]{:S(2)}) collective-permute-start(bf16[32,1792]{1,0:T(8,128)(2,1)S(1)} %get-tuple-element.31), channel_id=1, source_target_pairs={{0,5},{1,10},{2,7},{3,8},{4,1},{5,14},{6,3},{7,12},{8,13},{9,2},{1... | collective-permute-start | bytes 344072 | tf_op jit(solution)/shard_map/ppermute | solution.py:452
  10.4 7.9 %collective-permute-start.3 = (bf16[32,1792]{1,0:T(8,128)(2,1)S(1)}, bf16[32,1792]{1,0:T(8,128)(2,1)S(1)}, u32[]{:S(2)}, u32[]{:S(2)}) collective-permute-start(bf16[32,1792]{1,0:T(8,128)(2,1)S(1)} %get-tuple-element.32), channel_id=1, source_target_pairs={{0,9},{1,6},{2,11},{3,4},{4,13},{5,2},{6,15},{7,0},{8,1},{9,14},{1... | collective-permute-start | bytes 344072 | tf_op jit(solution)/shard_map/ppermute | solution.py:452
  10.6 9.3 %collective-permute-start.4 = (bf16[32,1792]{1,0:T(8,128)(2,1)S(1)}, bf16[32,1792]{1,0:T(8,128)(2,1)S(1)}, u32[]{:S(2)}, u32[]{:S(2)}) collective-permute-start(bf16[32,1792]{1,0:T(8,128)(2,1)S(1)} %get-tuple-element.33), channel_id=1, source_target_pairs={{0,13},{1,2},{2,15},{3,0},{4,9},{5,6},{6,11},{7,4},{8,5},{9,10},{1... | collective-permute-start | bytes 344072 | tf_op jit(solution)/shard_map/ppermute | solution.py:452
  15.0 4.9 %collective-permute-start.5 = (bf16[32,1792]{1,0:T(8,128)(2,1)S(1)}, bf16[32,1792]{1,0:T(8,128)(2,1)S(1)}, u32[]{:S(2)}, u32[]{:S(2)}) collective-permute-start(bf16[32,1792]{1,0:T(8,128)(2,1)S(1)} %collective-permute-done.1.refs_0_), channel_id=1, source_target_pairs={{0,1},{1,0},{2,3},{3,2},{4,5},{5,4},{6,7},{7,6},{8,9},{9,8},{10,11... | collective-permute-start | bytes 344072 | tf_op jit(solution)/shard_map/ppermute | solution.py:446
  17.7 2.2 %collective-permute-start.6 = (bf16[32,1792]{1,0:T(8,128)(2,1)S(1)}, bf16[32,1792]{1,0:T(8,128)(2,1)S(1)}, u32[]{:S(2)}, u32[]{:S(2)}) collective-permute-start(bf16[32,1792]{1,0:T(8,128)(2,1)S(1)} %collective-permute-done.2.refs_1_), channel_id=1, source_target_pairs={{0,1},{1,0},{2,3},{3,2},{4,5},{5,4},{6,7},{7,6},{8,9},{9,8},{10,11... | collective-permute-start | bytes 344072 | tf_op jit(solution)/shard_map/ppermute | solution.py:446
  18.3 2.6 %collective-permute-start.7 = (bf16[32,1792]{1,0:T(8,128)(2,1)S(1)}, bf16[32,1792]{1,0:T(8,128)(2,1)S(1)}, u32[]{:S(2)}, u32[]{:S(2)}) collective-permute-start(bf16[32,1792]{1,0:T(8,128)(2,1)S(1)} %collective-permute-done.3.refs_2_), channel_id=1, source_target_pairs={{0,1},{1,0},{2,3},{3,2},{4,5},{5,4},{6,7},{7,6},{8,9},{9,8},{10,11... | collective-permute-start | bytes 344072 | tf_op jit(solution)/shard_map/ppermute | solution.py:446
  19.9 1.3 %collective-permute-start.8 = (bf16[32,1792]{1,0:T(8,128)(2,1)S(1)}, bf16[32,1792]{1,0:T(8,128)(2,1)S(1)}, u32[]{:S(2)}, u32[]{:S(2)}) collective-permute-start(bf16[32,1792]{1,0:T(8,128)(2,1)S(1)} %collective-permute-done.4.refs_3_), channel_id=1, source_target_pairs={{0,1},{1,0},{2,3},{3,2},{4,5},{5,4},{6,7},{7,6},{8,9},{9,8},{10,11... | collective-permute-start | bytes 344072 | tf_op jit(solution)/shard_map/ppermute | solution.py:446
  24.9 1.4 %collective-permute-start.9 = (bf16[32,1792]{1,0:T(8,128)(2,1)S(1)}, bf16[32,1792]{1,0:T(8,128)(2,1)S(1)}, u32[]{:S(2)}, u32[]{:S(2)}) collective-permute-start(bf16[32,1792]{1,0:T(8,128)(2,1)S(1)} %get-tuple-element.38), channel_id=1, source_target_pairs={{0,1},{1,0},{2,3},{3,2},{4,5},{5,4},{6,7},{7,6},{8,9},{9,8},{10,11... | collective-permute-start | bytes 344072 | tf_op jit(solution)/shard_map/ppermute | solution.py:446
  25.1 3.7 %collective-permute-start.11 = (bf16[32,1792]{1,0:T(8,128)(2,1)S(1)}, bf16[32,1792]{1,0:T(8,128)(2,1)S(1)}, u32[]{:S(2)}, u32[]{:S(2)}) collective-permute-start(bf16[32,1792]{1,0:T(8,128)(2,1)S(1)} %get-tuple-element.40), channel_id=1, source_target_pairs={{0,1},{1,0},{2,3},{3,2},{4,5},{5,4},{6,7},{7,6},{8,9},{9,8},{10,11... | collective-permute-start | bytes 344072 | tf_op jit(solution)/shard_map/ppermute | solution.py:446
  25.4 3.8 %collective-permute-start.13 = (bf16[32,1792]{1,0:T(8,128)(2,1)S(1)}, bf16[32,1792]{1,0:T(8,128)(2,1)S(1)}, u32[]{:S(2)}, u32[]{:S(2)}) collective-permute-start(bf16[32,1792]{1,0:T(8,128)(2,1)S(1)} %get-tuple-element.42), channel_id=1, source_target_pairs={{0,1},{1,0},{2,3},{3,2},{4,5},{5,4},{6,7},{7,6},{8,9},{9,8},{10,11... | collective-permute-start | bytes 344072 | tf_op jit(solution)/shard_map/ppermute | solution.py:446
  25.6 6.1 %collective-permute-start.15 = (bf16[32,1792]{1,0:T(8,128)(2,1)S(1)}, bf16[32,1792]{1,0:T(8,128)(2,1)S(1)}, u32[]{:S(2)}, u32[]{:S(2)}) collective-permute-start(bf16[32,1792]{1,0:T(8,128)(2,1)S(1)} %get-tuple-element.44), channel_id=1, source_target_pairs={{0,1},{1,0},{2,3},{3,2},{4,5},{5,4},{6,7},{7,6},{8,9},{9,8},{10,11... | collective-permute-start | bytes 344072 | tf_op jit(solution)/shard_map/ppermute | solution.py:446
  26.3 5.8 %collective-permute-start.10 = (bf16[32,1792]{1,0:T(8,128)(2,1)S(1)}, bf16[32,1792]{1,0:T(8,128)(2,1)S(1)}, u32[]{:S(2)}, u32[]{:S(2)}) collective-permute-start(bf16[32,1792]{1,0:T(8,128)(2,1)S(1)} %add_convert_fusion.3), channel_id=1, source_target_pairs={{1,0},{14,1},{3,2},{12,3},{5,4},{10,5},{7,6},{8,7},{9,8},{6,9},{11... | collective-permute-start | bytes 344072 | tf_op jit(solution)/shard_map/ppermute | solution.py:455
  28.9 5.7 %collective-permute-start.12 = (bf16[32,1792]{1,0:T(8,128)(2,1)S(1)}, bf16[32,1792]{1,0:T(8,128)(2,1)S(1)}, u32[]{:S(2)}, u32[]{:S(2)}) collective-permute-start(bf16[32,1792]{1,0:T(8,128)(2,1)S(1)} %add_convert_fusion.2), channel_id=1, source_target_pairs={{5,0},{10,1},{7,2},{8,3},{1,4},{14,5},{3,6},{12,7},{13,8},{2,9},{1... | collective-permute-start | bytes 344072 | tf_op jit(solution)/shard_map/ppermute | solution.py:455
  29.3 10.0 %collective-permute-start.14 = (bf16[32,1792]{1,0:T(8,128)(2,1)S(1)}, bf16[32,1792]{1,0:T(8,128)(2,1)S(1)}, u32[]{:S(2)}, u32[]{:S(2)}) collective-permute-start(bf16[32,1792]{1,0:T(8,128)(2,1)S(1)} %add_convert_fusion.1), channel_id=1, source_target_pairs={{9,0},{6,1},{11,2},{4,3},{13,4},{2,5},{15,6},{0,7},{1,8},{14,9},{3... | collective-permute-start | bytes 344072 | tf_op jit(solution)/shard_map/ppermute | solution.py:455
  31.7 7.6 %collective-permute-start.16 = (bf16[32,1792]{1,0:T(8,128)(2,1)S(1)}, bf16[32,1792]{1,0:T(8,128)(2,1)S(1)}, u32[]{:S(2)}, u32[]{:S(2)}) collective-permute-start(bf16[32,1792]{1,0:T(8,128)(2,1)S(1)} %add_convert_fusion), channel_id=1, source_target_pairs={{13,0},{2,1},{15,2},{0,3},{9,4},{6,5},{11,6},{4,7},{5,8},{10,9},{7... | collective-permute-start | bytes 344072 | tf_op jit(solution)/shard_map/ppermute | solution.py:455
  39.6 1.6 %collective-permute-start.17 = (bf16[8,7168]{1,0:T(8,128)(2,1)S(1)}, bf16[8,7168]{1,0:T(8,128)(2,1)S(1)}, u32[]{:S(2)}, u32[]{:S(2)}) collective-permute-start(bf16[8,7168]{1,0:T(8,128)(2,1)S(1)} %get-tuple-element.46), channel_id=1, source_target_pairs={{0,1},{1,0},{2,3},{3,2},{4,5},{5,4},{6,7},{7,6},{8,9},{9,8},{10,11... | collective-permute-start | bytes 344072 | tf_op jit(solution)/shard_map/ppermute | solution.py:446

commit v12 on v11

--- a/solution.py
+++ b/solution.py
@@ -19,7 +19,7 @@
 MIB = 1 << 20
 VMEM = pl.BlockSpec(memory_space=pltpu.VMEM)
 HBM = pl.BlockSpec(memory_space=pltpu.HBM)
-TOGETHER = 4
+TOGETHER = 2
 
 
 def iota(shape, dim):
@@ -322,10 +322,9 @@
 
 
 def expert_kernel(turns, *refs):
-    own_refs, other_refs = refs[:turns], refs[turns : 2 * turns]
-    w_gate, w_upper, w_down = refs[2 * turns : 2 * turns + 3]
-    mine_refs = refs[2 * turns + 3 : 3 * turns + 3]
-    theirs_refs = refs[3 * turns + 3 :]
+    own_refs, other_refs = refs[:turns], refs[turns : -2 * turns - 3]
+    w_gate, w_upper, w_down = refs[-2 * turns - 3 : -2 * turns]
+    mine_refs, theirs_refs = refs[-2 * turns : -turns], refs[-turns:]
     lines, piece = own_refs[0].shape
     per = lines // PIECES
     half = turns * per
@@ -363,7 +362,7 @@
     results = pl.pallas_call(
         functools.partial(expert_kernel, turns),
         out_shape=[shape] * (2 * turns),
-        in_specs=[VMEM] * (2 * turns + 3),
+        in_specs=[VMEM] * (turns + len(other) + 3),
         out_specs=[VMEM] * (2 * turns),
         compiler_params=pltpu.CompilerParams(vmem_limit_bytes=32 * MIB),
         cost_estimate=pl.CostEstimate(
@@ -466,16 +465,20 @@
     own = [send(sent[t], t) for t in range(turns)]
     w_upper = stage(1, gate_up)
     mix = mixer(steps, chips, normed, normed_other)
-    own[0], w_upper = lax.optimization_barrier((own[0], w_upper))
-    other = [swap(x) for x in own]
-    summed = []
-    for t in range(0, turns, TOGETHER):
-        now = slice(t, t + TOGETHER)
-        mine, theirs = experts(own[now], other[now], w_gate, w_upper, w_down)
-        summed += [
+    own[:TOGETHER], w_upper = lax.optimization_barrier((own[:TOGETHER], w_upper))
+    backs = []
+    for first in range(0, turns, TOGETHER):
+        now = own[first : first + TOGETHER]
+        cut = 1 if first else 2
+        other = [jnp.concatenate([swap(part) for part in jnp.split(x, cut)]) for x in now]
+        mine, theirs = experts(now, other, w_gate, w_upper, w_down)
+        theirs, backs = lax.optimization_barrier((theirs, backs))
+        rest = own[first + TOGETHER :]
+        mine, own[first + TOGETHER :] = lax.optimization_barrier((mine, rest))
+        summed = [
             (a.astype(F32) + swap(b).astype(F32)).astype(BF16) for a, b in zip(mine, theirs)
         ]
-    backs = [send_back(summed[t], t) for t in range(turns)]
+        backs = backs + [send_back(x, first + i) for i, x in enumerate(summed)]
     kept, given = combine(mix, resid, backs)
     return finish(queries.shape, kept, swap(given))
 

time: 42.1 us -> 45.2 us (1.074)
  starting transfers between devices: 16.8 us -> 20 us
  waiting for transfers between devices: 13 us -> 9.8 us
  Pallas kernels: 11.9 us -> 15 us
    pallas_call x1 -> x2, Pallas kernels: 3.62 us -> 6.75 us  [experts(): pl.pallas_call(functools.partial(expert_kernel, turns), out_shape=[shape]...]
    ppermute x4, starting transfers between devices: 5.34 us -> 8.16 us  [send_back(): return lax.ppermute(x, 'afd', [(j, i) for i, j in route(t)])]
    ppermute x4, waiting for transfers between devices: 7.23 us -> 4.81 us  [send_back(): return lax.ppermute(x, 'afd', [(j, i) for i, j in route(t)])]
    ppermute x4, waiting for transfers between devices: 3.16 us -> 1.38 us  [send(): return lax.ppermute(x, 'afd', route(t))]
    ppermute x10 -> x12, waiting for transfers between devices: 2.59 us -> 3.61 us  [swap(): return lax.ppermute(x, 'afd', cores)]
    ppermute x10 -> x12, starting transfers between devices: 3.98 us -> 4.27 us  [swap(): return lax.ppermute(x, 'afd', cores)]
  transfers between devices with their start and end apart: 18 -> 20, of which waited for: 8 -> 9; matrix products, arithmetic and copies ran while one was open for 0% -> 0% of each run, Pallas kernels for 10% -> 25%
where the time goes in v12:
time: 45.2 us; the launch traced here: 45.1 us
  starting transfers between devices  20 us (44%)
  Pallas kernels  15 us (33%)
  waiting for transfers between devices  9.8 us (22%)
    ppermute x4, starting transfers between devices, send_back(): return lax.ppermute(x, 'afd', [(j, i) for i, j in route(t)])  8.16 us
    ppermute x4, starting transfers between devices, send(): return lax.ppermute(x, 'afd', route(t))  7.56 us
    pallas_call x2, Pallas kernels, experts(): pl.pallas_call(functools.partial(expert_kernel, turns), out_shape=[shape]...  6.75 us
    ppermute x4, waiting for transfers between devices, send_back(): return lax.ppermute(x, 'afd', [(j, i) for i, j in route(t)])  4.81 us
    ppermute x12, starting transfers between devices, swap(): return lax.ppermute(x, 'afd', cores)  4.27 us
    pallas_call x2, Pallas kernels, stage(): pl.pallas_call(functools.partial(stage_kernel, which), out_shape=jax.Shap...  4.08 us
    ppermute x12, waiting for transfers between devices, swap(): return lax.ppermute(x, 'afd', cores)  3.61 us
    pallas_call x1, Pallas kernels, attend(): pl.pallas_call(attend_kernel, out_shape=(jax.ShapeDtypeStruct((steps * ro...  2.39 us
  transfers between devices with their start and end apart: 20, of which 9 were waited for; matrix products, arithmetic and copies ran while one was open for 0% of the time, Pallas kernels for 25%

profile of v12, /device:TPU:0, one launch (start us, length us, event | category | flops | bytes accessed | tf_op | source)
XLA Modules:
  0.0 45.1 jit_solution(13753108808513305843)
XLA Ops:
  0.0 2.4 %attend.1 = (f32[8,7168]{1,0:T(8,128)S(1)}, bf16[8,7296]{1,0:T(8,128)(2,1)S(1)}, bf16[256,7168]{1,0:T(8,128)(2,1)S(1)}) custom-call(s32[4]{0:T(128)} %len_hbm.1, s32[3,2,4]{2,1,0:T(2,128)} %bitcast.6, f32[3,2,4]{2,1,0:T(2,128)} %bitcast.7, bf16[2,4,7168]{2,1,0:T(4,128)(2,1)} %q_hbm.1, bf16[2,4,448]{2,1,0:T(4,128)(2,1)} %fresh_hbm.1, ...), custom_call_target="tpu_custom_call" | custom-call | flops 300000000 | bytes 2000000 | tf_op jit(solution)/shard_map/attend/pallas_call | solution.py:175
  2.4 0.5 %collective-permute-start = (bf16[8,7296]{1,0:T(8,128)(2,1)S(1)}, bf16[8,7296]{1,0:T(8,128)(2,1)S(1)}, u32[]{:S(2)}, u32[]{:S(2)}) collective-permute-start(bf16[8,7296]{1,0:T(8,128)(2,1)S(1)} %get-tuple-element.39.own_ref), channel_id=1, source_target_pairs={{0,1},{1,0},{2,3},{3,2},{4,5},{5,4},{6,7},{7,6},{8,9},{9,8},{10,11... | collective-permute-start | bytes 350216 | tf_op jit(solution)/shard_map/ppermute | solution.py:445
  2.9 2.0 %stage.2.refs_4_ = bf16[256,7168]{1,0:T(8,128)(2,1)S(1)} custom-call(bf16[1,2,256,7168]{3,2,1,0:T(8,128)(2,1)} %gu_hbm.3), custom_call_target="tpu_custom_call" | custom-call | bytes 8000000 | tf_op jit(solution)/shard_map/stage/pallas_call | solution.py:292
  5.0 0.5 %pack.1 = (bf16[32,1792]{1,0:T(8,128)(2,1)S(1)}, bf16[32,1792]{1,0:T(8,128)(2,1)S(1)}, bf16[32,1792]{1,0:T(8,128)(2,1)S(1)}, bf16[32,1792]{1,0:T(8,128)(2,1)S(1)}) custom-call(bf16[8,7296]{1,0:T(8,128)(2,1)S(1)} %get-tuple-element.39.own_ref, bf16[8,7296]{1,0:T(8,128)(2,1)S(1)} %collective-permute-done.other_ref), custom_call_target="tpu_custom_call" | custom-call | flops 50000000 | bytes 2000000 | tf_op jit(solution)/shard_map/pack/pallas_call | solution.py:239
  5.6 4.8 %collective-permute-start.2 = (bf16[32,1792]{1,0:T(8,128)(2,1)S(1)}, bf16[32,1792]{1,0:T(8,128)(2,1)S(1)}, u32[]{:S(2)}, u32[]{:S(2)}) collective-permute-start(bf16[32,1792]{1,0:T(8,128)(2,1)S(1)} %get-tuple-element.43), channel_id=1, source_target_pairs={{0,5},{1,10},{2,7},{3,8},{4,1},{5,14},{6,3},{7,12},{8,13},{9,2},{1... | collective-permute-start | bytes 344072 | tf_op jit(solution)/shard_map/ppermute | solution.py:451
  10.4 2.0 %stage.3.refs_5_ = bf16[256,7168]{1,0:T(8,128)(2,1)S(1)} custom-call(bf16[1,2,256,7168]{3,2,1,0:T(8,128)(2,1)} %gu_hbm.3), custom_call_target="tpu_custom_call" | custom-call | bytes 8000000 | tf_op jit(solution)/shard_map/stage/pallas_call | solution.py:292
  12.7 2.4 %collective-permute-start.8 = (bf16[32,1792]{1,0:T(8,128)(2,1)S(1)}, bf16[32,1792]{1,0:T(8,128)(2,1)S(1)}, u32[]{:S(2)}, u32[]{:S(2)}) collective-permute-start(bf16[32,1792]{1,0:T(8,128)(2,1)S(1)} %get-tuple-element.52), channel_id=1, source_target_pairs={{0,13},{1,2},{2,15},{3,0},{4,9},{5,6},{6,11},{7,4},{8,5},{9,10},{1... | collective-permute-start | bytes 344072 | tf_op jit(solution)/shard_map/ppermute | solution.py:451
  15.1 1.4 %collective-permute-done.2.refs_1_ = bf16[32,1792]{1,0:T(8,128)(2,1)S(1)} collective-permute-done((bf16[32,1792]{1,0:T(8,128)(2,1)S(1)}, bf16[32,1792]{1,0:T(8,128)(2,1)S(1)}, u32[]{:S(2)}, u32[]{:S(2)}) %collective-permute-start.2) | collective-permute-done | bytes 114720 | tf_op jit(solution)/shard_map/ppermute | solution.py:451
  16.5 1.1 %collective-permute-start.3 = (bf16[16,1792]{1,0:T(8,128)(2,1)S(1)}, bf16[16,1792]{1,0:T(8,128)(2,1)S(1)}, u32[]{:S(2)}, u32[]{:S(2)}) collective-permute-start(bf16[16,1792]{1,0:T(8,128)(2,1)S(1)} %get-tuple-element.75), channel_id=1, source_target_pairs={{0,1},{1,0},{2,3},{3,2},{4,5},{5,4},{6,7},{7,6},{8,9},{9,8},{10,11... | collective-permute-start | bytes 172040 | tf_op jit(solution)/shard_map/ppermute | solution.py:445
  17.7 0.5 %collective-permute-start.5 = (bf16[16,1792]{1,0:T(8,128)(2,1)S(1)}, bf16[16,1792]{1,0:T(8,128)(2,1)S(1)}, u32[]{:S(2)}, u32[]{:S(2)}) collective-permute-start(bf16[16,1792]{1,0:T(8,128)(2,1)S(1)} %get-tuple-element.73), channel_id=1, source_target_pairs={{0,1},{1,0},{2,3},{3,2},{4,5},{5,4},{6,7},{7,6},{8,9},{9,8},{10,11... | collective-permute-start | bytes 172040 | tf_op jit(solution)/shard_map/ppermute | solution.py:445
  19.1 0.7 %collective-permute-done.6 = bf16[16,1792]{1,0:T(8,128)(2,1)S(1)} collective-permute-done((bf16[16,1792]{1,0:T(8,128)(2,1)S(1)}, bf16[16,1792]{1,0:T(8,128)(2,1)S(1)}, u32[]{:S(2)}, u32[]{:S(2)}) %collective-permute-start.6) | collective-permute-done | bytes 57376 | tf_op jit(solution)/shard_map/ppermute | solution.py:445
  19.7 3.4 %experts.2 = (bf16[32,1792]{1,0:T(8,128)(2,1)S(1)}, bf16[32,1792]{1,0:T(8,128)(2,1)S(1)}, bf16[32,1792]{1,0:T(8,128)(2,1)S(1)}, bf16[32,1792]{1,0:T(8,128)(2,1)S(1)}) custom-call(bf16[32,1792]{1,0:T(8,128)(2,1)S(1)} %collective-permute-done.1.refs_0_, bf16[32,1792]{1,0:T(8,128)(2,1)S(1)} %collective-permute-done.2.refs_1_, ...), custom_call_target="tpu_custom_call" | custom-call | flops 800000000 | bytes 12000000 | tf_op jit(solution)/shard_map/experts/pallas_call | solution.py:362
  23.1 0.4 collective-permute-start.13
  24.5 3.3 %collective-permute-start.14 = (bf16[32,1792]{1,0:T(8,128)(2,1)S(1)}, bf16[32,1792]{1,0:T(8,128)(2,1)S(1)}, u32[]{:S(2)}, u32[]{:S(2)}) collective-permute-start(bf16[32,1792]{1,0:T(8,128)(2,1)S(1)} %add_convert_fusion.2), channel_id=1, source_target_pairs={{5,0},{10,1},{7,2},{8,3},{1,4},{14,5},{3,6},{12,7},{13,8},{2,9},{1... | collective-permute-start | bytes 344072 | tf_op jit(solution)/shard_map/ppermute | solution.py:454
  27.9 1.5 %collective-permute-start.12 = (bf16[32,1792]{1,0:T(8,128)(2,1)S(1)}, bf16[32,1792]{1,0:T(8,128)(2,1)S(1)}, u32[]{:S(2)}, u32[]{:S(2)}) collective-permute-start(bf16[32,1792]{1,0:T(8,128)(2,1)S(1)} %add_convert_fusion.3), channel_id=1, source_target_pairs={{1,0},{14,1},{3,2},{12,3},{5,4},{10,5},{7,6},{8,7},{9,8},{6,9},{11... | collective-permute-start | bytes 344072 | tf_op jit(solution)/shard_map/ppermute | solution.py:454
  29.4 3.4 %experts.3 = (bf16[32,1792]{1,0:T(8,128)(2,1)S(1)}, bf16[32,1792]{1,0:T(8,128)(2,1)S(1)}, bf16[32,1792]{1,0:T(8,128)(2,1)S(1)}, bf16[32,1792]{1,0:T(8,128)(2,1)S(1)}) custom-call(bf16[32,1792]{1,0:T(8,128)(2,1)S(1)} %collective-permute-done.7.refs_0_, bf16[32,1792]{1,0:T(8,128)(2,1)S(1)} %collective-permute-done.8.refs_1_, ...), custom_call_target="tpu_custom_call" | custom-call | flops 800000000 | bytes 12000000 | tf_op jit(solution)/shard_map/experts/pallas_call | solution.py:362
  32.9 0.5 %collective-permute-start.17 = (bf16[32,1792]{1,0:T(8,128)(2,1)S(1)}, bf16[32,1792]{1,0:T(8,128)(2,1)S(1)}, u32[]{:S(2)}, u32[]{:S(2)}) collective-permute-start(bf16[32,1792]{1,0:T(8,128)(2,1)S(1)} %get-tuple-element.70), channel_id=1, source_target_pairs={{0,1},{1,0},{2,3},{3,2},{4,5},{5,4},{6,7},{7,6},{8,9},{9,8},{10,11... | collective-permute-start | bytes 344072 | tf_op jit(solution)/shard_map/ppermute | solution.py:445
  33.4 0.8 %collective-permute-done.15 = bf16[32,1792]{1,0:T(8,128)(2,1)S(1)} collective-permute-done((bf16[32,1792]{1,0:T(8,128)(2,1)S(1)}, bf16[32,1792]{1,0:T(8,128)(2,1)S(1)}, u32[]{:S(2)}, u32[]{:S(2)}) %collective-permute-start.15) | collective-permute-done | bytes 114720 | tf_op jit(solution)/shard_map/ppermute | solution.py:445
  34.2 1.6 %collective-permute-start.16 = (bf16[32,1792]{1,0:T(8,128)(2,1)S(1)}, bf16[32,1792]{1,0:T(8,128)(2,1)S(1)}, u32[]{:S(2)}, u32[]{:S(2)}) collective-permute-start(bf16[32,1792]{1,0:T(8,128)(2,1)S(1)} %add_convert_fusion.1), channel_id=1, source_target_pairs={{9,0},{6,1},{11,2},{4,3},{13,4},{2,5},{15,6},{0,7},{1,8},{14,9},{3... | collective-permute-start | bytes 344072 | tf_op jit(solution)/shard_map/ppermute | solution.py:454
  35.8 1.8 %collective-permute-start.18 = (bf16[32,1792]{1,0:T(8,128)(2,1)S(1)}, bf16[32,1792]{1,0:T(8,128)(2,1)S(1)}, u32[]{:S(2)}, u32[]{:S(2)}) collective-permute-start(bf16[32,1792]{1,0:T(8,128)(2,1)S(1)} %add_convert_fusion), channel_id=1, source_target_pairs={{13,0},{2,1},{15,2},{0,3},{9,4},{6,5},{11,6},{4,7},{5,8},{10,9},{7... | collective-permute-start | bytes 344072 | tf_op jit(solution)/shard_map/ppermute | solution.py:454
  37.9 2.7 %collective-permute-done.16.refs_2_ = bf16[32,1792]{1,0:T(8,128)(2,1)S(1)} collective-permute-done((bf16[32,1792]{1,0:T(8,128)(2,1)S(1)}, bf16[32,1792]{1,0:T(8,128)(2,1)S(1)}, u32[]{:S(2)}, u32[]{:S(2)}) %collective-permute-start.16) | collective-permute-done | bytes 114720 | tf_op jit(solution)/shard_map/ppermute | solution.py:454
  40.6 2.1 %collective-permute-done.18.refs_3_ = bf16[32,1792]{1,0:T(8,128)(2,1)S(1)} collective-permute-done((bf16[32,1792]{1,0:T(8,128)(2,1)S(1)}, bf16[32,1792]{1,0:T(8,128)(2,1)S(1)}, u32[]{:S(2)}, u32[]{:S(2)}) %collective-permute-start.18) | collective-permute-done | bytes 114720 | tf_op jit(solution)/shard_map/ppermute | solution.py:454
  43.1 1.3 %collective-permute-done.19.other_ref = bf16[8,7168]{1,0:T(8,128)(2,1)S(1)} collective-permute-done((bf16[8,7168]{1,0:T(8,128)(2,1)S(1)}, bf16[8,7168]{1,0:T(8,128)(2,1)S(1)}, u32[]{:S(2)}, u32[]{:S(2)}) %collective-permute-start.19) | collective-permute-done | bytes 114720 | tf_op jit(solution)/shard_map/ppermute | solution.py:445
  44.4 0.7 %finish.1 = bf16[2,4,7168]{2,1,0:T(4,128)(2,1)} custom-call(f32[8,7168]{1,0:T(8,128)S(1)} %get-tuple-element.71.kept_ref, bf16[8,7168]{1,0:T(8,128)(2,1)S(1)} %collective-permute-done.19.other_ref), custom_call_target="tpu_custom_call" | custom-call | flops 100000 | bytes 500000 | tf_op jit(solution)/shard_map/finish/pallas_call | solution.py:415
  (33 shorter events, 3.3 us)
Async XLA Ops:
  2.4 2.6 %collective-permute-start = (bf16[8,7296]{1,0:T(8,128)(2,1)S(1)}, bf16[8,7296]{1,0:T(8,128)(2,1)S(1)}, u32[]{:S(2)}, u32[]{:S(2)}) collective-permute-start(bf16[8,7296]{1,0:T(8,128)(2,1)S(1)} %get-tuple-element.39.own_ref), channel_id=1, source_target_pairs={{0,1},{1,0},{2,3},{3,2},{4,5},{5,4},{6,7},{7,6},{8,9},{9,8},{10,11... | collective-permute-start | bytes 350216 | tf_op jit(solution)/shard_map/ppermute | solution.py:445
  5.5 9.6 %collective-permute-start.1 = (bf16[32,1792]{1,0:T(8,128)(2,1)S(1)}, bf16[32,1792]{1,0:T(8,128)(2,1)S(1)}, u32[]{:S(2)}, u32[]{:S(2)}) collective-permute-start(bf16[32,1792]{1,0:T(8,128)(2,1)S(1)} %get-tuple-element.42), channel_id=1, source_target_pairs={{0,1},{1,14},{2,3},{3,12},{4,5},{5,10},{6,7},{7,8},{8,9},{9,6},{10... | collective-permute-start | bytes 344072 | tf_op jit(solution)/shard_map/ppermute | solution.py:451
  5.6 10.9 %collective-permute-start.2 = (bf16[32,1792]{1,0:T(8,128)(2,1)S(1)}, bf16[32,1792]{1,0:T(8,128)(2,1)S(1)}, u32[]{:S(2)}, u32[]{:S(2)}) collective-permute-start(bf16[32,1792]{1,0:T(8,128)(2,1)S(1)} %get-tuple-element.43), channel_id=1, source_target_pairs={{0,5},{1,10},{2,7},{3,8},{4,1},{5,14},{6,3},{7,12},{8,13},{9,2},{1... | collective-permute-start | bytes 344072 | tf_op jit(solution)/shard_map/ppermute | solution.py:451
  12.4 11.3 %collective-permute-start.7 = (bf16[32,1792]{1,0:T(8,128)(2,1)S(1)}, bf16[32,1792]{1,0:T(8,128)(2,1)S(1)}, u32[]{:S(2)}, u32[]{:S(2)}) collective-permute-start(bf16[32,1792]{1,0:T(8,128)(2,1)S(1)} %get-tuple-element.51), channel_id=1, source_target_pairs={{0,9},{1,6},{2,11},{3,4},{4,13},{5,2},{6,15},{7,0},{8,1},{9,14},{1... | collective-permute-start | bytes 344072 | tf_op jit(solution)/shard_map/ppermute | solution.py:451
  12.7 11.0 %collective-permute-start.8 = (bf16[32,1792]{1,0:T(8,128)(2,1)S(1)}, bf16[32,1792]{1,0:T(8,128)(2,1)S(1)}, u32[]{:S(2)}, u32[]{:S(2)}) collective-permute-start(bf16[32,1792]{1,0:T(8,128)(2,1)S(1)} %get-tuple-element.52), channel_id=1, source_target_pairs={{0,13},{1,2},{2,15},{3,0},{4,9},{5,6},{6,11},{7,4},{8,5},{9,10},{1... | collective-permute-start | bytes 344072 | tf_op jit(solution)/shard_map/ppermute | solution.py:451
  16.5 2.0 %collective-permute-start.3 = (bf16[16,1792]{1,0:T(8,128)(2,1)S(1)}, bf16[16,1792]{1,0:T(8,128)(2,1)S(1)}, u32[]{:S(2)}, u32[]{:S(2)}) collective-permute-start(bf16[16,1792]{1,0:T(8,128)(2,1)S(1)} %get-tuple-element.75), channel_id=1, source_target_pairs={{0,1},{1,0},{2,3},{3,2},{4,5},{5,4},{6,7},{7,6},{8,9},{9,8},{10,11... | collective-permute-start | bytes 172040 | tf_op jit(solution)/shard_map/ppermute | solution.py:445
  17.6 1.2 %collective-permute-start.4 = (bf16[16,1792]{1,0:T(8,128)(2,1)S(1)}, bf16[16,1792]{1,0:T(8,128)(2,1)S(1)}, u32[]{:S(2)}, u32[]{:S(2)}) collective-permute-start(bf16[16,1792]{1,0:T(8,128)(2,1)S(1)} %get-tuple-element.76), channel_id=1, source_target_pairs={{0,1},{1,0},{2,3},{3,2},{4,5},{5,4},{6,7},{7,6},{8,9},{9,8},{10,11... | collective-permute-start | bytes 172040 | tf_op jit(solution)/shard_map/ppermute | solution.py:445
  17.7 1.4 %collective-permute-start.5 = (bf16[16,1792]{1,0:T(8,128)(2,1)S(1)}, bf16[16,1792]{1,0:T(8,128)(2,1)S(1)}, u32[]{:S(2)}, u32[]{:S(2)}) collective-permute-start(bf16[16,1792]{1,0:T(8,128)(2,1)S(1)} %get-tuple-element.73), channel_id=1, source_target_pairs={{0,1},{1,0},{2,3},{3,2},{4,5},{5,4},{6,7},{7,6},{8,9},{9,8},{10,11... | collective-permute-start | bytes 172040 | tf_op jit(solution)/shard_map/ppermute | solution.py:445
  18.5 1.2 %collective-permute-start.6 = (bf16[16,1792]{1,0:T(8,128)(2,1)S(1)}, bf16[16,1792]{1,0:T(8,128)(2,1)S(1)}, u32[]{:S(2)}, u32[]{:S(2)}) collective-permute-start(bf16[16,1792]{1,0:T(8,128)(2,1)S(1)} %get-tuple-element.74), channel_id=1, source_target_pairs={{0,1},{1,0},{2,3},{3,2},{4,5},{5,4},{6,7},{7,6},{8,9},{9,8},{10,11... | collective-permute-start | bytes 172040 | tf_op jit(solution)/shard_map/ppermute | solution.py:445
  23.1 1.4 %collective-permute-start.13 = (bf16[32,1792]{1,0:T(8,128)(2,1)S(1)}, bf16[32,1792]{1,0:T(8,128)(2,1)S(1)}, u32[]{:S(2)}, u32[]{:S(2)}) collective-permute-start(bf16[32,1792]{1,0:T(8,128)(2,1)S(1)} %get-tuple-element.62), channel_id=1, source_target_pairs={{0,1},{1,0},{2,3},{3,2},{4,5},{5,4},{6,7},{7,6},{8,9},{9,8},{10,11... | collective-permute-start | bytes 344072 | tf_op jit(solution)/shard_map/ppermute | solution.py:445
  23.5 4.3 %collective-permute-start.11 = (bf16[32,1792]{1,0:T(8,128)(2,1)S(1)}, bf16[32,1792]{1,0:T(8,128)(2,1)S(1)}, u32[]{:S(2)}, u32[]{:S(2)}) collective-permute-start(bf16[32,1792]{1,0:T(8,128)(2,1)S(1)} %get-tuple-element.60), channel_id=1, source_target_pairs={{0,1},{1,0},{2,3},{3,2},{4,5},{5,4},{6,7},{7,6},{8,9},{9,8},{10,11... | collective-permute-start | bytes 344072 | tf_op jit(solution)/shard_map/ppermute | solution.py:445
  23.7 5.7 %collective-permute-start.9 = (bf16[32,1792]{1,0:T(8,128)(2,1)S(1)}, bf16[32,1792]{1,0:T(8,128)(2,1)S(1)}, u32[]{:S(2)}, u32[]{:S(2)}) collective-permute-start(bf16[32,1792]{1,0:T(8,128)(2,1)S(1)} %collective-permute-done.7.refs_0_), channel_id=1, source_target_pairs={{0,1},{1,0},{2,3},{3,2},{4,5},{5,4},{6,7},{7,6},{8,9},{9,8},{10,11... | collective-permute-start | bytes 344072 | tf_op jit(solution)/shard_map/ppermute | solution.py:445
  24.0 5.3 %collective-permute-start.10 = (bf16[32,1792]{1,0:T(8,128)(2,1)S(1)}, bf16[32,1792]{1,0:T(8,128)(2,1)S(1)}, u32[]{:S(2)}, u32[]{:S(2)}) collective-permute-start(bf16[32,1792]{1,0:T(8,128)(2,1)S(1)} %collective-permute-done.8.refs_1_), channel_id=1, source_target_pairs={{0,1},{1,0},{2,3},{3,2},{4,5},{5,4},{6,7},{7,6},{8,9},{9,8},{10,11... | collective-permute-start | bytes 344072 | tf_op jit(solution)/shard_map/ppermute | solution.py:445
  24.5 8.2 %collective-permute-start.14 = (bf16[32,1792]{1,0:T(8,128)(2,1)S(1)}, bf16[32,1792]{1,0:T(8,128)(2,1)S(1)}, u32[]{:S(2)}, u32[]{:S(2)}) collective-permute-start(bf16[32,1792]{1,0:T(8,128)(2,1)S(1)} %add_convert_fusion.2), channel_id=1, source_target_pairs={{5,0},{10,1},{7,2},{8,3},{1,4},{14,5},{3,6},{12,7},{13,8},{2,9},{1... | collective-permute-start | bytes 344072 | tf_op jit(solution)/shard_map/ppermute | solution.py:454
  27.9 4.9 %collective-permute-start.12 = (bf16[32,1792]{1,0:T(8,128)(2,1)S(1)}, bf16[32,1792]{1,0:T(8,128)(2,1)S(1)}, u32[]{:S(2)}, u32[]{:S(2)}) collective-permute-start(bf16[32,1792]{1,0:T(8,128)(2,1)S(1)} %add_convert_fusion.3), channel_id=1, source_target_pairs={{1,0},{14,1},{3,2},{12,3},{5,4},{10,5},{7,6},{8,7},{9,8},{6,9},{11... | collective-permute-start | bytes 344072 | tf_op jit(solution)/shard_map/ppermute | solution.py:454
  32.8 1.4 %collective-permute-start.15 = (bf16[32,1792]{1,0:T(8,128)(2,1)S(1)}, bf16[32,1792]{1,0:T(8,128)(2,1)S(1)}, u32[]{:S(2)}, u32[]{:S(2)}) collective-permute-start(bf16[32,1792]{1,0:T(8,128)(2,1)S(1)} %get-tuple-element.68), channel_id=1, source_target_pairs={{0,1},{1,0},{2,3},{3,2},{4,5},{5,4},{6,7},{7,6},{8,9},{9,8},{10,11... | collective-permute-start | bytes 344072 | tf_op jit(solution)/shard_map/ppermute | solution.py:445
  32.9 2.9 %collective-permute-start.17 = (bf16[32,1792]{1,0:T(8,128)(2,1)S(1)}, bf16[32,1792]{1,0:T(8,128)(2,1)S(1)}, u32[]{:S(2)}, u32[]{:S(2)}) collective-permute-start(bf16[32,1792]{1,0:T(8,128)(2,1)S(1)} %get-tuple-element.70), channel_id=1, source_target_pairs={{0,1},{1,0},{2,3},{3,2},{4,5},{5,4},{6,7},{7,6},{8,9},{9,8},{10,11... | collective-permute-start | bytes 344072 | tf_op jit(solution)/shard_map/ppermute | solution.py:445
  34.2 6.4 %collective-permute-start.16 = (bf16[32,1792]{1,0:T(8,128)(2,1)S(1)}, bf16[32,1792]{1,0:T(8,128)(2,1)S(1)}, u32[]{:S(2)}, u32[]{:S(2)}) collective-permute-start(bf16[32,1792]{1,0:T(8,128)(2,1)S(1)} %add_convert_fusion.1), channel_id=1, source_target_pairs={{9,0},{6,1},{11,2},{4,3},{13,4},{2,5},{15,6},{0,7},{1,8},{14,9},{3... | collective-permute-start | bytes 344072 | tf_op jit(solution)/shard_map/ppermute | solution.py:454
  35.8 6.9 %collective-permute-start.18 = (bf16[32,1792]{1,0:T(8,128)(2,1)S(1)}, bf16[32,1792]{1,0:T(8,128)(2,1)S(1)}, u32[]{:S(2)}, u32[]{:S(2)}) collective-permute-start(bf16[32,1792]{1,0:T(8,128)(2,1)S(1)} %add_convert_fusion), channel_id=1, source_target_pairs={{13,0},{2,1},{15,2},{0,3},{9,4},{6,5},{11,6},{4,7},{5,8},{10,9},{7... | collective-permute-start | bytes 344072 | tf_op jit(solution)/shard_map/ppermute | solution.py:454
  43.0 1.4 %collective-permute-start.19 = (bf16[8,7168]{1,0:T(8,128)(2,1)S(1)}, bf16[8,7168]{1,0:T(8,128)(2,1)S(1)}, u32[]{:S(2)}, u32[]{:S(2)}) collective-permute-start(bf16[8,7168]{1,0:T(8,128)(2,1)S(1)} %get-tuple-element.72), channel_id=1, source_target_pairs={{0,1},{1,0},{2,3},{3,2},{4,5},{5,4},{6,7},{7,6},{8,9},{9,8},{10,11... | collective-permute-start | bytes 344072 | tf_op jit(solution)/shard_map/ppermute | solution.py:445

commit v13 on v11

--- a/solution.py
+++ b/solution.py
@@ -43,7 +43,11 @@
 
 
 def distance(turn, core, chips):
-    return (2 * turn) ^ (core * (chips - 1))
+    bits = (chips // 2).bit_length() - 1
+    even = 0
+    for b in range(bits):
+        even = even + ((turn >> b) % 2 << (bits - b))
+    return even ^ (core * (chips - 1))
 
 
 def expert_at(turn, chips):
@@ -276,27 +280,29 @@
     return jnp.concatenate(parts, axis=0).astype(BF16)
 
 
-def stage_kernel(which, gu_hbm, out, sems):
-    step = out.shape[0] // 4
+def stage_kernel(gu_hbm, out, sems):
+    step = out.shape[1] // 4
     copies = []
-    for i in range(4):
-        part = pl.ds(i * step, step)
-        copies.append(pltpu.make_async_copy(gu_hbm.at[0, which, part], out.at[part], sems.at[i]))
+    for i in range(8):
+        part = pl.ds(i // 2 * step, step)
+        copies.append(
+            pltpu.make_async_copy(gu_hbm.at[0, i % 2, part], out.at[i % 2, part], sems.at[i])
+        )
     for copy in copies:
         copy.start()
     for copy in copies:
         copy.wait()
 
 
-def stage(which, gate_up):
+def stage(gate_up):
     return pl.pallas_call(
-        functools.partial(stage_kernel, which),
-        out_shape=jax.ShapeDtypeStruct(gate_up.shape[2:], BF16),
+        stage_kernel,
+        out_shape=jax.ShapeDtypeStruct(gate_up.shape[1:], BF16),
         in_specs=[HBM],
         out_specs=VMEM,
-        scratch_shapes=[pltpu.SemaphoreType.DMA((4,))],
+        scratch_shapes=[pltpu.SemaphoreType.DMA((8,))],
         compiler_params=pltpu.CompilerParams(vmem_limit_bytes=16 * MIB),
-        cost_estimate=pl.CostEstimate(flops=0, bytes_accessed=8_000_000, transcendentals=0),
+        cost_estimate=pl.CostEstimate(flops=0, bytes_accessed=16_000_000, transcendentals=0),
         name="stage",
     )(*in_hbm(gate_up))
 
@@ -323,9 +329,9 @@
 
 def expert_kernel(turns, *refs):
     own_refs, other_refs = refs[:turns], refs[turns : 2 * turns]
-    w_gate, w_upper, w_down = refs[2 * turns : 2 * turns + 3]
-    mine_refs = refs[2 * turns + 3 : 3 * turns + 3]
-    theirs_refs = refs[3 * turns + 3 :]
+    w_in, w_down = refs[2 * turns : 2 * turns + 2]
+    mine_refs = refs[2 * turns + 2 : 3 * turns + 2]
+    theirs_refs = refs[3 * turns + 2 :]
     lines, piece = own_refs[0].shape
     per = lines // PIECES
     half = turns * per
@@ -341,7 +347,7 @@
     for k in range(PIECES):
         x = jnp.concatenate([side[k * half : (k + 1) * half] for side in sides], axis=0)
         cols = pl.ds(k * piece, piece)
-        g, u = nt_dot(x, w_gate[:, cols]), nt_dot(x, w_upper[:, cols])
+        g, u = nt_dot(x, w_in[0, :, cols]), nt_dot(x, w_in[1, :, cols])
         gate, upper = (g, u) if k == 0 else (gate + g, upper + u)
     act = (gate / (1.0 + jnp.exp(-gate)) * upper).astype(BF16)
     mine = []
@@ -357,20 +363,20 @@
             ref[...] = out[t * lines : (t + 1) * lines]
 
 
-def experts(own, other, gate, upper, down):
+def experts(own, other, gate_up, down):
     turns = len(own)
     shape = jax.ShapeDtypeStruct(own[0].shape, BF16)
     results = pl.pallas_call(
         functools.partial(expert_kernel, turns),
         out_shape=[shape] * (2 * turns),
-        in_specs=[VMEM] * (2 * turns + 3),
+        in_specs=[VMEM] * (2 * turns + 2),
         out_specs=[VMEM] * (2 * turns),
         compiler_params=pltpu.CompilerParams(vmem_limit_bytes=32 * MIB),
         cost_estimate=pl.CostEstimate(
             flops=800_000_000, bytes_accessed=12_000_000, transcendentals=16384
         ),
         name="experts",
-    )(*own, *other, gate, upper, down)
+    )(*own, *other, gate_up, down)
     return results[:turns], results[turns:]
 
 
@@ -460,18 +466,16 @@
         cache_len, ids, weights, queries, fresh, kv_cache, hidden_state, norm_gain, down
     )
     normed_other = swap(normed)
-    w_gate = stage(0, gate_up)
-    w_gate, normed_other = lax.optimization_barrier((w_gate, normed_other))
     sent = pack(steps, chips, normed, normed_other)
     own = [send(sent[t], t) for t in range(turns)]
-    w_upper = stage(1, gate_up)
+    w_in = stage(gate_up)
     mix = mixer(steps, chips, normed, normed_other)
-    own[0], w_upper = lax.optimization_barrier((own[0], w_upper))
+    own[0], w_in = lax.optimization_barrier((own[0], w_in))
     other = [swap(x) for x in own]
     summed = []
     for t in range(0, turns, TOGETHER):
         now = slice(t, t + TOGETHER)
-        mine, theirs = experts(own[now], other[now], w_gate, w_upper, w_down)
+        mine, theirs = experts(own[now], other[now], w_in, w_down)
         summed += [
             (a.astype(F32) + swap(b).astype(F32)).astype(BF16) for a, b in zip(mine, theirs)
         ]

time: 42.1 us -> 42.1 us (level)
  starting transfers between devices: 16.8 us -> 20.4 us
  waiting for transfers between devices: 13 us -> 10.3 us
  Pallas kernels: 11.9 us -> 11 us
    ppermute x4, waiting for transfers between devices: 3.16 us -> 0.01 us  [send(): return lax.ppermute(x, 'afd', route(t))]
    ppermute x10, starting transfers between devices: 3.98 us -> 6.4 us  [swap(): return lax.ppermute(x, 'afd', cores)]
    pallas_call x2 -> x1, Pallas kernels: 4.08 us -> 3.17 us  [stage(): pl.pallas_call(stage_kernel, out_shape=jax.ShapeDtypeStruct(gate_up.shape...]
    ppermute x10, waiting for transfers between devices: 2.59 us -> 3.5 us  [swap(): return lax.ppermute(x, 'afd', cores)]
    ppermute x4, starting transfers between devices: 7.5 us -> 8.4 us  [send(): return lax.ppermute(x, 'afd', route(t))]
  transfers between devices with their start and end apart: 18 -> 18, of which waited for: 8 -> 9; matrix products, arithmetic and copies ran while one was open for 0% -> 0% of each run, Pallas kernels for 10% -> 8%
where the time goes in v13:
time: 42.1 us; the launch traced here: 42 us
  starting transfers between devices  20.4 us (48%)
  Pallas kernels  11 us (26%)
  waiting for transfers between devices  10.3 us (24%)
    ppermute x4, starting transfers between devices, send(): return lax.ppermute(x, 'afd', route(t))  8.4 us
    ppermute x4, waiting for transfers between devices, send_back(): return lax.ppermute(x, 'afd', [(j, i) for i, j in route(t)])  6.84 us
    ppermute x10, starting transfers between devices, swap(): return lax.ppermute(x, 'afd', cores)  6.4 us
    ppermute x4, starting transfers between devices, send_back(): return lax.ppermute(x, 'afd', [(j, i) for i, j in route(t)])  5.62 us
    pallas_call x1, Pallas kernels, experts(): pl.pallas_call(functools.partial(expert_kernel, turns), out_shape=[shape]...  3.62 us
    ppermute x10, waiting for transfers between devices, swap(): return lax.ppermute(x, 'afd', cores)  3.5 us
    pallas_call x1, Pallas kernels, stage(): pl.pallas_call(stage_kernel, out_shape=jax.ShapeDtypeStruct(gate_up.shape...  3.17 us
    pallas_call x1, Pallas kernels, attend(): pl.pallas_call(attend_kernel, out_shape=(jax.ShapeDtypeStruct((steps * ro...  2.39 us
  transfers between devices with their start and end apart: 18, of which 9 were waited for; matrix products, arithmetic and copies ran while one was open for 0% of the time, Pallas kernels for 8%

profile of v13, /device:TPU:0, one launch (start us, length us, event | category | flops | bytes accessed | tf_op | source)
XLA Modules:
  0.0 42.0 jit_solution(9394321227483050298)
XLA Ops:
  0.0 2.4 %attend.1 = (f32[8,7168]{1,0:T(8,128)S(1)}, bf16[8,7296]{1,0:T(8,128)(2,1)S(1)}, bf16[256,7168]{1,0:T(8,128)(2,1)S(1)}) custom-call(s32[4]{0:T(128)} %len_hbm.1, s32[3,2,4]{2,1,0:T(2,128)} %bitcast.6, f32[3,2,4]{2,1,0:T(2,128)} %bitcast.7, bf16[2,4,7168]{2,1,0:T(4,128)(2,1)} %q_hbm.1, bf16[2,4,448]{2,1,0:T(4,128)(2,1)} %fresh_hbm.1, ...), custom_call_target="tpu_custom_call" | custom-call | flops 300000000 | bytes 2000000 | tf_op jit(solution)/shard_map/attend/pallas_call | solution.py:179
  2.4 0.5 %collective-permute-start = (bf16[8,7296]{1,0:T(8,128)(2,1)S(1)}, bf16[8,7296]{1,0:T(8,128)(2,1)S(1)}, u32[]{:S(2)}, u32[]{:S(2)}) collective-permute-start(bf16[8,7296]{1,0:T(8,128)(2,1)S(1)} %get-tuple-element.24.own_ref), channel_id=1, source_target_pairs={{0,1},{1,0},{2,3},{3,2},{4,5},{5,4},{6,7},{7,6},{8,9},{9,8},{10,11... | collective-permute-start | bytes 350216 | tf_op jit(solution)/shard_map/ppermute | solution.py:452
  2.9 1.0 %collective-permute-done.other_ref = bf16[8,7296]{1,0:T(8,128)(2,1)S(1)} collective-permute-done((bf16[8,7296]{1,0:T(8,128)(2,1)S(1)}, bf16[8,7296]{1,0:T(8,128)(2,1)S(1)}, u32[]{:S(2)}, u32[]{:S(2)}) %collective-permute-start) | collective-permute-done | bytes 116768 | tf_op jit(solution)/shard_map/ppermute | solution.py:452
  3.9 0.5 %pack.1 = (bf16[32,1792]{1,0:T(8,128)(2,1)S(1)}, bf16[32,1792]{1,0:T(8,128)(2,1)S(1)}, bf16[32,1792]{1,0:T(8,128)(2,1)S(1)}, bf16[32,1792]{1,0:T(8,128)(2,1)S(1)}) custom-call(bf16[8,7296]{1,0:T(8,128)(2,1)S(1)} %get-tuple-element.24.own_ref, bf16[8,7296]{1,0:T(8,128)(2,1)S(1)} %collective-permute-done.other_ref), custom_call_target="tpu_custom_call" | custom-call | flops 50000000 | bytes 2000000 | tf_op jit(solution)/shard_map/pack/pallas_call | solution.py:243
  4.4 0.4 collective-permute-start.1
  4.8 4.7 %collective-permute-start.2 = (bf16[32,1792]{1,0:T(8,128)(2,1)S(1)}, bf16[32,1792]{1,0:T(8,128)(2,1)S(1)}, u32[]{:S(2)}, u32[]{:S(2)}) collective-permute-start(bf16[32,1792]{1,0:T(8,128)(2,1)S(1)} %get-tuple-element.28), channel_id=1, source_target_pairs={{0,9},{1,6},{2,11},{3,4},{4,13},{5,2},{6,15},{7,0},{8,1},{9,14},{1... | collective-permute-start | bytes 344072 | tf_op jit(solution)/shard_map/ppermute | solution.py:458
  9.6 3.2 %collective-permute-start.4 = (bf16[32,1792]{1,0:T(8,128)(2,1)S(1)}, bf16[32,1792]{1,0:T(8,128)(2,1)S(1)}, u32[]{:S(2)}, u32[]{:S(2)}) collective-permute-start(bf16[32,1792]{1,0:T(8,128)(2,1)S(1)} %get-tuple-element.30), channel_id=1, source_target_pairs={{0,13},{1,2},{2,15},{3,0},{4,9},{5,6},{6,11},{7,4},{8,5},{9,10},{1... | collective-permute-start | bytes 344072 | tf_op jit(solution)/shard_map/ppermute | solution.py:458
  12.8 3.2 %stage.1.refs_8_ = bf16[2,256,7168]{2,1,0:T(8,128)(2,1)S(1)} custom-call(bf16[1,2,256,7168]{3,2,1,0:T(8,128)(2,1)} %gu_hbm.1), custom_call_target="tpu_custom_call" | custom-call | bytes 16000000 | tf_op jit(solution)/shard_map/stage/pallas_call | solution.py:298
  16.0 3.3 %collective-permute-start.6 = (bf16[32,1792]{1,0:T(8,128)(2,1)S(1)}, bf16[32,1792]{1,0:T(8,128)(2,1)S(1)}, u32[]{:S(2)}, u32[]{:S(2)}) collective-permute-start(bf16[32,1792]{1,0:T(8,128)(2,1)S(1)} %collective-permute-done.2.refs_1_), channel_id=1, source_target_pairs={{0,1},{1,0},{2,3},{3,2},{4,5},{5,4},{6,7},{7,6},{8,9},{9,8},{10,11... | collective-permute-start | bytes 344072 | tf_op jit(solution)/shard_map/ppermute | solution.py:452
  19.3 0.5 %collective-permute-start.8 = (bf16[32,1792]{1,0:T(8,128)(2,1)S(1)}, bf16[32,1792]{1,0:T(8,128)(2,1)S(1)}, u32[]{:S(2)}, u32[]{:S(2)}) collective-permute-start(bf16[32,1792]{1,0:T(8,128)(2,1)S(1)} %collective-permute-done.4.refs_3_), channel_id=1, source_target_pairs={{0,1},{1,0},{2,3},{3,2},{4,5},{5,4},{6,7},{7,6},{8,9},{9,8},{10,11... | collective-permute-start | bytes 344072 | tf_op jit(solution)/shard_map/ppermute | solution.py:452
  19.9 0.4 collective-permute-done.6.refs_5_
  20.3 0.4 collective-permute-done.7.refs_6_
  20.8 0.3 collective-permute-done.5.refs_4_
  21.2 3.6 %experts.1 = (bf16[32,1792]{1,0:T(8,128)(2,1)S(1)}, bf16[32,1792]{1,0:T(8,128)(2,1)S(1)}, bf16[32,1792]{1,0:T(8,128)(2,1)S(1)}, bf16[32,1792]{1,0:T(8,128)(2,1)S...) custom-call(bf16[32,1792]{1,0:T(8,128)(2,1)S(1)} %collective-permute, ...), custom_call_target="tpu_custom_call" | custom-call | flops 800000000 | bytes 12000000 | tf_op jit(solution)/shard_map/experts/pallas_call | solution.py:369
  25.0 0.3 collective-permute-start.11
  25.5 0.3 collective-permute-start.15
  26.2 1.9 %collective-permute-start.10 = (bf16[32,1792]{1,0:T(8,128)(2,1)S(1)}, bf16[32,1792]{1,0:T(8,128)(2,1)S(1)}, u32[]{:S(2)}, u32[]{:S(2)}) collective-permute-start(bf16[32,1792]{1,0:T(8,128)(2,1)S(1)} %add_convert_fusion.3), channel_id=1, source_target_pairs={{1,0},{14,1},{3,2},{12,3},{5,4},{10,5},{7,6},{8,7},{9,8},{6,9},{11... | collective-permute-start | bytes 344072 | tf_op jit(solution)/shard_map/ppermute | solution.py:461
  28.3 3.6 %collective-permute-start.14 = (bf16[32,1792]{1,0:T(8,128)(2,1)S(1)}, bf16[32,1792]{1,0:T(8,128)(2,1)S(1)}, u32[]{:S(2)}, u32[]{:S(2)}) collective-permute-start(bf16[32,1792]{1,0:T(8,128)(2,1)S(1)} %add_convert_fusion.1), channel_id=1, source_target_pairs={{5,0},{10,1},{7,2},{8,3},{1,4},{14,5},{3,6},{12,7},{13,8},{2,9},{1... | collective-permute-start | bytes 344072 | tf_op jit(solution)/shard_map/ppermute | solution.py:461
  32.3 5.6 %collective-permute-done.12.refs_1_ = bf16[32,1792]{1,0:T(8,128)(2,1)S(1)} collective-permute-done((bf16[32,1792]{1,0:T(8,128)(2,1)S(1)}, bf16[32,1792]{1,0:T(8,128)(2,1)S(1)}, u32[]{:S(2)}, u32[]{:S(2)}) %collective-permute-start.12) | collective-permute-done | bytes 114720 | tf_op jit(solution)/shard_map/ppermute | solution.py:461
  37.9 1.2 %collective-permute-done.16.refs_3_ = bf16[32,1792]{1,0:T(8,128)(2,1)S(1)} collective-permute-done((bf16[32,1792]{1,0:T(8,128)(2,1)S(1)}, bf16[32,1792]{1,0:T(8,128)(2,1)S(1)}, u32[]{:S(2)}, u32[]{:S(2)}) %collective-permute-start.16) | collective-permute-done | bytes 114720 | tf_op jit(solution)/shard_map/ppermute | solution.py:461
  39.1 0.3 combine.1
  39.4 0.9 %collective-permute-start.17 = (bf16[8,7168]{1,0:T(8,128)(2,1)S(1)}, bf16[8,7168]{1,0:T(8,128)(2,1)S(1)}, u32[]{:S(2)}, u32[]{:S(2)}) collective-permute-start(bf16[8,7168]{1,0:T(8,128)(2,1)S(1)} %get-tuple-element.42), channel_id=1, source_target_pairs={{0,1},{1,0},{2,3},{3,2},{4,5},{5,4},{6,7},{7,6},{8,9},{9,8},{10,11... | collective-permute-start | bytes 344072 | tf_op jit(solution)/shard_map/ppermute | solution.py:452
  40.3 1.0 %collective-permute-done.17.other_ref = bf16[8,7168]{1,0:T(8,128)(2,1)S(1)} collective-permute-done((bf16[8,7168]{1,0:T(8,128)(2,1)S(1)}, bf16[8,7168]{1,0:T(8,128)(2,1)S(1)}, u32[]{:S(2)}, u32[]{:S(2)}) %collective-permute-start.17) | collective-permute-done | bytes 114720 | tf_op jit(solution)/shard_map/ppermute | solution.py:452
  41.3 0.7 %finish.1 = bf16[2,4,7168]{2,1,0:T(4,128)(2,1)} custom-call(f32[8,7168]{1,0:T(8,128)S(1)} %get-tuple-element.41.kept_ref, bf16[8,7168]{1,0:T(8,128)(2,1)S(1)} %collective-permute-done.17.other_ref), custom_call_target="tpu_custom_call" | custom-call | flops 100000 | bytes 500000 | tf_op jit(solution)/shard_map/finish/pallas_call | solution.py:422
  (23 shorter events, 1.6 us)
Async XLA Ops:
  2.4 1.5 %collective-permute-start = (bf16[8,7296]{1,0:T(8,128)(2,1)S(1)}, bf16[8,7296]{1,0:T(8,128)(2,1)S(1)}, u32[]{:S(2)}, u32[]{:S(2)}) collective-permute-start(bf16[8,7296]{1,0:T(8,128)(2,1)S(1)} %get-tuple-element.24.own_ref), channel_id=1, source_target_pairs={{0,1},{1,0},{2,3},{3,2},{4,5},{5,4},{6,7},{7,6},{8,9},{9,8},{10,11... | collective-permute-start | bytes 350216 | tf_op jit(solution)/shard_map/ppermute | solution.py:452
  4.4 11.6 %collective-permute-start.1 = (bf16[32,1792]{1,0:T(8,128)(2,1)S(1)}, bf16[32,1792]{1,0:T(8,128)(2,1)S(1)}, u32[]{:S(2)}, u32[]{:S(2)}) collective-permute-start(bf16[32,1792]{1,0:T(8,128)(2,1)S(1)} %get-tuple-element.26), channel_id=1, source_target_pairs={{0,1},{1,14},{2,3},{3,12},{4,5},{5,10},{6,7},{7,8},{8,9},{9,6},{10... | collective-permute-start | bytes 344072 | tf_op jit(solution)/shard_map/ppermute | solution.py:458
  4.8 11.2 %collective-permute-start.2 = (bf16[32,1792]{1,0:T(8,128)(2,1)S(1)}, bf16[32,1792]{1,0:T(8,128)(2,1)S(1)}, u32[]{:S(2)}, u32[]{:S(2)}) collective-permute-start(bf16[32,1792]{1,0:T(8,128)(2,1)S(1)} %get-tuple-element.28), channel_id=1, source_target_pairs={{0,9},{1,6},{2,11},{3,4},{4,13},{5,2},{6,15},{7,0},{8,1},{9,14},{1... | collective-permute-start | bytes 344072 | tf_op jit(solution)/shard_map/ppermute | solution.py:458
  9.5 9.8 %collective-permute-start.3 = (bf16[32,1792]{1,0:T(8,128)(2,1)S(1)}, bf16[32,1792]{1,0:T(8,128)(2,1)S(1)}, u32[]{:S(2)}, u32[]{:S(2)}) collective-permute-start(bf16[32,1792]{1,0:T(8,128)(2,1)S(1)} %get-tuple-element.29), channel_id=1, source_target_pairs={{0,5},{1,10},{2,7},{3,8},{4,1},{5,14},{6,3},{7,12},{8,13},{9,2},{1... | collective-permute-start | bytes 344072 | tf_op jit(solution)/shard_map/ppermute | solution.py:458
  9.6 9.7 %collective-permute-start.4 = (bf16[32,1792]{1,0:T(8,128)(2,1)S(1)}, bf16[32,1792]{1,0:T(8,128)(2,1)S(1)}, u32[]{:S(2)}, u32[]{:S(2)}) collective-permute-start(bf16[32,1792]{1,0:T(8,128)(2,1)S(1)} %get-tuple-element.30), channel_id=1, source_target_pairs={{0,13},{1,2},{2,15},{3,0},{4,9},{5,6},{6,11},{7,4},{8,5},{9,10},{1... | collective-permute-start | bytes 344072 | tf_op jit(solution)/shard_map/ppermute | solution.py:458
  16.0 4.3 %collective-permute-start.6 = (bf16[32,1792]{1,0:T(8,128)(2,1)S(1)}, bf16[32,1792]{1,0:T(8,128)(2,1)S(1)}, u32[]{:S(2)}, u32[]{:S(2)}) collective-permute-start(bf16[32,1792]{1,0:T(8,128)(2,1)S(1)} %collective-permute-done.2.refs_1_), channel_id=1, source_target_pairs={{0,1},{1,0},{2,3},{3,2},{4,5},{5,4},{6,7},{7,6},{8,9},{9,8},{10,11... | collective-permute-start | bytes 344072 | tf_op jit(solution)/shard_map/ppermute | solution.py:452
  19.3 1.3 %collective-permute-start.7 = (bf16[32,1792]{1,0:T(8,128)(2,1)S(1)}, bf16[32,1792]{1,0:T(8,128)(2,1)S(1)}, u32[]{:S(2)}, u32[]{:S(2)}) collective-permute-start(bf16[32,1792]{1,0:T(8,128)(2,1)S(1)} %collective-permute-done.3.refs_2_), channel_id=1, source_target_pairs={{0,1},{1,0},{2,3},{3,2},{4,5},{5,4},{6,7},{7,6},{8,9},{9,8},{10,11... | collective-permute-start | bytes 344072 | tf_op jit(solution)/shard_map/ppermute | solution.py:452
  19.3 1.5 %collective-permute-start.8 = (bf16[32,1792]{1,0:T(8,128)(2,1)S(1)}, bf16[32,1792]{1,0:T(8,128)(2,1)S(1)}, u32[]{:S(2)}, u32[]{:S(2)}) collective-permute-start(bf16[32,1792]{1,0:T(8,128)(2,1)S(1)} %collective-permute-done.4.refs_3_), channel_id=1, source_target_pairs={{0,1},{1,0},{2,3},{3,2},{4,5},{5,4},{6,7},{7,6},{8,9},{9,8},{10,11... | collective-permute-start | bytes 344072 | tf_op jit(solution)/shard_map/ppermute | solution.py:452
  19.8 1.3 %collective-permute-start.5 = (bf16[32,1792]{1,0:T(8,128)(2,1)S(1)}, bf16[32,1792]{1,0:T(8,128)(2,1)S(1)}, u32[]{:S(2)}, u32[]{:S(2)}) collective-permute-start(bf16[32,1792]{1,0:T(8,128)(2,1)S(1)} %collective-permute-done.1.refs_0_), channel_id=1, source_target_pairs={{0,1},{1,0},{2,3},{3,2},{4,5},{5,4},{6,7},{7,6},{8,9},{9,8},{10,11... | collective-permute-start | bytes 344072 | tf_op jit(solution)/shard_map/ppermute | solution.py:452
  24.8 1.4 %collective-permute-start.9 = (bf16[32,1792]{1,0:T(8,128)(2,1)S(1)}, bf16[32,1792]{1,0:T(8,128)(2,1)S(1)}, u32[]{:S(2)}, u32[]{:S(2)}) collective-permute-start(bf16[32,1792]{1,0:T(8,128)(2,1)S(1)} %get-tuple-element.34), channel_id=1, source_target_pairs={{0,1},{1,0},{2,3},{3,2},{4,5},{5,4},{6,7},{7,6},{8,9},{9,8},{10,11... | collective-permute-start | bytes 344072 | tf_op jit(solution)/shard_map/ppermute | solution.py:452
  25.0 3.1 %collective-permute-start.11 = (bf16[32,1792]{1,0:T(8,128)(2,1)S(1)}, bf16[32,1792]{1,0:T(8,128)(2,1)S(1)}, u32[]{:S(2)}, u32[]{:S(2)}) collective-permute-start(bf16[32,1792]{1,0:T(8,128)(2,1)S(1)} %get-tuple-element.36), channel_id=1, source_target_pairs={{0,1},{1,0},{2,3},{3,2},{4,5},{5,4},{6,7},{7,6},{8,9},{9,8},{10,11... | collective-permute-start | bytes 344072 | tf_op jit(solution)/shard_map/ppermute | solution.py:452
  25.4 2.9 %collective-permute-start.13 = (bf16[32,1792]{1,0:T(8,128)(2,1)S(1)}, bf16[32,1792]{1,0:T(8,128)(2,1)S(1)}, u32[]{:S(2)}, u32[]{:S(2)}) collective-permute-start(bf16[32,1792]{1,0:T(8,128)(2,1)S(1)} %get-tuple-element.38), channel_id=1, source_target_pairs={{0,1},{1,0},{2,3},{3,2},{4,5},{5,4},{6,7},{7,6},{8,9},{9,8},{10,11... | collective-permute-start | bytes 344072 | tf_op jit(solution)/shard_map/ppermute | solution.py:452
  25.5 6.3 %collective-permute-start.15 = (bf16[32,1792]{1,0:T(8,128)(2,1)S(1)}, bf16[32,1792]{1,0:T(8,128)(2,1)S(1)}, u32[]{:S(2)}, u32[]{:S(2)}) collective-permute-start(bf16[32,1792]{1,0:T(8,128)(2,1)S(1)} %get-tuple-element.40), channel_id=1, source_target_pairs={{0,1},{1,0},{2,3},{3,2},{4,5},{5,4},{6,7},{7,6},{8,9},{9,8},{10,11... | collective-permute-start | bytes 344072 | tf_op jit(solution)/shard_map/ppermute | solution.py:452
  26.2 6.0 %collective-permute-start.10 = (bf16[32,1792]{1,0:T(8,128)(2,1)S(1)}, bf16[32,1792]{1,0:T(8,128)(2,1)S(1)}, u32[]{:S(2)}, u32[]{:S(2)}) collective-permute-start(bf16[32,1792]{1,0:T(8,128)(2,1)S(1)} %add_convert_fusion.3), channel_id=1, source_target_pairs={{1,0},{14,1},{3,2},{12,3},{5,4},{10,5},{7,6},{8,7},{9,8},{6,9},{11... | collective-permute-start | bytes 344072 | tf_op jit(solution)/shard_map/ppermute | solution.py:461
  28.1 9.7 %collective-permute-start.12 = (bf16[32,1792]{1,0:T(8,128)(2,1)S(1)}, bf16[32,1792]{1,0:T(8,128)(2,1)S(1)}, u32[]{:S(2)}, u32[]{:S(2)}) collective-permute-start(bf16[32,1792]{1,0:T(8,128)(2,1)S(1)} %add_convert_fusion.2), channel_id=1, source_target_pairs={{9,0},{6,1},{11,2},{4,3},{13,4},{2,5},{15,6},{0,7},{1,8},{14,9},{3... | collective-permute-start | bytes 344072 | tf_op jit(solution)/shard_map/ppermute | solution.py:461
  28.3 9.6 %collective-permute-start.14 = (bf16[32,1792]{1,0:T(8,128)(2,1)S(1)}, bf16[32,1792]{1,0:T(8,128)(2,1)S(1)}, u32[]{:S(2)}, u32[]{:S(2)}) collective-permute-start(bf16[32,1792]{1,0:T(8,128)(2,1)S(1)} %add_convert_fusion.1), channel_id=1, source_target_pairs={{5,0},{10,1},{7,2},{8,3},{1,4},{14,5},{3,6},{12,7},{13,8},{2,9},{1... | collective-permute-start | bytes 344072 | tf_op jit(solution)/shard_map/ppermute | solution.py:461
  31.9 7.2 %collective-permute-start.16 = (bf16[32,1792]{1,0:T(8,128)(2,1)S(1)}, bf16[32,1792]{1,0:T(8,128)(2,1)S(1)}, u32[]{:S(2)}, u32[]{:S(2)}) collective-permute-start(bf16[32,1792]{1,0:T(8,128)(2,1)S(1)} %add_convert_fusion), channel_id=1, source_target_pairs={{13,0},{2,1},{15,2},{0,3},{9,4},{6,5},{11,6},{4,7},{5,8},{10,9},{7... | collective-permute-start | bytes 344072 | tf_op jit(solution)/shard_map/ppermute | solution.py:461
  39.4 1.9 %collective-permute-start.17 = (bf16[8,7168]{1,0:T(8,128)(2,1)S(1)}, bf16[8,7168]{1,0:T(8,128)(2,1)S(1)}, u32[]{:S(2)}, u32[]{:S(2)}) collective-permute-start(bf16[8,7168]{1,0:T(8,128)(2,1)S(1)} %get-tuple-element.42), channel_id=1, source_target_pairs={{0,1},{1,0},{2,3},{3,2},{4,5},{5,4},{6,7},{7,6},{8,9},{9,8},{10,11... | collective-permute-start | bytes 344072 | tf_op jit(solution)/shard_map/ppermute | solution.py:452

commit v14 on v13

--- a/solution.py
+++ b/solution.py
@@ -43,16 +43,16 @@
 
 
 def distance(turn, core, chips):
-    bits = (chips // 2).bit_length() - 1
-    even = 0
-    for b in range(bits):
-        even = even + ((turn >> b) % 2 << (bits - b))
-    return even ^ (core * (chips - 1))
+    return jnp.where(turn == 0, 0, (2 * turn) ^ (core * (chips - 1)))
 
 
 def expert_at(turn, chips):
     place = lax.axis_index("afd")
     return (distance(turn, place % 2, chips) ^ (place // 2)) // (chips // EXPERTS)
+
+
+def expert_across(chips):
+    return (lax.axis_index("afd") // 2 ^ (chips - 1)) // (chips // EXPERTS)
 
 
 def spread(ref, k, where, steps, rows, empty):
@@ -81,7 +81,27 @@
     return out.astype(BF16)
 
 
+def choose(steps, expert, place, lines, tails, parts):
+    both, width = parts[0].shape
+    rows = both // steps
+    piece = width // PIECES
+    stacked = jnp.concatenate([x.astype(F32) for x in tails] * PIECES, axis=0).astype(BF16)
+    count = stacked.shape[0]
+    line = iota((lines, LANES), 0)
+    named = nt_dot(one_hot(iota(line.shape, 1) == PARTS * EXPERTS + expert(line)), stacked)
+    at = iota((count, count), 0)
+    to = iota((count, count), 1)
+    before = one_hot((at // rows == to // rows) & (at < to))
+    rank = dot(named.astype(BF16), before)
+    line = iota(named.shape, 0)
+    same = place(line) == iota(named.shape, 1) // rows
+    picks = one_hot(same & (named > 0.5) & (rank == (line % CAP).astype(F32)))
+    data = [x[:, k * piece : (k + 1) * piece].astype(F32) for k in range(PIECES) for x in parts]
+    return dot(picks, jnp.concatenate(data, axis=0).astype(BF16)).astype(BF16)
+
+
 def attend_kernel(
+    chips,
     len_hbm,
     ids_hbm,
     weight_hbm,
@@ -93,6 +113,7 @@
     dn_hbm,
     resid_ref,
     out_ref,
+    across_ref,
     dn_ref,
     len_ref,
     ids_ref,
@@ -168,23 +189,29 @@
     gain = jnp.concatenate([gain[i : i + 1] for i in range(width // LANES)], axis=1)
     normed = resid * lax.rsqrt(meansq + 1e-06) * gain
     out_ref[:, :width] = normed.astype(BF16)
-    out_ref[:, width:] = tail(ids_ref, weight_ref, steps, rows)
+    ends = tail(ids_ref, weight_ref, steps, rows)
+    out_ref[:, width:] = ends
+    lines = across_ref.shape[0]
+    across_ref[...] = choose(
+        steps, lambda n: expert_across(chips), lambda n: n // CAP, lines, [ends], [normed]
+    )
     down.wait()
 
 
-def attend(cache_len, ids, weights, queries, fresh, kv_cache, hidden_state, norm_gain, down):
+def attend(chips, cache_len, ids, weights, queries, fresh, kv_cache, hidden_state, norm_gain, down):
     steps, rows, width = queries.shape
     kv = kv_cache.transpose(0, 2, 1)
     gain = norm_gain.reshape(width // LANES, LANES)
     return pl.pallas_call(
-        attend_kernel,
+        functools.partial(attend_kernel, chips),
         out_shape=(
             jax.ShapeDtypeStruct((steps * rows, width), F32),
             jax.ShapeDtypeStruct((steps * rows, width + LANES), BF16),
+            jax.ShapeDtypeStruct((PIECES * steps * CAP, width // PIECES), BF16),
             jax.ShapeDtypeStruct(down.shape[1:], BF16),
         ),
         in_specs=[HBM] * 9,
-        out_specs=(VMEM, VMEM, VMEM),
+        out_specs=(VMEM,) * 4,
         scratch_shapes=[
             pltpu.SMEM(cache_len.shape, jnp.int32),
             pltpu.SMEM(ids.shape, jnp.int32),
@@ -205,46 +232,38 @@
     )(*in_hbm(cache_len, ids, weights, queries, fresh, kv, hidden_state, gain, down))
 
 
-def pack_kernel(steps, chips, own_ref, other_ref, *outs):
-    both, width = own_ref.shape
-    width -= LANES
-    rows = both // steps
-    piece = width // PIECES
-    side_lines = steps * CAP
-    lines = PIECES * 2 * side_lines
-    tails = [ref[:, width:].astype(F32) for ref in (own_ref, other_ref)]
-    tails = jnp.concatenate(tails * PIECES, axis=0).astype(BF16)
-    count = 2 * both * PIECES
-    row = iota((len(outs) * lines, LANES), 0)
-    lane = iota((len(outs) * lines, LANES), 1)
-    wanted = one_hot(lane == PARTS * EXPERTS + expert_at(row // lines, chips))
-    named = nt_dot(wanted, tails)
-    at = iota((count, count), 0)
-    to = iota((count, count), 1)
-    before = one_hot((at // rows == to // rows) & (at < to))
-    rank = dot(named.astype(BF16), before)
-    line = iota(named.shape, 0)
-    col = iota(named.shape, 1)
-    same = (line // CAP) % (lines // CAP) == col // rows
-    picks = one_hot(same & (named > 0.5) & (rank == (line % CAP).astype(F32)))
-    parts = [ref[:, :width].astype(F32) for ref in (own_ref, other_ref)]
-    stacked = jnp.concatenate(
-        [part[:, k * piece : (k + 1) * piece] for k in range(PIECES) for part in parts], axis=0
-    ).astype(BF16)
-    sent = dot(picks, stacked).astype(BF16)
+def pack_kernel(steps, chips, own_ref, other_ref, home_ref, away_ref, *outs):
+    width = own_ref.shape[1] - LANES
+    lines = PIECES * 2 * steps * CAP
+
+    def place(n):
+        at = n // CAP % (lines // CAP)
+        side, k = at // (PIECES * steps), at // steps % PIECES
+        return jnp.where(n < lines, (k * 2 + side) * steps + at % steps, at)
+
+    sent = choose(
+        steps,
+        lambda n: expert_at(n // lines, chips),
+        place,
+        (1 + len(outs)) * lines,
+        [own_ref[:, width:], other_ref[:, width:]],
+        [own_ref[:, :width], other_ref[:, :width]],
+    )
+    home_ref[...] = sent[: lines // 2]
+    away_ref[...] = sent[lines // 2 : lines]
     for t, out in enumerate(outs):
-        out[...] = sent[t * lines : (t + 1) * lines]
+        out[...] = sent[(t + 1) * lines : (t + 2) * lines]
 
 
 def pack(steps, chips, own, other):
-    both, width = own.shape
-    shape = (PIECES * 2 * steps * CAP, (width - LANES) // PIECES)
-    turns = chips // 2
+    lines, piece = PIECES * 2 * steps * CAP, (own.shape[1] - LANES) // PIECES
+    half = jax.ShapeDtypeStruct((lines // 2, piece), BF16)
+    turns = [jax.ShapeDtypeStruct((lines, piece), BF16)] * (chips // 2 - 1)
     return pl.pallas_call(
         functools.partial(pack_kernel, steps, chips),
-        out_shape=[jax.ShapeDtypeStruct(shape, BF16)] * turns,
+        out_shape=[half, half, *turns],
         in_specs=[VMEM] * 2,
-        out_specs=[VMEM] * turns,
+        out_specs=[VMEM] * (2 + len(turns)),
         compiler_params=pltpu.CompilerParams(vmem_limit_bytes=24 * MIB),
         cost_estimate=pl.CostEstimate(
             flops=50_000_000, bytes_accessed=2_000_000, transcendentals=0
@@ -253,25 +272,21 @@
     )(own, other)
 
 
-def mixing(steps, chips, own_ref, other_ref):
-    both, width = own_ref.shape
-    width -= LANES
+def mixing(steps, expert, sides, lines, count, tails):
+    both = tails[0].shape[0]
     rows = both // steps
-    lines = PIECES * 2 * steps * CAP
-    tails = [ref[:, width:].astype(F32) for ref in (own_ref, other_ref)]
-    tails = jnp.concatenate(tails, axis=0).astype(BF16)
-    count = chips // 2 * lines
+    tails = jnp.concatenate([x.astype(F32) for x in tails], axis=0).astype(BF16)
     lane = iota((LANES, count), 0)
-    expert = expert_at(iota((LANES, count), 1) // lines, chips)
-    found = [dot(tails, one_hot(lane == part * EXPERTS + expert)) for part in range(PARTS + 1)]
-    at = iota((2 * both, 2 * both), 1)
-    to = iota((2 * both, 2 * both), 0)
+    named_by = expert(iota((LANES, count), 1) // lines)
+    found = [dot(tails, one_hot(lane == part * EXPERTS + named_by)) for part in range(PARTS + 1)]
+    at = iota((sides * both, sides * both), 1)
+    to = iota((sides * both, sides * both), 0)
     rank = dot(one_hot((at // rows == to // rows) & (at < to)), found[PARTS].astype(BF16))
-    line = iota((2 * both, count), 1)
-    row = iota((2 * both, count), 0)
-    same = (line // CAP) % (2 * steps) == row // rows
+    line = iota((sides * both, count), 1)
+    row = iota((sides * both, count), 0)
+    same = (line // CAP) % (sides * steps) == row // rows
     slot = same & (rank == (line % CAP).astype(F32))
-    k_of = line // (2 * steps * CAP) % PIECES
+    k_of = line // (sides * steps * CAP) % PIECES
     parts = [
         jnp.where(slot & (k_of == k), found[part], 0.0)
         for part in range(PARTS)
@@ -307,18 +322,36 @@
     )(*in_hbm(gate_up))
 
 
-def mix_kernel(steps, chips, own_ref, other_ref, mix_ref):
-    mix_ref[...] = mixing(steps, chips, own_ref, other_ref)
+def mix_kernel(steps, chips, own_ref, other_ref, mix_ref, last_ref):
+    width = own_ref.shape[1] - LANES
+    own, other = own_ref[:, width:], other_ref[:, width:]
+    lines = PIECES * steps * CAP
+    mix_ref[...] = mixing(
+        steps, lambda t: expert_at(t + 1, chips), 2, 2 * lines, mix_ref.shape[1], [own, other]
+    )
+    last_ref[...] = mixing(
+        steps,
+        lambda t: jnp.where(t == 0, expert_across(chips), expert_at(0 * t, chips)),
+        1,
+        lines,
+        last_ref.shape[1],
+        [own],
+    )
 
 
 def mixer(steps, chips, own, other):
-    lines = PIECES * 2 * steps * CAP
-    shape = (PARTS * PIECES * 2 * own.shape[0], chips // 2 * lines)
+    both = own.shape[0]
+    lines = PIECES * steps * CAP
     return pl.pallas_call(
         functools.partial(mix_kernel, steps, chips),
-        out_shape=jax.ShapeDtypeStruct(shape, BF16),
+        out_shape=(
+            jax.ShapeDtypeStruct(
+                (PARTS * PIECES * 2 * both, (chips // 2 - 1) * 2 * lines), BF16
+            ),
+            jax.ShapeDtypeStruct((PARTS * PIECES * both, 2 * lines), BF16),
+        ),
         in_specs=[VMEM, VMEM],
-        out_specs=VMEM,
+        out_specs=(VMEM, VMEM),
         compiler_params=pltpu.CompilerParams(vmem_limit_bytes=24 * MIB),
         cost_estimate=pl.CostEstimate(
             flops=10_000_000, bytes_accessed=1_000_000, transcendentals=0
@@ -327,25 +360,37 @@
     )(own, other)
 
 
-def expert_kernel(turns, *refs):
-    own_refs, other_refs = refs[:turns], refs[turns : 2 * turns]
-    w_in, w_down = refs[2 * turns : 2 * turns + 2]
-    mine_refs = refs[2 * turns + 2 : 3 * turns + 2]
-    theirs_refs = refs[3 * turns + 2 :]
-    lines, piece = own_refs[0].shape
-    per = lines // PIECES
-    half = turns * per
-    n = turns * lines
-    row = iota((n, n), 0)
-    col = iota((n, n), 1)
-    order = one_hot(col == row // per % turns * lines + row // half * per + row % per)
-    sides = [
-        dot(order, jnp.concatenate([ref[...] for ref in now], axis=0)).astype(BF16)
-        for now in (own_refs, other_refs)
+def regroup(heights, back):
+    n = sum(heights)
+    per_k = n // PIECES
+    target = iota((n, n), 1 if back else 0)
+    source = iota((n, n), 0 if back else 1)
+    k, x = target // per_k, target % per_k
+    line = target
+    start = 0
+    for height in heights:
+        per = height // PIECES
+        at = start + k * per + x - start // PIECES
+        line = jnp.where(x >= start // PIECES, at, line)
+        start += height
+    return one_hot(source == line)
+
+
+def expert_kernel(count, *refs):
+    sides = refs[:count], refs[count : 2 * count]
+    w_in, w_down = refs[2 * count : 2 * count + 2]
+    outs = refs[2 * count + 2 :]
+    heights = [ref.shape[0] for ref in sides[0]]
+    piece = sides[0][0].shape[1]
+    half = sum(heights) // PIECES
+    order = regroup(heights, False)
+    rows = [
+        dot(order, jnp.concatenate([ref[...] for ref in side], axis=0)).astype(BF16)
+        for side in sides
     ]
     gate = upper = None
     for k in range(PIECES):
-        x = jnp.concatenate([side[k * half : (k + 1) * half] for side in sides], axis=0)
+        x = jnp.concatenate([side[k * half : (k + 1) * half] for side in rows], axis=0)
         cols = pl.ds(k * piece, piece)
         g, u = nt_dot(x, w_in[0, :, cols]), nt_dot(x, w_in[1, :, cols])
         gate, upper = (g, u) if k == 0 else (gate + g, upper + u)
@@ -356,59 +401,65 @@
         part = dot(act, w_down[:, k * piece : (k + 1) * piece]).astype(BF16)
         mine.append(part[:half])
         theirs.append(part[half:])
-    back = one_hot(row == col // per % turns * lines + col // half * per + col % per)
-    for parts, now in ((theirs, theirs_refs), (mine, mine_refs)):
+    back = regroup(heights, True)
+    for parts, now in ((theirs, outs[len(outs) // 2 :]), (mine, outs[: len(outs) // 2])):
         out = dot(back, jnp.concatenate(parts, axis=0)).astype(BF16)
-        for t, ref in enumerate(now):
-            ref[...] = out[t * lines : (t + 1) * lines]
-
-
-def experts(own, other, gate_up, down):
-    turns = len(own)
-    shape = jax.ShapeDtypeStruct(own[0].shape, BF16)
+        start = 0
+        for ref in now:
+            ref[...] = out[start : start + ref.shape[0]]
+            start += ref.shape[0]
+
+
+def experts(own, other, heights, gate_up, down):
+    shapes = [jax.ShapeDtypeStruct((height, own[0].shape[1]), BF16) for height in heights]
     results = pl.pallas_call(
-        functools.partial(expert_kernel, turns),
-        out_shape=[shape] * (2 * turns),
-        in_specs=[VMEM] * (2 * turns + 2),
-        out_specs=[VMEM] * (2 * turns),
+        functools.partial(expert_kernel, len(own)),
+        out_shape=shapes + shapes,
+        in_specs=[VMEM] * (2 * len(own) + 2),
+        out_specs=[VMEM] * (2 * len(shapes)),
         compiler_params=pltpu.CompilerParams(vmem_limit_bytes=32 * MIB),
         cost_estimate=pl.CostEstimate(
             flops=800_000_000, bytes_accessed=12_000_000, transcendentals=16384
         ),
         name="experts",
     )(*own, *other, gate_up, down)
-    return results[:turns], results[turns:]
-
-
-def combine_kernel(mix_ref, resid_ref, *refs):
-    back_refs, (kept_ref, sent_ref) = refs[:-2], refs[-2:]
+    return results[: len(shapes)], results[len(shapes) :]
+
+
+def mixed(mix_ref, back_refs, rows):
+    product = dot(mix_ref[...], jnp.concatenate([ref[...] for ref in back_refs], axis=0))
+    n = PIECES * rows
+    total = product[:n] + product[n : 2 * n] + product[2 * n :]
+    return [total[k * rows : (k + 1) * rows] for k in range(PIECES)]
+
+
+def combine_kernel(mix_ref, last_ref, resid_ref, across_ref, home_ref, *refs):
+    back_refs, (kept_ref, given_ref) = refs[:-2], refs[-2:]
     both = resid_ref.shape[0]
-    piece = back_refs[0].shape[1]
-    product = dot(mix_ref[...], jnp.concatenate([ref[...] for ref in back_refs], axis=0))
-    n = PIECES * 2 * both
-    total = product[:n] + product[n : 2 * n] + product[2 * n :]
+    piece = home_ref.shape[1]
+    turns = mixed(mix_ref, back_refs, 2 * both)
+    last = mixed(last_ref, [across_ref, home_ref], both)
     for k in range(PIECES):
         cols = pl.ds(k * piece, piece)
-        first = k * 2 * both
-        kept_ref[:, cols] = resid_ref[:, cols] + total[first : first + both]
-        sent_ref[:, cols] = total[first + both : first + 2 * both].astype(BF16)
-
-
-def combine(mix, resid, backs):
+        kept_ref[:, cols] = resid_ref[:, cols] + turns[k][:both] + last[k]
+        given_ref[:, cols] = turns[k][both:].astype(BF16)
+
+
+def combine(mix, mix_last, resid, across, home, backs):
     return pl.pallas_call(
         combine_kernel,
         out_shape=(
             jax.ShapeDtypeStruct(resid.shape, F32),
             jax.ShapeDtypeStruct(resid.shape, BF16),
         ),
-        in_specs=[VMEM] * (2 + len(backs)),
+        in_specs=[VMEM] * (5 + len(backs)),
         out_specs=(VMEM, VMEM),
         compiler_params=pltpu.CompilerParams(vmem_limit_bytes=24 * MIB),
         cost_estimate=pl.CostEstimate(
             flops=100_000_000, bytes_accessed=1_000_000, transcendentals=0
         ),
         name="combine",
-    )(mix, resid, *backs)
+    )(mix, mix_last, resid, across, home, *backs)
 
 
 def finish_kernel(kept_ref, other_ref, out_ref):
@@ -452,35 +503,52 @@
         return lax.ppermute(x, "afd", cores)
 
     def route(t):
-        return [(i, (i // 2 ^ distance(t, i % 2, chips)) * 2 + 1 - i % 2) for i in range(owners)]
-
-    def send(x, t):
-        return lax.ppermute(x, "afd", route(t))
-
-    def send_back(x, t):
-        return lax.ppermute(x, "afd", [(j, i) for i, j in route(t)])
+        return [
+            (i, ((i // 2 ^ 2 * t ^ i % 2 * (chips - 1)) * 2 + 1 - i % 2)) for i in range(owners)
+        ]
+
+    def route_across():
+        return [
+            (i, (i // 2 ^ (chips - 1)) * 2 + (i % 2 ^ (i // 2 >= turns))) for i in range(owners)
+        ]
+
+    def send(x, to):
+        return lax.ppermute(x, "afd", to)
+
+    def send_back(x, to):
+        return lax.ppermute(x, "afd", [(j, i) for i, j in to])
 
     ids = expert_ids.transpose(2, 0, 1)
     weights = route_weight.transpose(2, 0, 1)
-    resid, normed, w_down = attend(
-        cache_len, ids, weights, queries, fresh, kv_cache, hidden_state, norm_gain, down
-    )
+    resid, normed, sent_across, w_down = attend(
+        chips, cache_len, ids, weights, queries, fresh, kv_cache, hidden_state, norm_gain, down
+    )
+    across = send(sent_across, route_across())
     normed_other = swap(normed)
-    sent = pack(steps, chips, normed, normed_other)
-    own = [send(sent[t], t) for t in range(turns)]
+    home, away, *sent = pack(steps, chips, normed, normed_other)
+    across, sent = lax.optimization_barrier((across, sent))
+    own = [send(x, route(t + 1)) for t, x in enumerate(sent)]
     w_in = stage(gate_up)
-    mix = mixer(steps, chips, normed, normed_other)
-    own[0], w_in = lax.optimization_barrier((own[0], w_in))
-    other = [swap(x) for x in own]
+    mix, mix_last = mixer(steps, chips, normed, normed_other)
+    own[0], w_in, mix = lax.optimization_barrier((own[0], w_in, mix))
+    mines = [across, home, *own[: TOGETHER - 1]]
+    others = [swap(across), away, *[swap(x) for x in own[: TOGETHER - 1]]]
+    small, large = sent_across.shape[0], sent[0].shape[0]
     summed = []
-    for t in range(0, turns, TOGETHER):
-        now = slice(t, t + TOGETHER)
-        mine, theirs = experts(own[now], other[now], w_in, w_down)
+    for first in range(0, turns, TOGETHER):
+        heights = [large] * TOGETHER
+        if first:
+            now = slice(first - 1, first + TOGETHER - 1)
+            mines = own[now]
+            others = [swap(x) for x in mines]
+        mine, theirs = experts(mines, others, heights, w_in, w_down)
         summed += [
             (a.astype(F32) + swap(b).astype(F32)).astype(BF16) for a, b in zip(mine, theirs)
         ]
-    backs = [send_back(summed[t], t) for t in range(turns)]
-    kept, given = combine(mix, resid, backs)
+    last, summed = summed[0], summed[1:]
+    backs = [send_back(x, route(t + 1)) for t, x in enumerate(summed)]
+    back_across = send_back(last[:small], route_across())
+    kept, given = combine(mix, mix_last, resid, back_across, last[small:], backs)
     return finish(queries.shape, kept, swap(given))
 
 

time: 42.1 us -> 44.5 us (1.057)
  the two profiles are of different devices: /device:TPU:0 before, /device:TPU:21 now
where the time goes in v14:
time: 44.5 us; the launch traced here: 44.3 us
  waiting for transfers between devices  17.7 us (40%)
  starting transfers between devices  15.2 us (34%)
  Pallas kernels  11.2 us (25%)
    ppermute x4, waiting for transfers between devices, send_back(): return lax.ppermute(x, 'afd', [(j, i) for i, j in to])  8.86 us
    ppermute x4, waiting for transfers between devices, send(): return lax.ppermute(x, 'afd', to)  6.31 us
    ppermute x4, starting transfers between devices, send(): return lax.ppermute(x, 'afd', to)  5.81 us
    ppermute x10, starting transfers between devices, swap(): return lax.ppermute(x, 'afd', cores)  5.03 us
    ppermute x4, starting transfers between devices, send_back(): return lax.ppermute(x, 'afd', [(j, i) for i, j in to])  4.38 us
    pallas_call x1, Pallas kernels, experts(): pl.pallas_call(functools.partial(expert_kernel, len(own)), out_shape=shap...  3.62 us
    pallas_call x1, Pallas kernels, stage(): pl.pallas_call(stage_kernel, out_shape=jax.ShapeDtypeStruct(gate_up.shape...  3.17 us
    ppermute x10, waiting for transfers between devices, swap(): return lax.ppermute(x, 'afd', cores)  2.53 us
  transfers between devices with their start and end apart: 18, of which 7 were waited for; matrix products, arithmetic and copies ran while one was open for 0% of the time, Pallas kernels for 9%

profile of v14, /device:TPU:21, one launch (start us, length us, event | category | flops | bytes accessed | tf_op | source)
XLA Modules:
  0.0 44.3 jit_solution(1461205515398895916)
XLA Ops:
  0.0 2.4 %attend.1 = (f32[8,7168]{1,0:T(8,128)S(1)}, bf16[8,7296]{1,0:T(8,128)(2,1)S(1)}, bf16[16,1792]{1,0:T(8,128)(2,1)S(1)}, bf16[256,7168]{1,0:T(8,128)(2,1)S(1)}) custom-call(s32[4]{0:T(128)} %len_hbm.1, s32[3,2,4]{2,1,0:T(2,128)} %bitcast.6, f32[3,2,4]{2,1,0:T(2,128)} %bitcast.7, bf16[2,4,7168]{2,1,0:T(4,128)(2,1)} %q_hbm.1, bf16[2,4,448]{2,1,0:T(4,128)(2,1)} %fresh_hbm.1, ...), custom_call_target="tpu_custom_call" | custom-call | flops 300000000 | bytes 2000000 | tf_op jit(solution)/shard_map/attend/pallas_call | solution.py:205
  2.4 0.7 %collective-permute-start.1 = (bf16[8,7296]{1,0:T(8,128)(2,1)S(1)}, bf16[8,7296]{1,0:T(8,128)(2,1)S(1)}, u32[]{:S(2)}, u32[]{:S(2)}) collective-permute-start(bf16[8,7296]{1,0:T(8,128)(2,1)S(1)} %get-tuple-element.34.own_ref), channel_id=1, source_target_pairs={{0,1},{1,0},{2,3},{3,2},{4,5},{5,4},{6,7},{7,6},{8,9},{9,8},{10,11... | collective-permute-start | bytes 350216 | tf_op jit(solution)/shard_map/ppermute | solution.py:503
  3.1 1.0 %collective-permute-start = (bf16[16,1792]{1,0:T(8,128)(2,1)S(1)}, bf16[16,1792]{1,0:T(8,128)(2,1)S(1)}, u32[]{:S(2)}, u32[]{:S(2)}) collective-permute-start(bf16[16,1792]{1,0:T(8,128)(2,1)S(1)} %get-tuple-element.33), channel_id=1, source_target_pairs={{0,14},{1,15},{2,12},{3,13},{4,10},{5,11},{6,8},{7,9},{8,7},{9,6},... | collective-permute-start | bytes 172040 | tf_op jit(solution)/shard_map/ppermute | solution.py:516
  4.2 0.5 %pack.1 = (bf16[16,1792]{1,0:T(8,128)(2,1)S(1)}, bf16[16,1792]{1,0:T(8,128)(2,1)S(1)}, bf16[32,1792]{1,0:T(8,128)(2,1)S(1)}, bf16[32,1792]{1,0:T(8,128)(2,1)S(1)}, bf16[32,1792]{1,0:T(8,128)(2,1)S(1)}) custom-call(bf16[8,7296]{1,0:T(8,128)(2,1)S(1)} %get-tuple-element.34.own_ref, bf16[8,7296]{1,0:T(8,128)(2,1)S(1)} %collective-permute-done.1.other_ref), custom_call_target="tpu_custom_call" | custom-call | flops 50000000 | bytes 2000000 | tf_op jit(solution)/shard_map/pack/pallas_call | solution.py:262
  4.7 2.8 %collective-permute-done.refs_0_ = bf16[16,1792]{1,0:T(8,128)(2,1)S(1)} collective-permute-done((bf16[16,1792]{1,0:T(8,128)(2,1)S(1)}, bf16[16,1792]{1,0:T(8,128)(2,1)S(1)}, u32[]{:S(2)}, u32[]{:S(2)}) %collective-permute-start) | collective-permute-done | bytes 57376 | tf_op jit(solution)/shard_map/ppermute | solution.py:516
  7.5 3.0 %collective-permute-start.2 = (bf16[32,1792]{1,0:T(8,128)(2,1)S(1)}, bf16[32,1792]{1,0:T(8,128)(2,1)S(1)}, u32[]{:S(2)}, u32[]{:S(2)}) collective-permute-start(bf16[32,1792]{1,0:T(8,128)(2,1)S(1)} %get-tuple-element.38), channel_id=1, source_target_pairs={{0,5},{1,10},{2,7},{3,8},{4,1},{5,14},{6,3},{7,12},{8,13},{9,2},{1... | collective-permute-start | bytes 344072 | tf_op jit(solution)/shard_map/ppermute | solution.py:516
  10.5 1.8 %collective-permute-start.3 = (bf16[32,1792]{1,0:T(8,128)(2,1)S(1)}, bf16[32,1792]{1,0:T(8,128)(2,1)S(1)}, u32[]{:S(2)}, u32[]{:S(2)}) collective-permute-start(bf16[32,1792]{1,0:T(8,128)(2,1)S(1)} %get-tuple-element.46), channel_id=1, source_target_pairs={{0,9},{1,6},{2,11},{3,4},{4,13},{5,2},{6,15},{7,0},{8,1},{9,14},{1... | collective-permute-start | bytes 344072 | tf_op jit(solution)/shard_map/ppermute | solution.py:516
  12.3 3.2 %stage.1.refs_10_ = bf16[2,256,7168]{2,1,0:T(8,128)(2,1)S(1)} custom-call(bf16[1,2,256,7168]{3,2,1,0:T(8,128)(2,1)} %gu_hbm.1), custom_call_target="tpu_custom_call" | custom-call | bytes 16000000 | tf_op jit(solution)/shard_map/stage/pallas_call | solution.py:313
  15.5 0.4 mixer.1
  15.9 0.8 %collective-permute-done.3.refs_3_ = bf16[32,1792]{1,0:T(8,128)(2,1)S(1)} collective-permute-done((bf16[32,1792]{1,0:T(8,128)(2,1)S(1)}, bf16[32,1792]{1,0:T(8,128)(2,1)S(1)}, u32[]{:S(2)}, u32[]{:S(2)}) %collective-permute-start.3) | collective-permute-done | bytes 114720 | tf_op jit(solution)/shard_map/ppermute | solution.py:516
  16.7 0.9 %collective-permute-start.7 = (bf16[32,1792]{1,0:T(8,128)(2,1)S(1)}, bf16[32,1792]{1,0:T(8,128)(2,1)S(1)}, u32[]{:S(2)}, u32[]{:S(2)}) collective-permute-start(bf16[32,1792]{1,0:T(8,128)(2,1)S(1)} %collective-permute-done.3.refs_3_), channel_id=1, source_target_pairs={{0,1},{1,0},{2,3},{3,2},{4,5},{5,4},{6,7},{7,6},{8,9},{9,8},{10,11... | collective-permute-start | bytes 344072 | tf_op jit(solution)/shard_map/ppermute | solution.py:503
  17.6 2.7 %collective-permute-done.4.refs_4_ = bf16[32,1792]{1,0:T(8,128)(2,1)S(1)} collective-permute-done((bf16[32,1792]{1,0:T(8,128)(2,1)S(1)}, bf16[32,1792]{1,0:T(8,128)(2,1)S(1)}, u32[]{:S(2)}, u32[]{:S(2)}) %collective-permute-start.4) | collective-permute-done | bytes 114720 | tf_op jit(solution)/shard_map/ppermute | solution.py:516
  20.3 0.5 %collective-permute-start.6 = (bf16[32,1792]{1,0:T(8,128)(2,1)S(1)}, bf16[32,1792]{1,0:T(8,128)(2,1)S(1)}, u32[]{:S(2)}, u32[]{:S(2)}) collective-permute-start(bf16[32,1792]{1,0:T(8,128)(2,1)S(1)} %collective-permute-done.2.refs_2_), channel_id=1, source_target_pairs={{0,1},{1,0},{2,3},{3,2},{4,5},{5,4},{6,7},{7,6},{8,9},{9,8},{10,11... | collective-permute-start | bytes 344072 | tf_op jit(solution)/shard_map/ppermute | solution.py:503
  20.8 1.2 %collective-permute-done.5.refs_5_ = bf16[16,1792]{1,0:T(8,128)(2,1)S(1)} collective-permute-done((bf16[16,1792]{1,0:T(8,128)(2,1)S(1)}, bf16[16,1792]{1,0:T(8,128)(2,1)S(1)}, u32[]{:S(2)}, u32[]{:S(2)}) %collective-permute-start.5) | collective-permute-done | bytes 57376 | tf_op jit(solution)/shard_map/ppermute | solution.py:503
  22.0 3.6 %experts.1 = (bf16[32,1792]{1,0:T(8,128)(2,1)S(1)}, bf16[32,1792]{1,0:T(8,128)(2,1)S(1)}, bf16[32,1792]{1,0:T(8,128)(2,1)S(1)}, bf16[32,1792]{1,0:T(8,128)(2,1)S...) custom-call(bf16[16,1792]{1,0:T(8,128)(2,1)S(1)} %collective-permute, ...), custom_call_target="tpu_custom_call" | custom-call | flops 800000000 | bytes 12000000 | tf_op jit(solution)/shard_map/experts/pallas_call | solution.py:415
  27.1 1.2 %collective-permute-start.12 = (bf16[32,1792]{1,0:T(8,128)(2,1)S(1)}, bf16[32,1792]{1,0:T(8,128)(2,1)S(1)}, u32[]{:S(2)}, u32[]{:S(2)}) collective-permute-start(bf16[32,1792]{1,0:T(8,128)(2,1)S(1)} %add_convert_fusion.2), channel_id=1, source_target_pairs={{5,0},{10,1},{7,2},{8,3},{1,4},{14,5},{3,6},{12,7},{13,8},{2,9},{1... | collective-permute-start | bytes 344072 | tf_op jit(solution)/shard_map/ppermute | solution.py:519
  28.3 1.9 %collective-permute-start.14 = (bf16[32,1792]{1,0:T(8,128)(2,1)S(1)}, bf16[32,1792]{1,0:T(8,128)(2,1)S(1)}, u32[]{:S(2)}, u32[]{:S(2)}) collective-permute-start(bf16[32,1792]{1,0:T(8,128)(2,1)S(1)} %add_convert_fusion.1), channel_id=1, source_target_pairs={{9,0},{6,1},{11,2},{4,3},{13,4},{2,5},{15,6},{0,7},{1,8},{14,9},{3... | collective-permute-start | bytes 344072 | tf_op jit(solution)/shard_map/ppermute | solution.py:519
  30.3 0.4 collective-permute-start.16
  30.7 0.9 %collective-permute-start.10 = (bf16[16,1792]{1,0:T(8,128)(2,1)S(1)}, bf16[16,1792]{1,0:T(8,128)(2,1)S(1)}, u32[]{:S(2)}, u32[]{:S(2)}) collective-permute-start(bf16[16,1792]{1,0:T(8,128)(2,1)S(1)} %get-tuple-element.62), channel_id=1, source_target_pairs={{14,0},{15,1},{12,2},{13,3},{10,4},{11,5},{8,6},{9,7},{7,8},{6,9},... | collective-permute-start | bytes 172040 | tf_op jit(solution)/shard_map/ppermute | solution.py:519
  31.6 8.8 %collective-permute-done.10.across_ref = bf16[16,1792]{1,0:T(8,128)(2,1)S(1)} collective-permute-done((bf16[16,1792]{1,0:T(8,128)(2,1)S(1)}, bf16[16,1792]{1,0:T(8,128)(2,1)S(1)}, u32[]{:S(2)}, u32[]{:S(2)}) %collective-permute-start.10) | collective-permute-done | bytes 57376 | tf_op jit(solution)/shard_map/ppermute | solution.py:519
  40.5 0.4 combine.1
  40.9 1.8 %collective-permute-start.17 = (bf16[8,7168]{1,0:T(8,128)(2,1)S(1)}, bf16[8,7168]{1,0:T(8,128)(2,1)S(1)}, u32[]{:S(2)}, u32[]{:S(2)}) collective-permute-start(bf16[8,7168]{1,0:T(8,128)(2,1)S(1)} %get-tuple-element.60), channel_id=1, source_target_pairs={{0,1},{1,0},{2,3},{3,2},{4,5},{5,4},{6,7},{7,6},{8,9},{9,8},{10,11... | collective-permute-start | bytes 344072 | tf_op jit(solution)/shard_map/ppermute | solution.py:503
  42.7 1.0 %collective-permute-done.17.other_ref = bf16[8,7168]{1,0:T(8,128)(2,1)S(1)} collective-permute-done((bf16[8,7168]{1,0:T(8,128)(2,1)S(1)}, bf16[8,7168]{1,0:T(8,128)(2,1)S(1)}, u32[]{:S(2)}, u32[]{:S(2)}) %collective-permute-start.17) | collective-permute-done | bytes 114720 | tf_op jit(solution)/shard_map/ppermute | solution.py:503
  43.6 0.7 %finish.1 = bf16[2,4,7168]{2,1,0:T(4,128)(2,1)} custom-call(f32[8,7168]{1,0:T(8,128)S(1)} %get-tuple-element.59.kept_ref, bf16[8,7168]{1,0:T(8,128)(2,1)S(1)} %collective-permute-done.17.other_ref), custom_call_target="tpu_custom_call" | custom-call | flops 100000 | bytes 500000 | tf_op jit(solution)/shard_map/finish/pallas_call | solution.py:473
  (24 shorter events, 1.6 us)
Async XLA Ops:
  2.4 1.8 %collective-permute-start.1 = (bf16[8,7296]{1,0:T(8,128)(2,1)S(1)}, bf16[8,7296]{1,0:T(8,128)(2,1)S(1)}, u32[]{:S(2)}, u32[]{:S(2)}) collective-permute-start(bf16[8,7296]{1,0:T(8,128)(2,1)S(1)} %get-tuple-element.34.own_ref), channel_id=1, source_target_pairs={{0,1},{1,0},{2,3},{3,2},{4,5},{5,4},{6,7},{7,6},{8,9},{9,8},{10,11... | collective-permute-start | bytes 350216 | tf_op jit(solution)/shard_map/ppermute | solution.py:503
  3.1 4.4 %collective-permute-start = (bf16[16,1792]{1,0:T(8,128)(2,1)S(1)}, bf16[16,1792]{1,0:T(8,128)(2,1)S(1)}, u32[]{:S(2)}, u32[]{:S(2)}) collective-permute-start(bf16[16,1792]{1,0:T(8,128)(2,1)S(1)} %get-tuple-element.33), channel_id=1, source_target_pairs={{0,14},{1,15},{2,12},{3,13},{4,10},{5,11},{6,8},{7,9},{8,7},{9,6},... | collective-permute-start | bytes 172040 | tf_op jit(solution)/shard_map/ppermute | solution.py:516
  7.5 8.4 %collective-permute-start.2 = (bf16[32,1792]{1,0:T(8,128)(2,1)S(1)}, bf16[32,1792]{1,0:T(8,128)(2,1)S(1)}, u32[]{:S(2)}, u32[]{:S(2)}) collective-permute-start(bf16[32,1792]{1,0:T(8,128)(2,1)S(1)} %get-tuple-element.38), channel_id=1, source_target_pairs={{0,5},{1,10},{2,7},{3,8},{4,1},{5,14},{6,3},{7,12},{8,13},{9,2},{1... | collective-permute-start | bytes 344072 | tf_op jit(solution)/shard_map/ppermute | solution.py:516
  10.5 6.2 %collective-permute-start.3 = (bf16[32,1792]{1,0:T(8,128)(2,1)S(1)}, bf16[32,1792]{1,0:T(8,128)(2,1)S(1)}, u32[]{:S(2)}, u32[]{:S(2)}) collective-permute-start(bf16[32,1792]{1,0:T(8,128)(2,1)S(1)} %get-tuple-element.46), channel_id=1, source_target_pairs={{0,9},{1,6},{2,11},{3,4},{4,13},{5,2},{6,15},{7,0},{8,1},{9,14},{1... | collective-permute-start | bytes 344072 | tf_op jit(solution)/shard_map/ppermute | solution.py:516
  12.3 8.0 %collective-permute-start.4 = (bf16[32,1792]{1,0:T(8,128)(2,1)S(1)}, bf16[32,1792]{1,0:T(8,128)(2,1)S(1)}, u32[]{:S(2)}, u32[]{:S(2)}) collective-permute-start(bf16[32,1792]{1,0:T(8,128)(2,1)S(1)} %get-tuple-element.47), channel_id=1, source_target_pairs={{0,13},{1,2},{2,15},{3,0},{4,9},{5,6},{6,11},{7,4},{8,5},{9,10},{1... | collective-permute-start | bytes 344072 | tf_op jit(solution)/shard_map/ppermute | solution.py:516
  16.7 5.4 %collective-permute-start.7 = (bf16[32,1792]{1,0:T(8,128)(2,1)S(1)}, bf16[32,1792]{1,0:T(8,128)(2,1)S(1)}, u32[]{:S(2)}, u32[]{:S(2)}) collective-permute-start(bf16[32,1792]{1,0:T(8,128)(2,1)S(1)} %collective-permute-done.3.refs_3_), channel_id=1, source_target_pairs={{0,1},{1,0},{2,3},{3,2},{4,5},{5,4},{6,7},{7,6},{8,9},{9,8},{10,11... | collective-permute-start | bytes 344072 | tf_op jit(solution)/shard_map/ppermute | solution.py:503
  20.3 1.8 %collective-permute-start.8 = (bf16[32,1792]{1,0:T(8,128)(2,1)S(1)}, bf16[32,1792]{1,0:T(8,128)(2,1)S(1)}, u32[]{:S(2)}, u32[]{:S(2)}) collective-permute-start(bf16[32,1792]{1,0:T(8,128)(2,1)S(1)} %collective-permute-done.4.refs_4_), channel_id=1, source_target_pairs={{0,1},{1,0},{2,3},{3,2},{4,5},{5,4},{6,7},{7,6},{8,9},{9,8},{10,11... | collective-permute-start | bytes 344072 | tf_op jit(solution)/shard_map/ppermute | solution.py:503
  20.3 1.8 %collective-permute-start.6 = (bf16[32,1792]{1,0:T(8,128)(2,1)S(1)}, bf16[32,1792]{1,0:T(8,128)(2,1)S(1)}, u32[]{:S(2)}, u32[]{:S(2)}) collective-permute-start(bf16[32,1792]{1,0:T(8,128)(2,1)S(1)} %collective-permute-done.2.refs_2_), channel_id=1, source_target_pairs={{0,1},{1,0},{2,3},{3,2},{4,5},{5,4},{6,7},{7,6},{8,9},{9,8},{10,11... | collective-permute-start | bytes 344072 | tf_op jit(solution)/shard_map/ppermute | solution.py:503
  20.8 1.2 %collective-permute-start.5 = (bf16[16,1792]{1,0:T(8,128)(2,1)S(1)}, bf16[16,1792]{1,0:T(8,128)(2,1)S(1)}, u32[]{:S(2)}, u32[]{:S(2)}) collective-permute-start(bf16[16,1792]{1,0:T(8,128)(2,1)S(1)} %collective-permute-done.refs_0_), channel_id=1, source_target_pairs={{0,1},{1,0},{2,3},{3,2},{4,5},{5,4},{6,7},{7,6},{8,9},{9,8},{10,11... | collective-permute-start | bytes 172040 | tf_op jit(solution)/shard_map/ppermute | solution.py:503
  25.7 1.4 %collective-permute-start.11 = (bf16[32,1792]{1,0:T(8,128)(2,1)S(1)}, bf16[32,1792]{1,0:T(8,128)(2,1)S(1)}, u32[]{:S(2)}, u32[]{:S(2)}) collective-permute-start(bf16[32,1792]{1,0:T(8,128)(2,1)S(1)} %get-tuple-element.54), channel_id=1, source_target_pairs={{0,1},{1,0},{2,3},{3,2},{4,5},{5,4},{6,7},{7,6},{8,9},{9,8},{10,11... | collective-permute-start | bytes 344072 | tf_op jit(solution)/shard_map/ppermute | solution.py:503
  25.9 4.8 %collective-permute-start.9 = (bf16[32,1792]{1,0:T(8,128)(2,1)S(1)}, bf16[32,1792]{1,0:T(8,128)(2,1)S(1)}, u32[]{:S(2)}, u32[]{:S(2)}) collective-permute-start(bf16[32,1792]{1,0:T(8,128)(2,1)S(1)} %get-tuple-element.52), channel_id=1, source_target_pairs={{0,1},{1,0},{2,3},{3,2},{4,5},{5,4},{6,7},{7,6},{8,9},{9,8},{10,11... | collective-permute-start | bytes 344072 | tf_op jit(solution)/shard_map/ppermute | solution.py:503
  26.2 2.1 %collective-permute-start.13 = (bf16[32,1792]{1,0:T(8,128)(2,1)S(1)}, bf16[32,1792]{1,0:T(8,128)(2,1)S(1)}, u32[]{:S(2)}, u32[]{:S(2)}) collective-permute-start(bf16[32,1792]{1,0:T(8,128)(2,1)S(1)} %get-tuple-element.56), channel_id=1, source_target_pairs={{0,1},{1,0},{2,3},{3,2},{4,5},{5,4},{6,7},{7,6},{8,9},{9,8},{10,11... | collective-permute-start | bytes 344072 | tf_op jit(solution)/shard_map/ppermute | solution.py:503
  26.4 3.8 %collective-permute-start.15 = (bf16[32,1792]{1,0:T(8,128)(2,1)S(1)}, bf16[32,1792]{1,0:T(8,128)(2,1)S(1)}, u32[]{:S(2)}, u32[]{:S(2)}) collective-permute-start(bf16[32,1792]{1,0:T(8,128)(2,1)S(1)} %get-tuple-element.58), channel_id=1, source_target_pairs={{0,1},{1,0},{2,3},{3,2},{4,5},{5,4},{6,7},{7,6},{8,9},{9,8},{10,11... | collective-permute-start | bytes 344072 | tf_op jit(solution)/shard_map/ppermute | solution.py:503
  27.1 13.4 %collective-permute-start.12 = (bf16[32,1792]{1,0:T(8,128)(2,1)S(1)}, bf16[32,1792]{1,0:T(8,128)(2,1)S(1)}, u32[]{:S(2)}, u32[]{:S(2)}) collective-permute-start(bf16[32,1792]{1,0:T(8,128)(2,1)S(1)} %add_convert_fusion.2), channel_id=1, source_target_pairs={{5,0},{10,1},{7,2},{8,3},{1,4},{14,5},{3,6},{12,7},{13,8},{2,9},{1... | collective-permute-start | bytes 344072 | tf_op jit(solution)/shard_map/ppermute | solution.py:519
  28.3 12.1 %collective-permute-start.14 = (bf16[32,1792]{1,0:T(8,128)(2,1)S(1)}, bf16[32,1792]{1,0:T(8,128)(2,1)S(1)}, u32[]{:S(2)}, u32[]{:S(2)}) collective-permute-start(bf16[32,1792]{1,0:T(8,128)(2,1)S(1)} %add_convert_fusion.1), channel_id=1, source_target_pairs={{9,0},{6,1},{11,2},{4,3},{13,4},{2,5},{15,6},{0,7},{1,8},{14,9},{3... | collective-permute-start | bytes 344072 | tf_op jit(solution)/shard_map/ppermute | solution.py:519
  30.3 10.2 %collective-permute-start.16 = (bf16[32,1792]{1,0:T(8,128)(2,1)S(1)}, bf16[32,1792]{1,0:T(8,128)(2,1)S(1)}, u32[]{:S(2)}, u32[]{:S(2)}) collective-permute-start(bf16[32,1792]{1,0:T(8,128)(2,1)S(1)} %add_convert_fusion), channel_id=1, source_target_pairs={{13,0},{2,1},{15,2},{0,3},{9,4},{6,5},{11,6},{4,7},{5,8},{10,9},{7... | collective-permute-start | bytes 344072 | tf_op jit(solution)/shard_map/ppermute | solution.py:519
  30.7 9.7 %collective-permute-start.10 = (bf16[16,1792]{1,0:T(8,128)(2,1)S(1)}, bf16[16,1792]{1,0:T(8,128)(2,1)S(1)}, u32[]{:S(2)}, u32[]{:S(2)}) collective-permute-start(bf16[16,1792]{1,0:T(8,128)(2,1)S(1)} %get-tuple-element.62), channel_id=1, source_target_pairs={{14,0},{15,1},{12,2},{13,3},{10,4},{11,5},{8,6},{9,7},{7,8},{6,9},... | collective-permute-start | bytes 172040 | tf_op jit(solution)/shard_map/ppermute | solution.py:519
  40.9 2.8 %collective-permute-start.17 = (bf16[8,7168]{1,0:T(8,128)(2,1)S(1)}, bf16[8,7168]{1,0:T(8,128)(2,1)S(1)}, u32[]{:S(2)}, u32[]{:S(2)}) collective-permute-start(bf16[8,7168]{1,0:T(8,128)(2,1)S(1)} %get-tuple-element.60), channel_id=1, source_target_pairs={{0,1},{1,0},{2,3},{3,2},{4,5},{5,4},{6,7},{7,6},{8,9},{9,8},{10,11... | collective-permute-start | bytes 344072 | tf_op jit(solution)/shard_map/ppermute | solution.py:503

commit v15 on v13

--- a/solution.py
+++ b/solution.py
@@ -105,33 +105,30 @@
     merged,
     sems,
 ):
-    copies = [
-        pltpu.make_async_copy(source, target, sems.at[i])
-        for i, (source, target) in enumerate(
-            (
-                (q_hbm, q_ref),
-                (kv_hbm, kv_ref),
-                (len_hbm, len_ref),
-                (ids_hbm, ids_ref),
-                (weight_hbm, weight_ref),
-                (fresh_hbm, fresh_ref),
-                (hid_hbm, hid_ref),
-                (gain_hbm, gain_ref),
-            )
-        )
-    ]
-    down = pltpu.make_async_copy(dn_hbm.at[0], dn_ref, sems.at[len(copies)])
-    for copy in [*copies, down]:
+    pairs = (
+        (q_hbm, q_ref),
+        (kv_hbm, kv_ref),
+        (fresh_hbm, fresh_ref),
+        (len_hbm, len_ref),
+        (hid_hbm, hid_ref),
+        (gain_hbm, gain_ref),
+        (ids_hbm, ids_ref),
+        (weight_hbm, weight_ref),
+        (dn_hbm.at[0], dn_ref),
+    )
+    copies = [pltpu.make_async_copy(a, b, sems.at[i]) for i, (a, b) in enumerate(pairs)]
+    for copy in copies:
         copy.start()
     steps, rows, width = q_ref.shape
     length = kv_ref.shape[2]
     both = steps * rows
     scale = HEAD ** (-0.5)
-    for copy in copies:
-        copy.wait()
+    copies[0].wait()
     q = jnp.concatenate([q_ref[s].astype(F32) for s in range(steps)], axis=0)
     heads = jnp.concatenate([q[:, h * HEAD : (h + 1) * HEAD] for h in range(HEADS)], axis=0)
     heads = heads.astype(BF16)
+    for copy in copies[1:4]:
+        copy.wait()
     kv = jnp.concatenate([kv_ref[r] for r in range(rows)], axis=1)
     new = jnp.concatenate([fresh_ref[s].astype(F32) for s in range(steps)], axis=0).astype(BF16)
 
@@ -155,11 +152,14 @@
     old_e = jnp.exp(old_s - top)
     new_e = jnp.exp(new_s - top)
     total = jnp.sum(old_e, axis=-1, keepdims=True) + jnp.sum(new_e, axis=-1, keepdims=True)
-    old_w = (old_e / total).reshape(HEADS * both, rows * length).astype(BF16)
-    new_w = (new_e / total).reshape(HEADS * both, both).astype(BF16)
+    share = 1.0 / total
+    old_w = (old_e * share).reshape(HEADS * both, rows * length).astype(BF16)
+    new_w = (new_e * share).reshape(HEADS * both, both).astype(BF16)
     attended = nt_dot(old_w, kv[HEAD:]) + dot(new_w, new[:, HEAD:])
     for h in range(HEADS):
         merged[:, h * HEAD : (h + 1) * HEAD] = attended[h * both : (h + 1) * both]
+    for copy in copies[4:8]:
+        copy.wait()
     hidden = jnp.concatenate([hid_ref[s].astype(F32) for s in range(steps)], axis=0)
     resid = hidden + merged[...]
     resid_ref[...] = resid
@@ -169,7 +169,7 @@
     normed = resid * lax.rsqrt(meansq + 1e-06) * gain
     out_ref[:, :width] = normed.astype(BF16)
     out_ref[:, width:] = tail(ids_ref, weight_ref, steps, rows)
-    down.wait()
+    copies[8].wait()
 
 
 def attend(cache_len, ids, weights, queries, fresh, kv_cache, hidden_state, norm_gain, down):
@@ -335,32 +335,21 @@
     lines, piece = own_refs[0].shape
     per = lines // PIECES
     half = turns * per
-    n = turns * lines
-    row = iota((n, n), 0)
-    col = iota((n, n), 1)
-    order = one_hot(col == row // per % turns * lines + row // half * per + row % per)
-    sides = [
-        dot(order, jnp.concatenate([ref[...] for ref in now], axis=0)).astype(BF16)
-        for now in (own_refs, other_refs)
-    ]
+    arrays = [ref[...].astype(F32) for ref in own_refs + other_refs]
     gate = upper = None
     for k in range(PIECES):
-        x = jnp.concatenate([side[k * half : (k + 1) * half] for side in sides], axis=0)
+        x = [array[k * per : (k + 1) * per] for array in arrays]
+        x = jnp.concatenate(x, axis=0).astype(BF16)
         cols = pl.ds(k * piece, piece)
         g, u = nt_dot(x, w_in[0, :, cols]), nt_dot(x, w_in[1, :, cols])
         gate, upper = (g, u) if k == 0 else (gate + g, upper + u)
     act = (gate / (1.0 + jnp.exp(-gate)) * upper).astype(BF16)
-    mine = []
-    theirs = []
-    for k in range(PIECES):
-        part = dot(act, w_down[:, k * piece : (k + 1) * piece]).astype(BF16)
-        mine.append(part[:half])
-        theirs.append(part[half:])
-    back = one_hot(row == col // per % turns * lines + col // half * per + col % per)
-    for parts, now in ((theirs, theirs_refs), (mine, mine_refs)):
-        out = dot(back, jnp.concatenate(parts, axis=0)).astype(BF16)
+    parts = [dot(act, w_down[:, k * piece : (k + 1) * piece]) for k in range(PIECES)]
+    for first, now in ((half, theirs_refs), (0, mine_refs)):
         for t, ref in enumerate(now):
-            ref[...] = out[t * lines : (t + 1) * lines]
+            start = first + t * per
+            out = [part[start : start + per] for part in parts]
+            ref[...] = jnp.concatenate(out, axis=0).astype(BF16)
 
 
 def experts(own, other, gate_up, down):

time: 42.1 us -> 41.5 us (0.986)
  Pallas kernels: 11 us -> 10.4 us
    pallas_call x1, Pallas kernels: 3.62 us -> 3.06 us  [experts(): pl.pallas_call(functools.partial(expert_kernel, turns), out_shape=[shape]...]
where the time goes in v15:
time: 41.5 us; the launch traced here: 41.4 us
  starting transfers between devices  20.4 us (49%)
  Pallas kernels  10.4 us (25%)
  waiting for transfers between devices  10.3 us (25%)
    ppermute x4, starting transfers between devices, send(): return lax.ppermute(x, 'afd', route(t))  8.4 us
    ppermute x4, waiting for transfers between devices, send_back(): return lax.ppermute(x, 'afd', [(j, i) for i, j in route(t)])  6.84 us
    ppermute x10, starting transfers between devices, swap(): return lax.ppermute(x, 'afd', cores)  6.4 us
    ppermute x4, starting transfers between devices, send_back(): return lax.ppermute(x, 'afd', [(j, i) for i, j in route(t)])  5.62 us
    ppermute x10, waiting for transfers between devices, swap(): return lax.ppermute(x, 'afd', cores)  3.5 us
    pallas_call x1, Pallas kernels, stage(): pl.pallas_call(stage_kernel, out_shape=jax.ShapeDtypeStruct(gate_up.shape...  3.17 us
    pallas_call x1, Pallas kernels, experts(): pl.pallas_call(functools.partial(expert_kernel, turns), out_shape=[shape]...  3.06 us
    pallas_call x1, Pallas kernels, attend(): pl.pallas_call(attend_kernel, out_shape=(jax.ShapeDtypeStruct((steps * ro...  2.39 us
  transfers between devices with their start and end apart: 18, of which 9 were waited for; matrix products, arithmetic and copies ran while one was open for 0% of the time, Pallas kernels for 8%

profile of v15, /device:TPU:0, one launch (start us, length us, event | category | flops | bytes accessed | tf_op | source)
XLA Modules:
  0.0 41.4 jit_solution(11654565373760109461)
XLA Ops:
  0.0 2.4 %attend.1 = (f32[8,7168]{1,0:T(8,128)S(1)}, bf16[8,7296]{1,0:T(8,128)(2,1)S(1)}, bf16[256,7168]{1,0:T(8,128)(2,1)S(1)}) custom-call(s32[4]{0:T(128)} %len_hbm.1, s32[3,2,4]{2,1,0:T(2,128)} %bitcast.6, f32[3,2,4]{2,1,0:T(2,128)} %bitcast.7, bf16[2,4,7168]{2,1,0:T(4,128)(2,1)} %q_hbm.1, bf16[2,4,448]{2,1,0:T(4,128)(2,1)} %fresh_hbm.1, ...), custom_call_target="tpu_custom_call" | custom-call | flops 300000000 | bytes 2000000 | tf_op jit(solution)/shard_map/attend/pallas_call | solution.py:179
  2.4 0.5 %collective-permute-start = (bf16[8,7296]{1,0:T(8,128)(2,1)S(1)}, bf16[8,7296]{1,0:T(8,128)(2,1)S(1)}, u32[]{:S(2)}, u32[]{:S(2)}) collective-permute-start(bf16[8,7296]{1,0:T(8,128)(2,1)S(1)} %get-tuple-element.24.own_ref), channel_id=1, source_target_pairs={{0,1},{1,0},{2,3},{3,2},{4,5},{5,4},{6,7},{7,6},{8,9},{9,8},{10,11... | collective-permute-start | bytes 350216 | tf_op jit(solution)/shard_map/ppermute | solution.py:441
  2.9 1.0 %collective-permute-done.other_ref = bf16[8,7296]{1,0:T(8,128)(2,1)S(1)} collective-permute-done((bf16[8,7296]{1,0:T(8,128)(2,1)S(1)}, bf16[8,7296]{1,0:T(8,128)(2,1)S(1)}, u32[]{:S(2)}, u32[]{:S(2)}) %collective-permute-start) | collective-permute-done | bytes 116768 | tf_op jit(solution)/shard_map/ppermute | solution.py:441
  3.9 0.5 %pack.1 = (bf16[32,1792]{1,0:T(8,128)(2,1)S(1)}, bf16[32,1792]{1,0:T(8,128)(2,1)S(1)}, bf16[32,1792]{1,0:T(8,128)(2,1)S(1)}, bf16[32,1792]{1,0:T(8,128)(2,1)S(1)}) custom-call(bf16[8,7296]{1,0:T(8,128)(2,1)S(1)} %get-tuple-element.24.own_ref, bf16[8,7296]{1,0:T(8,128)(2,1)S(1)} %collective-permute-done.other_ref), custom_call_target="tpu_custom_call" | custom-call | flops 50000000 | bytes 2000000 | tf_op jit(solution)/shard_map/pack/pallas_call | solution.py:243
  4.4 0.4 collective-permute-start.1
  4.8 4.7 %collective-permute-start.2 = (bf16[32,1792]{1,0:T(8,128)(2,1)S(1)}, bf16[32,1792]{1,0:T(8,128)(2,1)S(1)}, u32[]{:S(2)}, u32[]{:S(2)}) collective-permute-start(bf16[32,1792]{1,0:T(8,128)(2,1)S(1)} %get-tuple-element.28), channel_id=1, source_target_pairs={{0,9},{1,6},{2,11},{3,4},{4,13},{5,2},{6,15},{7,0},{8,1},{9,14},{1... | collective-permute-start | bytes 344072 | tf_op jit(solution)/shard_map/ppermute | solution.py:447
  9.6 3.2 %collective-permute-start.4 = (bf16[32,1792]{1,0:T(8,128)(2,1)S(1)}, bf16[32,1792]{1,0:T(8,128)(2,1)S(1)}, u32[]{:S(2)}, u32[]{:S(2)}) collective-permute-start(bf16[32,1792]{1,0:T(8,128)(2,1)S(1)} %get-tuple-element.30), channel_id=1, source_target_pairs={{0,13},{1,2},{2,15},{3,0},{4,9},{5,6},{6,11},{7,4},{8,5},{9,10},{1... | collective-permute-start | bytes 344072 | tf_op jit(solution)/shard_map/ppermute | solution.py:447
  12.8 3.2 %stage.1.refs_8_ = bf16[2,256,7168]{2,1,0:T(8,128)(2,1)S(1)} custom-call(bf16[1,2,256,7168]{3,2,1,0:T(8,128)(2,1)} %gu_hbm.1), custom_call_target="tpu_custom_call" | custom-call | bytes 16000000 | tf_op jit(solution)/shard_map/stage/pallas_call | solution.py:298
  16.0 3.3 %collective-permute-start.6 = (bf16[32,1792]{1,0:T(8,128)(2,1)S(1)}, bf16[32,1792]{1,0:T(8,128)(2,1)S(1)}, u32[]{:S(2)}, u32[]{:S(2)}) collective-permute-start(bf16[32,1792]{1,0:T(8,128)(2,1)S(1)} %collective-permute-done.2.refs_1_), channel_id=1, source_target_pairs={{0,1},{1,0},{2,3},{3,2},{4,5},{5,4},{6,7},{7,6},{8,9},{9,8},{10,11... | collective-permute-start | bytes 344072 | tf_op jit(solution)/shard_map/ppermute | solution.py:441
  19.3 0.5 %collective-permute-start.8 = (bf16[32,1792]{1,0:T(8,128)(2,1)S(1)}, bf16[32,1792]{1,0:T(8,128)(2,1)S(1)}, u32[]{:S(2)}, u32[]{:S(2)}) collective-permute-start(bf16[32,1792]{1,0:T(8,128)(2,1)S(1)} %collective-permute-done.4.refs_3_), channel_id=1, source_target_pairs={{0,1},{1,0},{2,3},{3,2},{4,5},{5,4},{6,7},{7,6},{8,9},{9,8},{10,11... | collective-permute-start | bytes 344072 | tf_op jit(solution)/shard_map/ppermute | solution.py:441
  19.9 0.4 collective-permute-done.6.refs_5_
  20.3 0.4 collective-permute-done.7.refs_6_
  20.8 0.3 collective-permute-done.5.refs_4_
  21.2 3.1 %experts.1 = (bf16[32,1792]{1,0:T(8,128)(2,1)S(1)}, bf16[32,1792]{1,0:T(8,128)(2,1)S(1)}, bf16[32,1792]{1,0:T(8,128)(2,1)S(1)}, bf16[32,1792]{1,0:T(8,128)(2,1)S...) custom-call(bf16[32,1792]{1,0:T(8,128)(2,1)S(1)} %collective-permute, ...), custom_call_target="tpu_custom_call" | custom-call | flops 800000000 | bytes 12000000 | tf_op jit(solution)/shard_map/experts/pallas_call | solution.py:358
  24.5 0.3 collective-permute-start.11
  25.0 0.3 collective-permute-start.15
  25.7 1.9 %collective-permute-start.10 = (bf16[32,1792]{1,0:T(8,128)(2,1)S(1)}, bf16[32,1792]{1,0:T(8,128)(2,1)S(1)}, u32[]{:S(2)}, u32[]{:S(2)}) collective-permute-start(bf16[32,1792]{1,0:T(8,128)(2,1)S(1)} %add_convert_fusion.3), channel_id=1, source_target_pairs={{1,0},{14,1},{3,2},{12,3},{5,4},{10,5},{7,6},{8,7},{9,8},{6,9},{11... | collective-permute-start | bytes 344072 | tf_op jit(solution)/shard_map/ppermute | solution.py:450
  27.7 3.6 %collective-permute-start.14 = (bf16[32,1792]{1,0:T(8,128)(2,1)S(1)}, bf16[32,1792]{1,0:T(8,128)(2,1)S(1)}, u32[]{:S(2)}, u32[]{:S(2)}) collective-permute-start(bf16[32,1792]{1,0:T(8,128)(2,1)S(1)} %add_convert_fusion.1), channel_id=1, source_target_pairs={{5,0},{10,1},{7,2},{8,3},{1,4},{14,5},{3,6},{12,7},{13,8},{2,9},{1... | collective-permute-start | bytes 344072 | tf_op jit(solution)/shard_map/ppermute | solution.py:450
  31.7 5.6 %collective-permute-done.12.refs_1_ = bf16[32,1792]{1,0:T(8,128)(2,1)S(1)} collective-permute-done((bf16[32,1792]{1,0:T(8,128)(2,1)S(1)}, bf16[32,1792]{1,0:T(8,128)(2,1)S(1)}, u32[]{:S(2)}, u32[]{:S(2)}) %collective-permute-start.12) | collective-permute-done | bytes 114720 | tf_op jit(solution)/shard_map/ppermute | solution.py:450
  37.3 1.2 %collective-permute-done.16.refs_3_ = bf16[32,1792]{1,0:T(8,128)(2,1)S(1)} collective-permute-done((bf16[32,1792]{1,0:T(8,128)(2,1)S(1)}, bf16[32,1792]{1,0:T(8,128)(2,1)S(1)}, u32[]{:S(2)}, u32[]{:S(2)}) %collective-permute-start.16) | collective-permute-done | bytes 114720 | tf_op jit(solution)/shard_map/ppermute | solution.py:450
  38.5 0.3 combine.1
  38.9 0.9 %collective-permute-start.17 = (bf16[8,7168]{1,0:T(8,128)(2,1)S(1)}, bf16[8,7168]{1,0:T(8,128)(2,1)S(1)}, u32[]{:S(2)}, u32[]{:S(2)}) collective-permute-start(bf16[8,7168]{1,0:T(8,128)(2,1)S(1)} %get-tuple-element.42), channel_id=1, source_target_pairs={{0,1},{1,0},{2,3},{3,2},{4,5},{5,4},{6,7},{7,6},{8,9},{9,8},{10,11... | collective-permute-start | bytes 344072 | tf_op jit(solution)/shard_map/ppermute | solution.py:441
  39.8 1.0 %collective-permute-done.17.other_ref = bf16[8,7168]{1,0:T(8,128)(2,1)S(1)} collective-permute-done((bf16[8,7168]{1,0:T(8,128)(2,1)S(1)}, bf16[8,7168]{1,0:T(8,128)(2,1)S(1)}, u32[]{:S(2)}, u32[]{:S(2)}) %collective-permute-start.17) | collective-permute-done | bytes 114720 | tf_op jit(solution)/shard_map/ppermute | solution.py:441
  40.7 0.7 %finish.1 = bf16[2,4,7168]{2,1,0:T(4,128)(2,1)} custom-call(f32[8,7168]{1,0:T(8,128)S(1)} %get-tuple-element.41.kept_ref, bf16[8,7168]{1,0:T(8,128)(2,1)S(1)} %collective-permute-done.17.other_ref), custom_call_target="tpu_custom_call" | custom-call | flops 100000 | bytes 500000 | tf_op jit(solution)/shard_map/finish/pallas_call | solution.py:411
  (23 shorter events, 1.6 us)
Async XLA Ops:
  2.4 1.5 %collective-permute-start = (bf16[8,7296]{1,0:T(8,128)(2,1)S(1)}, bf16[8,7296]{1,0:T(8,128)(2,1)S(1)}, u32[]{:S(2)}, u32[]{:S(2)}) collective-permute-start(bf16[8,7296]{1,0:T(8,128)(2,1)S(1)} %get-tuple-element.24.own_ref), channel_id=1, source_target_pairs={{0,1},{1,0},{2,3},{3,2},{4,5},{5,4},{6,7},{7,6},{8,9},{9,8},{10,11... | collective-permute-start | bytes 350216 | tf_op jit(solution)/shard_map/ppermute | solution.py:441
  4.4 11.6 %collective-permute-start.1 = (bf16[32,1792]{1,0:T(8,128)(2,1)S(1)}, bf16[32,1792]{1,0:T(8,128)(2,1)S(1)}, u32[]{:S(2)}, u32[]{:S(2)}) collective-permute-start(bf16[32,1792]{1,0:T(8,128)(2,1)S(1)} %get-tuple-element.26), channel_id=1, source_target_pairs={{0,1},{1,14},{2,3},{3,12},{4,5},{5,10},{6,7},{7,8},{8,9},{9,6},{10... | collective-permute-start | bytes 344072 | tf_op jit(solution)/shard_map/ppermute | solution.py:447
  4.8 11.2 %collective-permute-start.2 = (bf16[32,1792]{1,0:T(8,128)(2,1)S(1)}, bf16[32,1792]{1,0:T(8,128)(2,1)S(1)}, u32[]{:S(2)}, u32[]{:S(2)}) collective-permute-start(bf16[32,1792]{1,0:T(8,128)(2,1)S(1)} %get-tuple-element.28), channel_id=1, source_target_pairs={{0,9},{1,6},{2,11},{3,4},{4,13},{5,2},{6,15},{7,0},{8,1},{9,14},{1... | collective-permute-start | bytes 344072 | tf_op jit(solution)/shard_map/ppermute | solution.py:447
  9.5 9.8 %collective-permute-start.3 = (bf16[32,1792]{1,0:T(8,128)(2,1)S(1)}, bf16[32,1792]{1,0:T(8,128)(2,1)S(1)}, u32[]{:S(2)}, u32[]{:S(2)}) collective-permute-start(bf16[32,1792]{1,0:T(8,128)(2,1)S(1)} %get-tuple-element.29), channel_id=1, source_target_pairs={{0,5},{1,10},{2,7},{3,8},{4,1},{5,14},{6,3},{7,12},{8,13},{9,2},{1... | collective-permute-start | bytes 344072 | tf_op jit(solution)/shard_map/ppermute | solution.py:447
  9.6 9.7 %collective-permute-start.4 = (bf16[32,1792]{1,0:T(8,128)(2,1)S(1)}, bf16[32,1792]{1,0:T(8,128)(2,1)S(1)}, u32[]{:S(2)}, u32[]{:S(2)}) collective-permute-start(bf16[32,1792]{1,0:T(8,128)(2,1)S(1)} %get-tuple-element.30), channel_id=1, source_target_pairs={{0,13},{1,2},{2,15},{3,0},{4,9},{5,6},{6,11},{7,4},{8,5},{9,10},{1... | collective-permute-start | bytes 344072 | tf_op jit(solution)/shard_map/ppermute | solution.py:447
  16.0 4.3 %collective-permute-start.6 = (bf16[32,1792]{1,0:T(8,128)(2,1)S(1)}, bf16[32,1792]{1,0:T(8,128)(2,1)S(1)}, u32[]{:S(2)}, u32[]{:S(2)}) collective-permute-start(bf16[32,1792]{1,0:T(8,128)(2,1)S(1)} %collective-permute-done.2.refs_1_), channel_id=1, source_target_pairs={{0,1},{1,0},{2,3},{3,2},{4,5},{5,4},{6,7},{7,6},{8,9},{9,8},{10,11... | collective-permute-start | bytes 344072 | tf_op jit(solution)/shard_map/ppermute | solution.py:441
  19.3 1.3 %collective-permute-start.7 = (bf16[32,1792]{1,0:T(8,128)(2,1)S(1)}, bf16[32,1792]{1,0:T(8,128)(2,1)S(1)}, u32[]{:S(2)}, u32[]{:S(2)}) collective-permute-start(bf16[32,1792]{1,0:T(8,128)(2,1)S(1)} %collective-permute-done.3.refs_2_), channel_id=1, source_target_pairs={{0,1},{1,0},{2,3},{3,2},{4,5},{5,4},{6,7},{7,6},{8,9},{9,8},{10,11... | collective-permute-start | bytes 344072 | tf_op jit(solution)/shard_map/ppermute | solution.py:441
  19.3 1.5 %collective-permute-start.8 = (bf16[32,1792]{1,0:T(8,128)(2,1)S(1)}, bf16[32,1792]{1,0:T(8,128)(2,1)S(1)}, u32[]{:S(2)}, u32[]{:S(2)}) collective-permute-start(bf16[32,1792]{1,0:T(8,128)(2,1)S(1)} %collective-permute-done.4.refs_3_), channel_id=1, source_target_pairs={{0,1},{1,0},{2,3},{3,2},{4,5},{5,4},{6,7},{7,6},{8,9},{9,8},{10,11... | collective-permute-start | bytes 344072 | tf_op jit(solution)/shard_map/ppermute | solution.py:441
  19.8 1.3 %collective-permute-start.5 = (bf16[32,1792]{1,0:T(8,128)(2,1)S(1)}, bf16[32,1792]{1,0:T(8,128)(2,1)S(1)}, u32[]{:S(2)}, u32[]{:S(2)}) collective-permute-start(bf16[32,1792]{1,0:T(8,128)(2,1)S(1)} %collective-permute-done.1.refs_0_), channel_id=1, source_target_pairs={{0,1},{1,0},{2,3},{3,2},{4,5},{5,4},{6,7},{7,6},{8,9},{9,8},{10,11... | collective-permute-start | bytes 344072 | tf_op jit(solution)/shard_map/ppermute | solution.py:441
  24.2 1.4 %collective-permute-start.9 = (bf16[32,1792]{1,0:T(8,128)(2,1)S(1)}, bf16[32,1792]{1,0:T(8,128)(2,1)S(1)}, u32[]{:S(2)}, u32[]{:S(2)}) collective-permute-start(bf16[32,1792]{1,0:T(8,128)(2,1)S(1)} %get-tuple-element.34), channel_id=1, source_target_pairs={{0,1},{1,0},{2,3},{3,2},{4,5},{5,4},{6,7},{7,6},{8,9},{9,8},{10,11... | collective-permute-start | bytes 344072 | tf_op jit(solution)/shard_map/ppermute | solution.py:441
  24.5 3.1 %collective-permute-start.11 = (bf16[32,1792]{1,0:T(8,128)(2,1)S(1)}, bf16[32,1792]{1,0:T(8,128)(2,1)S(1)}, u32[]{:S(2)}, u32[]{:S(2)}) collective-permute-start(bf16[32,1792]{1,0:T(8,128)(2,1)S(1)} %get-tuple-element.36), channel_id=1, source_target_pairs={{0,1},{1,0},{2,3},{3,2},{4,5},{5,4},{6,7},{7,6},{8,9},{9,8},{10,11... | collective-permute-start | bytes 344072 | tf_op jit(solution)/shard_map/ppermute | solution.py:441
  24.8 2.9 %collective-permute-start.13 = (bf16[32,1792]{1,0:T(8,128)(2,1)S(1)}, bf16[32,1792]{1,0:T(8,128)(2,1)S(1)}, u32[]{:S(2)}, u32[]{:S(2)}) collective-permute-start(bf16[32,1792]{1,0:T(8,128)(2,1)S(1)} %get-tuple-element.38), channel_id=1, source_target_pairs={{0,1},{1,0},{2,3},{3,2},{4,5},{5,4},{6,7},{7,6},{8,9},{9,8},{10,11... | collective-permute-start | bytes 344072 | tf_op jit(solution)/shard_map/ppermute | solution.py:441
  25.0 6.3 %collective-permute-start.15 = (bf16[32,1792]{1,0:T(8,128)(2,1)S(1)}, bf16[32,1792]{1,0:T(8,128)(2,1)S(1)}, u32[]{:S(2)}, u32[]{:S(2)}) collective-permute-start(bf16[32,1792]{1,0:T(8,128)(2,1)S(1)} %get-tuple-element.40), channel_id=1, source_target_pairs={{0,1},{1,0},{2,3},{3,2},{4,5},{5,4},{6,7},{7,6},{8,9},{9,8},{10,11... | collective-permute-start | bytes 344072 | tf_op jit(solution)/shard_map/ppermute | solution.py:441
  25.7 6.0 %collective-permute-start.10 = (bf16[32,1792]{1,0:T(8,128)(2,1)S(1)}, bf16[32,1792]{1,0:T(8,128)(2,1)S(1)}, u32[]{:S(2)}, u32[]{:S(2)}) collective-permute-start(bf16[32,1792]{1,0:T(8,128)(2,1)S(1)} %add_convert_fusion.3), channel_id=1, source_target_pairs={{1,0},{14,1},{3,2},{12,3},{5,4},{10,5},{7,6},{8,7},{9,8},{6,9},{11... | collective-permute-start | bytes 344072 | tf_op jit(solution)/shard_map/ppermute | solution.py:450
  27.6 9.7 %collective-permute-start.12 = (bf16[32,1792]{1,0:T(8,128)(2,1)S(1)}, bf16[32,1792]{1,0:T(8,128)(2,1)S(1)}, u32[]{:S(2)}, u32[]{:S(2)}) collective-permute-start(bf16[32,1792]{1,0:T(8,128)(2,1)S(1)} %add_convert_fusion.2), channel_id=1, source_target_pairs={{9,0},{6,1},{11,2},{4,3},{13,4},{2,5},{15,6},{0,7},{1,8},{14,9},{3... | collective-permute-start | bytes 344072 | tf_op jit(solution)/shard_map/ppermute | solution.py:450
  27.7 9.6 %collective-permute-start.14 = (bf16[32,1792]{1,0:T(8,128)(2,1)S(1)}, bf16[32,1792]{1,0:T(8,128)(2,1)S(1)}, u32[]{:S(2)}, u32[]{:S(2)}) collective-permute-start(bf16[32,1792]{1,0:T(8,128)(2,1)S(1)} %add_convert_fusion.1), channel_id=1, source_target_pairs={{5,0},{10,1},{7,2},{8,3},{1,4},{14,5},{3,6},{12,7},{13,8},{2,9},{1... | collective-permute-start | bytes 344072 | tf_op jit(solution)/shard_map/ppermute | solution.py:450
  31.3 7.2 %collective-permute-start.16 = (bf16[32,1792]{1,0:T(8,128)(2,1)S(1)}, bf16[32,1792]{1,0:T(8,128)(2,1)S(1)}, u32[]{:S(2)}, u32[]{:S(2)}) collective-permute-start(bf16[32,1792]{1,0:T(8,128)(2,1)S(1)} %add_convert_fusion), channel_id=1, source_target_pairs={{13,0},{2,1},{15,2},{0,3},{9,4},{6,5},{11,6},{4,7},{5,8},{10,9},{7... | collective-permute-start | bytes 344072 | tf_op jit(solution)/shard_map/ppermute | solution.py:450
  38.9 1.9 %collective-permute-start.17 = (bf16[8,7168]{1,0:T(8,128)(2,1)S(1)}, bf16[8,7168]{1,0:T(8,128)(2,1)S(1)}, u32[]{:S(2)}, u32[]{:S(2)}) collective-permute-start(bf16[8,7168]{1,0:T(8,128)(2,1)S(1)} %get-tuple-element.42), channel_id=1, source_target_pairs={{0,1},{1,0},{2,3},{3,2},{4,5},{5,4},{6,7},{7,6},{8,9},{9,8},{10,11... | collective-permute-start | bytes 344072 | tf_op jit(solution)/shard_map/ppermute | solution.py:441

commit v16 on v15

--- a/solution.py
+++ b/solution.py
@@ -90,10 +90,8 @@
     kv_hbm,
     hid_hbm,
     gain_hbm,
-    dn_hbm,
     resid_ref,
     out_ref,
-    dn_ref,
     len_ref,
     ids_ref,
     weight_ref,
@@ -114,7 +112,6 @@
         (gain_hbm, gain_ref),
         (ids_hbm, ids_ref),
         (weight_hbm, weight_ref),
-        (dn_hbm.at[0], dn_ref),
     )
     copies = [pltpu.make_async_copy(a, b, sems.at[i]) for i, (a, b) in enumerate(pairs)]
     for copy in copies:
@@ -169,10 +166,9 @@
     normed = resid * lax.rsqrt(meansq + 1e-06) * gain
     out_ref[:, :width] = normed.astype(BF16)
     out_ref[:, width:] = tail(ids_ref, weight_ref, steps, rows)
-    copies[8].wait()
-
-
-def attend(cache_len, ids, weights, queries, fresh, kv_cache, hidden_state, norm_gain, down):
+
+
+def attend(cache_len, ids, weights, queries, fresh, kv_cache, hidden_state, norm_gain):
     steps, rows, width = queries.shape
     kv = kv_cache.transpose(0, 2, 1)
     gain = norm_gain.reshape(width // LANES, LANES)
@@ -181,10 +177,9 @@
         out_shape=(
             jax.ShapeDtypeStruct((steps * rows, width), F32),
             jax.ShapeDtypeStruct((steps * rows, width + LANES), BF16),
-            jax.ShapeDtypeStruct(down.shape[1:], BF16),
-        ),
-        in_specs=[HBM] * 9,
-        out_specs=(VMEM, VMEM, VMEM),
+        ),
+        in_specs=[HBM] * 8,
+        out_specs=(VMEM, VMEM),
         scratch_shapes=[
             pltpu.SMEM(cache_len.shape, jnp.int32),
             pltpu.SMEM(ids.shape, jnp.int32),
@@ -195,14 +190,14 @@
             pltpu.VMEM(hidden_state.shape, BF16),
             pltpu.VMEM(gain.shape, BF16),
             pltpu.VMEM((steps * rows, width), F32),
-            pltpu.SemaphoreType.DMA((9,)),
+            pltpu.SemaphoreType.DMA((8,)),
         ],
         compiler_params=pltpu.CompilerParams(vmem_limit_bytes=24 * MIB),
         cost_estimate=pl.CostEstimate(
             flops=300_000_000, bytes_accessed=2_000_000, transcendentals=131072
         ),
         name="attend",
-    )(*in_hbm(cache_len, ids, weights, queries, fresh, kv, hidden_state, gain, down))
+    )(*in_hbm(cache_len, ids, weights, queries, fresh, kv, hidden_state, gain))
 
 
 def pack_kernel(steps, chips, own_ref, other_ref, *outs):
@@ -280,31 +275,35 @@
     return jnp.concatenate(parts, axis=0).astype(BF16)
 
 
-def stage_kernel(gu_hbm, out, sems):
-    step = out.shape[1] // 4
-    copies = []
-    for i in range(8):
-        part = pl.ds(i // 2 * step, step)
-        copies.append(
-            pltpu.make_async_copy(gu_hbm.at[0, i % 2, part], out.at[i % 2, part], sems.at[i])
-        )
+def stage_kernel(gu_hbm, dn_hbm, gu, dn, sems):
+    step = dn.shape[0] // 4
+    pairs = []
+    for i in range(4):
+        part = pl.ds(i * step, step)
+        pairs.append((gu_hbm.at[0, 0, part], gu.at[0, part]))
+        pairs.append((gu_hbm.at[0, 1, part], gu.at[1, part]))
+        pairs.append((dn_hbm.at[0, part], dn.at[part]))
+    copies = [pltpu.make_async_copy(a, b, sems.at[i]) for i, (a, b) in enumerate(pairs)]
     for copy in copies:
         copy.start()
     for copy in copies:
         copy.wait()
 
 
-def stage(gate_up):
+def stage(gate_up, down):
     return pl.pallas_call(
         stage_kernel,
-        out_shape=jax.ShapeDtypeStruct(gate_up.shape[1:], BF16),
-        in_specs=[HBM],
-        out_specs=VMEM,
-        scratch_shapes=[pltpu.SemaphoreType.DMA((8,))],
+        out_shape=(
+            jax.ShapeDtypeStruct(gate_up.shape[1:], BF16),
+            jax.ShapeDtypeStruct(down.shape[1:], BF16),
+        ),
+        in_specs=[HBM, HBM],
+        out_specs=(VMEM, VMEM),
+        scratch_shapes=[pltpu.SemaphoreType.DMA((12,))],
         compiler_params=pltpu.CompilerParams(vmem_limit_bytes=16 * MIB),
-        cost_estimate=pl.CostEstimate(flops=0, bytes_accessed=16_000_000, transcendentals=0),
+        cost_estimate=pl.CostEstimate(flops=0, bytes_accessed=22_000_000, transcendentals=0),
         name="stage",
-    )(*in_hbm(gate_up))
+    )(*in_hbm(gate_up, down))
 
 
 def mix_kernel(steps, chips, own_ref, other_ref, mix_ref):
@@ -341,9 +340,9 @@
         x = [array[k * per : (k + 1) * per] for array in arrays]
         x = jnp.concatenate(x, axis=0).astype(BF16)
         cols = pl.ds(k * piece, piece)
-        g, u = nt_dot(x, w_in[0, :, cols]), nt_dot(x, w_in[1, :, cols])
+        g, u = nt_dot(w_in[0, :, cols], x), nt_dot(w_in[1, :, cols], x)
         gate, upper = (g, u) if k == 0 else (gate + g, upper + u)
-    act = (gate / (1.0 + jnp.exp(-gate)) * upper).astype(BF16)
+    act = (gate / (1.0 + jnp.exp(-gate)) * upper).T.astype(BF16)
     parts = [dot(act, w_down[:, k * piece : (k + 1) * piece]) for k in range(PIECES)]
     for first, now in ((half, theirs_refs), (0, mine_refs)):
         for t, ref in enumerate(now):
@@ -451,13 +450,13 @@
 
     ids = expert_ids.transpose(2, 0, 1)
     weights = route_weight.transpose(2, 0, 1)
-    resid, normed, w_down = attend(
-        cache_len, ids, weights, queries, fresh, kv_cache, hidden_state, norm_gain, down
+    resid, normed = attend(
+        cache_len, ids, weights, queries, fresh, kv_cache, hidden_state, norm_gain
     )
     normed_other = swap(normed)
     sent = pack(steps, chips, normed, normed_other)
     own = [send(sent[t], t) for t in range(turns)]
-    w_in = stage(gate_up)
+    w_in, w_down = stage(gate_up, down)
     mix = mixer(steps, chips, normed, normed_other)
     own[0], w_in = lax.optimization_barrier((own[0], w_in))
     other = [swap(x) for x in own]

time: 41.5 us -> 41.2 us (level)
  starting transfers between devices: 20.4 us -> 19.3 us
  Pallas kernels: 10.4 us -> 11.1 us
    pallas_call x1, Pallas kernels: 3.17 us -> 4.24 us  [stage(): pl.pallas_call(stage_kernel, out_shape=(jax.ShapeDtypeStruct(gate_up.shap...]
    ppermute x10, starting transfers between devices: 6.4 us -> 5.32 us  [swap(): return lax.ppermute(x, 'afd', cores)]
  transfers between devices with their start and end apart: 18 -> 18, of which waited for: 9 -> 10; matrix products, arithmetic and copies ran while one was open for 0% -> 0% of each run, Pallas kernels for 8% -> 11%
where the time goes in v16:
time: 41.2 us; the launch traced here: 41.1 us
  starting transfers between devices  19.3 us (47%)
  Pallas kernels  11.1 us (27%)
  waiting for transfers between devices  10.4 us (25%)
    ppermute x4, starting transfers between devices, send(): return lax.ppermute(x, 'afd', route(t))  8.4 us
    ppermute x4, waiting for transfers between devices, send_back(): return lax.ppermute(x, 'afd', [(j, i) for i, j in route(t)])  6.85 us
    ppermute x4, starting transfers between devices, send_back(): return lax.ppermute(x, 'afd', [(j, i) for i, j in route(t)])  5.59 us
    ppermute x10, starting transfers between devices, swap(): return lax.ppermute(x, 'afd', cores)  5.32 us
    pallas_call x1, Pallas kernels, stage(): pl.pallas_call(stage_kernel, out_shape=(jax.ShapeDtypeStruct(gate_up.shap...  4.24 us
    ppermute x10, waiting for transfers between devices, swap(): return lax.ppermute(x, 'afd', cores)  3.5 us
    pallas_call x1, Pallas kernels, experts(): pl.pallas_call(functools.partial(expert_kernel, turns), out_shape=[shape]...  2.82 us
    pallas_call x1, Pallas kernels, attend(): pl.pallas_call(attend_kernel, out_shape=(jax.ShapeDtypeStruct((steps * ro...  2.29 us
  transfers between devices with their start and end apart: 18, of which 10 were waited for; matrix products, arithmetic and copies ran while one was open for 0% of the time, Pallas kernels for 11%

profile of v16, /device:TPU:0, one launch (start us, length us, event | category | flops | bytes accessed | tf_op | source)
XLA Modules:
  0.0 41.1 jit_solution(9563784907233521329)
XLA Ops:
  0.0 2.3 %attend.1 = (f32[8,7168]{1,0:T(8,128)S(1)}, bf16[8,7296]{1,0:T(8,128)(2,1)S(1)}) custom-call(s32[4]{0:T(128)} %len_hbm.1, s32[3,2,4]{2,1,0:T(2,128)} %bitcast.6, f32[3,2,4]{2,1,0:T(2,128)} %bitcast.7, bf16[2,4,7168]{2,1,0:T(4,128)(2,1)} %q_hbm.1, bf16[2,4,448]{2,1,0:T(4,128)(2,1)} %fresh_hbm.1, bf16[4,448,128]{2,1,0:T(8,128)(2,1)} %bitcast.4, ...), custom_call_target="tpu_custom_call" | custom-call | flops 300000000 | bytes 2000000 | tf_op jit(solution)/shard_map/attend/pallas_call | solution.py:175
  2.3 0.5 %collective-permute-start = (bf16[8,7296]{1,0:T(8,128)(2,1)S(1)}, bf16[8,7296]{1,0:T(8,128)(2,1)S(1)}, u32[]{:S(2)}, u32[]{:S(2)}) collective-permute-start(bf16[8,7296]{1,0:T(8,128)(2,1)S(1)} %get-tuple-element.25.own_ref), channel_id=1, source_target_pairs={{0,1},{1,0},{2,3},{3,2},{4,5},{5,4},{6,7},{7,6},{8,9},{9,8},{10,11... | collective-permute-start | bytes 350216 | tf_op jit(solution)/shard_map/ppermute | solution.py:440
  2.8 1.0 %collective-permute-done.other_ref = bf16[8,7296]{1,0:T(8,128)(2,1)S(1)} collective-permute-done((bf16[8,7296]{1,0:T(8,128)(2,1)S(1)}, bf16[8,7296]{1,0:T(8,128)(2,1)S(1)}, u32[]{:S(2)}, u32[]{:S(2)}) %collective-permute-start) | collective-permute-done | bytes 116768 | tf_op jit(solution)/shard_map/ppermute | solution.py:440
  3.8 0.5 %pack.1 = (bf16[32,1792]{1,0:T(8,128)(2,1)S(1)}, bf16[32,1792]{1,0:T(8,128)(2,1)S(1)}, bf16[32,1792]{1,0:T(8,128)(2,1)S(1)}, bf16[32,1792]{1,0:T(8,128)(2,1)S(1)}) custom-call(bf16[8,7296]{1,0:T(8,128)(2,1)S(1)} %get-tuple-element.25.own_ref, bf16[8,7296]{1,0:T(8,128)(2,1)S(1)} %collective-permute-done.other_ref), custom_call_target="tpu_custom_call" | custom-call | flops 50000000 | bytes 2000000 | tf_op jit(solution)/shard_map/pack/pallas_call | solution.py:238
  4.3 0.4 %collective-permute-start.1 = (bf16[32,1792]{1,0:T(8,128)(2,1)S(1)}, bf16[32,1792]{1,0:T(8,128)(2,1)S(1)}, u32[]{:S(2)}, u32[]{:S(2)}) collective-permute-start(bf16[32,1792]{1,0:T(8,128)(2,1)S(1)} %get-tuple-element.27), channel_id=1, source_target_pairs={{0,1},{1,14},{2,3},{3,12},{4,5},{5,10},{6,7},{7,8},{8,9},{9,6},{10... | collective-permute-start | bytes 344072 | tf_op jit(solution)/shard_map/ppermute | solution.py:446
  4.7 4.7 %collective-permute-start.2 = (bf16[32,1792]{1,0:T(8,128)(2,1)S(1)}, bf16[32,1792]{1,0:T(8,128)(2,1)S(1)}, u32[]{:S(2)}, u32[]{:S(2)}) collective-permute-start(bf16[32,1792]{1,0:T(8,128)(2,1)S(1)} %get-tuple-element.30), channel_id=1, source_target_pairs={{0,9},{1,6},{2,11},{3,4},{4,13},{5,2},{6,15},{7,0},{8,1},{9,14},{1... | collective-permute-start | bytes 344072 | tf_op jit(solution)/shard_map/ppermute | solution.py:446
  9.5 3.2 %collective-permute-start.4 = (bf16[32,1792]{1,0:T(8,128)(2,1)S(1)}, bf16[32,1792]{1,0:T(8,128)(2,1)S(1)}, u32[]{:S(2)}, u32[]{:S(2)}) collective-permute-start(bf16[32,1792]{1,0:T(8,128)(2,1)S(1)} %get-tuple-element.32), channel_id=1, source_target_pairs={{0,13},{1,2},{2,15},{3,0},{4,9},{5,6},{6,11},{7,4},{8,5},{9,10},{1... | collective-permute-start | bytes 344072 | tf_op jit(solution)/shard_map/ppermute | solution.py:446
  12.7 4.2 %stage.1 = (bf16[2,256,7168]{2,1,0:T(8,128)(2,1)S(1)}, bf16[256,7168]{1,0:T(8,128)(2,1)S(1)}) custom-call(bf16[1,2,256,7168]{3,2,1,0:T(8,128)(2,1)} %gu_hbm.1, bf16[1,256,7168]{2,1,0:T(8,128)(2,1)} %dn_hbm.1), custom_call_target="tpu_custom_call" | custom-call | bytes 22000000 | tf_op jit(solution)/shard_map/stage/pallas_call | solution.py:294
  17.0 2.2 %collective-permute-start.6 = (bf16[32,1792]{1,0:T(8,128)(2,1)S(1)}, bf16[32,1792]{1,0:T(8,128)(2,1)S(1)}, u32[]{:S(2)}, u32[]{:S(2)}) collective-permute-start(bf16[32,1792]{1,0:T(8,128)(2,1)S(1)} %collective-permute-done.2.refs_1_), channel_id=1, source_target_pairs={{0,1},{1,0},{2,3},{3,2},{4,5},{5,4},{6,7},{7,6},{8,9},{9,8},{10,11... | collective-permute-start | bytes 344072 | tf_op jit(solution)/shard_map/ppermute | solution.py:440
  19.2 0.5 %collective-permute-start.8 = (bf16[32,1792]{1,0:T(8,128)(2,1)S(1)}, bf16[32,1792]{1,0:T(8,128)(2,1)S(1)}, u32[]{:S(2)}, u32[]{:S(2)}) collective-permute-start(bf16[32,1792]{1,0:T(8,128)(2,1)S(1)} %collective-permute-done.4.refs_3_), channel_id=1, source_target_pairs={{0,1},{1,0},{2,3},{3,2},{4,5},{5,4},{6,7},{7,6},{8,9},{9,8},{10,11... | collective-permute-start | bytes 344072 | tf_op jit(solution)/shard_map/ppermute | solution.py:440
  19.8 0.4 collective-permute-done.6.refs_5_
  20.2 0.4 collective-permute-done.7.refs_6_
  20.7 0.3 collective-permute-done.5.refs_4_
  21.1 2.8 %experts.1 = (bf16[32,1792]{1,0:T(8,128)(2,1)S(1)}, bf16[32,1792]{1,0:T(8,128)(2,1)S(1)}, bf16[32,1792]{1,0:T(8,128)(2,1)S(1)}, bf16[32,1792]{1,0:T(8,128)(2,1)S...) custom-call(bf16[32,1792]{1,0:T(8,128)(2,1)S(1)} %collective-permute, ...), custom_call_target="tpu_custom_call" | custom-call | flops 800000000 | bytes 12000000 | tf_op jit(solution)/shard_map/experts/pallas_call | solution.py:357
  24.1 0.3 collective-permute-start.11
  24.6 0.3 collective-permute-start.15
  25.3 2.6 %collective-permute-start.10 = (bf16[32,1792]{1,0:T(8,128)(2,1)S(1)}, bf16[32,1792]{1,0:T(8,128)(2,1)S(1)}, u32[]{:S(2)}, u32[]{:S(2)}) collective-permute-start(bf16[32,1792]{1,0:T(8,128)(2,1)S(1)} %add_convert_fusion.3), channel_id=1, source_target_pairs={{1,0},{14,1},{3,2},{12,3},{5,4},{10,5},{7,6},{8,7},{9,8},{6,9},{11... | collective-permute-start | bytes 344072 | tf_op jit(solution)/shard_map/ppermute | solution.py:449
  28.1 2.9 %collective-permute-start.14 = (bf16[32,1792]{1,0:T(8,128)(2,1)S(1)}, bf16[32,1792]{1,0:T(8,128)(2,1)S(1)}, u32[]{:S(2)}, u32[]{:S(2)}) collective-permute-start(bf16[32,1792]{1,0:T(8,128)(2,1)S(1)} %add_convert_fusion.1), channel_id=1, source_target_pairs={{5,0},{10,1},{7,2},{8,3},{1,4},{14,5},{3,6},{12,7},{13,8},{2,9},{1... | collective-permute-start | bytes 344072 | tf_op jit(solution)/shard_map/ppermute | solution.py:449
  31.5 5.4 %collective-permute-done.12.refs_1_ = bf16[32,1792]{1,0:T(8,128)(2,1)S(1)} collective-permute-done((bf16[32,1792]{1,0:T(8,128)(2,1)S(1)}, bf16[32,1792]{1,0:T(8,128)(2,1)S(1)}, u32[]{:S(2)}, u32[]{:S(2)}) %collective-permute-start.12) | collective-permute-done | bytes 114720 | tf_op jit(solution)/shard_map/ppermute | solution.py:449
  36.9 1.2 %collective-permute-done.16.refs_3_ = bf16[32,1792]{1,0:T(8,128)(2,1)S(1)} collective-permute-done((bf16[32,1792]{1,0:T(8,128)(2,1)S(1)}, bf16[32,1792]{1,0:T(8,128)(2,1)S(1)}, u32[]{:S(2)}, u32[]{:S(2)}) %collective-permute-start.16) | collective-permute-done | bytes 114720 | tf_op jit(solution)/shard_map/ppermute | solution.py:449
  38.2 0.3 combine.1
  38.5 0.9 %collective-permute-start.17 = (bf16[8,7168]{1,0:T(8,128)(2,1)S(1)}, bf16[8,7168]{1,0:T(8,128)(2,1)S(1)}, u32[]{:S(2)}, u32[]{:S(2)}) collective-permute-start(bf16[8,7168]{1,0:T(8,128)(2,1)S(1)} %get-tuple-element.44), channel_id=1, source_target_pairs={{0,1},{1,0},{2,3},{3,2},{4,5},{5,4},{6,7},{7,6},{8,9},{9,8},{10,11... | collective-permute-start | bytes 344072 | tf_op jit(solution)/shard_map/ppermute | solution.py:440
  39.4 1.0 %collective-permute-done.17.other_ref = bf16[8,7168]{1,0:T(8,128)(2,1)S(1)} collective-permute-done((bf16[8,7168]{1,0:T(8,128)(2,1)S(1)}, bf16[8,7168]{1,0:T(8,128)(2,1)S(1)}, u32[]{:S(2)}, u32[]{:S(2)}) %collective-permute-start.17) | collective-permute-done | bytes 114720 | tf_op jit(solution)/shard_map/ppermute | solution.py:440
  40.4 0.7 %finish.1 = bf16[2,4,7168]{2,1,0:T(4,128)(2,1)} custom-call(f32[8,7168]{1,0:T(8,128)S(1)} %get-tuple-element.43.kept_ref, bf16[8,7168]{1,0:T(8,128)(2,1)S(1)} %collective-permute-done.17.other_ref), custom_call_target="tpu_custom_call" | custom-call | flops 100000 | bytes 500000 | tf_op jit(solution)/shard_map/finish/pallas_call | solution.py:410
  (23 shorter events, 1.8 us)
Async XLA Ops:
  2.3 1.5 %collective-permute-start = (bf16[8,7296]{1,0:T(8,128)(2,1)S(1)}, bf16[8,7296]{1,0:T(8,128)(2,1)S(1)}, u32[]{:S(2)}, u32[]{:S(2)}) collective-permute-start(bf16[8,7296]{1,0:T(8,128)(2,1)S(1)} %get-tuple-element.25.own_ref), channel_id=1, source_target_pairs={{0,1},{1,0},{2,3},{3,2},{4,5},{5,4},{6,7},{7,6},{8,9},{9,8},{10,11... | collective-permute-start | bytes 350216 | tf_op jit(solution)/shard_map/ppermute | solution.py:440
  4.3 12.7 %collective-permute-start.1 = (bf16[32,1792]{1,0:T(8,128)(2,1)S(1)}, bf16[32,1792]{1,0:T(8,128)(2,1)S(1)}, u32[]{:S(2)}, u32[]{:S(2)}) collective-permute-start(bf16[32,1792]{1,0:T(8,128)(2,1)S(1)} %get-tuple-element.27), channel_id=1, source_target_pairs={{0,1},{1,14},{2,3},{3,12},{4,5},{5,10},{6,7},{7,8},{8,9},{9,6},{10... | collective-permute-start | bytes 344072 | tf_op jit(solution)/shard_map/ppermute | solution.py:446
  4.7 12.3 %collective-permute-start.2 = (bf16[32,1792]{1,0:T(8,128)(2,1)S(1)}, bf16[32,1792]{1,0:T(8,128)(2,1)S(1)}, u32[]{:S(2)}, u32[]{:S(2)}) collective-permute-start(bf16[32,1792]{1,0:T(8,128)(2,1)S(1)} %get-tuple-element.30), channel_id=1, source_target_pairs={{0,9},{1,6},{2,11},{3,4},{4,13},{5,2},{6,15},{7,0},{8,1},{9,14},{1... | collective-permute-start | bytes 344072 | tf_op jit(solution)/shard_map/ppermute | solution.py:446
  9.4 9.8 %collective-permute-start.3 = (bf16[32,1792]{1,0:T(8,128)(2,1)S(1)}, bf16[32,1792]{1,0:T(8,128)(2,1)S(1)}, u32[]{:S(2)}, u32[]{:S(2)}) collective-permute-start(bf16[32,1792]{1,0:T(8,128)(2,1)S(1)} %get-tuple-element.31), channel_id=1, source_target_pairs={{0,5},{1,10},{2,7},{3,8},{4,1},{5,14},{6,3},{7,12},{8,13},{9,2},{1... | collective-permute-start | bytes 344072 | tf_op jit(solution)/shard_map/ppermute | solution.py:446
  9.5 9.7 %collective-permute-start.4 = (bf16[32,1792]{1,0:T(8,128)(2,1)S(1)}, bf16[32,1792]{1,0:T(8,128)(2,1)S(1)}, u32[]{:S(2)}, u32[]{:S(2)}) collective-permute-start(bf16[32,1792]{1,0:T(8,128)(2,1)S(1)} %get-tuple-element.32), channel_id=1, source_target_pairs={{0,13},{1,2},{2,15},{3,0},{4,9},{5,6},{6,11},{7,4},{8,5},{9,10},{1... | collective-permute-start | bytes 344072 | tf_op jit(solution)/shard_map/ppermute | solution.py:446
  17.0 3.2 %collective-permute-start.6 = (bf16[32,1792]{1,0:T(8,128)(2,1)S(1)}, bf16[32,1792]{1,0:T(8,128)(2,1)S(1)}, u32[]{:S(2)}, u32[]{:S(2)}) collective-permute-start(bf16[32,1792]{1,0:T(8,128)(2,1)S(1)} %collective-permute-done.2.refs_1_), channel_id=1, source_target_pairs={{0,1},{1,0},{2,3},{3,2},{4,5},{5,4},{6,7},{7,6},{8,9},{9,8},{10,11... | collective-permute-start | bytes 344072 | tf_op jit(solution)/shard_map/ppermute | solution.py:440
  19.2 1.3 %collective-permute-start.7 = (bf16[32,1792]{1,0:T(8,128)(2,1)S(1)}, bf16[32,1792]{1,0:T(8,128)(2,1)S(1)}, u32[]{:S(2)}, u32[]{:S(2)}) collective-permute-start(bf16[32,1792]{1,0:T(8,128)(2,1)S(1)} %collective-permute-done.3.refs_2_), channel_id=1, source_target_pairs={{0,1},{1,0},{2,3},{3,2},{4,5},{5,4},{6,7},{7,6},{8,9},{9,8},{10,11... | collective-permute-start | bytes 344072 | tf_op jit(solution)/shard_map/ppermute | solution.py:440
  19.2 1.5 %collective-permute-start.8 = (bf16[32,1792]{1,0:T(8,128)(2,1)S(1)}, bf16[32,1792]{1,0:T(8,128)(2,1)S(1)}, u32[]{:S(2)}, u32[]{:S(2)}) collective-permute-start(bf16[32,1792]{1,0:T(8,128)(2,1)S(1)} %collective-permute-done.4.refs_3_), channel_id=1, source_target_pairs={{0,1},{1,0},{2,3},{3,2},{4,5},{5,4},{6,7},{7,6},{8,9},{9,8},{10,11... | collective-permute-start | bytes 344072 | tf_op jit(solution)/shard_map/ppermute | solution.py:440
  19.7 1.3 %collective-permute-start.5 = (bf16[32,1792]{1,0:T(8,128)(2,1)S(1)}, bf16[32,1792]{1,0:T(8,128)(2,1)S(1)}, u32[]{:S(2)}, u32[]{:S(2)}) collective-permute-start(bf16[32,1792]{1,0:T(8,128)(2,1)S(1)} %collective-permute-done.1.refs_0_), channel_id=1, source_target_pairs={{0,1},{1,0},{2,3},{3,2},{4,5},{5,4},{6,7},{7,6},{8,9},{9,8},{10,11... | collective-permute-start | bytes 344072 | tf_op jit(solution)/shard_map/ppermute | solution.py:440
  23.9 1.4 %collective-permute-start.9 = (bf16[32,1792]{1,0:T(8,128)(2,1)S(1)}, bf16[32,1792]{1,0:T(8,128)(2,1)S(1)}, u32[]{:S(2)}, u32[]{:S(2)}) collective-permute-start(bf16[32,1792]{1,0:T(8,128)(2,1)S(1)} %get-tuple-element.36), channel_id=1, source_target_pairs={{0,1},{1,0},{2,3},{3,2},{4,5},{5,4},{6,7},{7,6},{8,9},{9,8},{10,11... | collective-permute-start | bytes 344072 | tf_op jit(solution)/shard_map/ppermute | solution.py:440
  24.1 3.8 %collective-permute-start.11 = (bf16[32,1792]{1,0:T(8,128)(2,1)S(1)}, bf16[32,1792]{1,0:T(8,128)(2,1)S(1)}, u32[]{:S(2)}, u32[]{:S(2)}) collective-permute-start(bf16[32,1792]{1,0:T(8,128)(2,1)S(1)} %get-tuple-element.38), channel_id=1, source_target_pairs={{0,1},{1,0},{2,3},{3,2},{4,5},{5,4},{6,7},{7,6},{8,9},{9,8},{10,11... | collective-permute-start | bytes 344072 | tf_op jit(solution)/shard_map/ppermute | solution.py:440
  24.5 3.6 %collective-permute-start.13 = (bf16[32,1792]{1,0:T(8,128)(2,1)S(1)}, bf16[32,1792]{1,0:T(8,128)(2,1)S(1)}, u32[]{:S(2)}, u32[]{:S(2)}) collective-permute-start(bf16[32,1792]{1,0:T(8,128)(2,1)S(1)} %get-tuple-element.40), channel_id=1, source_target_pairs={{0,1},{1,0},{2,3},{3,2},{4,5},{5,4},{6,7},{7,6},{8,9},{9,8},{10,11... | collective-permute-start | bytes 344072 | tf_op jit(solution)/shard_map/ppermute | solution.py:440
  24.6 6.3 %collective-permute-start.15 = (bf16[32,1792]{1,0:T(8,128)(2,1)S(1)}, bf16[32,1792]{1,0:T(8,128)(2,1)S(1)}, u32[]{:S(2)}, u32[]{:S(2)}) collective-permute-start(bf16[32,1792]{1,0:T(8,128)(2,1)S(1)} %get-tuple-element.42), channel_id=1, source_target_pairs={{0,1},{1,0},{2,3},{3,2},{4,5},{5,4},{6,7},{7,6},{8,9},{9,8},{10,11... | collective-permute-start | bytes 344072 | tf_op jit(solution)/shard_map/ppermute | solution.py:440
  25.3 6.2 %collective-permute-start.10 = (bf16[32,1792]{1,0:T(8,128)(2,1)S(1)}, bf16[32,1792]{1,0:T(8,128)(2,1)S(1)}, u32[]{:S(2)}, u32[]{:S(2)}) collective-permute-start(bf16[32,1792]{1,0:T(8,128)(2,1)S(1)} %add_convert_fusion.3), channel_id=1, source_target_pairs={{1,0},{14,1},{3,2},{12,3},{5,4},{10,5},{7,6},{8,7},{9,8},{6,9},{11... | collective-permute-start | bytes 344072 | tf_op jit(solution)/shard_map/ppermute | solution.py:449
  28.0 9.0 %collective-permute-start.12 = (bf16[32,1792]{1,0:T(8,128)(2,1)S(1)}, bf16[32,1792]{1,0:T(8,128)(2,1)S(1)}, u32[]{:S(2)}, u32[]{:S(2)}) collective-permute-start(bf16[32,1792]{1,0:T(8,128)(2,1)S(1)} %add_convert_fusion.2), channel_id=1, source_target_pairs={{9,0},{6,1},{11,2},{4,3},{13,4},{2,5},{15,6},{0,7},{1,8},{14,9},{3... | collective-permute-start | bytes 344072 | tf_op jit(solution)/shard_map/ppermute | solution.py:449
  28.1 8.9 %collective-permute-start.14 = (bf16[32,1792]{1,0:T(8,128)(2,1)S(1)}, bf16[32,1792]{1,0:T(8,128)(2,1)S(1)}, u32[]{:S(2)}, u32[]{:S(2)}) collective-permute-start(bf16[32,1792]{1,0:T(8,128)(2,1)S(1)} %add_convert_fusion.1), channel_id=1, source_target_pairs={{5,0},{10,1},{7,2},{8,3},{1,4},{14,5},{3,6},{12,7},{13,8},{2,9},{1... | collective-permute-start | bytes 344072 | tf_op jit(solution)/shard_map/ppermute | solution.py:449
  31.0 7.2 %collective-permute-start.16 = (bf16[32,1792]{1,0:T(8,128)(2,1)S(1)}, bf16[32,1792]{1,0:T(8,128)(2,1)S(1)}, u32[]{:S(2)}, u32[]{:S(2)}) collective-permute-start(bf16[32,1792]{1,0:T(8,128)(2,1)S(1)} %add_convert_fusion), channel_id=1, source_target_pairs={{13,0},{2,1},{15,2},{0,3},{9,4},{6,5},{11,6},{4,7},{5,8},{10,9},{7... | collective-permute-start | bytes 344072 | tf_op jit(solution)/shard_map/ppermute | solution.py:449
  38.5 1.9 %collective-permute-start.17 = (bf16[8,7168]{1,0:T(8,128)(2,1)S(1)}, bf16[8,7168]{1,0:T(8,128)(2,1)S(1)}, u32[]{:S(2)}, u32[]{:S(2)}) collective-permute-start(bf16[8,7168]{1,0:T(8,128)(2,1)S(1)} %get-tuple-element.44), channel_id=1, source_target_pairs={{0,1},{1,0},{2,3},{3,2},{4,5},{5,4},{6,7},{7,6},{8,9},{9,8},{10,11... | collective-permute-start | bytes 344072 | tf_op jit(solution)/shard_map/ppermute | solution.py:440

commit v17 on v16

--- a/solution.py
+++ b/solution.py
@@ -464,8 +464,11 @@
     for t in range(0, turns, TOGETHER):
         now = slice(t, t + TOGETHER)
         mine, theirs = experts(own[now], other[now], w_in, w_down)
+        head = (mine[0].astype(F32) + swap(theirs[0]).astype(F32)).astype(BF16)
+        head, theirs = lax.optimization_barrier((head, theirs[1:]))
+        summed += [head]
         summed += [
-            (a.astype(F32) + swap(b).astype(F32)).astype(BF16) for a, b in zip(mine, theirs)
+            (a.astype(F32) + swap(b).astype(F32)).astype(BF16) for a, b in zip(mine[1:], theirs)
         ]
     backs = [send_back(summed[t], t) for t in range(turns)]
     kept, given = combine(mix, resid, backs)

time: 41.2 us -> 42.2 us (1.024)
  starting transfers between devices: 19.3 us -> 19.8 us
  waiting for transfers between devices: 10.4 us -> 10.9 us
    ppermute x10, waiting for transfers between devices: 3.5 us -> 4.35 us  [swap(): return lax.ppermute(x, 'afd', cores)]
where the time goes in v17:
time: 42.2 us; the launch traced here: 42.1 us
  starting transfers between devices  19.8 us (47%)
  Pallas kernels  11.1 us (26%)
  waiting for transfers between devices  10.9 us (26%)
    ppermute x4, starting transfers between devices, send(): return lax.ppermute(x, 'afd', route(t))  8.4 us
    ppermute x4, waiting for transfers between devices, send_back(): return lax.ppermute(x, 'afd', [(j, i) for i, j in route(t)])  6.54 us
    ppermute x4, starting transfers between devices, send_back(): return lax.ppermute(x, 'afd', [(j, i) for i, j in route(t)])  5.74 us
    ppermute x10, starting transfers between devices, swap(): return lax.ppermute(x, 'afd', cores)  5.67 us
    ppermute x10, waiting for transfers between devices, swap(): return lax.ppermute(x, 'afd', cores)  4.35 us
    pallas_call x1, Pallas kernels, stage(): pl.pallas_call(stage_kernel, out_shape=(jax.ShapeDtypeStruct(gate_up.shap...  4.24 us
    pallas_call x1, Pallas kernels, experts(): pl.pallas_call(functools.partial(expert_kernel, turns), out_shape=[shape]...  2.82 us
    pallas_call x1, Pallas kernels, attend(): pl.pallas_call(attend_kernel, out_shape=(jax.ShapeDtypeStruct((steps * ro...  2.29 us
  transfers between devices with their start and end apart: 18, of which 10 were waited for; matrix products, arithmetic and copies ran while one was open for 0% of the time, Pallas kernels for 11%

profile of v17, /device:TPU:0, one launch (start us, length us, event | category | flops | bytes accessed | tf_op | source)
XLA Modules:
  0.0 42.1 jit_solution(3901733426750102881)
XLA Ops:
  0.0 2.3 %attend.1 = (f32[8,7168]{1,0:T(8,128)S(1)}, bf16[8,7296]{1,0:T(8,128)(2,1)S(1)}) custom-call(s32[4]{0:T(128)} %len_hbm.1, s32[3,2,4]{2,1,0:T(2,128)} %bitcast.6, f32[3,2,4]{2,1,0:T(2,128)} %bitcast.7, bf16[2,4,7168]{2,1,0:T(4,128)(2,1)} %q_hbm.1, bf16[2,4,448]{2,1,0:T(4,128)(2,1)} %fresh_hbm.1, bf16[4,448,128]{2,1,0:T(8,128)(2,1)} %bitcast.4, ...), custom_call_target="tpu_custom_call" | custom-call | flops 300000000 | bytes 2000000 | tf_op jit(solution)/shard_map/attend/pallas_call | solution.py:175
  2.3 0.5 %collective-permute-start = (bf16[8,7296]{1,0:T(8,128)(2,1)S(1)}, bf16[8,7296]{1,0:T(8,128)(2,1)S(1)}, u32[]{:S(2)}, u32[]{:S(2)}) collective-permute-start(bf16[8,7296]{1,0:T(8,128)(2,1)S(1)} %get-tuple-element.29.own_ref), channel_id=1, source_target_pairs={{0,1},{1,0},{2,3},{3,2},{4,5},{5,4},{6,7},{7,6},{8,9},{9,8},{10,11... | collective-permute-start | bytes 350216 | tf_op jit(solution)/shard_map/ppermute | solution.py:440
  2.8 1.0 %collective-permute-done.other_ref = bf16[8,7296]{1,0:T(8,128)(2,1)S(1)} collective-permute-done((bf16[8,7296]{1,0:T(8,128)(2,1)S(1)}, bf16[8,7296]{1,0:T(8,128)(2,1)S(1)}, u32[]{:S(2)}, u32[]{:S(2)}) %collective-permute-start) | collective-permute-done | bytes 116768 | tf_op jit(solution)/shard_map/ppermute | solution.py:440
  3.8 0.5 %pack.1 = (bf16[32,1792]{1,0:T(8,128)(2,1)S(1)}, bf16[32,1792]{1,0:T(8,128)(2,1)S(1)}, bf16[32,1792]{1,0:T(8,128)(2,1)S(1)}, bf16[32,1792]{1,0:T(8,128)(2,1)S(1)}) custom-call(bf16[8,7296]{1,0:T(8,128)(2,1)S(1)} %get-tuple-element.29.own_ref, bf16[8,7296]{1,0:T(8,128)(2,1)S(1)} %collective-permute-done.other_ref), custom_call_target="tpu_custom_call" | custom-call | flops 50000000 | bytes 2000000 | tf_op jit(solution)/shard_map/pack/pallas_call | solution.py:238
  4.3 0.4 collective-permute-start.1
  4.7 4.7 %collective-permute-start.2 = (bf16[32,1792]{1,0:T(8,128)(2,1)S(1)}, bf16[32,1792]{1,0:T(8,128)(2,1)S(1)}, u32[]{:S(2)}, u32[]{:S(2)}) collective-permute-start(bf16[32,1792]{1,0:T(8,128)(2,1)S(1)} %get-tuple-element.34), channel_id=1, source_target_pairs={{0,9},{1,6},{2,11},{3,4},{4,13},{5,2},{6,15},{7,0},{8,1},{9,14},{1... | collective-permute-start | bytes 344072 | tf_op jit(solution)/shard_map/ppermute | solution.py:446
  9.5 3.2 %collective-permute-start.4 = (bf16[32,1792]{1,0:T(8,128)(2,1)S(1)}, bf16[32,1792]{1,0:T(8,128)(2,1)S(1)}, u32[]{:S(2)}, u32[]{:S(2)}) collective-permute-start(bf16[32,1792]{1,0:T(8,128)(2,1)S(1)} %get-tuple-element.36), channel_id=1, source_target_pairs={{0,13},{1,2},{2,15},{3,0},{4,9},{5,6},{6,11},{7,4},{8,5},{9,10},{1... | collective-permute-start | bytes 344072 | tf_op jit(solution)/shard_map/ppermute | solution.py:446
  12.7 4.2 %stage.1 = (bf16[2,256,7168]{2,1,0:T(8,128)(2,1)S(1)}, bf16[256,7168]{1,0:T(8,128)(2,1)S(1)}) custom-call(bf16[1,2,256,7168]{3,2,1,0:T(8,128)(2,1)} %gu_hbm.1, bf16[1,256,7168]{2,1,0:T(8,128)(2,1)} %dn_hbm.1), custom_call_target="tpu_custom_call" | custom-call | bytes 22000000 | tf_op jit(solution)/shard_map/stage/pallas_call | solution.py:294
  17.0 2.2 %collective-permute-start.6 = (bf16[32,1792]{1,0:T(8,128)(2,1)S(1)}, bf16[32,1792]{1,0:T(8,128)(2,1)S(1)}, u32[]{:S(2)}, u32[]{:S(2)}) collective-permute-start(bf16[32,1792]{1,0:T(8,128)(2,1)S(1)} %collective-permute-done.2.refs_1_), channel_id=1, source_target_pairs={{0,1},{1,0},{2,3},{3,2},{4,5},{5,4},{6,7},{7,6},{8,9},{9,8},{10,11... | collective-permute-start | bytes 344072 | tf_op jit(solution)/shard_map/ppermute | solution.py:440
  19.2 0.5 %collective-permute-start.8 = (bf16[32,1792]{1,0:T(8,128)(2,1)S(1)}, bf16[32,1792]{1,0:T(8,128)(2,1)S(1)}, u32[]{:S(2)}, u32[]{:S(2)}) collective-permute-start(bf16[32,1792]{1,0:T(8,128)(2,1)S(1)} %collective-permute-done.4.refs_3_), channel_id=1, source_target_pairs={{0,1},{1,0},{2,3},{3,2},{4,5},{5,4},{6,7},{7,6},{8,9},{9,8},{10,11... | collective-permute-start | bytes 344072 | tf_op jit(solution)/shard_map/ppermute | solution.py:440
  19.8 0.4 collective-permute-done.6.refs_5_
  20.2 0.4 collective-permute-done.7.refs_6_
  21.1 2.8 %experts.1 = (bf16[32,1792]{1,0:T(8,128)(2,1)S(1)}, bf16[32,1792]{1,0:T(8,128)(2,1)S(1)}, bf16[32,1792]{1,0:T(8,128)(2,1)S(1)}, bf16[32,1792]{1,0:T(8,128)(2,1)S...) custom-call(bf16[32,1792]{1,0:T(8,128)(2,1)S(1)} %collective-permute, ...), custom_call_target="tpu_custom_call" | custom-call | flops 800000000 | bytes 12000000 | tf_op jit(solution)/shard_map/experts/pallas_call | solution.py:357
  24.1 1.2 %collective-permute-done.9 = bf16[32,1792]{1,0:T(8,128)(2,1)S(1)} collective-permute-done((bf16[32,1792]{1,0:T(8,128)(2,1)S(1)}, bf16[32,1792]{1,0:T(8,128)(2,1)S(1)}, u32[]{:S(2)}, u32[]{:S(2)}) %collective-permute-start.9) | collective-permute-done | bytes 114720 | tf_op jit(solution)/shard_map/ppermute | solution.py:440
  25.5 2.6 %collective-permute-start.10 = (bf16[32,1792]{1,0:T(8,128)(2,1)S(1)}, bf16[32,1792]{1,0:T(8,128)(2,1)S(1)}, u32[]{:S(2)}, u32[]{:S(2)}) collective-permute-start(bf16[32,1792]{1,0:T(8,128)(2,1)S(1)} %add_convert_fusion.3), channel_id=1, source_target_pairs={{1,0},{14,1},{3,2},{12,3},{5,4},{10,5},{7,6},{8,7},{9,8},{6,9},{11... | collective-permute-start | bytes 344072 | tf_op jit(solution)/shard_map/ppermute | solution.py:449
  28.1 0.5 %collective-permute-start.15 = (bf16[32,1792]{1,0:T(8,128)(2,1)S(1)}, bf16[32,1792]{1,0:T(8,128)(2,1)S(1)}, u32[]{:S(2)}, u32[]{:S(2)}) collective-permute-start(bf16[32,1792]{1,0:T(8,128)(2,1)S(1)} %get-tuple-element.50), channel_id=1, source_target_pairs={{0,1},{1,0},{2,3},{3,2},{4,5},{5,4},{6,7},{7,6},{8,9},{9,8},{10,11... | collective-permute-start | bytes 344072 | tf_op jit(solution)/shard_map/ppermute | solution.py:440
  28.7 1.0 %collective-permute-start.12 = (bf16[32,1792]{1,0:T(8,128)(2,1)S(1)}, bf16[32,1792]{1,0:T(8,128)(2,1)S(1)}, u32[]{:S(2)}, u32[]{:S(2)}) collective-permute-start(bf16[32,1792]{1,0:T(8,128)(2,1)S(1)} %add_convert_fusion.2), channel_id=1, source_target_pairs={{9,0},{6,1},{11,2},{4,3},{13,4},{2,5},{15,6},{0,7},{1,8},{14,9},{3... | collective-permute-start | bytes 344072 | tf_op jit(solution)/shard_map/ppermute | solution.py:449
  29.7 2.1 %collective-permute-start.14 = (bf16[32,1792]{1,0:T(8,128)(2,1)S(1)}, bf16[32,1792]{1,0:T(8,128)(2,1)S(1)}, u32[]{:S(2)}, u32[]{:S(2)}) collective-permute-start(bf16[32,1792]{1,0:T(8,128)(2,1)S(1)} %add_convert_fusion.1), channel_id=1, source_target_pairs={{5,0},{10,1},{7,2},{8,3},{1,4},{14,5},{3,6},{12,7},{13,8},{2,9},{1... | collective-permute-start | bytes 344072 | tf_op jit(solution)/shard_map/ppermute | solution.py:449
  32.2 3.6 %collective-permute-done.12.refs_1_ = bf16[32,1792]{1,0:T(8,128)(2,1)S(1)} collective-permute-done((bf16[32,1792]{1,0:T(8,128)(2,1)S(1)}, bf16[32,1792]{1,0:T(8,128)(2,1)S(1)}, u32[]{:S(2)}, u32[]{:S(2)}) %collective-permute-start.12) | collective-permute-done | bytes 114720 | tf_op jit(solution)/shard_map/ppermute | solution.py:449
  35.9 0.8 %collective-permute-done.14.refs_2_ = bf16[32,1792]{1,0:T(8,128)(2,1)S(1)} collective-permute-done((bf16[32,1792]{1,0:T(8,128)(2,1)S(1)}, bf16[32,1792]{1,0:T(8,128)(2,1)S(1)}, u32[]{:S(2)}, u32[]{:S(2)}) %collective-permute-start.14) | collective-permute-done | bytes 114720 | tf_op jit(solution)/shard_map/ppermute | solution.py:449
  36.7 2.1 %collective-permute-done.16.refs_3_ = bf16[32,1792]{1,0:T(8,128)(2,1)S(1)} collective-permute-done((bf16[32,1792]{1,0:T(8,128)(2,1)S(1)}, bf16[32,1792]{1,0:T(8,128)(2,1)S(1)}, u32[]{:S(2)}, u32[]{:S(2)}) %collective-permute-start.16) | collective-permute-done | bytes 114720 | tf_op jit(solution)/shard_map/ppermute | solution.py:449
  39.1 1.4 %collective-permute-start.17 = (bf16[8,7168]{1,0:T(8,128)(2,1)S(1)}, bf16[8,7168]{1,0:T(8,128)(2,1)S(1)}, u32[]{:S(2)}, u32[]{:S(2)}) collective-permute-start(bf16[8,7168]{1,0:T(8,128)(2,1)S(1)} %get-tuple-element.52), channel_id=1, source_target_pairs={{0,1},{1,0},{2,3},{3,2},{4,5},{5,4},{6,7},{7,6},{8,9},{9,8},{10,11... | collective-permute-start | bytes 344072 | tf_op jit(solution)/shard_map/ppermute | solution.py:440
  40.5 1.0 %collective-permute-done.17.other_ref = bf16[8,7168]{1,0:T(8,128)(2,1)S(1)} collective-permute-done((bf16[8,7168]{1,0:T(8,128)(2,1)S(1)}, bf16[8,7168]{1,0:T(8,128)(2,1)S(1)}, u32[]{:S(2)}, u32[]{:S(2)}) %collective-permute-start.17) | collective-permute-done | bytes 114720 | tf_op jit(solution)/shard_map/ppermute | solution.py:440
  41.4 0.7 %finish.1 = bf16[2,4,7168]{2,1,0:T(4,128)(2,1)} custom-call(f32[8,7168]{1,0:T(8,128)S(1)} %get-tuple-element.51.kept_ref, bf16[8,7168]{1,0:T(8,128)(2,1)S(1)} %collective-permute-done.17.other_ref), custom_call_target="tpu_custom_call" | custom-call | flops 100000 | bytes 500000 | tf_op jit(solution)/shard_map/finish/pallas_call | solution.py:410
  (23 shorter events, 2.0 us)
Async XLA Ops:
  2.3 1.5 %collective-permute-start = (bf16[8,7296]{1,0:T(8,128)(2,1)S(1)}, bf16[8,7296]{1,0:T(8,128)(2,1)S(1)}, u32[]{:S(2)}, u32[]{:S(2)}) collective-permute-start(bf16[8,7296]{1,0:T(8,128)(2,1)S(1)} %get-tuple-element.29.own_ref), channel_id=1, source_target_pairs={{0,1},{1,0},{2,3},{3,2},{4,5},{5,4},{6,7},{7,6},{8,9},{9,8},{10,11... | collective-permute-start | bytes 350216 | tf_op jit(solution)/shard_map/ppermute | solution.py:440
  4.3 12.7 %collective-permute-start.1 = (bf16[32,1792]{1,0:T(8,128)(2,1)S(1)}, bf16[32,1792]{1,0:T(8,128)(2,1)S(1)}, u32[]{:S(2)}, u32[]{:S(2)}) collective-permute-start(bf16[32,1792]{1,0:T(8,128)(2,1)S(1)} %get-tuple-element.31), channel_id=1, source_target_pairs={{0,1},{1,14},{2,3},{3,12},{4,5},{5,10},{6,7},{7,8},{8,9},{9,6},{10... | collective-permute-start | bytes 344072 | tf_op jit(solution)/shard_map/ppermute | solution.py:446
  4.7 12.3 %collective-permute-start.2 = (bf16[32,1792]{1,0:T(8,128)(2,1)S(1)}, bf16[32,1792]{1,0:T(8,128)(2,1)S(1)}, u32[]{:S(2)}, u32[]{:S(2)}) collective-permute-start(bf16[32,1792]{1,0:T(8,128)(2,1)S(1)} %get-tuple-element.34), channel_id=1, source_target_pairs={{0,9},{1,6},{2,11},{3,4},{4,13},{5,2},{6,15},{7,0},{8,1},{9,14},{1... | collective-permute-start | bytes 344072 | tf_op jit(solution)/shard_map/ppermute | solution.py:446
  9.4 9.8 %collective-permute-start.3 = (bf16[32,1792]{1,0:T(8,128)(2,1)S(1)}, bf16[32,1792]{1,0:T(8,128)(2,1)S(1)}, u32[]{:S(2)}, u32[]{:S(2)}) collective-permute-start(bf16[32,1792]{1,0:T(8,128)(2,1)S(1)} %get-tuple-element.35), channel_id=1, source_target_pairs={{0,5},{1,10},{2,7},{3,8},{4,1},{5,14},{6,3},{7,12},{8,13},{9,2},{1... | collective-permute-start | bytes 344072 | tf_op jit(solution)/shard_map/ppermute | solution.py:446
  9.5 9.7 %collective-permute-start.4 = (bf16[32,1792]{1,0:T(8,128)(2,1)S(1)}, bf16[32,1792]{1,0:T(8,128)(2,1)S(1)}, u32[]{:S(2)}, u32[]{:S(2)}) collective-permute-start(bf16[32,1792]{1,0:T(8,128)(2,1)S(1)} %get-tuple-element.36), channel_id=1, source_target_pairs={{0,13},{1,2},{2,15},{3,0},{4,9},{5,6},{6,11},{7,4},{8,5},{9,10},{1... | collective-permute-start | bytes 344072 | tf_op jit(solution)/shard_map/ppermute | solution.py:446
  17.0 3.2 %collective-permute-start.6 = (bf16[32,1792]{1,0:T(8,128)(2,1)S(1)}, bf16[32,1792]{1,0:T(8,128)(2,1)S(1)}, u32[]{:S(2)}, u32[]{:S(2)}) collective-permute-start(bf16[32,1792]{1,0:T(8,128)(2,1)S(1)} %collective-permute-done.2.refs_1_), channel_id=1, source_target_pairs={{0,1},{1,0},{2,3},{3,2},{4,5},{5,4},{6,7},{7,6},{8,9},{9,8},{10,11... | collective-permute-start | bytes 344072 | tf_op jit(solution)/shard_map/ppermute | solution.py:440
  19.2 1.3 %collective-permute-start.7 = (bf16[32,1792]{1,0:T(8,128)(2,1)S(1)}, bf16[32,1792]{1,0:T(8,128)(2,1)S(1)}, u32[]{:S(2)}, u32[]{:S(2)}) collective-permute-start(bf16[32,1792]{1,0:T(8,128)(2,1)S(1)} %collective-permute-done.3.refs_2_), channel_id=1, source_target_pairs={{0,1},{1,0},{2,3},{3,2},{4,5},{5,4},{6,7},{7,6},{8,9},{9,8},{10,11... | collective-permute-start | bytes 344072 | tf_op jit(solution)/shard_map/ppermute | solution.py:440
  19.2 1.5 %collective-permute-start.8 = (bf16[32,1792]{1,0:T(8,128)(2,1)S(1)}, bf16[32,1792]{1,0:T(8,128)(2,1)S(1)}, u32[]{:S(2)}, u32[]{:S(2)}) collective-permute-start(bf16[32,1792]{1,0:T(8,128)(2,1)S(1)} %collective-permute-done.4.refs_3_), channel_id=1, source_target_pairs={{0,1},{1,0},{2,3},{3,2},{4,5},{5,4},{6,7},{7,6},{8,9},{9,8},{10,11... | collective-permute-start | bytes 344072 | tf_op jit(solution)/shard_map/ppermute | solution.py:440
  19.7 1.3 %collective-permute-start.5 = (bf16[32,1792]{1,0:T(8,128)(2,1)S(1)}, bf16[32,1792]{1,0:T(8,128)(2,1)S(1)}, u32[]{:S(2)}, u32[]{:S(2)}) collective-permute-start(bf16[32,1792]{1,0:T(8,128)(2,1)S(1)} %collective-permute-done.1.refs_0_), channel_id=1, source_target_pairs={{0,1},{1,0},{2,3},{3,2},{4,5},{5,4},{6,7},{7,6},{8,9},{9,8},{10,11... | collective-permute-start | bytes 344072 | tf_op jit(solution)/shard_map/ppermute | solution.py:440
  23.9 1.4 %collective-permute-start.9 = (bf16[32,1792]{1,0:T(8,128)(2,1)S(1)}, bf16[32,1792]{1,0:T(8,128)(2,1)S(1)}, u32[]{:S(2)}, u32[]{:S(2)}) collective-permute-start(bf16[32,1792]{1,0:T(8,128)(2,1)S(1)} %get-tuple-element.40), channel_id=1, source_target_pairs={{0,1},{1,0},{2,3},{3,2},{4,5},{5,4},{6,7},{7,6},{8,9},{9,8},{10,11... | collective-permute-start | bytes 344072 | tf_op jit(solution)/shard_map/ppermute | solution.py:440
  25.3 3.3 %collective-permute-start.11 = (bf16[32,1792]{1,0:T(8,128)(2,1)S(1)}, bf16[32,1792]{1,0:T(8,128)(2,1)S(1)}, u32[]{:S(2)}, u32[]{:S(2)}) collective-permute-start(bf16[32,1792]{1,0:T(8,128)(2,1)S(1)} %get-tuple-element.46), channel_id=1, source_target_pairs={{0,1},{1,0},{2,3},{3,2},{4,5},{5,4},{6,7},{7,6},{8,9},{9,8},{10,11... | collective-permute-start | bytes 344072 | tf_op jit(solution)/shard_map/ppermute | solution.py:440
  25.5 6.7 %collective-permute-start.10 = (bf16[32,1792]{1,0:T(8,128)(2,1)S(1)}, bf16[32,1792]{1,0:T(8,128)(2,1)S(1)}, u32[]{:S(2)}, u32[]{:S(2)}) collective-permute-start(bf16[32,1792]{1,0:T(8,128)(2,1)S(1)} %add_convert_fusion.3), channel_id=1, source_target_pairs={{1,0},{14,1},{3,2},{12,3},{5,4},{10,5},{7,6},{8,7},{9,8},{6,9},{11... | collective-permute-start | bytes 344072 | tf_op jit(solution)/shard_map/ppermute | solution.py:449
  28.1 1.5 %collective-permute-start.13 = (bf16[32,1792]{1,0:T(8,128)(2,1)S(1)}, bf16[32,1792]{1,0:T(8,128)(2,1)S(1)}, u32[]{:S(2)}, u32[]{:S(2)}) collective-permute-start(bf16[32,1792]{1,0:T(8,128)(2,1)S(1)} %get-tuple-element.48), channel_id=1, source_target_pairs={{0,1},{1,0},{2,3},{3,2},{4,5},{5,4},{6,7},{7,6},{8,9},{9,8},{10,11... | collective-permute-start | bytes 344072 | tf_op jit(solution)/shard_map/ppermute | solution.py:440
  28.1 3.7 %collective-permute-start.15 = (bf16[32,1792]{1,0:T(8,128)(2,1)S(1)}, bf16[32,1792]{1,0:T(8,128)(2,1)S(1)}, u32[]{:S(2)}, u32[]{:S(2)}) collective-permute-start(bf16[32,1792]{1,0:T(8,128)(2,1)S(1)} %get-tuple-element.50), channel_id=1, source_target_pairs={{0,1},{1,0},{2,3},{3,2},{4,5},{5,4},{6,7},{7,6},{8,9},{9,8},{10,11... | collective-permute-start | bytes 344072 | tf_op jit(solution)/shard_map/ppermute | solution.py:440
  28.7 7.2 %collective-permute-start.12 = (bf16[32,1792]{1,0:T(8,128)(2,1)S(1)}, bf16[32,1792]{1,0:T(8,128)(2,1)S(1)}, u32[]{:S(2)}, u32[]{:S(2)}) collective-permute-start(bf16[32,1792]{1,0:T(8,128)(2,1)S(1)} %add_convert_fusion.2), channel_id=1, source_target_pairs={{9,0},{6,1},{11,2},{4,3},{13,4},{2,5},{15,6},{0,7},{1,8},{14,9},{3... | collective-permute-start | bytes 344072 | tf_op jit(solution)/shard_map/ppermute | solution.py:449
  29.7 7.0 %collective-permute-start.14 = (bf16[32,1792]{1,0:T(8,128)(2,1)S(1)}, bf16[32,1792]{1,0:T(8,128)(2,1)S(1)}, u32[]{:S(2)}, u32[]{:S(2)}) collective-permute-start(bf16[32,1792]{1,0:T(8,128)(2,1)S(1)} %add_convert_fusion.1), channel_id=1, source_target_pairs={{5,0},{10,1},{7,2},{8,3},{1,4},{14,5},{3,6},{12,7},{13,8},{2,9},{1... | collective-permute-start | bytes 344072 | tf_op jit(solution)/shard_map/ppermute | solution.py:449
  31.8 6.9 %collective-permute-start.16 = (bf16[32,1792]{1,0:T(8,128)(2,1)S(1)}, bf16[32,1792]{1,0:T(8,128)(2,1)S(1)}, u32[]{:S(2)}, u32[]{:S(2)}) collective-permute-start(bf16[32,1792]{1,0:T(8,128)(2,1)S(1)} %add_convert_fusion), channel_id=1, source_target_pairs={{13,0},{2,1},{15,2},{0,3},{9,4},{6,5},{11,6},{4,7},{5,8},{10,9},{7... | collective-permute-start | bytes 344072 | tf_op jit(solution)/shard_map/ppermute | solution.py:449
  39.1 2.3 %collective-permute-start.17 = (bf16[8,7168]{1,0:T(8,128)(2,1)S(1)}, bf16[8,7168]{1,0:T(8,128)(2,1)S(1)}, u32[]{:S(2)}, u32[]{:S(2)}) collective-permute-start(bf16[8,7168]{1,0:T(8,128)(2,1)S(1)} %get-tuple-element.52), channel_id=1, source_target_pairs={{0,1},{1,0},{2,3},{3,2},{4,5},{5,4},{6,7},{7,6},{8,9},{9,8},{10,11... | collective-permute-start | bytes 344072 | tf_op jit(solution)/shard_map/ppermute | solution.py:440

commit v18 on v16

--- a/solution.py
+++ b/solution.py
@@ -455,10 +455,10 @@
     )
     normed_other = swap(normed)
     sent = pack(steps, chips, normed, normed_other)
-    own = [send(sent[t], t) for t in range(turns)]
     w_in, w_down = stage(gate_up, down)
+    last, w_in = lax.optimization_barrier((sent[-1], w_in))
+    own = [send(x, t) for t, x in enumerate([*sent[:-1], last])]
     mix = mixer(steps, chips, normed, normed_other)
-    own[0], w_in = lax.optimization_barrier((own[0], w_in))
     other = [swap(x) for x in own]
     summed = []
     for t in range(0, turns, TOGETHER):

time: 41.2 us -> 44 us (1.068)
  starting transfers between devices: 19.3 us -> 23.3 us
  waiting for transfers between devices: 10.4 us -> 9.19 us
    ppermute x10, starting transfers between devices: 5.32 us -> 9.12 us  [swap(): return lax.ppermute(x, 'afd', cores)]
    ppermute x10, waiting for transfers between devices: 3.5 us -> 2.25 us  [swap(): return lax.ppermute(x, 'afd', cores)]
  transfers between devices with their start and end apart: 18 -> 18, of which waited for: 10 -> 6; matrix products, arithmetic and copies ran while one was open for 0% -> 0% of each run, Pallas kernels for 11% -> 10%
where the time goes in v18:
time: 44 us; the launch traced here: 43.9 us
  starting transfers between devices  23.3 us (53%)
  Pallas kernels  11.2 us (25%)
  waiting for transfers between devices  9.19 us (21%)
    ppermute x10, starting transfers between devices, swap(): return lax.ppermute(x, 'afd', cores)  9.12 us
    ppermute x4, starting transfers between devices, send(): return lax.ppermute(x, 'afd', route(t))  8.4 us
    ppermute x4, waiting for transfers between devices, send_back(): return lax.ppermute(x, 'afd', [(j, i) for i, j in route(t)])  6.93 us
    ppermute x4, starting transfers between devices, send_back(): return lax.ppermute(x, 'afd', [(j, i) for i, j in route(t)])  5.76 us
    pallas_call x1, Pallas kernels, stage(): pl.pallas_call(stage_kernel, out_shape=(jax.ShapeDtypeStruct(gate_up.shap...  4.24 us
    pallas_call x1, Pallas kernels, experts(): pl.pallas_call(functools.partial(expert_kernel, turns), out_shape=[shape]...  2.82 us
    pallas_call x1, Pallas kernels, attend(): pl.pallas_call(attend_kernel, out_shape=(jax.ShapeDtypeStruct((steps * ro...  2.29 us
    ppermute x10, waiting for transfers between devices, swap(): return lax.ppermute(x, 'afd', cores)  2.25 us
  transfers between devices with their start and end apart: 18, of which 6 were waited for; matrix products, arithmetic and copies ran while one was open for 0% of the time, Pallas kernels for 10%

profile of v18, /device:TPU:0, one launch (start us, length us, event | category | flops | bytes accessed | tf_op | source)
XLA Modules:
  0.0 43.9 jit_solution(5371381150272971540)
XLA Ops:
  0.0 2.3 %attend.1 = (f32[8,7168]{1,0:T(8,128)S(1)}, bf16[8,7296]{1,0:T(8,128)(2,1)S(1)}) custom-call(s32[4]{0:T(128)} %len_hbm.1, s32[3,2,4]{2,1,0:T(2,128)} %bitcast.6, f32[3,2,4]{2,1,0:T(2,128)} %bitcast.7, bf16[2,4,7168]{2,1,0:T(4,128)(2,1)} %q_hbm.1, bf16[2,4,448]{2,1,0:T(4,128)(2,1)} %fresh_hbm.1, bf16[4,448,128]{2,1,0:T(8,128)(2,1)} %bitcast.4, ...), custom_call_target="tpu_custom_call" | custom-call | flops 300000000 | bytes 2000000 | tf_op jit(solution)/shard_map/attend/pallas_call | solution.py:175
  2.3 0.5 %collective-permute-start = (bf16[8,7296]{1,0:T(8,128)(2,1)S(1)}, bf16[8,7296]{1,0:T(8,128)(2,1)S(1)}, u32[]{:S(2)}, u32[]{:S(2)}) collective-permute-start(bf16[8,7296]{1,0:T(8,128)(2,1)S(1)} %get-tuple-element.25.own_ref), channel_id=1, source_target_pairs={{0,1},{1,0},{2,3},{3,2},{4,5},{5,4},{6,7},{7,6},{8,9},{9,8},{10,11... | collective-permute-start | bytes 350216 | tf_op jit(solution)/shard_map/ppermute | solution.py:440
  2.8 4.2 %stage.1 = (bf16[2,256,7168]{2,1,0:T(8,128)(2,1)S(1)}, bf16[256,7168]{1,0:T(8,128)(2,1)S(1)}) custom-call(bf16[1,2,256,7168]{3,2,1,0:T(8,128)(2,1)} %gu_hbm.1, bf16[1,256,7168]{2,1,0:T(8,128)(2,1)} %dn_hbm.1), custom_call_target="tpu_custom_call" | custom-call | bytes 22000000 | tf_op jit(solution)/shard_map/stage/pallas_call | solution.py:294
  7.1 0.5 %pack.1 = (bf16[32,1792]{1,0:T(8,128)(2,1)S(1)}, bf16[32,1792]{1,0:T(8,128)(2,1)S(1)}, bf16[32,1792]{1,0:T(8,128)(2,1)S(1)}, bf16[32,1792]{1,0:T(8,128)(2,1)S(1)}) custom-call(bf16[8,7296]{1,0:T(8,128)(2,1)S(1)} %get-tuple-element.25.own_ref, bf16[8,7296]{1,0:T(8,128)(2,1)S(1)} %collective-permute-done.other_ref), custom_call_target="tpu_custom_call" | custom-call | flops 50000000 | bytes 2000000 | tf_op jit(solution)/shard_map/pack/pallas_call | solution.py:238
  7.7 4.6 %collective-permute-start.2 = (bf16[32,1792]{1,0:T(8,128)(2,1)S(1)}, bf16[32,1792]{1,0:T(8,128)(2,1)S(1)}, u32[]{:S(2)}, u32[]{:S(2)}) collective-permute-start(bf16[32,1792]{1,0:T(8,128)(2,1)S(1)} %get-tuple-element.28), channel_id=1, source_target_pairs={{0,9},{1,6},{2,11},{3,4},{4,13},{5,2},{6,15},{7,0},{8,1},{9,14},{1... | collective-permute-start | bytes 344072 | tf_op jit(solution)/shard_map/ppermute | solution.py:446
  12.5 3.5 %collective-permute-start.4 = (bf16[32,1792]{1,0:T(8,128)(2,1)S(1)}, bf16[32,1792]{1,0:T(8,128)(2,1)S(1)}, u32[]{:S(2)}, u32[]{:S(2)}) collective-permute-start(bf16[32,1792]{1,0:T(8,128)(2,1)S(1)} %get-tuple-element.32), channel_id=1, source_target_pairs={{0,13},{1,2},{2,15},{3,0},{4,9},{5,6},{6,11},{7,4},{8,5},{9,10},{1... | collective-permute-start | bytes 344072 | tf_op jit(solution)/shard_map/ppermute | solution.py:446
  16.0 0.3 collective-permute-start.5
  16.3 5.9 %collective-permute-start.6 = (bf16[32,1792]{1,0:T(8,128)(2,1)S(1)}, bf16[32,1792]{1,0:T(8,128)(2,1)S(1)}, u32[]{:S(2)}, u32[]{:S(2)}) collective-permute-start(bf16[32,1792]{1,0:T(8,128)(2,1)S(1)} %collective-permute-done.2.refs_1_), channel_id=1, source_target_pairs={{0,1},{1,0},{2,3},{3,2},{4,5},{5,4},{6,7},{7,6},{8,9},{9,8},{10,11... | collective-permute-start | bytes 344072 | tf_op jit(solution)/shard_map/ppermute | solution.py:440
  22.2 0.5 %collective-permute-start.8 = (bf16[32,1792]{1,0:T(8,128)(2,1)S(1)}, bf16[32,1792]{1,0:T(8,128)(2,1)S(1)}, u32[]{:S(2)}, u32[]{:S(2)}) collective-permute-start(bf16[32,1792]{1,0:T(8,128)(2,1)S(1)} %collective-permute-done.4.refs_3_), channel_id=1, source_target_pairs={{0,1},{1,0},{2,3},{3,2},{4,5},{5,4},{6,7},{7,6},{8,9},{9,8},{10,11... | collective-permute-start | bytes 344072 | tf_op jit(solution)/shard_map/ppermute | solution.py:440
  22.7 0.4 %collective-permute-done.6.refs_5_ = bf16[32,1792]{1,0:T(8,128)(2,1)S(1)} collective-permute-done((bf16[32,1792]{1,0:T(8,128)(2,1)S(1)}, bf16[32,1792]{1,0:T(8,128)(2,1)S(1)}, u32[]{:S(2)}, u32[]{:S(2)}) %collective-permute-start.6) | collective-permute-done | bytes 114720 | tf_op jit(solution)/shard_map/ppermute | solution.py:440
  23.2 0.4 collective-permute-done.7.refs_6_
  23.5 0.2 collective-permute-done.8.refs_7_
  23.7 2.8 %experts.1 = (bf16[32,1792]{1,0:T(8,128)(2,1)S(1)}, bf16[32,1792]{1,0:T(8,128)(2,1)S(1)}, bf16[32,1792]{1,0:T(8,128)(2,1)S(1)}, bf16[32,1792]{1,0:T(8,128)(2,1)S...) custom-call(bf16[32,1792]{1,0:T(8,128)(2,1)S(1)} %collective-permute, ...), custom_call_target="tpu_custom_call" | custom-call | flops 800000000 | bytes 12000000 | tf_op jit(solution)/shard_map/experts/pallas_call | solution.py:357
  26.5 0.4 collective-permute-start.9
  27.1 0.3 collective-permute-start.13
  27.6 0.3 collective-permute-done.9
  27.9 2.1 %collective-permute-start.10 = (bf16[32,1792]{1,0:T(8,128)(2,1)S(1)}, bf16[32,1792]{1,0:T(8,128)(2,1)S(1)}, u32[]{:S(2)}, u32[]{:S(2)}) collective-permute-start(bf16[32,1792]{1,0:T(8,128)(2,1)S(1)} %add_convert_fusion.3), channel_id=1, source_target_pairs={{1,0},{14,1},{3,2},{12,3},{5,4},{10,5},{7,6},{8,7},{9,8},{6,9},{11... | collective-permute-start | bytes 344072 | tf_op jit(solution)/shard_map/ppermute | solution.py:449
  30.2 3.6 %collective-permute-start.14 = (bf16[32,1792]{1,0:T(8,128)(2,1)S(1)}, bf16[32,1792]{1,0:T(8,128)(2,1)S(1)}, u32[]{:S(2)}, u32[]{:S(2)}) collective-permute-start(bf16[32,1792]{1,0:T(8,128)(2,1)S(1)} %add_convert_fusion.1), channel_id=1, source_target_pairs={{5,0},{10,1},{7,2},{8,3},{1,4},{14,5},{3,6},{12,7},{13,8},{2,9},{1... | collective-permute-start | bytes 344072 | tf_op jit(solution)/shard_map/ppermute | solution.py:449
  33.8 0.3 mixer.1.mix_ref
  34.1 6.9 %collective-permute-done.12.refs_1_ = bf16[32,1792]{1,0:T(8,128)(2,1)S(1)} collective-permute-done((bf16[32,1792]{1,0:T(8,128)(2,1)S(1)}, bf16[32,1792]{1,0:T(8,128)(2,1)S(1)}, u32[]{:S(2)}, u32[]{:S(2)}) %collective-permute-start.12) | collective-permute-done | bytes 114720 | tf_op jit(solution)/shard_map/ppermute | solution.py:449
  41.1 0.3 combine.1
  41.4 0.8 %collective-permute-start.17 = (bf16[8,7168]{1,0:T(8,128)(2,1)S(1)}, bf16[8,7168]{1,0:T(8,128)(2,1)S(1)}, u32[]{:S(2)}, u32[]{:S(2)}) collective-permute-start(bf16[8,7168]{1,0:T(8,128)(2,1)S(1)} %get-tuple-element.44), channel_id=1, source_target_pairs={{0,1},{1,0},{2,3},{3,2},{4,5},{5,4},{6,7},{7,6},{8,9},{9,8},{10,11... | collective-permute-start | bytes 344072 | tf_op jit(solution)/shard_map/ppermute | solution.py:440
  42.2 1.0 %collective-permute-done.17.other_ref = bf16[8,7168]{1,0:T(8,128)(2,1)S(1)} collective-permute-done((bf16[8,7168]{1,0:T(8,128)(2,1)S(1)}, bf16[8,7168]{1,0:T(8,128)(2,1)S(1)}, u32[]{:S(2)}, u32[]{:S(2)}) %collective-permute-start.17) | collective-permute-done | bytes 114720 | tf_op jit(solution)/shard_map/ppermute | solution.py:440
  43.2 0.7 %finish.1 = bf16[2,4,7168]{2,1,0:T(4,128)(2,1)} custom-call(f32[8,7168]{1,0:T(8,128)S(1)} %get-tuple-element.43.kept_ref, bf16[8,7168]{1,0:T(8,128)(2,1)S(1)} %collective-permute-done.17.other_ref), custom_call_target="tpu_custom_call" | custom-call | flops 100000 | bytes 500000 | tf_op jit(solution)/shard_map/finish/pallas_call | solution.py:410
  (23 shorter events, 0.8 us)
Async XLA Ops:
  2.3 4.8 %collective-permute-start = (bf16[8,7296]{1,0:T(8,128)(2,1)S(1)}, bf16[8,7296]{1,0:T(8,128)(2,1)S(1)}, u32[]{:S(2)}, u32[]{:S(2)}) collective-permute-start(bf16[8,7296]{1,0:T(8,128)(2,1)S(1)} %get-tuple-element.25.own_ref), channel_id=1, source_target_pairs={{0,1},{1,0},{2,3},{3,2},{4,5},{5,4},{6,7},{7,6},{8,9},{9,8},{10,11... | collective-permute-start | bytes 350216 | tf_op jit(solution)/shard_map/ppermute | solution.py:440
  7.6 8.4 %collective-permute-start.1 = (bf16[32,1792]{1,0:T(8,128)(2,1)S(1)}, bf16[32,1792]{1,0:T(8,128)(2,1)S(1)}, u32[]{:S(2)}, u32[]{:S(2)}) collective-permute-start(bf16[32,1792]{1,0:T(8,128)(2,1)S(1)} %get-tuple-element.27), channel_id=1, source_target_pairs={{0,1},{1,14},{2,3},{3,12},{4,5},{5,10},{6,7},{7,8},{8,9},{9,6},{10... | collective-permute-start | bytes 344072 | tf_op jit(solution)/shard_map/ppermute | solution.py:446
  7.7 8.6 %collective-permute-start.2 = (bf16[32,1792]{1,0:T(8,128)(2,1)S(1)}, bf16[32,1792]{1,0:T(8,128)(2,1)S(1)}, u32[]{:S(2)}, u32[]{:S(2)}) collective-permute-start(bf16[32,1792]{1,0:T(8,128)(2,1)S(1)} %get-tuple-element.28), channel_id=1, source_target_pairs={{0,9},{1,6},{2,11},{3,4},{4,13},{5,2},{6,15},{7,0},{8,1},{9,14},{1... | collective-permute-start | bytes 344072 | tf_op jit(solution)/shard_map/ppermute | solution.py:446
  12.4 9.8 %collective-permute-start.3 = (bf16[32,1792]{1,0:T(8,128)(2,1)S(1)}, bf16[32,1792]{1,0:T(8,128)(2,1)S(1)}, u32[]{:S(2)}, u32[]{:S(2)}) collective-permute-start(bf16[32,1792]{1,0:T(8,128)(2,1)S(1)} %get-tuple-element.29), channel_id=1, source_target_pairs={{0,5},{1,10},{2,7},{3,8},{4,1},{5,14},{6,3},{7,12},{8,13},{9,2},{1... | collective-permute-start | bytes 344072 | tf_op jit(solution)/shard_map/ppermute | solution.py:446
  12.5 9.7 %collective-permute-start.4 = (bf16[32,1792]{1,0:T(8,128)(2,1)S(1)}, bf16[32,1792]{1,0:T(8,128)(2,1)S(1)}, u32[]{:S(2)}, u32[]{:S(2)}) collective-permute-start(bf16[32,1792]{1,0:T(8,128)(2,1)S(1)} %get-tuple-element.32), channel_id=1, source_target_pairs={{0,13},{1,2},{2,15},{3,0},{4,9},{5,6},{6,11},{7,4},{8,5},{9,10},{1... | collective-permute-start | bytes 344072 | tf_op jit(solution)/shard_map/ppermute | solution.py:446
  16.0 6.7 %collective-permute-start.5 = (bf16[32,1792]{1,0:T(8,128)(2,1)S(1)}, bf16[32,1792]{1,0:T(8,128)(2,1)S(1)}, u32[]{:S(2)}, u32[]{:S(2)}) collective-permute-start(bf16[32,1792]{1,0:T(8,128)(2,1)S(1)} %collective-permute-done.1.refs_0_), channel_id=1, source_target_pairs={{0,1},{1,0},{2,3},{3,2},{4,5},{5,4},{6,7},{7,6},{8,9},{9,8},{10,11... | collective-permute-start | bytes 344072 | tf_op jit(solution)/shard_map/ppermute | solution.py:440
  16.3 6.8 %collective-permute-start.6 = (bf16[32,1792]{1,0:T(8,128)(2,1)S(1)}, bf16[32,1792]{1,0:T(8,128)(2,1)S(1)}, u32[]{:S(2)}, u32[]{:S(2)}) collective-permute-start(bf16[32,1792]{1,0:T(8,128)(2,1)S(1)} %collective-permute-done.2.refs_1_), channel_id=1, source_target_pairs={{0,1},{1,0},{2,3},{3,2},{4,5},{5,4},{6,7},{7,6},{8,9},{9,8},{10,11... | collective-permute-start | bytes 344072 | tf_op jit(solution)/shard_map/ppermute | solution.py:440
  22.2 1.3 %collective-permute-start.7 = (bf16[32,1792]{1,0:T(8,128)(2,1)S(1)}, bf16[32,1792]{1,0:T(8,128)(2,1)S(1)}, u32[]{:S(2)}, u32[]{:S(2)}) collective-permute-start(bf16[32,1792]{1,0:T(8,128)(2,1)S(1)} %collective-permute-done.3.refs_2_), channel_id=1, source_target_pairs={{0,1},{1,0},{2,3},{3,2},{4,5},{5,4},{6,7},{7,6},{8,9},{9,8},{10,11... | collective-permute-start | bytes 344072 | tf_op jit(solution)/shard_map/ppermute | solution.py:440
  22.2 1.5 %collective-permute-start.8 = (bf16[32,1792]{1,0:T(8,128)(2,1)S(1)}, bf16[32,1792]{1,0:T(8,128)(2,1)S(1)}, u32[]{:S(2)}, u32[]{:S(2)}) collective-permute-start(bf16[32,1792]{1,0:T(8,128)(2,1)S(1)} %collective-permute-done.4.refs_3_), channel_id=1, source_target_pairs={{0,1},{1,0},{2,3},{3,2},{4,5},{5,4},{6,7},{7,6},{8,9},{9,8},{10,11... | collective-permute-start | bytes 344072 | tf_op jit(solution)/shard_map/ppermute | solution.py:440
  26.5 1.4 %collective-permute-start.9 = (bf16[32,1792]{1,0:T(8,128)(2,1)S(1)}, bf16[32,1792]{1,0:T(8,128)(2,1)S(1)}, u32[]{:S(2)}, u32[]{:S(2)}) collective-permute-start(bf16[32,1792]{1,0:T(8,128)(2,1)S(1)} %get-tuple-element.36), channel_id=1, source_target_pairs={{0,1},{1,0},{2,3},{3,2},{4,5},{5,4},{6,7},{7,6},{8,9},{9,8},{10,11... | collective-permute-start | bytes 344072 | tf_op jit(solution)/shard_map/ppermute | solution.py:440
  26.9 3.1 %collective-permute-start.11 = (bf16[32,1792]{1,0:T(8,128)(2,1)S(1)}, bf16[32,1792]{1,0:T(8,128)(2,1)S(1)}, u32[]{:S(2)}, u32[]{:S(2)}) collective-permute-start(bf16[32,1792]{1,0:T(8,128)(2,1)S(1)} %get-tuple-element.38), channel_id=1, source_target_pairs={{0,1},{1,0},{2,3},{3,2},{4,5},{5,4},{6,7},{7,6},{8,9},{9,8},{10,11... | collective-permute-start | bytes 344072 | tf_op jit(solution)/shard_map/ppermute | solution.py:440
  27.1 3.0 %collective-permute-start.13 = (bf16[32,1792]{1,0:T(8,128)(2,1)S(1)}, bf16[32,1792]{1,0:T(8,128)(2,1)S(1)}, u32[]{:S(2)}, u32[]{:S(2)}) collective-permute-start(bf16[32,1792]{1,0:T(8,128)(2,1)S(1)} %get-tuple-element.40), channel_id=1, source_target_pairs={{0,1},{1,0},{2,3},{3,2},{4,5},{5,4},{6,7},{7,6},{8,9},{9,8},{10,11... | collective-permute-start | bytes 344072 | tf_op jit(solution)/shard_map/ppermute | solution.py:440
  27.4 6.3 %collective-permute-start.15 = (bf16[32,1792]{1,0:T(8,128)(2,1)S(1)}, bf16[32,1792]{1,0:T(8,128)(2,1)S(1)}, u32[]{:S(2)}, u32[]{:S(2)}) collective-permute-start(bf16[32,1792]{1,0:T(8,128)(2,1)S(1)} %get-tuple-element.42), channel_id=1, source_target_pairs={{0,1},{1,0},{2,3},{3,2},{4,5},{5,4},{6,7},{7,6},{8,9},{9,8},{10,11... | collective-permute-start | bytes 344072 | tf_op jit(solution)/shard_map/ppermute | solution.py:440
  27.9 6.2 %collective-permute-start.10 = (bf16[32,1792]{1,0:T(8,128)(2,1)S(1)}, bf16[32,1792]{1,0:T(8,128)(2,1)S(1)}, u32[]{:S(2)}, u32[]{:S(2)}) collective-permute-start(bf16[32,1792]{1,0:T(8,128)(2,1)S(1)} %add_convert_fusion.3), channel_id=1, source_target_pairs={{1,0},{14,1},{3,2},{12,3},{5,4},{10,5},{7,6},{8,7},{9,8},{6,9},{11... | collective-permute-start | bytes 344072 | tf_op jit(solution)/shard_map/ppermute | solution.py:449
  30.1 11.0 %collective-permute-start.12 = (bf16[32,1792]{1,0:T(8,128)(2,1)S(1)}, bf16[32,1792]{1,0:T(8,128)(2,1)S(1)}, u32[]{:S(2)}, u32[]{:S(2)}) collective-permute-start(bf16[32,1792]{1,0:T(8,128)(2,1)S(1)} %add_convert_fusion.2), channel_id=1, source_target_pairs={{9,0},{6,1},{11,2},{4,3},{13,4},{2,5},{15,6},{0,7},{1,8},{14,9},{3... | collective-permute-start | bytes 344072 | tf_op jit(solution)/shard_map/ppermute | solution.py:449
  30.2 10.9 %collective-permute-start.14 = (bf16[32,1792]{1,0:T(8,128)(2,1)S(1)}, bf16[32,1792]{1,0:T(8,128)(2,1)S(1)}, u32[]{:S(2)}, u32[]{:S(2)}) collective-permute-start(bf16[32,1792]{1,0:T(8,128)(2,1)S(1)} %add_convert_fusion.1), channel_id=1, source_target_pairs={{5,0},{10,1},{7,2},{8,3},{1,4},{14,5},{3,6},{12,7},{13,8},{2,9},{1... | collective-permute-start | bytes 344072 | tf_op jit(solution)/shard_map/ppermute | solution.py:449
  33.8 7.3 %collective-permute-start.16 = (bf16[32,1792]{1,0:T(8,128)(2,1)S(1)}, bf16[32,1792]{1,0:T(8,128)(2,1)S(1)}, u32[]{:S(2)}, u32[]{:S(2)}) collective-permute-start(bf16[32,1792]{1,0:T(8,128)(2,1)S(1)} %add_convert_fusion), channel_id=1, source_target_pairs={{13,0},{2,1},{15,2},{0,3},{9,4},{6,5},{11,6},{4,7},{5,8},{10,9},{7... | collective-permute-start | bytes 344072 | tf_op jit(solution)/shard_map/ppermute | solution.py:449
  41.4 1.8 %collective-permute-start.17 = (bf16[8,7168]{1,0:T(8,128)(2,1)S(1)}, bf16[8,7168]{1,0:T(8,128)(2,1)S(1)}, u32[]{:S(2)}, u32[]{:S(2)}) collective-permute-start(bf16[8,7168]{1,0:T(8,128)(2,1)S(1)} %get-tuple-element.44), channel_id=1, source_target_pairs={{0,1},{1,0},{2,3},{3,2},{4,5},{5,4},{6,7},{7,6},{8,9},{9,8},{10,11... | collective-permute-start | bytes 344072 | tf_op jit(solution)/shard_map/ppermute | solution.py:440

commit v19 on v16

--- a/solution.py
+++ b/solution.py
@@ -124,7 +124,7 @@
     q = jnp.concatenate([q_ref[s].astype(F32) for s in range(steps)], axis=0)
     heads = jnp.concatenate([q[:, h * HEAD : (h + 1) * HEAD] for h in range(HEADS)], axis=0)
     heads = heads.astype(BF16)
-    for copy in copies[1:4]:
+    for copy in copies[1:]:
         copy.wait()
     kv = jnp.concatenate([kv_ref[r] for r in range(rows)], axis=1)
     new = jnp.concatenate([fresh_ref[s].astype(F32) for s in range(steps)], axis=0).astype(BF16)
@@ -155,8 +155,6 @@
     attended = nt_dot(old_w, kv[HEAD:]) + dot(new_w, new[:, HEAD:])
     for h in range(HEADS):
         merged[:, h * HEAD : (h + 1) * HEAD] = attended[h * both : (h + 1) * both]
-    for copy in copies[4:8]:
-        copy.wait()
     hidden = jnp.concatenate([hid_ref[s].astype(F32) for s in range(steps)], axis=0)
     resid = hidden + merged[...]
     resid_ref[...] = resid
@@ -335,13 +333,13 @@
     per = lines // PIECES
     half = turns * per
     arrays = [ref[...].astype(F32) for ref in own_refs + other_refs]
-    gate = upper = None
+    x = []
     for k in range(PIECES):
-        x = [array[k * per : (k + 1) * per] for array in arrays]
-        x = jnp.concatenate(x, axis=0).astype(BF16)
-        cols = pl.ds(k * piece, piece)
-        g, u = nt_dot(w_in[0, :, cols], x), nt_dot(w_in[1, :, cols], x)
-        gate, upper = (g, u) if k == 0 else (gate + g, upper + u)
+        rows = [array[k * per : (k + 1) * per] for array in arrays]
+        x.append(jnp.concatenate(rows, axis=0).astype(BF16))
+    _, hidden, width = w_in.shape
+    both = nt_dot(w_in[...].reshape(2 * hidden, width), jnp.concatenate(x, axis=1))
+    gate, upper = both[:hidden], both[hidden:]
     act = (gate / (1.0 + jnp.exp(-gate)) * upper).T.astype(BF16)
     parts = [dot(act, w_down[:, k * piece : (k + 1) * piece]) for k in range(PIECES)]
     for first, now in ((half, theirs_refs), (0, mine_refs)):

time: 41.2 us -> 42 us (1.019)
  Pallas kernels: 11.1 us -> 12 us
    pallas_call x1, Pallas kernels: 2.82 us -> 3.69 us  [experts(): pl.pallas_call(functools.partial(expert_kernel, turns), out_shape=[shape]...]
where the time goes in v19:
time: 42 us; the launch traced here: 41.9 us
  starting transfers between devices  19.3 us (46%)
  Pallas kernels  12 us (29%)
  waiting for transfers between devices  10.4 us (25%)
    ppermute x4, starting transfers between devices, send(): return lax.ppermute(x, 'afd', route(t))  8.4 us
    ppermute x4, waiting for transfers between devices, send_back(): return lax.ppermute(x, 'afd', [(j, i) for i, j in route(t)])  6.85 us
    ppermute x4, starting transfers between devices, send_back(): return lax.ppermute(x, 'afd', [(j, i) for i, j in route(t)])  5.58 us
    ppermute x10, starting transfers between devices, swap(): return lax.ppermute(x, 'afd', cores)  5.32 us
    pallas_call x1, Pallas kernels, stage(): pl.pallas_call(stage_kernel, out_shape=(jax.ShapeDtypeStruct(gate_up.shap...  4.24 us
    pallas_call x1, Pallas kernels, experts(): pl.pallas_call(functools.partial(expert_kernel, turns), out_shape=[shape]...  3.69 us
    ppermute x10, waiting for transfers between devices, swap(): return lax.ppermute(x, 'afd', cores)  3.5 us
    pallas_call x1, Pallas kernels, attend(): pl.pallas_call(attend_kernel, out_shape=(jax.ShapeDtypeStruct((steps * ro...  2.23 us
  transfers between devices with their start and end apart: 18, of which 10 were waited for; matrix products, arithmetic and copies ran while one was open for 0% of the time, Pallas kernels for 11%

profile of v19, /device:TPU:0, one launch (start us, length us, event | category | flops | bytes accessed | tf_op | source)
XLA Modules:
  0.0 41.9 jit_solution(10342342060251438963)
XLA Ops:
  0.0 2.2 %attend.1 = (f32[8,7168]{1,0:T(8,128)S(1)}, bf16[8,7296]{1,0:T(8,128)(2,1)S(1)}) custom-call(s32[4]{0:T(128)} %len_hbm.1, s32[3,2,4]{2,1,0:T(2,128)} %bitcast.6, f32[3,2,4]{2,1,0:T(2,128)} %bitcast.7, bf16[2,4,7168]{2,1,0:T(4,128)(2,1)} %q_hbm.1, bf16[2,4,448]{2,1,0:T(4,128)(2,1)} %fresh_hbm.1, bf16[4,448,128]{2,1,0:T(8,128)(2,1)} %bitcast.4, ...), custom_call_target="tpu_custom_call" | custom-call | flops 300000000 | bytes 2000000 | tf_op jit(solution)/shard_map/attend/pallas_call | solution.py:173
  2.2 0.5 %collective-permute-start = (bf16[8,7296]{1,0:T(8,128)(2,1)S(1)}, bf16[8,7296]{1,0:T(8,128)(2,1)S(1)}, u32[]{:S(2)}, u32[]{:S(2)}) collective-permute-start(bf16[8,7296]{1,0:T(8,128)(2,1)S(1)} %get-tuple-element.25.own_ref), channel_id=1, source_target_pairs={{0,1},{1,0},{2,3},{3,2},{4,5},{5,4},{6,7},{7,6},{8,9},{9,8},{10,11... | collective-permute-start | bytes 350216 | tf_op jit(solution)/shard_map/ppermute | solution.py:438
  2.8 1.0 %collective-permute-done.other_ref = bf16[8,7296]{1,0:T(8,128)(2,1)S(1)} collective-permute-done((bf16[8,7296]{1,0:T(8,128)(2,1)S(1)}, bf16[8,7296]{1,0:T(8,128)(2,1)S(1)}, u32[]{:S(2)}, u32[]{:S(2)}) %collective-permute-start) | collective-permute-done | bytes 116768 | tf_op jit(solution)/shard_map/ppermute | solution.py:438
  3.7 0.5 %pack.1 = (bf16[32,1792]{1,0:T(8,128)(2,1)S(1)}, bf16[32,1792]{1,0:T(8,128)(2,1)S(1)}, bf16[32,1792]{1,0:T(8,128)(2,1)S(1)}, bf16[32,1792]{1,0:T(8,128)(2,1)S(1)}) custom-call(bf16[8,7296]{1,0:T(8,128)(2,1)S(1)} %get-tuple-element.25.own_ref, bf16[8,7296]{1,0:T(8,128)(2,1)S(1)} %collective-permute-done.other_ref), custom_call_target="tpu_custom_call" | custom-call | flops 50000000 | bytes 2000000 | tf_op jit(solution)/shard_map/pack/pallas_call | solution.py:236
  4.2 0.4 collective-permute-start.1
  4.7 4.7 %collective-permute-start.2 = (bf16[32,1792]{1,0:T(8,128)(2,1)S(1)}, bf16[32,1792]{1,0:T(8,128)(2,1)S(1)}, u32[]{:S(2)}, u32[]{:S(2)}) collective-permute-start(bf16[32,1792]{1,0:T(8,128)(2,1)S(1)} %get-tuple-element.30), channel_id=1, source_target_pairs={{0,9},{1,6},{2,11},{3,4},{4,13},{5,2},{6,15},{7,0},{8,1},{9,14},{1... | collective-permute-start | bytes 344072 | tf_op jit(solution)/shard_map/ppermute | solution.py:444
  9.5 3.2 %collective-permute-start.4 = (bf16[32,1792]{1,0:T(8,128)(2,1)S(1)}, bf16[32,1792]{1,0:T(8,128)(2,1)S(1)}, u32[]{:S(2)}, u32[]{:S(2)}) collective-permute-start(bf16[32,1792]{1,0:T(8,128)(2,1)S(1)} %get-tuple-element.32), channel_id=1, source_target_pairs={{0,13},{1,2},{2,15},{3,0},{4,9},{5,6},{6,11},{7,4},{8,5},{9,10},{1... | collective-permute-start | bytes 344072 | tf_op jit(solution)/shard_map/ppermute | solution.py:444
  12.6 4.2 %stage.1 = (bf16[2,256,7168]{2,1,0:T(8,128)(2,1)S(1)}, bf16[256,7168]{1,0:T(8,128)(2,1)S(1)}) custom-call(bf16[1,2,256,7168]{3,2,1,0:T(8,128)(2,1)} %gu_hbm.1, bf16[1,256,7168]{2,1,0:T(8,128)(2,1)} %dn_hbm.1), custom_call_target="tpu_custom_call" | custom-call | bytes 22000000 | tf_op jit(solution)/shard_map/stage/pallas_call | solution.py:292
  16.9 2.2 %collective-permute-start.6 = (bf16[32,1792]{1,0:T(8,128)(2,1)S(1)}, bf16[32,1792]{1,0:T(8,128)(2,1)S(1)}, u32[]{:S(2)}, u32[]{:S(2)}) collective-permute-start(bf16[32,1792]{1,0:T(8,128)(2,1)S(1)} %collective-permute-done.2.refs_1_), channel_id=1, source_target_pairs={{0,1},{1,0},{2,3},{3,2},{4,5},{5,4},{6,7},{7,6},{8,9},{9,8},{10,11... | collective-permute-start | bytes 344072 | tf_op jit(solution)/shard_map/ppermute | solution.py:438
  19.2 0.5 %collective-permute-start.8 = (bf16[32,1792]{1,0:T(8,128)(2,1)S(1)}, bf16[32,1792]{1,0:T(8,128)(2,1)S(1)}, u32[]{:S(2)}, u32[]{:S(2)}) collective-permute-start(bf16[32,1792]{1,0:T(8,128)(2,1)S(1)} %collective-permute-done.4.refs_3_), channel_id=1, source_target_pairs={{0,1},{1,0},{2,3},{3,2},{4,5},{5,4},{6,7},{7,6},{8,9},{9,8},{10,11... | collective-permute-start | bytes 344072 | tf_op jit(solution)/shard_map/ppermute | solution.py:438
  19.8 0.4 collective-permute-done.6.refs_5_
  20.1 0.4 collective-permute-done.7.refs_6_
  20.7 0.3 collective-permute-done.5.refs_4_
  21.0 3.7 %experts.1 = (bf16[32,1792]{1,0:T(8,128)(2,1)S(1)}, bf16[32,1792]{1,0:T(8,128)(2,1)S(1)}, bf16[32,1792]{1,0:T(8,128)(2,1)S(1)}, bf16[32,1792]{1,0:T(8,128)(2,1)S...) custom-call(bf16[32,1792]{1,0:T(8,128)(2,1)S(1)} %collective-permute, ...), custom_call_target="tpu_custom_call" | custom-call | flops 800000000 | bytes 12000000 | tf_op jit(solution)/shard_map/experts/pallas_call | solution.py:355
  24.9 0.3 collective-permute-start.11
  25.5 0.3 collective-permute-start.15
  26.1 2.6 %collective-permute-start.10 = (bf16[32,1792]{1,0:T(8,128)(2,1)S(1)}, bf16[32,1792]{1,0:T(8,128)(2,1)S(1)}, u32[]{:S(2)}, u32[]{:S(2)}) collective-permute-start(bf16[32,1792]{1,0:T(8,128)(2,1)S(1)} %add_convert_fusion.3), channel_id=1, source_target_pairs={{1,0},{14,1},{3,2},{12,3},{5,4},{10,5},{7,6},{8,7},{9,8},{6,9},{11... | collective-permute-start | bytes 344072 | tf_op jit(solution)/shard_map/ppermute | solution.py:447
  28.9 2.9 %collective-permute-start.14 = (bf16[32,1792]{1,0:T(8,128)(2,1)S(1)}, bf16[32,1792]{1,0:T(8,128)(2,1)S(1)}, u32[]{:S(2)}, u32[]{:S(2)}) collective-permute-start(bf16[32,1792]{1,0:T(8,128)(2,1)S(1)} %add_convert_fusion.1), channel_id=1, source_target_pairs={{5,0},{10,1},{7,2},{8,3},{1,4},{14,5},{3,6},{12,7},{13,8},{2,9},{1... | collective-permute-start | bytes 344072 | tf_op jit(solution)/shard_map/ppermute | solution.py:447
  32.3 5.4 %collective-permute-done.12.refs_1_ = bf16[32,1792]{1,0:T(8,128)(2,1)S(1)} collective-permute-done((bf16[32,1792]{1,0:T(8,128)(2,1)S(1)}, bf16[32,1792]{1,0:T(8,128)(2,1)S(1)}, u32[]{:S(2)}, u32[]{:S(2)}) %collective-permute-start.12) | collective-permute-done | bytes 114720 | tf_op jit(solution)/shard_map/ppermute | solution.py:447
  37.8 1.2 %collective-permute-done.16.refs_3_ = bf16[32,1792]{1,0:T(8,128)(2,1)S(1)} collective-permute-done((bf16[32,1792]{1,0:T(8,128)(2,1)S(1)}, bf16[32,1792]{1,0:T(8,128)(2,1)S(1)}, u32[]{:S(2)}, u32[]{:S(2)}) %collective-permute-start.16) | collective-permute-done | bytes 114720 | tf_op jit(solution)/shard_map/ppermute | solution.py:447
  39.0 0.3 combine.1
  39.3 0.9 %collective-permute-start.17 = (bf16[8,7168]{1,0:T(8,128)(2,1)S(1)}, bf16[8,7168]{1,0:T(8,128)(2,1)S(1)}, u32[]{:S(2)}, u32[]{:S(2)}) collective-permute-start(bf16[8,7168]{1,0:T(8,128)(2,1)S(1)} %get-tuple-element.44), channel_id=1, source_target_pairs={{0,1},{1,0},{2,3},{3,2},{4,5},{5,4},{6,7},{7,6},{8,9},{9,8},{10,11... | collective-permute-start | bytes 344072 | tf_op jit(solution)/shard_map/ppermute | solution.py:438
  40.2 1.0 %collective-permute-done.17.other_ref = bf16[8,7168]{1,0:T(8,128)(2,1)S(1)} collective-permute-done((bf16[8,7168]{1,0:T(8,128)(2,1)S(1)}, bf16[8,7168]{1,0:T(8,128)(2,1)S(1)}, u32[]{:S(2)}, u32[]{:S(2)}) %collective-permute-start.17) | collective-permute-done | bytes 114720 | tf_op jit(solution)/shard_map/ppermute | solution.py:438
  41.2 0.7 %finish.1 = bf16[2,4,7168]{2,1,0:T(4,128)(2,1)} custom-call(f32[8,7168]{1,0:T(8,128)S(1)} %get-tuple-element.43.kept_ref, bf16[8,7168]{1,0:T(8,128)(2,1)S(1)} %collective-permute-done.17.other_ref), custom_call_target="tpu_custom_call" | custom-call | flops 100000 | bytes 500000 | tf_op jit(solution)/shard_map/finish/pallas_call | solution.py:408
  (23 shorter events, 1.8 us)
Async XLA Ops:
  2.2 1.5 %collective-permute-start = (bf16[8,7296]{1,0:T(8,128)(2,1)S(1)}, bf16[8,7296]{1,0:T(8,128)(2,1)S(1)}, u32[]{:S(2)}, u32[]{:S(2)}) collective-permute-start(bf16[8,7296]{1,0:T(8,128)(2,1)S(1)} %get-tuple-element.25.own_ref), channel_id=1, source_target_pairs={{0,1},{1,0},{2,3},{3,2},{4,5},{5,4},{6,7},{7,6},{8,9},{9,8},{10,11... | collective-permute-start | bytes 350216 | tf_op jit(solution)/shard_map/ppermute | solution.py:438
  4.2 12.7 %collective-permute-start.1 = (bf16[32,1792]{1,0:T(8,128)(2,1)S(1)}, bf16[32,1792]{1,0:T(8,128)(2,1)S(1)}, u32[]{:S(2)}, u32[]{:S(2)}) collective-permute-start(bf16[32,1792]{1,0:T(8,128)(2,1)S(1)} %get-tuple-element.27), channel_id=1, source_target_pairs={{0,1},{1,14},{2,3},{3,12},{4,5},{5,10},{6,7},{7,8},{8,9},{9,6},{10... | collective-permute-start | bytes 344072 | tf_op jit(solution)/shard_map/ppermute | solution.py:444
  4.7 12.3 %collective-permute-start.2 = (bf16[32,1792]{1,0:T(8,128)(2,1)S(1)}, bf16[32,1792]{1,0:T(8,128)(2,1)S(1)}, u32[]{:S(2)}, u32[]{:S(2)}) collective-permute-start(bf16[32,1792]{1,0:T(8,128)(2,1)S(1)} %get-tuple-element.30), channel_id=1, source_target_pairs={{0,9},{1,6},{2,11},{3,4},{4,13},{5,2},{6,15},{7,0},{8,1},{9,14},{1... | collective-permute-start | bytes 344072 | tf_op jit(solution)/shard_map/ppermute | solution.py:444
  9.3 9.8 %collective-permute-start.3 = (bf16[32,1792]{1,0:T(8,128)(2,1)S(1)}, bf16[32,1792]{1,0:T(8,128)(2,1)S(1)}, u32[]{:S(2)}, u32[]{:S(2)}) collective-permute-start(bf16[32,1792]{1,0:T(8,128)(2,1)S(1)} %get-tuple-element.31), channel_id=1, source_target_pairs={{0,5},{1,10},{2,7},{3,8},{4,1},{5,14},{6,3},{7,12},{8,13},{9,2},{1... | collective-permute-start | bytes 344072 | tf_op jit(solution)/shard_map/ppermute | solution.py:444
  9.5 9.7 %collective-permute-start.4 = (bf16[32,1792]{1,0:T(8,128)(2,1)S(1)}, bf16[32,1792]{1,0:T(8,128)(2,1)S(1)}, u32[]{:S(2)}, u32[]{:S(2)}) collective-permute-start(bf16[32,1792]{1,0:T(8,128)(2,1)S(1)} %get-tuple-element.32), channel_id=1, source_target_pairs={{0,13},{1,2},{2,15},{3,0},{4,9},{5,6},{6,11},{7,4},{8,5},{9,10},{1... | collective-permute-start | bytes 344072 | tf_op jit(solution)/shard_map/ppermute | solution.py:444
  16.9 3.2 %collective-permute-start.6 = (bf16[32,1792]{1,0:T(8,128)(2,1)S(1)}, bf16[32,1792]{1,0:T(8,128)(2,1)S(1)}, u32[]{:S(2)}, u32[]{:S(2)}) collective-permute-start(bf16[32,1792]{1,0:T(8,128)(2,1)S(1)} %collective-permute-done.2.refs_1_), channel_id=1, source_target_pairs={{0,1},{1,0},{2,3},{3,2},{4,5},{5,4},{6,7},{7,6},{8,9},{9,8},{10,11... | collective-permute-start | bytes 344072 | tf_op jit(solution)/shard_map/ppermute | solution.py:438
  19.2 1.3 %collective-permute-start.7 = (bf16[32,1792]{1,0:T(8,128)(2,1)S(1)}, bf16[32,1792]{1,0:T(8,128)(2,1)S(1)}, u32[]{:S(2)}, u32[]{:S(2)}) collective-permute-start(bf16[32,1792]{1,0:T(8,128)(2,1)S(1)} %collective-permute-done.3.refs_2_), channel_id=1, source_target_pairs={{0,1},{1,0},{2,3},{3,2},{4,5},{5,4},{6,7},{7,6},{8,9},{9,8},{10,11... | collective-permute-start | bytes 344072 | tf_op jit(solution)/shard_map/ppermute | solution.py:438
  19.2 1.5 %collective-permute-start.8 = (bf16[32,1792]{1,0:T(8,128)(2,1)S(1)}, bf16[32,1792]{1,0:T(8,128)(2,1)S(1)}, u32[]{:S(2)}, u32[]{:S(2)}) collective-permute-start(bf16[32,1792]{1,0:T(8,128)(2,1)S(1)} %collective-permute-done.4.refs_3_), channel_id=1, source_target_pairs={{0,1},{1,0},{2,3},{3,2},{4,5},{5,4},{6,7},{7,6},{8,9},{9,8},{10,11... | collective-permute-start | bytes 344072 | tf_op jit(solution)/shard_map/ppermute | solution.py:438
  19.7 1.3 %collective-permute-start.5 = (bf16[32,1792]{1,0:T(8,128)(2,1)S(1)}, bf16[32,1792]{1,0:T(8,128)(2,1)S(1)}, u32[]{:S(2)}, u32[]{:S(2)}) collective-permute-start(bf16[32,1792]{1,0:T(8,128)(2,1)S(1)} %collective-permute-done.1.refs_0_), channel_id=1, source_target_pairs={{0,1},{1,0},{2,3},{3,2},{4,5},{5,4},{6,7},{7,6},{8,9},{9,8},{10,11... | collective-permute-start | bytes 344072 | tf_op jit(solution)/shard_map/ppermute | solution.py:438
  24.7 1.4 %collective-permute-start.9 = (bf16[32,1792]{1,0:T(8,128)(2,1)S(1)}, bf16[32,1792]{1,0:T(8,128)(2,1)S(1)}, u32[]{:S(2)}, u32[]{:S(2)}) collective-permute-start(bf16[32,1792]{1,0:T(8,128)(2,1)S(1)} %get-tuple-element.36), channel_id=1, source_target_pairs={{0,1},{1,0},{2,3},{3,2},{4,5},{5,4},{6,7},{7,6},{8,9},{9,8},{10,11... | collective-permute-start | bytes 344072 | tf_op jit(solution)/shard_map/ppermute | solution.py:438
  24.9 3.8 %collective-permute-start.11 = (bf16[32,1792]{1,0:T(8,128)(2,1)S(1)}, bf16[32,1792]{1,0:T(8,128)(2,1)S(1)}, u32[]{:S(2)}, u32[]{:S(2)}) collective-permute-start(bf16[32,1792]{1,0:T(8,128)(2,1)S(1)} %get-tuple-element.38), channel_id=1, source_target_pairs={{0,1},{1,0},{2,3},{3,2},{4,5},{5,4},{6,7},{7,6},{8,9},{9,8},{10,11... | collective-permute-start | bytes 344072 | tf_op jit(solution)/shard_map/ppermute | solution.py:438
  25.3 3.6 %collective-permute-start.13 = (bf16[32,1792]{1,0:T(8,128)(2,1)S(1)}, bf16[32,1792]{1,0:T(8,128)(2,1)S(1)}, u32[]{:S(2)}, u32[]{:S(2)}) collective-permute-start(bf16[32,1792]{1,0:T(8,128)(2,1)S(1)} %get-tuple-element.40), channel_id=1, source_target_pairs={{0,1},{1,0},{2,3},{3,2},{4,5},{5,4},{6,7},{7,6},{8,9},{9,8},{10,11... | collective-permute-start | bytes 344072 | tf_op jit(solution)/shard_map/ppermute | solution.py:438
  25.5 6.3 %collective-permute-start.15 = (bf16[32,1792]{1,0:T(8,128)(2,1)S(1)}, bf16[32,1792]{1,0:T(8,128)(2,1)S(1)}, u32[]{:S(2)}, u32[]{:S(2)}) collective-permute-start(bf16[32,1792]{1,0:T(8,128)(2,1)S(1)} %get-tuple-element.42), channel_id=1, source_target_pairs={{0,1},{1,0},{2,3},{3,2},{4,5},{5,4},{6,7},{7,6},{8,9},{9,8},{10,11... | collective-permute-start | bytes 344072 | tf_op jit(solution)/shard_map/ppermute | solution.py:438
  26.1 6.2 %collective-permute-start.10 = (bf16[32,1792]{1,0:T(8,128)(2,1)S(1)}, bf16[32,1792]{1,0:T(8,128)(2,1)S(1)}, u32[]{:S(2)}, u32[]{:S(2)}) collective-permute-start(bf16[32,1792]{1,0:T(8,128)(2,1)S(1)} %add_convert_fusion.3), channel_id=1, source_target_pairs={{1,0},{14,1},{3,2},{12,3},{5,4},{10,5},{7,6},{8,7},{9,8},{6,9},{11... | collective-permute-start | bytes 344072 | tf_op jit(solution)/shard_map/ppermute | solution.py:447
  28.8 9.0 %collective-permute-start.12 = (bf16[32,1792]{1,0:T(8,128)(2,1)S(1)}, bf16[32,1792]{1,0:T(8,128)(2,1)S(1)}, u32[]{:S(2)}, u32[]{:S(2)}) collective-permute-start(bf16[32,1792]{1,0:T(8,128)(2,1)S(1)} %add_convert_fusion.2), channel_id=1, source_target_pairs={{9,0},{6,1},{11,2},{4,3},{13,4},{2,5},{15,6},{0,7},{1,8},{14,9},{3... | collective-permute-start | bytes 344072 | tf_op jit(solution)/shard_map/ppermute | solution.py:447
  28.9 8.9 %collective-permute-start.14 = (bf16[32,1792]{1,0:T(8,128)(2,1)S(1)}, bf16[32,1792]{1,0:T(8,128)(2,1)S(1)}, u32[]{:S(2)}, u32[]{:S(2)}) collective-permute-start(bf16[32,1792]{1,0:T(8,128)(2,1)S(1)} %add_convert_fusion.1), channel_id=1, source_target_pairs={{5,0},{10,1},{7,2},{8,3},{1,4},{14,5},{3,6},{12,7},{13,8},{2,9},{1... | collective-permute-start | bytes 344072 | tf_op jit(solution)/shard_map/ppermute | solution.py:447
  31.8 7.2 %collective-permute-start.16 = (bf16[32,1792]{1,0:T(8,128)(2,1)S(1)}, bf16[32,1792]{1,0:T(8,128)(2,1)S(1)}, u32[]{:S(2)}, u32[]{:S(2)}) collective-permute-start(bf16[32,1792]{1,0:T(8,128)(2,1)S(1)} %add_convert_fusion), channel_id=1, source_target_pairs={{13,0},{2,1},{15,2},{0,3},{9,4},{6,5},{11,6},{4,7},{5,8},{10,9},{7... | collective-permute-start | bytes 344072 | tf_op jit(solution)/shard_map/ppermute | solution.py:447
  39.3 1.9 %collective-permute-start.17 = (bf16[8,7168]{1,0:T(8,128)(2,1)S(1)}, bf16[8,7168]{1,0:T(8,128)(2,1)S(1)}, u32[]{:S(2)}, u32[]{:S(2)}) collective-permute-start(bf16[8,7168]{1,0:T(8,128)(2,1)S(1)} %get-tuple-element.44), channel_id=1, source_target_pairs={{0,1},{1,0},{2,3},{3,2},{4,5},{5,4},{6,7},{7,6},{8,9},{9,8},{10,11... | collective-permute-start | bytes 344072 | tf_op jit(solution)/shard_map/ppermute | solution.py:438

commit v20 on v16

--- a/solution.py
+++ b/solution.py
@@ -370,7 +370,8 @@
 
 def combine_kernel(mix_ref, resid_ref, *refs):
     back_refs, (kept_ref, sent_ref) = refs[:-2], refs[-2:]
-    both = resid_ref.shape[0]
+    steps, rows, _ = kept_ref.shape
+    both = steps * rows
     piece = back_refs[0].shape[1]
     product = dot(mix_ref[...], jnp.concatenate([ref[...] for ref in back_refs], axis=0))
     n = PIECES * 2 * both
@@ -378,16 +379,19 @@
     for k in range(PIECES):
         cols = pl.ds(k * piece, piece)
         first = k * 2 * both
-        kept_ref[:, cols] = resid_ref[:, cols] + total[first : first + both]
-        sent_ref[:, cols] = total[first + both : first + 2 * both].astype(BF16)
-
-
-def combine(mix, resid, backs):
+        kept = resid_ref[:, cols] + total[first : first + both]
+        sent = total[first + both : first + 2 * both].astype(BF16)
+        for s in range(steps):
+            kept_ref[s, :, cols] = kept[s * rows : (s + 1) * rows]
+            sent_ref[s, :, cols] = sent[s * rows : (s + 1) * rows]
+
+
+def combine(shape, mix, resid, backs):
     return pl.pallas_call(
         combine_kernel,
         out_shape=(
-            jax.ShapeDtypeStruct(resid.shape, F32),
-            jax.ShapeDtypeStruct(resid.shape, BF16),
+            jax.ShapeDtypeStruct(shape, F32),
+            jax.ShapeDtypeStruct(shape, BF16),
         ),
         in_specs=[VMEM] * (2 + len(backs)),
         out_specs=(VMEM, VMEM),
@@ -397,25 +401,6 @@
         ),
         name="combine",
     )(mix, resid, *backs)
-
-
-def finish_kernel(kept_ref, other_ref, out_ref):
-    steps, rows, _ = out_ref.shape
-    done = (kept_ref[...] + other_ref[...].astype(F32)).astype(BF16)
-    for s in range(steps):
-        out_ref[s] = done[s * rows : (s + 1) * rows]
-
-
-def finish(shape, kept, other):
-    return pl.pallas_call(
-        finish_kernel,
-        out_shape=jax.ShapeDtypeStruct(shape, BF16),
-        in_specs=[VMEM, VMEM],
-        out_specs=VMEM,
-        compiler_params=pltpu.CompilerParams(vmem_limit_bytes=24 * MIB),
-        cost_estimate=pl.CostEstimate(flops=100_000, bytes_accessed=500_000, transcendentals=0),
-        name="finish",
-    )(kept, other)
 
 
 def per_device(
@@ -468,8 +453,8 @@
             (a.astype(F32) + swap(b).astype(F32)).astype(BF16) for a, b in zip(mine, theirs)
         ]
     backs = [send_back(summed[t], t) for t in range(turns)]
-    kept, given = combine(mix, resid, backs)
-    return finish(queries.shape, kept, swap(given))
+    kept, given = combine(queries.shape, mix, resid, backs)
+    return (kept + swap(given).astype(F32)).astype(BF16)
 
 
 def solution(mesh):

time: 41.2 us -> 41.2 us (level)
  other arithmetic: 0.12 us -> 0.83 us
  Pallas kernels: 11.1 us -> 10.5 us
    convert_element_type x0 -> x1, other arithmetic: none -> 0.71 us  [per_device(): return (kept + swap(given).astype(F32)).astype(BF16)]
    pallas_call x2 -> x1, Pallas kernels: 1 us -> 0.33 us  [combine(): pl.pallas_call(combine_kernel, out_shape=(jax.ShapeDtypeStruct(shape, F32...]
where the time goes in v20:
time: 41.2 us; the launch traced here: 41.1 us
  starting transfers between devices  19.3 us (47%)
  Pallas kernels  10.5 us (25%)
  waiting for transfers between devices  10.4 us (25%)
  other arithmetic  0.83 us (2%)
    ppermute x4, starting transfers between devices, send(): return lax.ppermute(x, 'afd', route(t))  8.4 us
    ppermute x4, waiting for transfers between devices, send_back(): return lax.ppermute(x, 'afd', [(j, i) for i, j in route(t)])  6.85 us
    ppermute x4, starting transfers between devices, send_back(): return lax.ppermute(x, 'afd', [(j, i) for i, j in route(t)])  5.59 us
    ppermute x10, starting transfers between devices, swap(): return lax.ppermute(x, 'afd', cores)  5.32 us
    pallas_call x1, Pallas kernels, stage(): pl.pallas_call(stage_kernel, out_shape=(jax.ShapeDtypeStruct(gate_up.shap...  4.24 us
    ppermute x10, waiting for transfers between devices, swap(): return lax.ppermute(x, 'afd', cores)  3.5 us
    pallas_call x1, Pallas kernels, experts(): pl.pallas_call(functools.partial(expert_kernel, turns), out_shape=[shape]...  2.82 us
    pallas_call x1, Pallas kernels, attend(): pl.pallas_call(attend_kernel, out_shape=(jax.ShapeDtypeStruct((steps * ro...  2.29 us
  transfers between devices with their start and end apart: 18, of which 10 were waited for; matrix products, arithmetic and copies ran while one was open for 0% of the time, Pallas kernels for 11%

profile of v20, /device:TPU:0, one launch (start us, length us, event | category | flops | bytes accessed | tf_op | source)
XLA Modules:
  0.0 41.1 jit_solution(4192362576971774155)
XLA Ops:
  0.0 2.3 %attend.1 = (f32[8,7168]{1,0:T(8,128)S(1)}, bf16[8,7296]{1,0:T(8,128)(2,1)S(1)}) custom-call(s32[4]{0:T(128)} %len_hbm.1, s32[3,2,4]{2,1,0:T(2,128)} %bitcast.6, f32[3,2,4]{2,1,0:T(2,128)} %bitcast.7, bf16[2,4,7168]{2,1,0:T(4,128)(2,1)} %q_hbm.1, bf16[2,4,448]{2,1,0:T(4,128)(2,1)} %fresh_hbm.1, bf16[4,448,128]{2,1,0:T(8,128)(2,1)} %bitcast.4, ...), custom_call_target="tpu_custom_call" | custom-call | flops 300000000 | bytes 2000000 | tf_op jit(solution)/shard_map/attend/pallas_call | solution.py:175
  2.3 0.5 %collective-permute-start = (bf16[8,7296]{1,0:T(8,128)(2,1)S(1)}, bf16[8,7296]{1,0:T(8,128)(2,1)S(1)}, u32[]{:S(2)}, u32[]{:S(2)}) collective-permute-start(bf16[8,7296]{1,0:T(8,128)(2,1)S(1)} %get-tuple-element.25.own_ref), channel_id=1, source_target_pairs={{0,1},{1,0},{2,3},{3,2},{4,5},{5,4},{6,7},{7,6},{8,9},{9,8},{10,11... | collective-permute-start | bytes 350216 | tf_op jit(solution)/shard_map/ppermute | solution.py:425
  2.8 1.0 %collective-permute-done.other_ref = bf16[8,7296]{1,0:T(8,128)(2,1)S(1)} collective-permute-done((bf16[8,7296]{1,0:T(8,128)(2,1)S(1)}, bf16[8,7296]{1,0:T(8,128)(2,1)S(1)}, u32[]{:S(2)}, u32[]{:S(2)}) %collective-permute-start) | collective-permute-done | bytes 116768 | tf_op jit(solution)/shard_map/ppermute | solution.py:425
  3.8 0.5 %pack.1 = (bf16[32,1792]{1,0:T(8,128)(2,1)S(1)}, bf16[32,1792]{1,0:T(8,128)(2,1)S(1)}, bf16[32,1792]{1,0:T(8,128)(2,1)S(1)}, bf16[32,1792]{1,0:T(8,128)(2,1)S(1)}) custom-call(bf16[8,7296]{1,0:T(8,128)(2,1)S(1)} %get-tuple-element.25.own_ref, bf16[8,7296]{1,0:T(8,128)(2,1)S(1)} %collective-permute-done.other_ref), custom_call_target="tpu_custom_call" | custom-call | flops 50000000 | bytes 2000000 | tf_op jit(solution)/shard_map/pack/pallas_call | solution.py:238
  4.3 0.4 %collective-permute-start.1 = (bf16[32,1792]{1,0:T(8,128)(2,1)S(1)}, bf16[32,1792]{1,0:T(8,128)(2,1)S(1)}, u32[]{:S(2)}, u32[]{:S(2)}) collective-permute-start(bf16[32,1792]{1,0:T(8,128)(2,1)S(1)} %get-tuple-element.27), channel_id=1, source_target_pairs={{0,1},{1,14},{2,3},{3,12},{4,5},{5,10},{6,7},{7,8},{8,9},{9,6},{10... | collective-permute-start | bytes 344072 | tf_op jit(solution)/shard_map/ppermute | solution.py:431
  4.7 4.7 %collective-permute-start.2 = (bf16[32,1792]{1,0:T(8,128)(2,1)S(1)}, bf16[32,1792]{1,0:T(8,128)(2,1)S(1)}, u32[]{:S(2)}, u32[]{:S(2)}) collective-permute-start(bf16[32,1792]{1,0:T(8,128)(2,1)S(1)} %get-tuple-element.30), channel_id=1, source_target_pairs={{0,9},{1,6},{2,11},{3,4},{4,13},{5,2},{6,15},{7,0},{8,1},{9,14},{1... | collective-permute-start | bytes 344072 | tf_op jit(solution)/shard_map/ppermute | solution.py:431
  9.5 3.2 %collective-permute-start.4 = (bf16[32,1792]{1,0:T(8,128)(2,1)S(1)}, bf16[32,1792]{1,0:T(8,128)(2,1)S(1)}, u32[]{:S(2)}, u32[]{:S(2)}) collective-permute-start(bf16[32,1792]{1,0:T(8,128)(2,1)S(1)} %get-tuple-element.32), channel_id=1, source_target_pairs={{0,13},{1,2},{2,15},{3,0},{4,9},{5,6},{6,11},{7,4},{8,5},{9,10},{1... | collective-permute-start | bytes 344072 | tf_op jit(solution)/shard_map/ppermute | solution.py:431
  12.7 4.2 %stage.1 = (bf16[2,256,7168]{2,1,0:T(8,128)(2,1)S(1)}, bf16[256,7168]{1,0:T(8,128)(2,1)S(1)}) custom-call(bf16[1,2,256,7168]{3,2,1,0:T(8,128)(2,1)} %gu_hbm.1, bf16[1,256,7168]{2,1,0:T(8,128)(2,1)} %dn_hbm.1), custom_call_target="tpu_custom_call" | custom-call | bytes 22000000 | tf_op jit(solution)/shard_map/stage/pallas_call | solution.py:294
  17.0 2.2 %collective-permute-start.6 = (bf16[32,1792]{1,0:T(8,128)(2,1)S(1)}, bf16[32,1792]{1,0:T(8,128)(2,1)S(1)}, u32[]{:S(2)}, u32[]{:S(2)}) collective-permute-start(bf16[32,1792]{1,0:T(8,128)(2,1)S(1)} %collective-permute-done.2.refs_1_), channel_id=1, source_target_pairs={{0,1},{1,0},{2,3},{3,2},{4,5},{5,4},{6,7},{7,6},{8,9},{9,8},{10,11... | collective-permute-start | bytes 344072 | tf_op jit(solution)/shard_map/ppermute | solution.py:425
  19.2 0.5 %collective-permute-start.8 = (bf16[32,1792]{1,0:T(8,128)(2,1)S(1)}, bf16[32,1792]{1,0:T(8,128)(2,1)S(1)}, u32[]{:S(2)}, u32[]{:S(2)}) collective-permute-start(bf16[32,1792]{1,0:T(8,128)(2,1)S(1)} %collective-permute-done.4.refs_3_), channel_id=1, source_target_pairs={{0,1},{1,0},{2,3},{3,2},{4,5},{5,4},{6,7},{7,6},{8,9},{9,8},{10,11... | collective-permute-start | bytes 344072 | tf_op jit(solution)/shard_map/ppermute | solution.py:425
  19.8 0.4 collective-permute-done.6.refs_5_
  20.2 0.4 collective-permute-done.7.refs_6_
  20.7 0.3 collective-permute-done.5.refs_4_
  21.1 2.8 %experts.1 = (bf16[32,1792]{1,0:T(8,128)(2,1)S(1)}, bf16[32,1792]{1,0:T(8,128)(2,1)S(1)}, bf16[32,1792]{1,0:T(8,128)(2,1)S(1)}, bf16[32,1792]{1,0:T(8,128)(2,1)S...) custom-call(bf16[32,1792]{1,0:T(8,128)(2,1)S(1)} %collective-permute, ...), custom_call_target="tpu_custom_call" | custom-call | flops 800000000 | bytes 12000000 | tf_op jit(solution)/shard_map/experts/pallas_call | solution.py:357
  24.1 0.3 collective-permute-start.11
  24.6 0.3 collective-permute-start.15
  25.3 2.6 %collective-permute-start.10 = (bf16[32,1792]{1,0:T(8,128)(2,1)S(1)}, bf16[32,1792]{1,0:T(8,128)(2,1)S(1)}, u32[]{:S(2)}, u32[]{:S(2)}) collective-permute-start(bf16[32,1792]{1,0:T(8,128)(2,1)S(1)} %add_convert_fusion.4), channel_id=1, source_target_pairs={{1,0},{14,1},{3,2},{12,3},{5,4},{10,5},{7,6},{8,7},{9,8},{6,9},{11... | collective-permute-start | bytes 344072 | tf_op jit(solution)/shard_map/ppermute | solution.py:434
  28.1 2.9 %collective-permute-start.14 = (bf16[32,1792]{1,0:T(8,128)(2,1)S(1)}, bf16[32,1792]{1,0:T(8,128)(2,1)S(1)}, u32[]{:S(2)}, u32[]{:S(2)}) collective-permute-start(bf16[32,1792]{1,0:T(8,128)(2,1)S(1)} %add_convert_fusion.2), channel_id=1, source_target_pairs={{5,0},{10,1},{7,2},{8,3},{1,4},{14,5},{3,6},{12,7},{13,8},{2,9},{1... | collective-permute-start | bytes 344072 | tf_op jit(solution)/shard_map/ppermute | solution.py:434
  31.5 5.4 %collective-permute-done.12.refs_1_ = bf16[32,1792]{1,0:T(8,128)(2,1)S(1)} collective-permute-done((bf16[32,1792]{1,0:T(8,128)(2,1)S(1)}, bf16[32,1792]{1,0:T(8,128)(2,1)S(1)}, u32[]{:S(2)}, u32[]{:S(2)}) %collective-permute-start.12) | collective-permute-done | bytes 114720 | tf_op jit(solution)/shard_map/ppermute | solution.py:434
  36.9 1.2 %collective-permute-done.16.refs_3_ = bf16[32,1792]{1,0:T(8,128)(2,1)S(1)} collective-permute-done((bf16[32,1792]{1,0:T(8,128)(2,1)S(1)}, bf16[32,1792]{1,0:T(8,128)(2,1)S(1)}, u32[]{:S(2)}, u32[]{:S(2)}) %collective-permute-start.16) | collective-permute-done | bytes 114720 | tf_op jit(solution)/shard_map/ppermute | solution.py:434
  38.2 0.3 combine.1
  38.5 0.9 %collective-permute-start.17 = (bf16[2,4,7168]{2,1,0:T(4,128)(2,1)S(1)}, bf16[2,4,7168]{2,1,0:T(4,128)(2,1)S(1)}, u32[]{:S(2)}, u32[]{:S(2)}) collective-permute-start(bf16[2,4,7168]{2,1,0:T(4,128)(2,1)S(1)} %get-tuple-element.44), channel_id=1, source_target_pairs={{0,1},{1,0},{2,3},{3,2},{4,5},{5,4},{6,7},{7,6},{8,9},{9,8},{10,11... | collective-permute-start | bytes 344072 | tf_op jit(solution)/shard_map/ppermute | solution.py:425
  39.4 1.0 %collective-permute-done.17 = bf16[2,4,7168]{2,1,0:T(4,128)(2,1)S(1)} collective-permute-done((bf16[2,4,7168]{2,1,0:T(4,128)(2,1)S(1)}, bf16[2,4,7168]{2,1,0:T(4,128)(2,1)S(1)}, u32[]{:S(2)}, u32[]{:S(2)}) %collective-permute-start.17) | collective-permute-done | bytes 114720 | tf_op jit(solution)/shard_map/ppermute | solution.py:425
  40.4 0.7 %add_convert_fusion = bf16[2,4,7168]{2,1,0:T(4,128)(2,1)} fusion(f32[2,4,7168]{2,1,0:T(4,128)S(1)} %get-tuple-element.43, bf16[2,4,7168]{2,1,0:T(4,128)(2,1)S(1)} %collective-permute-done.17), kind=kLoop, calls=%fused_computation | loop fusion | flops 172032 | bytes 458752 | tf_op jit(solution)/shard_map/convert_element_type | solution.py:457
  (23 shorter events, 1.8 us)
Async XLA Ops:
  2.3 1.5 %collective-permute-start = (bf16[8,7296]{1,0:T(8,128)(2,1)S(1)}, bf16[8,7296]{1,0:T(8,128)(2,1)S(1)}, u32[]{:S(2)}, u32[]{:S(2)}) collective-permute-start(bf16[8,7296]{1,0:T(8,128)(2,1)S(1)} %get-tuple-element.25.own_ref), channel_id=1, source_target_pairs={{0,1},{1,0},{2,3},{3,2},{4,5},{5,4},{6,7},{7,6},{8,9},{9,8},{10,11... | collective-permute-start | bytes 350216 | tf_op jit(solution)/shard_map/ppermute | solution.py:425
  4.3 12.7 %collective-permute-start.1 = (bf16[32,1792]{1,0:T(8,128)(2,1)S(1)}, bf16[32,1792]{1,0:T(8,128)(2,1)S(1)}, u32[]{:S(2)}, u32[]{:S(2)}) collective-permute-start(bf16[32,1792]{1,0:T(8,128)(2,1)S(1)} %get-tuple-element.27), channel_id=1, source_target_pairs={{0,1},{1,14},{2,3},{3,12},{4,5},{5,10},{6,7},{7,8},{8,9},{9,6},{10... | collective-permute-start | bytes 344072 | tf_op jit(solution)/shard_map/ppermute | solution.py:431
  4.7 12.3 %collective-permute-start.2 = (bf16[32,1792]{1,0:T(8,128)(2,1)S(1)}, bf16[32,1792]{1,0:T(8,128)(2,1)S(1)}, u32[]{:S(2)}, u32[]{:S(2)}) collective-permute-start(bf16[32,1792]{1,0:T(8,128)(2,1)S(1)} %get-tuple-element.30), channel_id=1, source_target_pairs={{0,9},{1,6},{2,11},{3,4},{4,13},{5,2},{6,15},{7,0},{8,1},{9,14},{1... | collective-permute-start | bytes 344072 | tf_op jit(solution)/shard_map/ppermute | solution.py:431
  9.4 9.8 %collective-permute-start.3 = (bf16[32,1792]{1,0:T(8,128)(2,1)S(1)}, bf16[32,1792]{1,0:T(8,128)(2,1)S(1)}, u32[]{:S(2)}, u32[]{:S(2)}) collective-permute-start(bf16[32,1792]{1,0:T(8,128)(2,1)S(1)} %get-tuple-element.31), channel_id=1, source_target_pairs={{0,5},{1,10},{2,7},{3,8},{4,1},{5,14},{6,3},{7,12},{8,13},{9,2},{1... | collective-permute-start | bytes 344072 | tf_op jit(solution)/shard_map/ppermute | solution.py:431
  9.5 9.7 %collective-permute-start.4 = (bf16[32,1792]{1,0:T(8,128)(2,1)S(1)}, bf16[32,1792]{1,0:T(8,128)(2,1)S(1)}, u32[]{:S(2)}, u32[]{:S(2)}) collective-permute-start(bf16[32,1792]{1,0:T(8,128)(2,1)S(1)} %get-tuple-element.32), channel_id=1, source_target_pairs={{0,13},{1,2},{2,15},{3,0},{4,9},{5,6},{6,11},{7,4},{8,5},{9,10},{1... | collective-permute-start | bytes 344072 | tf_op jit(solution)/shard_map/ppermute | solution.py:431
  17.0 3.2 %collective-permute-start.6 = (bf16[32,1792]{1,0:T(8,128)(2,1)S(1)}, bf16[32,1792]{1,0:T(8,128)(2,1)S(1)}, u32[]{:S(2)}, u32[]{:S(2)}) collective-permute-start(bf16[32,1792]{1,0:T(8,128)(2,1)S(1)} %collective-permute-done.2.refs_1_), channel_id=1, source_target_pairs={{0,1},{1,0},{2,3},{3,2},{4,5},{5,4},{6,7},{7,6},{8,9},{9,8},{10,11... | collective-permute-start | bytes 344072 | tf_op jit(solution)/shard_map/ppermute | solution.py:425
  19.2 1.3 %collective-permute-start.7 = (bf16[32,1792]{1,0:T(8,128)(2,1)S(1)}, bf16[32,1792]{1,0:T(8,128)(2,1)S(1)}, u32[]{:S(2)}, u32[]{:S(2)}) collective-permute-start(bf16[32,1792]{1,0:T(8,128)(2,1)S(1)} %collective-permute-done.3.refs_2_), channel_id=1, source_target_pairs={{0,1},{1,0},{2,3},{3,2},{4,5},{5,4},{6,7},{7,6},{8,9},{9,8},{10,11... | collective-permute-start | bytes 344072 | tf_op jit(solution)/shard_map/ppermute | solution.py:425
  19.2 1.5 %collective-permute-start.8 = (bf16[32,1792]{1,0:T(8,128)(2,1)S(1)}, bf16[32,1792]{1,0:T(8,128)(2,1)S(1)}, u32[]{:S(2)}, u32[]{:S(2)}) collective-permute-start(bf16[32,1792]{1,0:T(8,128)(2,1)S(1)} %collective-permute-done.4.refs_3_), channel_id=1, source_target_pairs={{0,1},{1,0},{2,3},{3,2},{4,5},{5,4},{6,7},{7,6},{8,9},{9,8},{10,11... | collective-permute-start | bytes 344072 | tf_op jit(solution)/shard_map/ppermute | solution.py:425
  19.7 1.3 %collective-permute-start.5 = (bf16[32,1792]{1,0:T(8,128)(2,1)S(1)}, bf16[32,1792]{1,0:T(8,128)(2,1)S(1)}, u32[]{:S(2)}, u32[]{:S(2)}) collective-permute-start(bf16[32,1792]{1,0:T(8,128)(2,1)S(1)} %collective-permute-done.1.refs_0_), channel_id=1, source_target_pairs={{0,1},{1,0},{2,3},{3,2},{4,5},{5,4},{6,7},{7,6},{8,9},{9,8},{10,11... | collective-permute-start | bytes 344072 | tf_op jit(solution)/shard_map/ppermute | solution.py:425
  23.9 1.4 %collective-permute-start.9 = (bf16[32,1792]{1,0:T(8,128)(2,1)S(1)}, bf16[32,1792]{1,0:T(8,128)(2,1)S(1)}, u32[]{:S(2)}, u32[]{:S(2)}) collective-permute-start(bf16[32,1792]{1,0:T(8,128)(2,1)S(1)} %get-tuple-element.36), channel_id=1, source_target_pairs={{0,1},{1,0},{2,3},{3,2},{4,5},{5,4},{6,7},{7,6},{8,9},{9,8},{10,11... | collective-permute-start | bytes 344072 | tf_op jit(solution)/shard_map/ppermute | solution.py:425
  24.1 3.8 %collective-permute-start.11 = (bf16[32,1792]{1,0:T(8,128)(2,1)S(1)}, bf16[32,1792]{1,0:T(8,128)(2,1)S(1)}, u32[]{:S(2)}, u32[]{:S(2)}) collective-permute-start(bf16[32,1792]{1,0:T(8,128)(2,1)S(1)} %get-tuple-element.38), channel_id=1, source_target_pairs={{0,1},{1,0},{2,3},{3,2},{4,5},{5,4},{6,7},{7,6},{8,9},{9,8},{10,11... | collective-permute-start | bytes 344072 | tf_op jit(solution)/shard_map/ppermute | solution.py:425
  24.5 3.6 %collective-permute-start.13 = (bf16[32,1792]{1,0:T(8,128)(2,1)S(1)}, bf16[32,1792]{1,0:T(8,128)(2,1)S(1)}, u32[]{:S(2)}, u32[]{:S(2)}) collective-permute-start(bf16[32,1792]{1,0:T(8,128)(2,1)S(1)} %get-tuple-element.40), channel_id=1, source_target_pairs={{0,1},{1,0},{2,3},{3,2},{4,5},{5,4},{6,7},{7,6},{8,9},{9,8},{10,11... | collective-permute-start | bytes 344072 | tf_op jit(solution)/shard_map/ppermute | solution.py:425
  24.6 6.3 %collective-permute-start.15 = (bf16[32,1792]{1,0:T(8,128)(2,1)S(1)}, bf16[32,1792]{1,0:T(8,128)(2,1)S(1)}, u32[]{:S(2)}, u32[]{:S(2)}) collective-permute-start(bf16[32,1792]{1,0:T(8,128)(2,1)S(1)} %get-tuple-element.42), channel_id=1, source_target_pairs={{0,1},{1,0},{2,3},{3,2},{4,5},{5,4},{6,7},{7,6},{8,9},{9,8},{10,11... | collective-permute-start | bytes 344072 | tf_op jit(solution)/shard_map/ppermute | solution.py:425
  25.3 6.2 %collective-permute-start.10 = (bf16[32,1792]{1,0:T(8,128)(2,1)S(1)}, bf16[32,1792]{1,0:T(8,128)(2,1)S(1)}, u32[]{:S(2)}, u32[]{:S(2)}) collective-permute-start(bf16[32,1792]{1,0:T(8,128)(2,1)S(1)} %add_convert_fusion.4), channel_id=1, source_target_pairs={{1,0},{14,1},{3,2},{12,3},{5,4},{10,5},{7,6},{8,7},{9,8},{6,9},{11... | collective-permute-start | bytes 344072 | tf_op jit(solution)/shard_map/ppermute | solution.py:434
  28.0 9.0 %collective-permute-start.12 = (bf16[32,1792]{1,0:T(8,128)(2,1)S(1)}, bf16[32,1792]{1,0:T(8,128)(2,1)S(1)}, u32[]{:S(2)}, u32[]{:S(2)}) collective-permute-start(bf16[32,1792]{1,0:T(8,128)(2,1)S(1)} %add_convert_fusion.3), channel_id=1, source_target_pairs={{9,0},{6,1},{11,2},{4,3},{13,4},{2,5},{15,6},{0,7},{1,8},{14,9},{3... | collective-permute-start | bytes 344072 | tf_op jit(solution)/shard_map/ppermute | solution.py:434
  28.1 8.9 %collective-permute-start.14 = (bf16[32,1792]{1,0:T(8,128)(2,1)S(1)}, bf16[32,1792]{1,0:T(8,128)(2,1)S(1)}, u32[]{:S(2)}, u32[]{:S(2)}) collective-permute-start(bf16[32,1792]{1,0:T(8,128)(2,1)S(1)} %add_convert_fusion.2), channel_id=1, source_target_pairs={{5,0},{10,1},{7,2},{8,3},{1,4},{14,5},{3,6},{12,7},{13,8},{2,9},{1... | collective-permute-start | bytes 344072 | tf_op jit(solution)/shard_map/ppermute | solution.py:434
  31.0 7.2 %collective-permute-start.16 = (bf16[32,1792]{1,0:T(8,128)(2,1)S(1)}, bf16[32,1792]{1,0:T(8,128)(2,1)S(1)}, u32[]{:S(2)}, u32[]{:S(2)}) collective-permute-start(bf16[32,1792]{1,0:T(8,128)(2,1)S(1)} %add_convert_fusion.1), channel_id=1, source_target_pairs={{13,0},{2,1},{15,2},{0,3},{9,4},{6,5},{11,6},{4,7},{5,8},{10,9},{7... | collective-permute-start | bytes 344072 | tf_op jit(solution)/shard_map/ppermute | solution.py:434
  38.5 1.9 %collective-permute-start.17 = (bf16[2,4,7168]{2,1,0:T(4,128)(2,1)S(1)}, bf16[2,4,7168]{2,1,0:T(4,128)(2,1)S(1)}, u32[]{:S(2)}, u32[]{:S(2)}) collective-permute-start(bf16[2,4,7168]{2,1,0:T(4,128)(2,1)S(1)} %get-tuple-element.44), channel_id=1, source_target_pairs={{0,1},{1,0},{2,3},{3,2},{4,5},{5,4},{6,7},{7,6},{8,9},{9,8},{10,11... | collective-permute-start | bytes 344072 | tf_op jit(solution)/shard_map/ppermute | solution.py:425

commit v21 on v16

--- a/solution.py
+++ b/solution.py
@@ -339,9 +339,11 @@
     for k in range(PIECES):
         x = [array[k * per : (k + 1) * per] for array in arrays]
         x = jnp.concatenate(x, axis=0).astype(BF16)
-        cols = pl.ds(k * piece, piece)
-        g, u = nt_dot(w_in[0, :, cols], x), nt_dot(w_in[1, :, cols], x)
-        gate, upper = (g, u) if k == 0 else (gate + g, upper + u)
+        for part in range(2):
+            cut = x[:, part * piece // 2 : (part + 1) * piece // 2]
+            cols = pl.ds(k * piece + part * piece // 2, piece // 2)
+            g, u = nt_dot(w_in[0, :, cols], cut), nt_dot(w_in[1, :, cols], cut)
+            gate, upper = (g, u) if gate is None else (gate + g, upper + u)
     act = (gate / (1.0 + jnp.exp(-gate)) * upper).T.astype(BF16)
     parts = [dot(act, w_down[:, k * piece : (k + 1) * piece]) for k in range(PIECES)]
     for first, now in ((half, theirs_refs), (0, mine_refs)):

time: 41.2 us -> 41.2 us (level)
  no operation moved by 1% of the time
where the time goes in v21:
time: 41.2 us; the launch traced here: 41.1 us
  starting transfers between devices  19.3 us (47%)
  Pallas kernels  11.2 us (27%)
  waiting for transfers between devices  10.4 us (25%)
    ppermute x4, starting transfers between devices, send(): return lax.ppermute(x, 'afd', route(t))  8.4 us
    ppermute x4, waiting for transfers between devices, send_back(): return lax.ppermute(x, 'afd', [(j, i) for i, j in route(t)])  6.85 us
    ppermute x4, starting transfers between devices, send_back(): return lax.ppermute(x, 'afd', [(j, i) for i, j in route(t)])  5.59 us
    ppermute x10, starting transfers between devices, swap(): return lax.ppermute(x, 'afd', cores)  5.32 us
    pallas_call x1, Pallas kernels, stage(): pl.pallas_call(stage_kernel, out_shape=(jax.ShapeDtypeStruct(gate_up.shap...  4.24 us
    ppermute x10, waiting for transfers between devices, swap(): return lax.ppermute(x, 'afd', cores)  3.5 us
    pallas_call x1, Pallas kernels, experts(): pl.pallas_call(functools.partial(expert_kernel, turns), out_shape=[shape]...  2.84 us
    pallas_call x1, Pallas kernels, attend(): pl.pallas_call(attend_kernel, out_shape=(jax.ShapeDtypeStruct((steps * ro...  2.29 us
  transfers between devices with their start and end apart: 18, of which 10 were waited for; matrix products, arithmetic and copies ran while one was open for 0% of the time, Pallas kernels for 11%

profile of v21, /device:TPU:0, one launch (start us, length us, event | category | flops | bytes accessed | tf_op | source)
XLA Modules:
  0.0 41.1 jit_solution(14861168915839542019)
XLA Ops:
  0.0 2.3 %attend.1 = (f32[8,7168]{1,0:T(8,128)S(1)}, bf16[8,7296]{1,0:T(8,128)(2,1)S(1)}) custom-call(s32[4]{0:T(128)} %len_hbm.1, s32[3,2,4]{2,1,0:T(2,128)} %bitcast.6, f32[3,2,4]{2,1,0:T(2,128)} %bitcast.7, bf16[2,4,7168]{2,1,0:T(4,128)(2,1)} %q_hbm.1, bf16[2,4,448]{2,1,0:T(4,128)(2,1)} %fresh_hbm.1, bf16[4,448,128]{2,1,0:T(8,128)(2,1)} %bitcast.4, ...), custom_call_target="tpu_custom_call" | custom-call | flops 300000000 | bytes 2000000 | tf_op jit(solution)/shard_map/attend/pallas_call | solution.py:175
  2.3 0.5 %collective-permute-start = (bf16[8,7296]{1,0:T(8,128)(2,1)S(1)}, bf16[8,7296]{1,0:T(8,128)(2,1)S(1)}, u32[]{:S(2)}, u32[]{:S(2)}) collective-permute-start(bf16[8,7296]{1,0:T(8,128)(2,1)S(1)} %get-tuple-element.25.own_ref), channel_id=1, source_target_pairs={{0,1},{1,0},{2,3},{3,2},{4,5},{5,4},{6,7},{7,6},{8,9},{9,8},{10,11... | collective-permute-start | bytes 350216 | tf_op jit(solution)/shard_map/ppermute | solution.py:442
  2.8 1.0 %collective-permute-done.other_ref = bf16[8,7296]{1,0:T(8,128)(2,1)S(1)} collective-permute-done((bf16[8,7296]{1,0:T(8,128)(2,1)S(1)}, bf16[8,7296]{1,0:T(8,128)(2,1)S(1)}, u32[]{:S(2)}, u32[]{:S(2)}) %collective-permute-start) | collective-permute-done | bytes 116768 | tf_op jit(solution)/shard_map/ppermute | solution.py:442
  3.8 0.5 %pack.1 = (bf16[32,1792]{1,0:T(8,128)(2,1)S(1)}, bf16[32,1792]{1,0:T(8,128)(2,1)S(1)}, bf16[32,1792]{1,0:T(8,128)(2,1)S(1)}, bf16[32,1792]{1,0:T(8,128)(2,1)S(1)}) custom-call(bf16[8,7296]{1,0:T(8,128)(2,1)S(1)} %get-tuple-element.25.own_ref, bf16[8,7296]{1,0:T(8,128)(2,1)S(1)} %collective-permute-done.other_ref), custom_call_target="tpu_custom_call" | custom-call | flops 50000000 | bytes 2000000 | tf_op jit(solution)/shard_map/pack/pallas_call | solution.py:238
  4.3 0.4 %collective-permute-start.1 = (bf16[32,1792]{1,0:T(8,128)(2,1)S(1)}, bf16[32,1792]{1,0:T(8,128)(2,1)S(1)}, u32[]{:S(2)}, u32[]{:S(2)}) collective-permute-start(bf16[32,1792]{1,0:T(8,128)(2,1)S(1)} %get-tuple-element.27), channel_id=1, source_target_pairs={{0,1},{1,14},{2,3},{3,12},{4,5},{5,10},{6,7},{7,8},{8,9},{9,6},{10... | collective-permute-start | bytes 344072 | tf_op jit(solution)/shard_map/ppermute | solution.py:448
  4.7 4.7 %collective-permute-start.2 = (bf16[32,1792]{1,0:T(8,128)(2,1)S(1)}, bf16[32,1792]{1,0:T(8,128)(2,1)S(1)}, u32[]{:S(2)}, u32[]{:S(2)}) collective-permute-start(bf16[32,1792]{1,0:T(8,128)(2,1)S(1)} %get-tuple-element.30), channel_id=1, source_target_pairs={{0,9},{1,6},{2,11},{3,4},{4,13},{5,2},{6,15},{7,0},{8,1},{9,14},{1... | collective-permute-start | bytes 344072 | tf_op jit(solution)/shard_map/ppermute | solution.py:448
  9.5 3.2 %collective-permute-start.4 = (bf16[32,1792]{1,0:T(8,128)(2,1)S(1)}, bf16[32,1792]{1,0:T(8,128)(2,1)S(1)}, u32[]{:S(2)}, u32[]{:S(2)}) collective-permute-start(bf16[32,1792]{1,0:T(8,128)(2,1)S(1)} %get-tuple-element.32), channel_id=1, source_target_pairs={{0,13},{1,2},{2,15},{3,0},{4,9},{5,6},{6,11},{7,4},{8,5},{9,10},{1... | collective-permute-start | bytes 344072 | tf_op jit(solution)/shard_map/ppermute | solution.py:448
  12.7 4.2 %stage.1 = (bf16[2,256,7168]{2,1,0:T(8,128)(2,1)S(1)}, bf16[256,7168]{1,0:T(8,128)(2,1)S(1)}) custom-call(bf16[1,2,256,7168]{3,2,1,0:T(8,128)(2,1)} %gu_hbm.1, bf16[1,256,7168]{2,1,0:T(8,128)(2,1)} %dn_hbm.1), custom_call_target="tpu_custom_call" | custom-call | bytes 22000000 | tf_op jit(solution)/shard_map/stage/pallas_call | solution.py:294
  17.0 2.2 %collective-permute-start.6 = (bf16[32,1792]{1,0:T(8,128)(2,1)S(1)}, bf16[32,1792]{1,0:T(8,128)(2,1)S(1)}, u32[]{:S(2)}, u32[]{:S(2)}) collective-permute-start(bf16[32,1792]{1,0:T(8,128)(2,1)S(1)} %collective-permute-done.2.refs_1_), channel_id=1, source_target_pairs={{0,1},{1,0},{2,3},{3,2},{4,5},{5,4},{6,7},{7,6},{8,9},{9,8},{10,11... | collective-permute-start | bytes 344072 | tf_op jit(solution)/shard_map/ppermute | solution.py:442
  19.2 0.5 %collective-permute-start.8 = (bf16[32,1792]{1,0:T(8,128)(2,1)S(1)}, bf16[32,1792]{1,0:T(8,128)(2,1)S(1)}, u32[]{:S(2)}, u32[]{:S(2)}) collective-permute-start(bf16[32,1792]{1,0:T(8,128)(2,1)S(1)} %collective-permute-done.4.refs_3_), channel_id=1, source_target_pairs={{0,1},{1,0},{2,3},{3,2},{4,5},{5,4},{6,7},{7,6},{8,9},{9,8},{10,11... | collective-permute-start | bytes 344072 | tf_op jit(solution)/shard_map/ppermute | solution.py:442
  19.8 0.4 collective-permute-done.6.refs_5_
  20.2 0.4 collective-permute-done.7.refs_6_
  20.7 0.3 collective-permute-done.5.refs_4_
  21.1 2.8 %experts.1 = (bf16[32,1792]{1,0:T(8,128)(2,1)S(1)}, bf16[32,1792]{1,0:T(8,128)(2,1)S(1)}, bf16[32,1792]{1,0:T(8,128)(2,1)S(1)}, bf16[32,1792]{1,0:T(8,128)(2,1)S...) custom-call(bf16[32,1792]{1,0:T(8,128)(2,1)S(1)} %collective-permute, ...), custom_call_target="tpu_custom_call" | custom-call | flops 800000000 | bytes 12000000 | tf_op jit(solution)/shard_map/experts/pallas_call | solution.py:359
  24.1 0.3 collective-permute-start.11
  24.7 0.3 collective-permute-start.15
  25.3 2.6 %collective-permute-start.10 = (bf16[32,1792]{1,0:T(8,128)(2,1)S(1)}, bf16[32,1792]{1,0:T(8,128)(2,1)S(1)}, u32[]{:S(2)}, u32[]{:S(2)}) collective-permute-start(bf16[32,1792]{1,0:T(8,128)(2,1)S(1)} %add_convert_fusion.3), channel_id=1, source_target_pairs={{1,0},{14,1},{3,2},{12,3},{5,4},{10,5},{7,6},{8,7},{9,8},{6,9},{11... | collective-permute-start | bytes 344072 | tf_op jit(solution)/shard_map/ppermute | solution.py:451
  28.1 2.9 %collective-permute-start.14 = (bf16[32,1792]{1,0:T(8,128)(2,1)S(1)}, bf16[32,1792]{1,0:T(8,128)(2,1)S(1)}, u32[]{:S(2)}, u32[]{:S(2)}) collective-permute-start(bf16[32,1792]{1,0:T(8,128)(2,1)S(1)} %add_convert_fusion.1), channel_id=1, source_target_pairs={{5,0},{10,1},{7,2},{8,3},{1,4},{14,5},{3,6},{12,7},{13,8},{2,9},{1... | collective-permute-start | bytes 344072 | tf_op jit(solution)/shard_map/ppermute | solution.py:451
  31.5 5.4 %collective-permute-done.12.refs_1_ = bf16[32,1792]{1,0:T(8,128)(2,1)S(1)} collective-permute-done((bf16[32,1792]{1,0:T(8,128)(2,1)S(1)}, bf16[32,1792]{1,0:T(8,128)(2,1)S(1)}, u32[]{:S(2)}, u32[]{:S(2)}) %collective-permute-start.12) | collective-permute-done | bytes 114720 | tf_op jit(solution)/shard_map/ppermute | solution.py:451
  37.0 1.2 %collective-permute-done.16.refs_3_ = bf16[32,1792]{1,0:T(8,128)(2,1)S(1)} collective-permute-done((bf16[32,1792]{1,0:T(8,128)(2,1)S(1)}, bf16[32,1792]{1,0:T(8,128)(2,1)S(1)}, u32[]{:S(2)}, u32[]{:S(2)}) %collective-permute-start.16) | collective-permute-done | bytes 114720 | tf_op jit(solution)/shard_map/ppermute | solution.py:451
  38.2 0.3 combine.1
  38.5 0.9 %collective-permute-start.17 = (bf16[8,7168]{1,0:T(8,128)(2,1)S(1)}, bf16[8,7168]{1,0:T(8,128)(2,1)S(1)}, u32[]{:S(2)}, u32[]{:S(2)}) collective-permute-start(bf16[8,7168]{1,0:T(8,128)(2,1)S(1)} %get-tuple-element.44), channel_id=1, source_target_pairs={{0,1},{1,0},{2,3},{3,2},{4,5},{5,4},{6,7},{7,6},{8,9},{9,8},{10,11... | collective-permute-start | bytes 344072 | tf_op jit(solution)/shard_map/ppermute | solution.py:442
  39.4 1.0 %collective-permute-done.17.other_ref = bf16[8,7168]{1,0:T(8,128)(2,1)S(1)} collective-permute-done((bf16[8,7168]{1,0:T(8,128)(2,1)S(1)}, bf16[8,7168]{1,0:T(8,128)(2,1)S(1)}, u32[]{:S(2)}, u32[]{:S(2)}) %collective-permute-start.17) | collective-permute-done | bytes 114720 | tf_op jit(solution)/shard_map/ppermute | solution.py:442
  40.4 0.7 %finish.1 = bf16[2,4,7168]{2,1,0:T(4,128)(2,1)} custom-call(f32[8,7168]{1,0:T(8,128)S(1)} %get-tuple-element.43.kept_ref, bf16[8,7168]{1,0:T(8,128)(2,1)S(1)} %collective-permute-done.17.other_ref), custom_call_target="tpu_custom_call" | custom-call | flops 100000 | bytes 500000 | tf_op jit(solution)/shard_map/finish/pallas_call | solution.py:412
  (23 shorter events, 1.8 us)
Async XLA Ops:
  2.3 1.5 %collective-permute-start = (bf16[8,7296]{1,0:T(8,128)(2,1)S(1)}, bf16[8,7296]{1,0:T(8,128)(2,1)S(1)}, u32[]{:S(2)}, u32[]{:S(2)}) collective-permute-start(bf16[8,7296]{1,0:T(8,128)(2,1)S(1)} %get-tuple-element.25.own_ref), channel_id=1, source_target_pairs={{0,1},{1,0},{2,3},{3,2},{4,5},{5,4},{6,7},{7,6},{8,9},{9,8},{10,11... | collective-permute-start | bytes 350216 | tf_op jit(solution)/shard_map/ppermute | solution.py:442
  4.3 12.7 %collective-permute-start.1 = (bf16[32,1792]{1,0:T(8,128)(2,1)S(1)}, bf16[32,1792]{1,0:T(8,128)(2,1)S(1)}, u32[]{:S(2)}, u32[]{:S(2)}) collective-permute-start(bf16[32,1792]{1,0:T(8,128)(2,1)S(1)} %get-tuple-element.27), channel_id=1, source_target_pairs={{0,1},{1,14},{2,3},{3,12},{4,5},{5,10},{6,7},{7,8},{8,9},{9,6},{10... | collective-permute-start | bytes 344072 | tf_op jit(solution)/shard_map/ppermute | solution.py:448
  4.7 12.3 %collective-permute-start.2 = (bf16[32,1792]{1,0:T(8,128)(2,1)S(1)}, bf16[32,1792]{1,0:T(8,128)(2,1)S(1)}, u32[]{:S(2)}, u32[]{:S(2)}) collective-permute-start(bf16[32,1792]{1,0:T(8,128)(2,1)S(1)} %get-tuple-element.30), channel_id=1, source_target_pairs={{0,9},{1,6},{2,11},{3,4},{4,13},{5,2},{6,15},{7,0},{8,1},{9,14},{1... | collective-permute-start | bytes 344072 | tf_op jit(solution)/shard_map/ppermute | solution.py:448
  9.4 9.8 %collective-permute-start.3 = (bf16[32,1792]{1,0:T(8,128)(2,1)S(1)}, bf16[32,1792]{1,0:T(8,128)(2,1)S(1)}, u32[]{:S(2)}, u32[]{:S(2)}) collective-permute-start(bf16[32,1792]{1,0:T(8,128)(2,1)S(1)} %get-tuple-element.31), channel_id=1, source_target_pairs={{0,5},{1,10},{2,7},{3,8},{4,1},{5,14},{6,3},{7,12},{8,13},{9,2},{1... | collective-permute-start | bytes 344072 | tf_op jit(solution)/shard_map/ppermute | solution.py:448
  9.5 9.7 %collective-permute-start.4 = (bf16[32,1792]{1,0:T(8,128)(2,1)S(1)}, bf16[32,1792]{1,0:T(8,128)(2,1)S(1)}, u32[]{:S(2)}, u32[]{:S(2)}) collective-permute-start(bf16[32,1792]{1,0:T(8,128)(2,1)S(1)} %get-tuple-element.32), channel_id=1, source_target_pairs={{0,13},{1,2},{2,15},{3,0},{4,9},{5,6},{6,11},{7,4},{8,5},{9,10},{1... | collective-permute-start | bytes 344072 | tf_op jit(solution)/shard_map/ppermute | solution.py:448
  17.0 3.2 %collective-permute-start.6 = (bf16[32,1792]{1,0:T(8,128)(2,1)S(1)}, bf16[32,1792]{1,0:T(8,128)(2,1)S(1)}, u32[]{:S(2)}, u32[]{:S(2)}) collective-permute-start(bf16[32,1792]{1,0:T(8,128)(2,1)S(1)} %collective-permute-done.2.refs_1_), channel_id=1, source_target_pairs={{0,1},{1,0},{2,3},{3,2},{4,5},{5,4},{6,7},{7,6},{8,9},{9,8},{10,11... | collective-permute-start | bytes 344072 | tf_op jit(solution)/shard_map/ppermute | solution.py:442
  19.2 1.3 %collective-permute-start.7 = (bf16[32,1792]{1,0:T(8,128)(2,1)S(1)}, bf16[32,1792]{1,0:T(8,128)(2,1)S(1)}, u32[]{:S(2)}, u32[]{:S(2)}) collective-permute-start(bf16[32,1792]{1,0:T(8,128)(2,1)S(1)} %collective-permute-done.3.refs_2_), channel_id=1, source_target_pairs={{0,1},{1,0},{2,3},{3,2},{4,5},{5,4},{6,7},{7,6},{8,9},{9,8},{10,11... | collective-permute-start | bytes 344072 | tf_op jit(solution)/shard_map/ppermute | solution.py:442
  19.2 1.5 %collective-permute-start.8 = (bf16[32,1792]{1,0:T(8,128)(2,1)S(1)}, bf16[32,1792]{1,0:T(8,128)(2,1)S(1)}, u32[]{:S(2)}, u32[]{:S(2)}) collective-permute-start(bf16[32,1792]{1,0:T(8,128)(2,1)S(1)} %collective-permute-done.4.refs_3_), channel_id=1, source_target_pairs={{0,1},{1,0},{2,3},{3,2},{4,5},{5,4},{6,7},{7,6},{8,9},{9,8},{10,11... | collective-permute-start | bytes 344072 | tf_op jit(solution)/shard_map/ppermute | solution.py:442
  19.7 1.3 %collective-permute-start.5 = (bf16[32,1792]{1,0:T(8,128)(2,1)S(1)}, bf16[32,1792]{1,0:T(8,128)(2,1)S(1)}, u32[]{:S(2)}, u32[]{:S(2)}) collective-permute-start(bf16[32,1792]{1,0:T(8,128)(2,1)S(1)} %collective-permute-done.1.refs_0_), channel_id=1, source_target_pairs={{0,1},{1,0},{2,3},{3,2},{4,5},{5,4},{6,7},{7,6},{8,9},{9,8},{10,11... | collective-permute-start | bytes 344072 | tf_op jit(solution)/shard_map/ppermute | solution.py:442
  23.9 1.4 %collective-permute-start.9 = (bf16[32,1792]{1,0:T(8,128)(2,1)S(1)}, bf16[32,1792]{1,0:T(8,128)(2,1)S(1)}, u32[]{:S(2)}, u32[]{:S(2)}) collective-permute-start(bf16[32,1792]{1,0:T(8,128)(2,1)S(1)} %get-tuple-element.36), channel_id=1, source_target_pairs={{0,1},{1,0},{2,3},{3,2},{4,5},{5,4},{6,7},{7,6},{8,9},{9,8},{10,11... | collective-permute-start | bytes 344072 | tf_op jit(solution)/shard_map/ppermute | solution.py:442
  24.1 3.8 %collective-permute-start.11 = (bf16[32,1792]{1,0:T(8,128)(2,1)S(1)}, bf16[32,1792]{1,0:T(8,128)(2,1)S(1)}, u32[]{:S(2)}, u32[]{:S(2)}) collective-permute-start(bf16[32,1792]{1,0:T(8,128)(2,1)S(1)} %get-tuple-element.38), channel_id=1, source_target_pairs={{0,1},{1,0},{2,3},{3,2},{4,5},{5,4},{6,7},{7,6},{8,9},{9,8},{10,11... | collective-permute-start | bytes 344072 | tf_op jit(solution)/shard_map/ppermute | solution.py:442
  24.5 3.6 %collective-permute-start.13 = (bf16[32,1792]{1,0:T(8,128)(2,1)S(1)}, bf16[32,1792]{1,0:T(8,128)(2,1)S(1)}, u32[]{:S(2)}, u32[]{:S(2)}) collective-permute-start(bf16[32,1792]{1,0:T(8,128)(2,1)S(1)} %get-tuple-element.40), channel_id=1, source_target_pairs={{0,1},{1,0},{2,3},{3,2},{4,5},{5,4},{6,7},{7,6},{8,9},{9,8},{10,11... | collective-permute-start | bytes 344072 | tf_op jit(solution)/shard_map/ppermute | solution.py:442
  24.7 6.3 %collective-permute-start.15 = (bf16[32,1792]{1,0:T(8,128)(2,1)S(1)}, bf16[32,1792]{1,0:T(8,128)(2,1)S(1)}, u32[]{:S(2)}, u32[]{:S(2)}) collective-permute-start(bf16[32,1792]{1,0:T(8,128)(2,1)S(1)} %get-tuple-element.42), channel_id=1, source_target_pairs={{0,1},{1,0},{2,3},{3,2},{4,5},{5,4},{6,7},{7,6},{8,9},{9,8},{10,11... | collective-permute-start | bytes 344072 | tf_op jit(solution)/shard_map/ppermute | solution.py:442
  25.3 6.2 %collective-permute-start.10 = (bf16[32,1792]{1,0:T(8,128)(2,1)S(1)}, bf16[32,1792]{1,0:T(8,128)(2,1)S(1)}, u32[]{:S(2)}, u32[]{:S(2)}) collective-permute-start(bf16[32,1792]{1,0:T(8,128)(2,1)S(1)} %add_convert_fusion.3), channel_id=1, source_target_pairs={{1,0},{14,1},{3,2},{12,3},{5,4},{10,5},{7,6},{8,7},{9,8},{6,9},{11... | collective-permute-start | bytes 344072 | tf_op jit(solution)/shard_map/ppermute | solution.py:451
  28.0 9.0 %collective-permute-start.12 = (bf16[32,1792]{1,0:T(8,128)(2,1)S(1)}, bf16[32,1792]{1,0:T(8,128)(2,1)S(1)}, u32[]{:S(2)}, u32[]{:S(2)}) collective-permute-start(bf16[32,1792]{1,0:T(8,128)(2,1)S(1)} %add_convert_fusion.2), channel_id=1, source_target_pairs={{9,0},{6,1},{11,2},{4,3},{13,4},{2,5},{15,6},{0,7},{1,8},{14,9},{3... | collective-permute-start | bytes 344072 | tf_op jit(solution)/shard_map/ppermute | solution.py:451
  28.1 8.9 %collective-permute-start.14 = (bf16[32,1792]{1,0:T(8,128)(2,1)S(1)}, bf16[32,1792]{1,0:T(8,128)(2,1)S(1)}, u32[]{:S(2)}, u32[]{:S(2)}) collective-permute-start(bf16[32,1792]{1,0:T(8,128)(2,1)S(1)} %add_convert_fusion.1), channel_id=1, source_target_pairs={{5,0},{10,1},{7,2},{8,3},{1,4},{14,5},{3,6},{12,7},{13,8},{2,9},{1... | collective-permute-start | bytes 344072 | tf_op jit(solution)/shard_map/ppermute | solution.py:451
  31.0 7.2 %collective-permute-start.16 = (bf16[32,1792]{1,0:T(8,128)(2,1)S(1)}, bf16[32,1792]{1,0:T(8,128)(2,1)S(1)}, u32[]{:S(2)}, u32[]{:S(2)}) collective-permute-start(bf16[32,1792]{1,0:T(8,128)(2,1)S(1)} %add_convert_fusion), channel_id=1, source_target_pairs={{13,0},{2,1},{15,2},{0,3},{9,4},{6,5},{11,6},{4,7},{5,8},{10,9},{7... | collective-permute-start | bytes 344072 | tf_op jit(solution)/shard_map/ppermute | solution.py:451
  38.5 1.9 %collective-permute-start.17 = (bf16[8,7168]{1,0:T(8,128)(2,1)S(1)}, bf16[8,7168]{1,0:T(8,128)(2,1)S(1)}, u32[]{:S(2)}, u32[]{:S(2)}) collective-permute-start(bf16[8,7168]{1,0:T(8,128)(2,1)S(1)} %get-tuple-element.44), channel_id=1, source_target_pairs={{0,1},{1,0},{2,3},{3,2},{4,5},{5,4},{6,7},{7,6},{8,9},{9,8},{10,11... | collective-permute-start | bytes 344072 | tf_op jit(solution)/shard_map/ppermute | solution.py:442
